TPU v7x, 256 devices: a whole 4x4x8 slice. The times are simulated.
256 devices in a mesh: gx: 16 (over y, z_hi), gy: 16 (over x, z_lo, core).
Axes of the slice: x: 4, y: 4, z: 8 (z_hi: 4, z_lo: 2; z = z_hi * 2 + z_lo), core: 2. Of those that a mesh axis runs over, the one named last changes fastest.
Arguments:
- charges: float32 [512, 512, 256], P('gx', 'gy'), may hold values from -6 to 6
- kernel_taps: float32 [3, 3, 21], replicated, may hold values from -1.08 to 1.08
Outputs:
- potential: float32 [512, 512, 256], P('gx', 'gy')
All inputs are finite; a program needn't handle non-finite values.
Results may differ from a plain program's by a relative error of at most 0.035.
Values sent between devices are 32-bit elements; how exact they have to be, the bound alone decides.
No kernel may reach another device: no remote copies, remote signals or barrier semaphores. Data moves between devices by JAX's collectives and lax.ppermute only.
A program may use at most 128 MiB of HBM per device.

v0:
```python
import jax
import jax.numpy as jnp
from jax import lax
from jax.sharding import PartitionSpec as P

SPLINE = (0.125, 0.5, 0.75, 0.5, 0.125)


def padded_2(x, sides, width):
    for axis, dim in sides:
        peers, length = (lax.axis_size(axis), x.shape[dim])
        up = [(i, (i + 1) % peers) for i in range(peers)]
        down = [(j, i) for i, j in up]
        last = lax.slice_in_dim(x, length - width, length, axis=dim)
        first = lax.slice_in_dim(x, 0, width, axis=dim)
        before = lax.ppermute(last, axis, up)
        after = lax.ppermute(first, axis, down)
        x = jnp.concatenate([before, x, after], axis=dim)
    return x


def from_everyone(x, axis):
    peers = lax.axis_size(axis)
    return lax.all_to_all(jnp.broadcast_to(x[None], (peers, *x.shape)), axis, 0, 0, tiled=True)


def in_order(pieces, dim):
    shape = list(pieces.shape[1:])
    shape[dim] *= pieces.shape[0]
    return jnp.moveaxis(pieces, 0, dim).reshape(shape)


def gathered_copies(x, axis, dim):
    pieces = from_everyone(x, axis)
    return in_order(pieces, dim)


def contract(formula, left, right):
    return jnp.einsum(formula, left, right, precision=lax.Precision.HIGHEST)


def grid_ids(count_rows, count_cols):
    row_ids = lax.broadcasted_iota(jnp.int32, (count_rows, count_cols), 0)
    col_ids = lax.broadcasted_iota(jnp.int32, (count_rows, count_cols), 1)
    return (row_ids, col_ids)


def spline_table(offsets):
    table = jnp.zeros(offsets.shape, jnp.float32)
    for position in range(5):
        table = table + SPLINE[position] * (offsets == position).astype(jnp.float32)
    return table


def band_taps(taps, count_rows, count_cols):
    row_ids, col_ids = grid_ids(count_rows, count_cols)
    offsets = col_ids - row_ids
    tap_count = taps.shape[1]
    inside = (offsets >= 0) & (offsets < tap_count)
    picked = jnp.take(taps, jnp.clip(offsets, 0, tap_count - 1), axis=1)
    return jnp.where(inside[None], picked, 0.0)


def cycle_taps(taps, length):
    tap_count = taps.shape[1]
    radius = tap_count // 2
    wrapped = (jnp.arange(tap_count, dtype=jnp.int32) - radius) % length
    onehot = (wrapped[:, None] == jnp.arange(length, dtype=jnp.int32)[None, :]).astype(jnp.float32)
    profile = jnp.dot(
        taps, onehot, preferred_element_type=jnp.float32, precision=lax.Precision.HIGHEST
    )
    row_ids, col_ids = grid_ids(length, length)
    return jnp.take(profile, (col_ids - row_ids) % length, axis=1)


def restrict_band(count_rows, count_cols, margin):
    row_ids, col_ids = grid_ids(count_rows, count_cols)
    return spline_table(col_ids - margin - 2 * row_ids + 2)


def restrict_cycle(length):
    row_ids, col_ids = grid_ids(length // 2, length)
    return spline_table((col_ids - 2 * row_ids + 2) % length)


def prolong_band(count_rows, count_cols):
    row_ids, col_ids = grid_ids(count_rows, count_cols)
    return spline_table(row_ids - 2 * col_ids + 4)


def prolong_cycle(count_rows, coarse_len, offset):
    row_ids, col_ids = grid_ids(count_rows, coarse_len)
    return spline_table((offset + row_ids - 2 * col_ids + 2) % (2 * coarse_len))


def body(charges, kernel_taps):
    radius = kernel_taps.shape[2] // 2
    margin = radius + 1
    term_count = kernel_taps.shape[1]
    rows_x, rows_y, cells_z = charges.shape
    half_x, half_y, half_z = (rows_x // 2, rows_y // 2, cells_z // 2)
    quarter_x, quarter_z = (rows_x // 4, cells_z // 4)
    count_x = lax.axis_size("gx")
    count_y = lax.axis_size("gy")
    wide_y = rows_y * count_y
    quarter_y = wide_y // 4
    taps_fine, taps_middle, taps_top = (kernel_taps[0], kernel_taps[1], kernel_taps[2])
    padded = padded_2(charges, (("gx", 0), ("gy", 1)), radius)
    across_x = band_taps(taps_fine, rows_x, rows_x + 2 * radius)
    across_y = band_taps(taps_fine, rows_y, rows_y + 2 * radius)
    across_z = cycle_taps(taps_fine, cells_z)
    direct_fine = jnp.zeros(charges.shape, jnp.float32)
    for member in range(term_count):
        sectioned = contract("mc,cyz->myz", across_x[member], padded)
        sectioned = contract("nc,mcz->mnz", across_y[member], sectioned)
        direct_fine = direct_fine + contract("mnz,wz->mnw", sectioned, across_z[member])
    coarse = contract("mc,cyz->myz", restrict_band(half_x, rows_x + 2 * radius, radius), padded)
    coarse = contract("nc,mcz->mnz", restrict_band(half_y, rows_y + 2 * radius, radius), coarse)
    coarse = contract("mnz,wz->mnw", coarse, restrict_cycle(cells_z))
    middle_x = band_taps(taps_middle, half_x + 2, half_x + 2 * margin)
    middle_z = cycle_taps(taps_middle, half_z)
    down_x = restrict_band(quarter_x, half_x + 2 * margin, margin)
    down_z = restrict_cycle(half_z)
    up_z = prolong_cycle(half_z, quarter_z, 0)
    rimmed = padded_2(coarse, (("gx", 0), ("gy", 1)), margin)
    middle_y = band_taps(taps_middle, half_y + 2, half_y + 2 * margin)
    direct_middle = jnp.zeros((half_x + 2, half_y + 2, half_z), jnp.float32)
    for member in range(term_count):
        sectioned = contract("mc,cyz->myz", middle_x[member], rimmed)
        sectioned = contract("nc,mcz->mnz", middle_y[member], sectioned)
        direct_middle = direct_middle + contract("mnz,wz->mnw", sectioned, middle_z[member])
    summit = contract("mc,cyz->myz", down_x, rimmed)
    summit = contract(
        "nc,mcz->mnz", restrict_band(half_y // 2, half_y + 2 * margin, margin), summit
    )
    summit = contract("mnz,wz->mnw", summit, down_z)
    lift_y = prolong_cycle(half_y + 2, quarter_y, lax.axis_index("gy") * half_y - 1)
    spread_y = prolong_band(rows_y, half_y + 2)
    top_y = cycle_taps(taps_top, quarter_y)
    top_z = cycle_taps(taps_top, quarter_z)
    full_x = quarter_x * count_x
    top_x = cycle_taps(taps_top, full_x)
    along_z = jnp.stack(
        [contract("mnz,wz->mnw", summit, top_z[member]) for member in range(term_count)]
    )
    portion = lax.all_to_all(along_z, "gy", split_axis=3, concat_axis=2, tiled=True)
    turned_yz = jnp.stack(
        [contract("nc,mcw->mnw", top_y[member], portion[member]) for member in range(term_count)]
    )
    up_x = prolong_cycle(2 * full_x, full_x, 0)
    portion = lax.all_to_all(turned_yz, "gx", split_axis=2, concat_axis=1, tiled=True)
    result = jnp.zeros(portion.shape[1:], jnp.float32)
    for member in range(term_count):
        result = result + contract("mc,cnw->mnw", top_x[member], portion[member])
    refined = contract("jm,mnw->jnw", up_x, result)
    rest_shape = refined.shape[1:]
    blocks = refined.reshape((count_x, half_x) + rest_shape)
    leading = jnp.roll(refined, 1, 0).reshape((count_x, half_x) + rest_shape)[:, :1]
    trailing = jnp.roll(refined, -1, 0).reshape((count_x, half_x) + rest_shape)[:, -1:]
    windows = jnp.concatenate([leading, blocks, trailing], axis=1)
    back_rows = lax.all_to_all(windows, "gx", split_axis=0, concat_axis=2, tiled=True)[0]
    returned = gathered_copies(back_rows, "gy", 2)
    lifted = contract("jn,mnw->mjw", lift_y, returned)
    lifted = contract("mjz,wz->mjw", lifted, up_z)
    middle = direct_middle + lifted
    refined = contract("jm,myz->jyz", prolong_band(rows_x, half_x + 2), middle)
    refined = contract("jn,mnz->mjz", spread_y, refined)
    refined = contract("mjz,wz->mjw", refined, prolong_cycle(cells_z, half_z, 0))
    return direct_fine + refined


def solution(mesh):
    return jax.shard_map(
        body,
        mesh=mesh,
        in_specs=(P("gx", "gy", None), P()),
        out_specs=P("gx", "gy", None),
        check_vma=False,
    )
```

profile of v0, /device:TPU:1, one launch (start us, length us, event | category | flops | bytes accessed | tf_op | source)
XLA Modules:
  0.0 526.8 jit_solution(14871646554281594508)
XLA Ops:
  2.9 3.8 collective-permute-start
  6.7 5.5 %collective-permute-start.1 = (f32[10,32,256]{2,0,1:T(8,128)}, f32[10,32,256]{2,0,1:T(8,128)}, u32[]{:S(2)}, u32[]{:S(2)}) collective-permute-start(f32[10,32,256]{2,0,1:T(8,128)} %get-tuple-element.11), channel_id=1, source_target_pairs={{16,0},{32,16},{48,32},{64,48},{80,64},{96,80},{112,96},{128,112},... | collective-permute-start | bytes 983048 | tf_op jit(solution)/shard_map/ppermute | solution.py:17
  24.4 3.2 gather_fusion.2
  28.6 10.8 %gather_fusion.1 = f32[4096,3]{1,0:T(8,128)S(1)} fusion(f32[3,64]{0,1:T(8,128)S(1)} %copy.63, s32[4096]{0:T(1024)S(1)} %broadcast_clamp_fusion.1), kind=kCustom, calls=%fused_computation.5 | custom fusion | bytes 114688 | tf_op jit(solution)/shard_map/jit(_take)/gather | solution.py:73
  47.5 54.8 %gather_fusion.5 = f32[16384,3]{1,0:T(8,128)} fusion(f32[3,128]{0,1:T(8,128)S(1)} %copy.59, s32[16384]{0:T(1024)S(1)} %bitcast_clamp_fusion), kind=kCustom, calls=%fused_computation.3.clone | custom fusion | bytes 458752 | tf_op jit(solution)/shard_map/jit(_take)/gather | solution.py:73
  102.3 5.2 copy.84
  107.5 54.8 %gather_fusion.4 = f32[16384,3]{1,0:T(8,128)} fusion(f32[3,128]{0,1:T(8,128)S(1)} %copy.53, s32[16384]{0:T(1024)S(1)} %bitcast_clamp_fusion), kind=kCustom, calls=%fused_computation.2.clone | custom fusion | bytes 458752 | tf_op jit(solution)/shard_map/jit(_take)/gather | solution.py:73
  162.3 5.2 copy.54
  167.6 217.0 %gather_fusion = f32[65536,3]{1,0:T(8,128)} fusion(f32[3,256]{0,1:T(8,128)S(1)} %copy.44, s32[65536]{0:T(1024)S(1)} %broadcast_clamp_fusion), kind=kCustom, calls=%fused_computation.4 | custom fusion | bytes 1835008 | tf_op jit(solution)/shard_map/jit(_take)/gather | solution.py:73
  384.6 18.9 %copy.83 = f32[256,256,3]{1,0,2:T(8,128)S(1)} copy(f32[256,256,3]{2,1,0:T(8,128)} %bitcast.274) | data formatting | bytes 1572864 | tf_op jit(solution)/shard_map/jit(_take)/gather | solution.py:73
  404.3 3.3 fusion.191
  409.6 5.7 %collective-permute-start.5 = (f32[11,16,128]{2,1,0:T(8,128)S(1)}, f32[11,16,128]{2,1,0:T(8,128)S(1)}, u32[]{:S(2)}, u32[]{:S(2)}) collective-permute-start(f32[11,16,128]{2,1,0:T(8,128)S(1)} %get-tuple-element.21), channel_id=1, source_target_pairs={{16,0},{32,16},{48,32},{64,48},{80,64},{96,80},{112,96},{128,112},... | collective-permute-start | bytes 270344 | tf_op jit(solution)/shard_map/ppermute | solution.py:17
  415.3 3.3 fusion.158
  420.9 3.3 fusion.157
  428.7 3.6 fusion.159
  440.9 5.7 %collective-permute-done.7 = f32[38,11,128]{2,1,0:T(8,128)S(1)} collective-permute-done((f32[38,11,128]{2,1,0:T(8,128)S(1)}, f32[38,11,128]{2,1,0:T(8,128)S(1)}, u32[]{:S(2)}, u32[]{:S(2)}) %collective-permute-start.7) | collective-permute-done | bytes 214048 | tf_op jit(solution)/shard_map/ppermute | solution.py:17
  450.4 6.3 %all-to-all-start = ((f32[16,1,768]{2,1,0:T(1,128)}), f32[16,1,768]{2,1,0:T(1,128)S(1)}, u32[]{:S(2)}, u32[]{:S(2)}) async-start(f32[16,1,768]{2,1,0:T(1,128)} %reshape.323), calls=%async_computation | async-start | bytes 98304 | tf_op jit(solution)/shard_map/all_to_all | solution.py:146
  458.1 4.5 all-to-all-done
  467.9 4.4 all-to-all-start.1
  473.5 7.8 %all-to-all-done.1 = f32[16,1,768]{2,1,0:T(1,128)S(1)} async-done(((f32[16,1,768]{2,1,0:T(1,128)}), f32[16,1,768]{2,1,0:T(1,128)S(1)}, u32[]{:S(2)}, u32[]{:S(2)}) %all-to-all-start.1) | async-done | bytes 49184 | tf_op jit(solution)/shard_map/all_to_all | solution.py:151
  489.4 3.5 all-to-all-start.2
  494.1 7.7 %all-to-all-done.2 = f32[16,1,576]{2,1,0:T(1,128)S(1)} async-done(((f32[16,1,576]{2,1,0:T(1,128)}), f32[16,1,576]{2,1,0:T(1,128)S(1)}, u32[]{:S(2)}, u32[]{:S(2)}) %all-to-all-start.2) | async-done | bytes 36896 | tf_op jit(solution)/shard_map/all_to_all | solution.py:161
  503.9 6.3 %all-to-all-start.3 = ((f32[16,18,128,4]{2,3,1,0:T(4,128)}), f32[16,18,128,4]{2,3,1,0:T(4,128)S(1)}, u32[]{:S(2)}, u32[]{:S(2)}) async-start(f32[16,18,128,4]{2,3,1,0:T(4,128)} %broadcast_in_dim.109), calls=%async_computation.3 | async-start | bytes 1179648 | tf_op jit(solution)/shard_map/all_to_all | solution.py:24
  513.7 7.1 %all-to-all-done.3 = f32[16,18,128,4]{2,3,1,0:T(4,128)S(1)} async-done(((f32[16,18,128,4]{2,3,1,0:T(4,128)}), f32[16,18,128,4]{2,3,1,0:T(4,128)S(1)}, u32[]{:S(2)}, u32[]{:S(2)}) %all-to-all-start.3) | async-done | bytes 589856 | tf_op jit(solution)/shard_map/all_to_all | solution.py:24
  (186 shorter events, 73.7 us)
Async XLA Ops:
  0.0 15.6 %copy-start.9 = (f32[3,3,21]{2,1,0:T(4,128)S(1)}, f32[3,3,21]{2,1,0:T(4,128)}, u32[]{:S(2)}) copy-start(f32[3,3,21]{2,1,0:T(4,128)} %param.9) | copy-start | bytes 2272
  2.9 40.4 %collective-permute-start = (f32[10,32,256]{2,0,1:T(8,128)}, f32[10,32,256]{2,0,1:T(8,128)}, u32[]{:S(2)}, u32[]{:S(2)}) collective-permute-start(f32[10,32,256]{2,0,1:T(8,128)} %get-tuple-element.10), channel_id=1, source_target_pairs={{0,16},{16,32},{32,48},{48,64},{64,80},{80,96},{96,112},{112,128},... | collective-permute-start | bytes 983048 | tf_op jit(solution)/shard_map/ppermute | solution.py:16
  6.7 36.6 %collective-permute-start.1 = (f32[10,32,256]{2,0,1:T(8,128)}, f32[10,32,256]{2,0,1:T(8,128)}, u32[]{:S(2)}, u32[]{:S(2)}) collective-permute-start(f32[10,32,256]{2,0,1:T(8,128)} %get-tuple-element.11), channel_id=1, source_target_pairs={{16,0},{32,16},{48,32},{64,48},{80,64},{96,80},{112,96},{128,112},... | collective-permute-start | bytes 983048 | tf_op jit(solution)/shard_map/ppermute | solution.py:17
  41.5 430.8 %copy-start.5 = (f32[3,18,38]{2,1,0:T(8,128)}, f32[3,18,38]{2,1,0:T(8,128)S(1)}, u32[]{:S(2)}) copy-start(f32[3,18,38]{2,1,0:T(8,128)S(1)} %bitcast_select_fusion.1) | copy-start | bytes 24628
  45.6 358.7 %collective-permute-start.2 = (f32[52,10,256]{2,0,1:T(8,128)}, f32[52,10,256]{2,0,1:T(8,128)}, u32[]{:S(2)}, u32[]{:S(2)}) collective-permute-start(f32[52,10,256]{2,0,1:T(8,128)} %get-tuple-element.6), channel_id=1, source_target_pairs={{0,1},{1,2},{2,3},{3,4},{4,5},{5,6},{6,7},{7,8},{8,9},{9,10},{10,1... | collective-permute-start | bytes 1597448 | tf_op jit(solution)/shard_map/ppermute | solution.py:16
  47.2 357.1 %collective-permute-start.3 = (f32[52,10,256]{2,0,1:T(8,128)}, f32[52,10,256]{2,0,1:T(8,128)}, u32[]{:S(2)}, u32[]{:S(2)}) collective-permute-start(f32[52,10,256]{2,0,1:T(8,128)} %get-tuple-element.8), channel_id=1, source_target_pairs={{1,0},{2,1},{3,2},{4,3},{5,4},{6,5},{7,6},{8,7},{9,8},{10,9},{11,1... | collective-permute-start | bytes 1597448 | tf_op jit(solution)/shard_map/ppermute | solution.py:17
  384.6 18.9 %copy-start.7 = (pred[128,128]{1,0:T(8,128)(4,1)S(1)}, pred[128,128]{1,0:T(8,128)(4,1)}, u32[]{:S(2)}) copy-start(pred[128,128]{1,0:T(8,128)(4,1)} %compare_and_fusion.1) | copy-start | bytes 49156
  384.6 19.6 %copy-start.6 = (pred[256,256]{1,0:T(8,128)(4,1)S(1)}, pred[256,256]{1,0:T(8,128)(4,1)}, u32[]{:S(2)}) copy-start(pred[256,256]{1,0:T(8,128)(4,1)} %compare_and_fusion) | copy-start | bytes 196612
  384.6 19.7 %copy-start.16 = (s32[52]{0:T(128)S(1)}, s32[52]{0:T(128)}, u32[]{:S(2)}) copy-start(s32[52]{0:T(128)} %iota_add_fusion.2) | copy-start | bytes 628
  384.6 19.7 %copy-start.17 = (s32[16]{0:T(128)S(1)}, s32[16]{0:T(128)}, u32[]{:S(2)}) copy-start(s32[16]{0:T(128)} %iota_multiply_fusion.3) | copy-start | bytes 196
  404.2 61.7 %copy-start = (f32[3,128,128]{2,1,0:T(8,128)}, f32[3,128,128]{2,1,0:T(8,128)S(1)}, u32[]{:S(2)}) copy-start(f32[3,128,128]{2,1,0:T(8,128)S(1)} %get-tuple-element.26) | copy-start | bytes 589828
  409.3 25.2 %collective-permute-start.4 = (f32[11,16,128]{2,1,0:T(8,128)S(1)}, f32[11,16,128]{2,1,0:T(8,128)S(1)}, u32[]{:S(2)}, u32[]{:S(2)}) collective-permute-start(f32[11,16,128]{2,1,0:T(8,128)S(1)} %get-tuple-element.20), channel_id=1, source_target_pairs={{0,16},{16,32},{32,48},{48,64},{64,80},{80,96},{96,112},{112,128},... | collective-permute-start | bytes 270344 | tf_op jit(solution)/shard_map/ppermute | solution.py:16
  409.6 25.0 %collective-permute-start.5 = (f32[11,16,128]{2,1,0:T(8,128)S(1)}, f32[11,16,128]{2,1,0:T(8,128)S(1)}, u32[]{:S(2)}, u32[]{:S(2)}) collective-permute-start(f32[11,16,128]{2,1,0:T(8,128)S(1)} %get-tuple-element.21), channel_id=1, source_target_pairs={{16,0},{32,16},{48,32},{64,48},{80,64},{96,80},{112,96},{128,112},... | collective-permute-start | bytes 270344 | tf_op jit(solution)/shard_map/ppermute | solution.py:17
  434.6 12.1 %copy-start.11 = (s32[38]{0:T(128)S(1)}, s32[38]{0:T(128)}, u32[]{:S(2)}) copy-start(s32[38]{0:T(128)} %iota_add_fusion.1) | copy-start | bytes 460
  434.6 12.1 %copy-start.12 = (s32[8]{0:T(128)S(1)}, s32[8]{0:T(128)}, u32[]{:S(2)}) copy-start(s32[8]{0:T(128)} %iota_multiply_fusion.1) | copy-start | bytes 100
  434.7 6.2 %collective-permute-start.6 = (f32[38,11,128]{2,1,0:T(8,128)S(1)}, f32[38,11,128]{2,1,0:T(8,128)S(1)}, u32[]{:S(2)}, u32[]{:S(2)}) collective-permute-start(f32[38,11,128]{2,1,0:T(8,128)S(1)} %get-tuple-element.18), channel_id=1, source_target_pairs={{0,1},{1,2},{2,3},{3,4},{4,5},{5,6},{6,7},{7,8},{8,9},{9,10},{10,1... | collective-permute-start | bytes 642056 | tf_op jit(solution)/shard_map/ppermute | solution.py:16
  437.1 9.5 %collective-permute-start.7 = (f32[38,11,128]{2,1,0:T(8,128)S(1)}, f32[38,11,128]{2,1,0:T(8,128)S(1)}, u32[]{:S(2)}, u32[]{:S(2)}) collective-permute-start(f32[38,11,128]{2,1,0:T(8,128)S(1)} %get-tuple-element.19), channel_id=1, source_target_pairs={{1,0},{2,1},{3,2},{4,3},{5,4},{6,5},{7,6},{8,7},{9,8},{10,9},{11,1... | collective-permute-start | bytes 642056 | tf_op jit(solution)/shard_map/ppermute | solution.py:17
  450.4 12.2 %all-to-all-start = ((f32[16,1,768]{2,1,0:T(1,128)}), f32[16,1,768]{2,1,0:T(1,128)S(1)}, u32[]{:S(2)}, u32[]{:S(2)}) async-start(f32[16,1,768]{2,1,0:T(1,128)} %reshape.323), calls=%async_computation | async-start | bytes 98304 | tf_op jit(solution)/shard_map/all_to_all | solution.py:146
  467.9 13.3 %all-to-all-start.1 = ((f32[16,1,768]{2,1,0:T(1,128)}), f32[16,1,768]{2,1,0:T(1,128)S(1)}, u32[]{:S(2)}, u32[]{:S(2)}) async-start(f32[16,1,768]{2,1,0:T(1,128)} %reshape.325), calls=%async_computation.1 | async-start | bytes 98304 | tf_op jit(solution)/shard_map/all_to_all | solution.py:151
  488.1 22.1 %copy-start.4 = (f32[3,128,128]{2,1,0:T(8,128)S(1)}, f32[3,128,128]{2,1,0:T(8,128)}, u32[]{:S(2)}) copy-start(f32[3,128,128]{2,1,0:T(8,128)} %get-tuple-element.27) | copy-start | bytes 589828
  489.4 12.3 %all-to-all-start.2 = ((f32[16,1,576]{2,1,0:T(1,128)}), f32[16,1,576]{2,1,0:T(1,128)S(1)}, u32[]{:S(2)}, u32[]{:S(2)}) async-start(f32[16,1,576]{2,1,0:T(1,128)} %reshape.327), calls=%async_computation.2 | async-start | bytes 81920 | tf_op jit(solution)/shard_map/all_to_all | solution.py:161
  492.9 20.1 %copy-start.3 = (f32[18,18,128]{2,1,0:T(8,128)S(1)}, f32[18,18,128]{2,1,0:T(8,128)}, u32[]{:S(2)}) copy-start(f32[18,18,128]{2,1,0:T(8,128)} %convolution_bitcast_fusion.4) | copy-start | bytes 497668
  503.9 17.0 %all-to-all-start.3 = ((f32[16,18,128,4]{2,3,1,0:T(4,128)}), f32[16,18,128,4]{2,3,1,0:T(4,128)S(1)}, u32[]{:S(2)}, u32[]{:S(2)}) async-start(f32[16,18,128,4]{2,3,1,0:T(4,128)} %broadcast_in_dim.109), calls=%async_computation.3 | async-start | bytes 1179648 | tf_op jit(solution)/shard_map/all_to_all | solution.py:24
  510.6 12.4 %copy-start.10 = (s32[18]{0:T(128)S(1)}, s32[18]{0:T(128)}, u32[]{:S(2)}) copy-start(s32[18]{0:T(128)} %iota_multiply_fusion.4) | copy-start | bytes 220
  (6 other events, 37.1 us)
where the time goes:
time: 536 us; the launch traced here: 527 us
  local copies, waits for them, and re-layouts  391 us (73%)
  matrix products  44.1 us (8%)
  starting transfers between devices  41.4 us (8%)
  waiting for transfers between devices  34 us (6%)
  other arithmetic  14.7 us (3%)
    gather x8, local copies, waits for them, and re-layouts, cycle_taps(): return jnp.take(profile, (col_ids - row_ids) % length, axis=1)  368 us
    dot_general x39, matrix products, contract(): return jnp.einsum(formula, left, right, precision=lax.Precision.HIGHEST)  41.5 us
    ppermute x4, starting transfers between devices, padded_2(): after = lax.ppermute(first, axis, down)  12.7 us
  transfers between devices with their start and end apart: 12, of which 6 were waited for; matrix products, arithmetic and copies ran while one was open for 79% of the time, Pallas kernels for 0%

commit v1 on v0

v1 whole, which is shorter than its diff:
```python
import functools

import jax
import jax.numpy as jnp
import numpy as np
from jax import lax
from jax.experimental import pallas as pl
from jax.experimental.pallas import tpu as pltpu
from jax.sharding import PartitionSpec as P

SPLINE = (0.125, 0.5, 0.75, 0.5, 0.125)
RADIUS = 10
TAPS = 21
BF = jnp.bfloat16
F32 = jnp.float32
VMEM_LIMIT = 48 * 1024 * 1024


def weight(offset):
    return SPLINE[offset + 2] if -2 <= offset <= 2 else 0.0


def restrict_table(coarse, fine):
    return np.array([[weight(f - 2 * c) for f in fine] for c in coarse], np.float32)


def prolong_cyclic(coarse_len):
    table = np.zeros((coarse_len, 2 * coarse_len), np.float32)
    for c in range(coarse_len):
        for k in range(-2, 3):
            table[c, (2 * c + k) % (2 * coarse_len)] += weight(k)
    return table


def tap_basis(rows, positions):
    basis = np.zeros((TAPS, len(rows), len(positions)), np.float32)
    for r, row in enumerate(rows):
        for c, position in enumerate(positions):
            if position is not None and 0 <= position - row + RADIUS < TAPS:
                basis[position - row + RADIUS, r, c] = 1.0
    return basis


def tables():
    ry = np.zeros((24, 32), np.float32)
    ry[:18] = restrict_table(range(-1, 17), range(32))
    rz = prolong_cyclic(128).T
    ry2 = np.zeros((16, 24), np.float32)
    ry2[:11, :18] = restrict_table(range(-1, 10), range(-1, 17))
    half = prolong_cyclic(64).T
    rz2 = np.zeros((256, 128), np.float32)
    rz2[:128, :64] = half
    rz2[128:, 64:] = half
    none = [None] * 6
    place0 = list(range(32)) + list(range(-10, 0)) + none + list(range(32, 42)) + none
    offsets0 = np.full((32, 64), -1, np.int32)
    for n in range(32):
        for c, position in enumerate(place0):
            if position is not None:
                offsets0[n, c] = position - n + RADIUS
    offsets0 = np.tile(offsets0, (1, 3))
    place1 = list(range(-11, 1)) + list(range(-1, 17)) + list(range(15, 27)) + none
    lift1 = restrict_table(range(-1, 17), range(32)).T
    basis1 = np.einsum("nm,dmc->dnc", lift1, tap_basis(range(-1, 17), place1))
    place2 = (
        list(range(-1, 10)) + [None] * 5 + list(range(-9, 2)) + list(range(7, 18))
        + list(range(-11, -6)) + list(range(15, 20))
    )
    lift2 = lift1 @ restrict_table(range(-1, 10), range(-1, 17)).T
    basis2 = np.einsum("nm,dmc->dnc", lift2, tap_basis(range(-1, 10), place2))
    basis1 = np.tile(basis1, (1, 1, 3))
    basis2 = np.tile(basis2, (1, 1, 3))
    up2 = prolong_cyclic(64)
    up1 = prolong_cyclic(128)
    return ry, rz, ry2, rz2, offsets0, basis1, basis2, up2, up1


def halves(x):
    high = x.astype(BF)
    return high, (x - high.astype(F32)).astype(BF)


def dot(a, b):
    return jnp.dot(a, b, preferred_element_type=F32)


def spline_sum(read, center, low, high):
    total = None
    for k in range(-2, 3):
        if low <= 2 * center + k <= high:
            term = SPLINE[k + 2] * read(2 * center + k)
            total = term if total is None else total + term
    return total


def matrices_kernel(taps, offsets0, basis1, basis2, up2, y0, y1, y2, z0h, z0l, z1h, z1l, z2h, z2l):
    def cycle(level, member, length):
        rows = lax.broadcasted_iota(jnp.int32, (length, length), 0)
        cols = lax.broadcasted_iota(jnp.int32, (length, length), 1)
        offsets = (rows - cols + RADIUS) & (length - 1)
        table = jnp.zeros((length, length), F32)
        for k in range(TAPS):
            table = jnp.where(offsets == k, taps[level, member * TAPS + k], table)
        return table

    for member in range(3):
        rows = pl.ds(32 * member, 32)
        table = jnp.zeros((32, 192), F32)
        for k in range(TAPS):
            table = jnp.where(offsets0[...] == k, taps[0, member * TAPS + k], table)
        high, low = halves(table)
        lanes = lax.broadcasted_iota(jnp.int32, (32, 192), 1)
        y0[rows] = jnp.where(lanes < 128, high.astype(F32), low.astype(F32)).astype(BF)
        lanes = lax.broadcasted_iota(jnp.int32, (32, 144), 1)
        for level, basis, out in ((1, basis1, y1), (2, basis2, y2)):
            table = jnp.zeros((32, 144), F32)
            for k in range(TAPS):
                table = table + taps[level, member * TAPS + k] * basis[k]
            high, low = halves(table)
            out[rows] = jnp.where(lanes < 96, high.astype(F32), low.astype(F32)).astype(BF)
        high, low = halves(cycle(0, member, 256))
        z0h[pl.ds(256 * member, 256)] = high
        z0l[pl.ds(256 * member, 256)] = low
        high, low = halves(cycle(1, member, 128))
        z1h[pl.ds(128 * member, 128)] = high
        z1l[pl.ds(128 * member, 128)] = low
        high, low = halves(cycle(2, member, 64))
        table = dot(high, up2[...]) + dot(low, up2[...])
        high, low = halves(table)
        z2h[pl.ds(128 * member, 64)] = high
        z2l[pl.ds(128 * member, 64)] = low
        z2h[pl.ds(128 * member + 64, 64)] = jnp.zeros((64, 128), BF)
        z2l[pl.ds(128 * member + 64, 64)] = jnp.zeros((64, 128), BF)


def restrict_kernel(c, ry, rz, ry2, rz2, l1, l2, up1, down1, two, s1, s2):
    for i in range(-1, 17):
        high, low = halves(spline_sum(lambda r: c[r], i, 0, 31))
        s1[i + 1] = dot(ry[...], high) + dot(ry[...], low)
    high, low = halves(s1[...].reshape(18 * 24, 256))
    l1[...] = (dot(high, rz[...]) + dot(low, rz[...])).reshape(18, 24, 128)
    for i in range(-1, 10):
        high, low = halves(spline_sum(lambda r: l1[r + 1], i, -1, 16))
        s2[i + 1] = dot(ry2[...], high) + dot(ry2[...], low)
    s2[11] = jnp.zeros((16, 128), F32)
    first = s2[pl.ds(0, 6)].reshape(96, 128)
    second = s2[pl.ds(6, 6)].reshape(96, 128)
    total = jnp.zeros((96, 128), F32)
    for part, rows in ((first, pl.ds(0, 128)), (second, pl.ds(128, 128))):
        high, low = halves(part)
        total = total + dot(high, rz2[rows]) + dot(low, rz2[rows])
    total = total.reshape(6, 16, 128)
    l2[...] = total
    up1[pl.ds(64, 8)] = jnp.zeros((8, 128), F32)
    down1[pl.ds(64, 8)] = jnp.zeros((8, 128), F32)
    two[pl.ds(48, 8)] = jnp.zeros((8, 128), F32)
    for j in range(6):
        up1[pl.ds(11 * j, 11)] = total[j, :11]
        down1[pl.ds(11 * j, 11)] = total[j, :11]
        if j < 5:
            two[pl.ds(11 * j, 11)] = total[j, :11]
    for r in range(12):
        up1[pl.ds(72 + 18 * r, 18)] = l1[6 + r, :18]
        down1[pl.ds(72 + 18 * r, 18)] = l1[r, :18]


def face_kernel(c, before, after, up, down):
    for i in range(52):
        read = before if i < 10 else c if i < 42 else after
        row = i if i < 10 else i - 10 if i < 42 else i - 42
        up[pl.ds(10 * i, 10)] = read[row, 22:32]
        down[pl.ds(10 * i, 10)] = read[row, 0:10]
    up[pl.ds(520, 8)] = jnp.zeros((8, 256), F32)
    down[pl.ds(520, 8)] = jnp.zeros((8, 256), F32)


def gather_x_kernel(l1, l2, left, right, left2, right2, l1x, l2x, up1, down1, up2, down2):
    for i in range(38):
        if i < 12:
            l1x[i, :18] = left[pl.ds(72 + 18 * i, 18)]
            l1x[i, pl.ds(18, 6)] = jnp.zeros((6, 128), F32)
        elif i >= 26:
            l1x[i, :18] = right[pl.ds(72 + 18 * (i - 26), 18)]
            l1x[i, pl.ds(18, 6)] = jnp.zeros((6, 128), F32)
        if 10 <= i < 12 or 26 <= i < 28:
            l1x[i] = l1x[i] + l1[i - 10]
        elif 12 <= i < 26:
            l1x[i] = l1[i - 10]
    lanes = lax.broadcasted_iota(jnp.int32, (11, 128), 1)
    lower = lanes < 64
    rolled = lambda x: pltpu.roll(x, 64, 1)
    for j in range(16):
        low = []
        high = []
        if j < 5:
            low.append(rolled(left2[pl.ds(11 * j, 11)]))
        if 2 <= j < 8:
            low.append(left[pl.ds(11 * (j - 2), 11)])
        if 8 <= j < 13:
            low.append(rolled(left[pl.ds(11 * (j - 8), 11)]))
        if j >= 10:
            low.append(l2[j - 10, :11])
        if j < 5:
            high.append(l2[j, :11])
        if 2 <= j < 8:
            high.append(rolled(right[pl.ds(11 * (j - 2), 11)]))
        if 8 <= j < 13:
            high.append(right[pl.ds(11 * (j - 8), 11)])
        if 10 <= j < 15:
            high.append(rolled(right2[pl.ds(11 * (j - 10), 11)]))
        row = jnp.where(lower, sum(low, jnp.zeros((11, 128), F32)), sum(high, jnp.zeros((11, 128), F32)))
        l2x[j, :11] = row
        l2x[j, pl.ds(11, 5)] = jnp.zeros((5, 128), F32)
        up1[pl.ds(11 * j, 11)] = row
        down1[pl.ds(11 * j, 11)] = row
        up2[pl.ds(5 * j, 5)] = row[6:11]
        down2[pl.ds(5 * j, 5)] = row[0:5]
    for i in range(38):
        up1[pl.ds(176 + 12 * i, 12)] = l1x[i, 6:18]
        down1[pl.ds(176 + 12 * i, 12)] = l1x[i, 0:12]


def upper_kernel(taps, l1x, l2x, left, right, left2, right2, y1, y2, z1h, z1l, z2h, z2l, out,
                 f1, f2, v1, v2, w1, w2, mid):
    for i in range(38):
        f1[i, pl.ds(0, 12)] = left[pl.ds(176 + 12 * i, 12)]
        f1[i, pl.ds(12, 18)] = l1x[i, :18]
        f1[i, pl.ds(30, 12)] = right[pl.ds(176 + 12 * i, 12)]
        f1[i, pl.ds(42, 6)] = jnp.zeros((6, 128), F32)
    for j in range(16):
        f2[j, pl.ds(0, 16)] = l2x[j]
        f2[j, pl.ds(16, 11)] = left[pl.ds(11 * j, 11)]
        f2[j, pl.ds(27, 11)] = right[pl.ds(11 * j, 11)]
        f2[j, pl.ds(38, 5)] = left2[pl.ds(5 * j, 5)]
        f2[j, pl.ds(43, 5)] = right2[pl.ds(5 * j, 5)]

    @pl.loop(0, 38, unroll=2)
    def _(i):
        high, low = halves(f1[i])
        v1[i] = dot(y1[...], jnp.concatenate([high, low, high], 0))

    @pl.loop(0, 16, unroll=2)
    def _(j):
        high, low = halves(f2[j])
        v = dot(y2[...], jnp.concatenate([high, low, high], 0))
        v2[j] = v
        v2[16 + j] = pltpu.roll(v, 64, 1)

    def correlate_x(level, v, w, count, g):
        member = g // 4
        rows = pl.ds(pl.multiple_of(8 * g, 8), 8)
        scale = [taps[level, member * TAPS + k] for k in range(TAPS)]
        for base in range(0, count, 9 if count == 18 else 11):
            many = 9 if count == 18 else 11
            sums = [None] * many
            for i in range(base, base + many + TAPS - 1):
                value = v[i, rows]
                for m in range(many):
                    k = i - base - m
                    if 0 <= k < TAPS:
                        term = scale[k] * value
                        sums[m] = term if sums[m] is None else sums[m] + term
            for m in range(many):
                w[base + m, rows] = sums[m]

    @pl.loop(0, 12)
    def _(g):
        correlate_x(1, v1, w1, 18, g)
        correlate_x(2, v2, w2, 11, g)

    def correlate_z(w, count, high_table, low_table):
        total = jnp.zeros((count * 32, 128), F32)
        for member in range(3):
            high, low = halves(w[:, pl.ds(32 * member, 32)].reshape(count * 32, 128))
            rows = pl.ds(128 * member, 128)
            total = total + dot(high, high_table[rows]) + dot(low, high_table[rows]) + dot(high, low_table[rows])
        return total.reshape(count, 32, 128)

    v2[pl.ds(0, 11), pl.ds(0, 32)] = correlate_z(w2, 11, z2h, z2l)
    mid[...] = correlate_z(w1, 18, z1h, z1l)
    top = lambda i: v2[i + 1, pl.ds(0, 32)]
    for a in range(-1, 9):
        if a >= 0:
            mid[2 * a + 1] = mid[2 * a + 1] + (0.75 * top(a) + 0.125 * (top(a - 1) + top(a + 1)))
        if a < 8:
            mid[2 * a + 2] = mid[2 * a + 2] + 0.5 * (top(a) + top(a + 1))
    for a in range(16):
        out[2 * a] = 0.75 * mid[a + 1] + 0.125 * (mid[a] + mid[a + 2])
        out[2 * a + 1] = 0.5 * (mid[a + 1] + mid[a + 2])


def finest_kernel(taps, c, before, after, left, right, middle, y0, z0h, z0l, up1, out, v, wh, wl):
    def section(own, i, base, at):
        b = left[pl.ds(base, 48)][10 * at:10 * at + 16]
        a = right[pl.ds(base, 48)][10 * at:10 * at + 16]
        high, low = halves(jnp.concatenate([own, b, a], 0))
        v[i] = dot(y0[...], jnp.concatenate([high, low, high], 0))

    for i in range(10):
        section(before[i], i, 40 * (i // 4), i % 4)
    for i in (10, 11):
        section(c[i - 10], i, 40 * (i // 4), i % 4)

    @pl.loop(3, 10)
    def _(q):
        base = pl.multiple_of(40 * q, 8)
        for at in range(4):
            i = 4 * q + at
            section(c[i - 10], i, base, at)

    for i in (40, 41):
        section(c[i - 10], i, 40 * (i // 4), i % 4)
    for i in range(42, 52):
        section(after[i - 42], i, 40 * (i // 4), i % 4)

    @pl.loop(0, 4)
    def _(g):
        for member in range(3):
            rows = pl.ds(pl.multiple_of(32 * member + 8 * g, 8), 8)
            scale = [taps[0, member * TAPS + k] for k in range(TAPS)]
            for h in range(2):
                lanes = pl.ds(128 * h, 128)
                for base in range(0, 32, 8):
                    sums = [None] * 8
                    for i in range(base, base + 8 + TAPS - 1):
                        value = v[i, rows, lanes]
                        for m in range(8):
                            k = i - base - m
                            if 0 <= k < TAPS:
                                term = scale[k] * value
                                sums[m] = term if sums[m] is None else sums[m] + term
                    for m in range(0, 8, 2):
                        high, low = halves(jnp.concatenate([sums[m], sums[m + 1]], 0))
                        at = (pl.ds(8 * (base + m), 16), pl.ds(256 * member + 128 * h, 128))
                        wh[at] = high
                        wl[at] = low
        cols = pl.ds(pl.multiple_of(8 * g, 8), 8)
        total = dot(wh[...], z0h[...]) + dot(wl[...], z0h[...]) + dot(wh[...], z0l[...])
        high, low = halves(middle[:, cols].reshape(256, 128))
        total = total + dot(high, up1[...]) + dot(low, up1[...])
        out[:, cols] = total.reshape(32, 8, 256)


def call(kernel, outs, scratch=(), scalars=0, count=0, flops=0, moved=0, name=None):
    vmem = pl.BlockSpec(memory_space=pltpu.VMEM)
    smem = pl.BlockSpec(memory_space=pltpu.SMEM)
    shapes = [jax.ShapeDtypeStruct(*o) for o in outs]
    return pl.pallas_call(
        kernel,
        out_shape=shapes,
        in_specs=[smem] * scalars + [vmem] * (count - scalars),
        out_specs=[vmem] * len(shapes),
        scratch_shapes=[pltpu.VMEM(*s) for s in scratch],
        compiler_params=pltpu.CompilerParams(vmem_limit_bytes=VMEM_LIMIT),
        cost_estimate=pl.CostEstimate(flops=flops, bytes_accessed=moved, transcendentals=0),
        name=name,
    )


def shift(x, axis, by):
    n = lax.axis_size(axis)
    return lax.ppermute(x, axis, [(i, (i + by) % n) for i in range(n)])


def body(charges, kernel_taps):
    ry, rz, ry2, rz2, offsets0, basis1, basis2, up2, up1 = tables()
    taps = kernel_taps.reshape(3, 63)
    b16 = lambda x: jnp.asarray(x, BF)
    before = shift(charges[22:], "gx", 1)
    after = shift(charges[:10], "gx", -1)
    l1, l2, s_up, s_down, s_two = call(
        restrict_kernel,
        [((18, 24, 128), F32), ((6, 16, 128), F32), ((288, 128), F32), ((288, 128), F32), ((56, 128), F32)],
        [((18, 24, 256), F32), ((12, 16, 128), F32)], 0, 5, 10**8, 2 * 10**6, name="restrict",
    )(charges, b16(ry), b16(rz), b16(ry2), b16(rz2))
    x_left = shift(s_up, "gx", 1)
    x_right = shift(s_down, "gx", -1)
    x_left2 = shift(s_two, "gx", 2)
    x_right2 = shift(s_two, "gx", -2)
    y0, y1, y2, z0h, z0l, z1h, z1l, z2h, z2l = call(
        matrices_kernel,
        [((96, 192), BF), ((96, 144), BF), ((96, 144), BF), ((768, 256), BF), ((768, 256), BF),
         ((384, 128), BF), ((384, 128), BF), ((384, 128), BF), ((384, 128), BF)],
        [], 1, 5, 10**8, 4 * 10**6, name="matrices",
    )(taps, jnp.asarray(offsets0), jnp.asarray(basis1), jnp.asarray(basis2), b16(up2))
    l1x, l2x, t_up, t_down, t_up2, t_down2 = call(
        gather_x_kernel,
        [((38, 24, 128), F32), ((16, 16, 128), F32), ((632, 128), F32), ((632, 128), F32),
         ((80, 128), F32), ((80, 128), F32)],
        [], 0, 6, 10**6, 2 * 10**6, name="gather_x",
    )(l1, l2, x_left, x_right, x_left2, x_right2)
    f_up, f_down = call(
        face_kernel, [((528, 256), F32), ((528, 256), F32)], [], 0, 3, 10**6, 3 * 10**6, name="faces",
    )(charges, before, after)
    left = shift(f_up, "gy", 1)
    right = shift(f_down, "gy", -1)
    y_left = shift(t_up, "gy", 1)
    y_right = shift(t_down, "gy", -1)
    y_left2 = shift(t_up2, "gy", 2)
    y_right2 = shift(t_down2, "gy", -2)
    middle, = call(
        upper_kernel, [((32, 32, 128), F32)],
        [((38, 48, 128), F32), ((16, 48, 128), F32), ((38, 96, 128), F32), ((32, 96, 128), F32),
         ((18, 96, 128), F32), ((11, 96, 128), F32), ((18, 32, 128), F32)],
        1, 13, 4 * 10**8, 4 * 10**6, name="upper",
    )(taps, l1x, l2x, y_left, y_right, y_left2, y_right2, y1, y2, z1h, z1l, z2h, z2l)
    result, = call(
        finest_kernel, [((32, 32, 256), F32)],
        [((52, 96, 256), F32), ((256, 768), BF), ((256, 768), BF)],
        1, 11, 2 * 10**9, 6 * 10**6, name="finest",
    )(taps, charges, before, after, left, right, middle, y0, z0h, z0l, b16(up1))
    return result


def solution(mesh):
    return jax.shard_map(
        body,
        mesh=mesh,
        in_specs=(P("gx", "gy", None), P()),
        out_specs=P("gx", "gy", None),
        check_vma=False,
    )
```

time: 536 us -> 102 us (0.19); the launches traced: 527 us -> 101 us
  local copies, waits for them, and re-layouts: 391 us -> 4.77 us
  matrix products: 44.1 us -> 0 us
  Pallas kernels: 0 us -> 26.5 us
  other arithmetic: 14.7 us -> 0 us
  starting transfers between devices: 41.4 us -> 34.8 us
    gather x14 -> x0, local copies, waits for them, and re-layouts: 375 us -> none  [the longest x8 368 us: cycle_taps(): return jnp.take(profile, (col_ids - row_ids) % length, axis=1)]
    dot_general x43 -> x0, matrix products: 44.1 us -> none  [the longest x39 41.5 us: contract(): return jnp.einsum(formula, left, right, precision=lax.Precision.HIGHEST)]
    ppermute x8 -> x12, waiting for transfers between devices: 6.92 us -> 35.1 us  [shift(): return lax.ppermute(x, axis, [(i, (i + by) % n) for i in range(n)])]
    all_to_all x4 -> x0, waiting for transfers between devices: 27.1 us -> none  [the longest x1 7.8 us: body(): lax.all_to_all(turned_yz, 'gx', split_axis=2, concat_axis=1, tiled=True)]
    pallas_call x0 -> x6, Pallas kernels: none -> 26.5 us  [the longest x1 11.1 us: body(): call(finest_kernel, [((32, 32, 256), F32)], [((52, 96, 256), F32), ((256,...]
    all_to_all x4 -> x0, starting transfers between devices: 20.6 us -> none  [the longest x1 6.35 us: from_everyone(): lax.all_to_all(jnp.broadcast_to(x[None], (peers, *x.shape)), axis, 0, 0,...]
    ppermute x8 -> x12, starting transfers between devices: 20.8 us -> 34.8 us  [shift(): return lax.ppermute(x, axis, [(i, (i + by) % n) for i in range(n)])]
  transfers between devices with their start and end apart: 12 -> 12, of which waited for: 6 -> 5; matrix products, arithmetic and copies ran while one was open for 79% -> 1% of each run, Pallas kernels for 0% -> 14%
where the time goes in v1:
time: 102 us; the launch traced here: 101 us
  waiting for transfers between devices  35.1 us (34%)
  starting transfers between devices  34.8 us (34%)
  Pallas kernels  26.5 us (26%)
  local copies, waits for them, and re-layouts  4.77 us (5%)
    ppermute x12, waiting for transfers between devices, shift(): return lax.ppermute(x, axis, [(i, (i + by) % n) for i in range(n)])  35.1 us
    ppermute x12, starting transfers between devices, shift(): return lax.ppermute(x, axis, [(i, (i + by) % n) for i in range(n)])  34.8 us
    pallas_call x1, Pallas kernels, body(): call(finest_kernel, [((32, 32, 256), F32)], [((52, 96, 256), F32), ((256,...  11.1 us
    pallas_call x1, Pallas kernels, body(): call(upper_kernel, [((32, 32, 128), F32)], [((38, 48, 128), F32), ((16, 4...  9.36 us
    pallas_call x1, Pallas kernels, body(): call(matrices_kernel, [((96, 192), BF), ((96, 144), BF), ((96, 144), BF),...  3.05 us
    unnamed x28, local copies, waits for them, and re-layouts  2.79 us
  transfers between devices with their start and end apart: 12, of which 5 were waited for; matrix products, arithmetic and copies ran while one was open for 1% of the time, Pallas kernels for 14%

profile of v1, /device:TPU:1, one launch (start us, length us, event | category | flops | bytes accessed | tf_op | source)
XLA Modules:
  0.0 101.4 jit_solution(11105026465092907052)
XLA Ops:
  0.0 1.2 %fusion = (f32[10,32,256]{2,1,0:T(8,128)S(1)}, f32[10,32,256]{2,1,0:T(8,128)S(1)}) fusion(f32[32,32,256]{2,1,0:T(8,128)} %c.5), kind=kLoop, calls=%fused_computation | loop fusion | bytes 1310720 | tf_op jit(solution)/shard_map/slice | solution.py:370
  1.2 3.9 %collective-permute-start = (f32[10,32,256]{2,1,0:T(8,128)S(1)}, f32[10,32,256]{2,1,0:T(8,128)S(1)}, u32[]{:S(2)}, u32[]{:S(2)}) collective-permute-start(f32[10,32,256]{2,1,0:T(8,128)S(1)} %get-tuple-element.50), channel_id=1, source_target_pairs={{0,16},{16,32},{32,48},{48,64},{64,80},{80,96},{96,112},{112,128},... | collective-permute-start | bytes 983048 | tf_op jit(solution)/shard_map/ppermute | solution.py:362
  5.1 5.6 %collective-permute-start.1 = (f32[10,32,256]{2,1,0:T(8,128)S(1)}, f32[10,32,256]{2,1,0:T(8,128)S(1)}, u32[]{:S(2)}, u32[]{:S(2)}) collective-permute-start(f32[10,32,256]{2,1,0:T(8,128)S(1)} %get-tuple-element.49), channel_id=1, source_target_pairs={{0,240},{16,0},{32,16},{48,32},{64,48},{80,64},{96,80},{112,96},{1... | collective-permute-start | bytes 983048 | tf_op jit(solution)/shard_map/ppermute | solution.py:362
  10.7 9.3 %collective-permute-done.before = f32[10,32,256]{2,1,0:T(8,128)S(1)} collective-permute-done((f32[10,32,256]{2,1,0:T(8,128)S(1)}, f32[10,32,256]{2,1,0:T(8,128)S(1)}, u32[]{:S(2)}, u32[]{:S(2)}) %collective-permute-start) | collective-permute-done | bytes 327712 | tf_op jit(solution)/shard_map/ppermute | solution.py:362
  20.0 4.0 %collective-permute-done.1.after = f32[10,32,256]{2,1,0:T(8,128)S(1)} collective-permute-done((f32[10,32,256]{2,1,0:T(8,128)S(1)}, f32[10,32,256]{2,1,0:T(8,128)S(1)}, u32[]{:S(2)}, u32[]{:S(2)}) %collective-permute-start.1) | collective-permute-done | bytes 327712 | tf_op jit(solution)/shard_map/ppermute | solution.py:362
  24.1 1.1 %faces.1 = (f32[528,256]{1,0:T(8,128)}, f32[528,256]{1,0:T(8,128)}) custom-call(f32[32,32,256]{2,1,0:T(8,128)S(1)} %copy-done, f32[10,32,256]{2,1,0:T(8,128)S(1)} %collective-permute-done.before, f32[10,32,256]{2,1,0:T(8,128)S(1)} %collective-permute-done.1.after), custom_call_target="tpu_custom_call" | custom-call | flops 1000000 | bytes 3000000 | tf_op jit(solution)/shard_map/faces/pallas_call | solution.py:392
  25.2 2.9 %collective-permute-start.2 = (f32[528,256]{1,0:T(8,128)}, f32[528,256]{1,0:T(8,128)}, u32[]{:S(2)}, u32[]{:S(2)}) collective-permute-start(f32[528,256]{1,0:T(8,128)} %get-tuple-element.27), channel_id=1, source_target_pairs={{0,1},{1,2},{2,3},{3,4},{4,5},{5,6},{6,7},{7,8},{8,9},{9,10},{10,1... | collective-permute-start | bytes 1622024 | tf_op jit(solution)/shard_map/ppermute | solution.py:362
  28.1 0.9 restrict.1
  29.0 1.9 %collective-permute-start.4 = (f32[288,128]{1,0:T(8,128)S(1)}, f32[288,128]{1,0:T(8,128)S(1)}, u32[]{:S(2)}, u32[]{:S(2)}) collective-permute-start(f32[288,128]{1,0:T(8,128)S(1)} %get-tuple-element.31), channel_id=1, source_target_pairs={{0,16},{16,32},{32,48},{48,64},{64,80},{80,96},{96,112},{112,128},... | collective-permute-start | bytes 442376 | tf_op jit(solution)/shard_map/ppermute | solution.py:362
  30.9 3.9 %collective-permute-start.5 = (f32[288,128]{1,0:T(8,128)S(1)}, f32[288,128]{1,0:T(8,128)S(1)}, u32[]{:S(2)}, u32[]{:S(2)}) collective-permute-start(f32[288,128]{1,0:T(8,128)S(1)} %get-tuple-element.32), channel_id=1, source_target_pairs={{0,240},{16,0},{32,16},{48,32},{64,48},{80,64},{96,80},{112,96},{1... | collective-permute-start | bytes 442376 | tf_op jit(solution)/shard_map/ppermute | solution.py:362
  34.8 10.7 %collective-permute-done.6.left2 = f32[56,128]{1,0:T(8,128)S(1)} collective-permute-done((f32[56,128]{1,0:T(8,128)S(1)}, f32[56,128]{1,0:T(8,128)S(1)}, u32[]{:S(2)}, u32[]{:S(2)}) %collective-permute-start.6) | collective-permute-done | bytes 28704 | tf_op jit(solution)/shard_map/ppermute | solution.py:362
  45.4 3.4 %collective-permute-start.7 = (f32[56,128]{1,0:T(8,128)S(1)}, f32[56,128]{1,0:T(8,128)S(1)}, u32[]{:S(2)}, u32[]{:S(2)}) collective-permute-start(f32[56,128]{1,0:T(8,128)S(1)} %get-tuple-element.33), channel_id=1, source_target_pairs={{0,224},{16,240},{32,0},{48,16},{64,32},{80,48},{96,64},{112,80},{... | collective-permute-start | bytes 86024 | tf_op jit(solution)/shard_map/ppermute | solution.py:362
  48.8 3.9 %collective-permute-done.7.right2 = f32[56,128]{1,0:T(8,128)S(1)} collective-permute-done((f32[56,128]{1,0:T(8,128)S(1)}, f32[56,128]{1,0:T(8,128)S(1)}, u32[]{:S(2)}, u32[]{:S(2)}) %collective-permute-start.7) | collective-permute-done | bytes 28704 | tf_op jit(solution)/shard_map/ppermute | solution.py:362
  52.7 1.0 gather_x.1
  54.4 7.2 %collective-permute-start.8 = (f32[632,128]{1,0:T(8,128)}, f32[632,128]{1,0:T(8,128)}, u32[]{:S(2)}, u32[]{:S(2)}) collective-permute-start(f32[632,128]{1,0:T(8,128)} %get-tuple-element.36), channel_id=1, source_target_pairs={{0,1},{1,2},{2,3},{3,4},{4,5},{5,6},{6,7},{7,8},{8,9},{9,10},{10,1... | collective-permute-start | bytes 970760 | tf_op jit(solution)/shard_map/ppermute | solution.py:362
  61.6 1.5 %collective-permute-start.10 = (f32[80,128]{1,0:T(8,128)S(1)}, f32[80,128]{1,0:T(8,128)S(1)}, u32[]{:S(2)}, u32[]{:S(2)}) collective-permute-start(f32[80,128]{1,0:T(8,128)S(1)} %get-tuple-element.38), channel_id=1, source_target_pairs={{0,2},{1,3},{2,4},{3,5},{4,6},{5,7},{6,8},{7,9},{8,10},{9,11},{10,... | collective-permute-start | bytes 122888 | tf_op jit(solution)/shard_map/ppermute | solution.py:362
  63.1 7.2 %collective-permute-done.10.left2 = f32[80,128]{1,0:T(8,128)S(1)} collective-permute-done((f32[80,128]{1,0:T(8,128)S(1)}, f32[80,128]{1,0:T(8,128)S(1)}, u32[]{:S(2)}, u32[]{:S(2)}) %collective-permute-start.10) | collective-permute-done | bytes 40992 | tf_op jit(solution)/shard_map/ppermute | solution.py:362
  70.9 4.6 %collective-permute-start.11 = (f32[80,128]{1,0:T(8,128)}, f32[80,128]{1,0:T(8,128)}, u32[]{:S(2)}, u32[]{:S(2)}) collective-permute-start(f32[80,128]{1,0:T(8,128)} %get-tuple-element.39), channel_id=1, source_target_pairs={{0,14},{1,15},{2,0},{3,1},{4,2},{5,3},{6,4},{7,5},{8,6},{9,7},{10,... | collective-permute-start | bytes 122888 | tf_op jit(solution)/shard_map/ppermute | solution.py:362
  75.5 0.8 reshape.3.taps
  76.3 0.8 copy-done.9
  77.0 0.7 copy-done.10
  77.8 3.1 %matrices.1 = (bf16[96,192]{1,0:T(8,128)(2,1)S(1)}, bf16[96,144]{1,0:T(8,128)(2,1)S(1)}, bf16[96,144]{1,0:T(8,128)(2,1)S(1)}, bf16[768,256]{1,0:T(8,128)(2,1)S(1...) custom-call(f32[3,63]{1,0:T(4,128)S(1)} %reshape.3.taps, ...), custom_call_target="tpu_custom_call" | custom-call | flops 100000000 | bytes 4000000 | tf_op jit(solution)/shard_map/matrices/pallas_call | solution.py:380
  80.9 9.4 %upper.1.middle = f32[32,32,128]{2,1,0:T(8,128)S(1)} custom-call(f32[3,63]{1,0:T(4,128)S(1)} %reshape.3.taps, f32[38,24,128]{2,1,0:T(8,128)S(1)} %get-tuple-element.34.l1x, f32[16,16,128]{2,1,0:T(8,128)S(1)} %copy-done.4, f32[632,128]{1,0:T(8,128)} %collective-permute-done.8.left, f32[632,128]{1,0:T(8,128)} %collective-permute-done.9.right, ...), custom_call_target="tpu_custom_call" | custom-call | flops 400000000 | bytes 4000000 | tf_op jit(solution)/shard_map/upper/pallas_call | solution.py:401
  90.3 11.1 %finest.1 = f32[32,32,256]{2,1,0:T(8,128)} custom-call(f32[3,63]{1,0:T(4,128)S(1)} %reshape.3.taps, f32[32,32,256]{2,1,0:T(8,128)S(1)} %copy-done, f32[10,32,256]{2,1,0:T(8,128)S(1)} %collective-permute-done.before, f32[10,32,256]{2,1,0:T(8,128)S(1)} %collective-permute-done.1.after, f32[528,256]{1,0:T(8,128)} %collective-permute-done.2.left, ...), custom_call_target="tpu_custom_call" | custom-call | flops 2000000000 | bytes 6000000 | tf_op jit(solution)/shard_map/finest/pallas_call | solution.py:407
  (36 shorter events, 1.3 us)
Async XLA Ops:
  0.0 24.0 %copy-start = (f32[32,32,256]{2,1,0:T(8,128)S(1)}, f32[32,32,256]{2,1,0:T(8,128)}, u32[]{:S(2)}) copy-start(f32[32,32,256]{2,1,0:T(8,128)} %c.5) | copy-start | bytes 3145732
  1.2 18.8 %collective-permute-start = (f32[10,32,256]{2,1,0:T(8,128)S(1)}, f32[10,32,256]{2,1,0:T(8,128)S(1)}, u32[]{:S(2)}, u32[]{:S(2)}) collective-permute-start(f32[10,32,256]{2,1,0:T(8,128)S(1)} %get-tuple-element.50), channel_id=1, source_target_pairs={{0,16},{16,32},{32,48},{48,64},{64,80},{80,96},{96,112},{112,128},... | collective-permute-start | bytes 983048 | tf_op jit(solution)/shard_map/ppermute | solution.py:362
  5.1 23.0 %copy-start.5 = (bf16[256,128]{1,0:T(8,128)(2,1)S(1)}, bf16[256,128]{1,0:T(8,128)(2,1)}, u32[]{:S(2)}) copy-start(bf16[256,128]{1,0:T(8,128)(2,1)} %constant.19.clone.rz) | copy-start | bytes 196612
  5.1 23.0 %copy-start.6 = (bf16[256,128]{1,0:T(8,128)(2,1)S(1)}, bf16[256,128]{1,0:T(8,128)(2,1)}, u32[]{:S(2)}) copy-start(bf16[256,128]{1,0:T(8,128)(2,1)} %constant.21.clone.rz2) | copy-start | bytes 196612
  5.1 18.9 %collective-permute-start.1 = (f32[10,32,256]{2,1,0:T(8,128)S(1)}, f32[10,32,256]{2,1,0:T(8,128)S(1)}, u32[]{:S(2)}, u32[]{:S(2)}) collective-permute-start(f32[10,32,256]{2,1,0:T(8,128)S(1)} %get-tuple-element.49), channel_id=1, source_target_pairs={{0,240},{16,0},{32,16},{48,32},{64,48},{80,64},{96,80},{112,96},{1... | collective-permute-start | bytes 983048 | tf_op jit(solution)/shard_map/ppermute | solution.py:362
  24.1 4.0 %copy-start.11 = (bf16[24,32]{1,0:T(8,128)(2,1)S(1)}, bf16[24,32]{1,0:T(8,128)(2,1)}, u32[]{:S(2)}) copy-start(bf16[24,32]{1,0:T(8,128)(2,1)} %constant.18.clone.ry) | copy-start | bytes 4612
  24.1 4.1 %copy-start.12 = (bf16[16,24]{1,0:T(8,128)(2,1)S(1)}, bf16[16,24]{1,0:T(8,128)(2,1)}, u32[]{:S(2)}) copy-start(bf16[16,24]{1,0:T(8,128)(2,1)} %constant.20.clone.ry2) | copy-start | bytes 2308
  25.2 65.0 %collective-permute-start.2 = (f32[528,256]{1,0:T(8,128)}, f32[528,256]{1,0:T(8,128)}, u32[]{:S(2)}, u32[]{:S(2)}) collective-permute-start(f32[528,256]{1,0:T(8,128)} %get-tuple-element.27), channel_id=1, source_target_pairs={{0,1},{1,2},{2,3},{3,4},{4,5},{5,6},{6,7},{7,8},{8,9},{9,10},{10,1... | collective-permute-start | bytes 1622024 | tf_op jit(solution)/shard_map/ppermute | solution.py:362
  28.1 48.2 %copy-start.1 = (f32[21,32,144]{2,1,0:T(8,128)S(1)}, f32[21,32,144]{2,1,0:T(8,128)}, u32[]{:S(2)}) copy-start(f32[21,32,144]{2,1,0:T(8,128)} %constant.23.clone.basis1) | copy-start | bytes 1161220
  28.1 48.2 %copy-start.2 = (f32[21,32,144]{2,1,0:T(8,128)S(1)}, f32[21,32,144]{2,1,0:T(8,128)}, u32[]{:S(2)}) copy-start(f32[21,32,144]{2,1,0:T(8,128)} %constant.24.clone.basis2) | copy-start | bytes 1161220
  28.1 62.2 %collective-permute-start.3 = (f32[528,256]{1,0:T(8,128)}, f32[528,256]{1,0:T(8,128)}, u32[]{:S(2)}, u32[]{:S(2)}) collective-permute-start(f32[528,256]{1,0:T(8,128)} %get-tuple-element.28), channel_id=1, source_target_pairs={{0,15},{1,0},{2,1},{3,2},{4,3},{5,4},{6,5},{7,6},{8,7},{9,8},{10,9... | collective-permute-start | bytes 1622024 | tf_op jit(solution)/shard_map/ppermute | solution.py:362
  29.0 23.7 %collective-permute-start.4 = (f32[288,128]{1,0:T(8,128)S(1)}, f32[288,128]{1,0:T(8,128)S(1)}, u32[]{:S(2)}, u32[]{:S(2)}) collective-permute-start(f32[288,128]{1,0:T(8,128)S(1)} %get-tuple-element.31), channel_id=1, source_target_pairs={{0,16},{16,32},{32,48},{48,64},{64,80},{80,96},{96,112},{112,128},... | collective-permute-start | bytes 442376 | tf_op jit(solution)/shard_map/ppermute | solution.py:362
  30.9 21.8 %collective-permute-start.5 = (f32[288,128]{1,0:T(8,128)S(1)}, f32[288,128]{1,0:T(8,128)S(1)}, u32[]{:S(2)}, u32[]{:S(2)}) collective-permute-start(f32[288,128]{1,0:T(8,128)S(1)} %get-tuple-element.32), channel_id=1, source_target_pairs={{0,240},{16,0},{32,16},{48,32},{64,48},{80,64},{96,80},{112,96},{1... | collective-permute-start | bytes 442376 | tf_op jit(solution)/shard_map/ppermute | solution.py:362
  34.8 10.7 %collective-permute-start.6 = (f32[56,128]{1,0:T(8,128)S(1)}, f32[56,128]{1,0:T(8,128)S(1)}, u32[]{:S(2)}, u32[]{:S(2)}) collective-permute-start(f32[56,128]{1,0:T(8,128)S(1)} %get-tuple-element.33), channel_id=1, source_target_pairs={{0,32},{16,48},{32,64},{48,80},{64,96},{80,112},{96,128},{112,144}... | collective-permute-start | bytes 86024 | tf_op jit(solution)/shard_map/ppermute | solution.py:362
  45.4 7.3 %collective-permute-start.7 = (f32[56,128]{1,0:T(8,128)S(1)}, f32[56,128]{1,0:T(8,128)S(1)}, u32[]{:S(2)}, u32[]{:S(2)}) collective-permute-start(f32[56,128]{1,0:T(8,128)S(1)} %get-tuple-element.33), channel_id=1, source_target_pairs={{0,224},{16,240},{32,0},{48,16},{64,32},{80,48},{96,64},{112,80},{... | collective-permute-start | bytes 86024 | tf_op jit(solution)/shard_map/ppermute | solution.py:362
  54.4 26.4 %collective-permute-start.8 = (f32[632,128]{1,0:T(8,128)}, f32[632,128]{1,0:T(8,128)}, u32[]{:S(2)}, u32[]{:S(2)}) collective-permute-start(f32[632,128]{1,0:T(8,128)} %get-tuple-element.36), channel_id=1, source_target_pairs={{0,1},{1,2},{2,3},{3,4},{4,5},{5,6},{6,7},{7,8},{8,9},{9,10},{10,1... | collective-permute-start | bytes 970760 | tf_op jit(solution)/shard_map/ppermute | solution.py:362
  61.6 19.2 %collective-permute-start.9 = (f32[632,128]{1,0:T(8,128)}, f32[632,128]{1,0:T(8,128)}, u32[]{:S(2)}, u32[]{:S(2)}) collective-permute-start(f32[632,128]{1,0:T(8,128)} %get-tuple-element.37), channel_id=1, source_target_pairs={{0,15},{1,0},{2,1},{3,2},{4,3},{5,4},{6,5},{7,6},{8,7},{9,8},{10,9... | collective-permute-start | bytes 970760 | tf_op jit(solution)/shard_map/ppermute | solution.py:362
  61.6 8.7 %collective-permute-start.10 = (f32[80,128]{1,0:T(8,128)S(1)}, f32[80,128]{1,0:T(8,128)S(1)}, u32[]{:S(2)}, u32[]{:S(2)}) collective-permute-start(f32[80,128]{1,0:T(8,128)S(1)} %get-tuple-element.38), channel_id=1, source_target_pairs={{0,2},{1,3},{2,4},{3,5},{4,6},{5,7},{6,8},{7,9},{8,10},{9,11},{10,... | collective-permute-start | bytes 122888 | tf_op jit(solution)/shard_map/ppermute | solution.py:362
  70.9 9.9 %collective-permute-start.11 = (f32[80,128]{1,0:T(8,128)}, f32[80,128]{1,0:T(8,128)}, u32[]{:S(2)}, u32[]{:S(2)}) collective-permute-start(f32[80,128]{1,0:T(8,128)} %get-tuple-element.39), channel_id=1, source_target_pairs={{0,14},{1,15},{2,0},{3,1},{4,2},{5,3},{6,4},{7,5},{8,6},{9,7},{10,... | collective-permute-start | bytes 122888 | tf_op jit(solution)/shard_map/ppermute | solution.py:362
  76.3 0.8 copy-start.9
  77.0 0.7 copy-start.10
  77.8 3.1 %copy-start.4 = (f32[16,16,128]{2,1,0:T(8,128)S(1)}, f32[16,16,128]{2,1,0:T(8,128)}, u32[]{:S(2)}) copy-start(f32[16,16,128]{2,1,0:T(8,128)} %copy-done.3) | copy-start | bytes 393220
  77.8 3.1 %copy-start.8 = (f32[80,128]{1,0:T(8,128)S(1)}, f32[80,128]{1,0:T(8,128)}, u32[]{:S(2)}) copy-start(f32[80,128]{1,0:T(8,128)} %copy-done.7) | copy-start | bytes 122884
  80.9 9.4 %copy-start.13 = (bf16[128,256]{1,0:T(8,128)(2,1)S(1)}, bf16[128,256]{1,0:T(8,128)(2,1)}, u32[]{:S(2)}) copy-start(bf16[128,256]{1,0:T(8,128)(2,1)} %constant.26.clone.up1) | copy-start | bytes 196612
  (2 other events, 1.3 us)

commit v2 on v1

--- a/solution.py
+++ b/solution.py
@@ -42,15 +42,6 @@
 
 
 def tables():
-    ry = np.zeros((24, 32), np.float32)
-    ry[:18] = restrict_table(range(-1, 17), range(32))
-    rz = prolong_cyclic(128).T
-    ry2 = np.zeros((16, 24), np.float32)
-    ry2[:11, :18] = restrict_table(range(-1, 10), range(-1, 17))
-    half = prolong_cyclic(64).T
-    rz2 = np.zeros((256, 128), np.float32)
-    rz2[:128, :64] = half
-    rz2[128:, 64:] = half
     none = [None] * 6
     place0 = list(range(32)) + list(range(-10, 0)) + none + list(range(32, 42)) + none
     offsets0 = np.full((32, 64), -1, np.int32)
@@ -72,7 +63,7 @@
     basis2 = np.tile(basis2, (1, 1, 3))
     up2 = prolong_cyclic(64)
     up1 = prolong_cyclic(128)
-    return ry, rz, ry2, rz2, offsets0, basis1, basis2, up2, up1
+    return offsets0, basis1, basis2, up2, up1
 
 
 def halves(x):
@@ -133,48 +124,85 @@
         z2l[pl.ds(128 * member + 64, 64)] = jnp.zeros((64, 128), BF)
 
 
-def restrict_kernel(c, ry, rz, ry2, rz2, l1, l2, up1, down1, two, s1, s2):
+def spline_iota(shape, offset, coarse_dim, fine_dim, keep=None):
+    fine = lax.broadcasted_iota(jnp.int32, shape, fine_dim)
+    coarse = lax.broadcasted_iota(jnp.int32, shape, coarse_dim)
+    delta = fine - 2 * coarse + offset
+    if keep is not None:
+        delta = jnp.where(coarse < keep, delta, 99)
+    return spline_of(delta)
+
+
+def spline_of(delta):
+    far = jnp.abs(delta)
+    return jnp.where(far == 0, 0.75, jnp.where(far == 1, 0.5, jnp.where(far == 2, 0.125, 0.0)))
+
+
+def cyclic_iota(shape, coarse_dim, fine_dim, fine_len):
+    fine = lax.broadcasted_iota(jnp.int32, shape, fine_dim)
+    coarse = lax.broadcasted_iota(jnp.int32, shape, coarse_dim)
+    return spline_of(((fine - 2 * coarse + 2) & (fine_len - 1)) - 2)
+
+
+def restrict_kernel(c, l1, l2, up1, down1, face_up, face_down, s1, s2):
+    for i in range(32):
+        face_up[pl.ds(10 * i, 10)] = c[i, 22:32]
+        face_down[pl.ds(10 * i, 10)] = c[i, 0:10]
+    face_up[pl.ds(320, 8)] = jnp.zeros((8, 256), F32)
+    face_down[pl.ds(320, 8)] = jnp.zeros((8, 256), F32)
+    ry = spline_iota((24, 32), 2, 0, 1, 18).astype(BF)
     for i in range(-1, 17):
         high, low = halves(spline_sum(lambda r: c[r], i, 0, 31))
-        s1[i + 1] = dot(ry[...], high) + dot(ry[...], low)
+        s1[i + 1] = dot(ry, high) + dot(ry, low)
+    rz = cyclic_iota((256, 128), 1, 0, 256).astype(BF)
     high, low = halves(s1[...].reshape(18 * 24, 256))
-    l1[...] = (dot(high, rz[...]) + dot(low, rz[...])).reshape(18, 24, 128)
+    l1[...] = (dot(high, rz) + dot(low, rz)).reshape(18, 24, 128)
+    ry2 = spline_iota((16, 24), 1, 0, 1, 11).astype(BF)
     for i in range(-1, 10):
         high, low = halves(spline_sum(lambda r: l1[r + 1], i, -1, 16))
-        s2[i + 1] = dot(ry2[...], high) + dot(ry2[...], low)
+        s2[i + 1] = dot(ry2, high) + dot(ry2, low)
     s2[11] = jnp.zeros((16, 128), F32)
-    first = s2[pl.ds(0, 6)].reshape(96, 128)
-    second = s2[pl.ds(6, 6)].reshape(96, 128)
+    near = s2[pl.ds(0, 6)].reshape(96, 128)
+    far = s2[pl.ds(6, 6)].reshape(96, 128)
+    lanes = lax.broadcasted_iota(jnp.int32, (128, 128), 1)
+    both = spline_of(((lax.broadcasted_iota(jnp.int32, (128, 128), 0) - 2 * (lanes & 63) + 2) & 127) - 2)
     total = jnp.zeros((96, 128), F32)
-    for part, rows in ((first, pl.ds(0, 128)), (second, pl.ds(128, 128))):
+    for part, upper in ((near, False), (far, True)):
+        weights = jnp.where((lanes >= 64) == upper, both, 0.0).astype(BF)
         high, low = halves(part)
-        total = total + dot(high, rz2[rows]) + dot(low, rz2[rows])
+        total = total + dot(high, weights) + dot(low, weights)
     total = total.reshape(6, 16, 128)
     l2[...] = total
     up1[pl.ds(64, 8)] = jnp.zeros((8, 128), F32)
     down1[pl.ds(64, 8)] = jnp.zeros((8, 128), F32)
-    two[pl.ds(48, 8)] = jnp.zeros((8, 128), F32)
     for j in range(6):
         up1[pl.ds(11 * j, 11)] = total[j, :11]
         down1[pl.ds(11 * j, 11)] = total[j, :11]
-        if j < 5:
-            two[pl.ds(11 * j, 11)] = total[j, :11]
     for r in range(12):
         up1[pl.ds(72 + 18 * r, 18)] = l1[6 + r, :18]
         down1[pl.ds(72 + 18 * r, 18)] = l1[r, :18]
 
 
-def face_kernel(c, before, after, up, down):
-    for i in range(52):
-        read = before if i < 10 else c if i < 42 else after
-        row = i if i < 10 else i - 10 if i < 42 else i - 42
-        up[pl.ds(10 * i, 10)] = read[row, 22:32]
-        down[pl.ds(10 * i, 10)] = read[row, 0:10]
-    up[pl.ds(520, 8)] = jnp.zeros((8, 256), F32)
-    down[pl.ds(520, 8)] = jnp.zeros((8, 256), F32)
-
-
-def gather_x_kernel(l1, l2, left, right, left2, right2, l1x, l2x, up1, down1, up2, down2):
+def paired(base, count, j):
+    return (pl.ds(base + count * (j // 2), count), pl.ds(128 * (j % 2), 128))
+
+
+def face_x_kernel(c, left, right, up, down):
+    for r in range(10):
+        up[pl.ds(32 * r, 32)] = c[22 + r]
+        down[pl.ds(32 * r, 32)] = c[r]
+    for j in range(5):
+        up[paired(320, 11, j)] = left[pl.ds(11 * j, 11)]
+        down[paired(320, 11, j)] = right[pl.ds(11 * j, 11)]
+
+
+def gather_x_kernel(before, after, l1, l2, left, right, l1x, l2x, up, down):
+    for i in range(20):
+        row = before[pl.ds(32 * i, 32)] if i < 10 else after[pl.ds(32 * (i - 10), 32)]
+        up[pl.ds(10 * i, 10)] = row[22:32]
+        down[pl.ds(10 * i, 10)] = row[0:10]
+    up[pl.ds(200, 8)] = jnp.zeros((8, 256), F32)
+    down[pl.ds(200, 8)] = jnp.zeros((8, 256), F32)
     for i in range(38):
         if i < 12:
             l1x[i, :18] = left[pl.ds(72 + 18 * i, 18)]
@@ -193,7 +221,7 @@
         low = []
         high = []
         if j < 5:
-            low.append(rolled(left2[pl.ds(11 * j, 11)]))
+            low.append(rolled(before[paired(320, 11, j)]))
         if 2 <= j < 8:
             low.append(left[pl.ds(11 * (j - 2), 11)])
         if 8 <= j < 13:
@@ -207,30 +235,35 @@
         if 8 <= j < 13:
             high.append(right[pl.ds(11 * (j - 8), 11)])
         if 10 <= j < 15:
-            high.append(rolled(right2[pl.ds(11 * (j - 10), 11)]))
+            high.append(rolled(after[paired(320, 11, j - 10)]))
         row = jnp.where(lower, sum(low, jnp.zeros((11, 128), F32)), sum(high, jnp.zeros((11, 128), F32)))
         l2x[j, :11] = row
         l2x[j, pl.ds(11, 5)] = jnp.zeros((5, 128), F32)
-        up1[pl.ds(11 * j, 11)] = row
-        down1[pl.ds(11 * j, 11)] = row
-        up2[pl.ds(5 * j, 5)] = row[6:11]
-        down2[pl.ds(5 * j, 5)] = row[0:5]
+        up[paired(208, 11, j)] = row
+        down[paired(208, 11, j)] = row
     for i in range(38):
-        up1[pl.ds(176 + 12 * i, 12)] = l1x[i, 6:18]
-        down1[pl.ds(176 + 12 * i, 12)] = l1x[i, 0:12]
-
-
-def upper_kernel(taps, l1x, l2x, left, right, left2, right2, y1, y2, z1h, z1l, z2h, z2l, out,
-                 f1, f2, v1, v2, w1, w2, mid):
+        up[paired(296, 12, i)] = l1x[i, 6:18]
+        down[paired(296, 12, i)] = l1x[i, 0:12]
+
+
+def second_kernel(left, right, up, down):
+    for j in range(16):
+        rows, lanes = paired(208, 11, j)
+        up[pl.ds(5 * j, 5)] = left[pl.ds(rows.start + 6, 5), lanes]
+        down[pl.ds(5 * j, 5)] = right[pl.ds(rows.start, 5), lanes]
+
+
+def upper_kernel(taps, l1x, l2x, left, right, left2, right2, y1, y2, z1h, z1l, z2h, z2l, up1, direct,
+                 out, f1, f2, v1, v2, w1, w2, mid, fine):
     for i in range(38):
-        f1[i, pl.ds(0, 12)] = left[pl.ds(176 + 12 * i, 12)]
+        f1[i, pl.ds(0, 12)] = left[paired(296, 12, i)]
         f1[i, pl.ds(12, 18)] = l1x[i, :18]
-        f1[i, pl.ds(30, 12)] = right[pl.ds(176 + 12 * i, 12)]
+        f1[i, pl.ds(30, 12)] = right[paired(296, 12, i)]
         f1[i, pl.ds(42, 6)] = jnp.zeros((6, 128), F32)
     for j in range(16):
         f2[j, pl.ds(0, 16)] = l2x[j]
-        f2[j, pl.ds(16, 11)] = left[pl.ds(11 * j, 11)]
-        f2[j, pl.ds(27, 11)] = right[pl.ds(11 * j, 11)]
+        f2[j, pl.ds(16, 11)] = left[paired(208, 11, j)]
+        f2[j, pl.ds(27, 11)] = right[paired(208, 11, j)]
         f2[j, pl.ds(38, 5)] = left2[pl.ds(5 * j, 5)]
         f2[j, pl.ds(43, 5)] = right2[pl.ds(5 * j, 5)]
 
@@ -285,33 +318,28 @@
         if a < 8:
             mid[2 * a + 2] = mid[2 * a + 2] + 0.5 * (top(a) + top(a + 1))
     for a in range(16):
-        out[2 * a] = 0.75 * mid[a + 1] + 0.125 * (mid[a] + mid[a + 2])
-        out[2 * a + 1] = 0.5 * (mid[a + 1] + mid[a + 2])
-
-
-def finest_kernel(taps, c, before, after, left, right, middle, y0, z0h, z0l, up1, out, v, wh, wl):
-    def section(own, i, base, at):
-        b = left[pl.ds(base, 48)][10 * at:10 * at + 16]
-        a = right[pl.ds(base, 48)][10 * at:10 * at + 16]
-        high, low = halves(jnp.concatenate([own, b, a], 0))
-        v[i] = dot(y0[...], jnp.concatenate([high, low, high], 0))
-
-    for i in range(10):
-        section(before[i], i, 40 * (i // 4), i % 4)
-    for i in (10, 11):
-        section(c[i - 10], i, 40 * (i // 4), i % 4)
-
-    @pl.loop(3, 10)
+        fine[2 * a] = 0.75 * mid[a + 1] + 0.125 * (mid[a] + mid[a + 2])
+        fine[2 * a + 1] = 0.5 * (mid[a + 1] + mid[a + 2])
+    for q in range(4):
+        rows = pl.ds(8 * q, 8)
+        high, low = halves(fine[rows].reshape(256, 128))
+        out[rows] = direct[rows] + (dot(high, up1[...]) + dot(low, up1[...])).reshape(8, 32, 256)
+
+
+def section(table, own, left, right, base, at):
+    b = left[pl.ds(base, 48)][10 * at:10 * at + 16]
+    a = right[pl.ds(base, 48)][10 * at:10 * at + 16]
+    high, low = halves(jnp.concatenate([own, b, a], 0))
+    return dot(table[...], jnp.concatenate([high, low, high], 0))
+
+
+def inner_kernel(taps, c, left, right, y0, w, v):
+    @pl.loop(0, 8)
     def _(q):
         base = pl.multiple_of(40 * q, 8)
         for at in range(4):
             i = 4 * q + at
-            section(c[i - 10], i, base, at)
-
-    for i in (40, 41):
-        section(c[i - 10], i, 40 * (i // 4), i % 4)
-    for i in range(42, 52):
-        section(after[i - 42], i, 40 * (i // 4), i % 4)
+            v[i] = section(y0, c[i], left, right, base, at)
 
     @pl.loop(0, 4)
     def _(g):
@@ -322,22 +350,48 @@
                 lanes = pl.ds(128 * h, 128)
                 for base in range(0, 32, 8):
                     sums = [None] * 8
-                    for i in range(base, base + 8 + TAPS - 1):
+                    for i in range(max(base - RADIUS, 0), min(base + 8 + RADIUS, 32)):
                         value = v[i, rows, lanes]
                         for m in range(8):
-                            k = i - base - m
+                            k = i - base - m + RADIUS
                             if 0 <= k < TAPS:
                                 term = scale[k] * value
                                 sums[m] = term if sums[m] is None else sums[m] + term
-                    for m in range(0, 8, 2):
-                        high, low = halves(jnp.concatenate([sums[m], sums[m + 1]], 0))
-                        at = (pl.ds(8 * (base + m), 16), pl.ds(256 * member + 128 * h, 128))
-                        wh[at] = high
-                        wl[at] = low
+                    for m in range(8):
+                        w[base + m, rows, lanes] = sums[m]
+
+
+def finest_kernel(taps, before, after, left, right, y0, z0h, z0l, w, out, v, wh, wl):
+    for i in range(20):
+        own = before[pl.ds(32 * i, 32)] if i < 10 else after[pl.ds(32 * (i - 10), 32)]
+        b = left[pl.ds(10 * i, 16)]
+        a = right[pl.ds(10 * i, 16)]
+        high, low = halves(jnp.concatenate([own, b, a], 0))
+        v[i] = dot(y0[...], jnp.concatenate([high, low, high], 0))
+
+    @pl.loop(0, 4)
+    def _(g):
+        for member in range(3):
+            rows = pl.ds(pl.multiple_of(32 * member + 8 * g, 8), 8)
+            scale = [taps[0, member * TAPS + k] for k in range(TAPS)]
+            for h in range(2):
+                lanes = pl.ds(128 * h, 128)
+                for base in range(0, 32, 2):
+                    sums = []
+                    for m in (base, base + 1):
+                        total = w[m, rows, lanes]
+                        for r in range(10):
+                            if r >= m:
+                                total = total + scale[r - m] * v[r, rows, lanes]
+                            if r <= m - 22:
+                                total = total + scale[42 + r - m] * v[10 + r, rows, lanes]
+                        sums.append(total)
+                    high, low = halves(jnp.concatenate(sums, 0))
+                    at = (pl.ds(8 * base, 16), pl.ds(256 * member + 128 * h, 128))
+                    wh[at] = high
+                    wl[at] = low
         cols = pl.ds(pl.multiple_of(8 * g, 8), 8)
         total = dot(wh[...], z0h[...]) + dot(wl[...], z0h[...]) + dot(wh[...], z0l[...])
-        high, low = halves(middle[:, cols].reshape(256, 128))
-        total = total + dot(high, up1[...]) + dot(low, up1[...])
         out[:, cols] = total.reshape(32, 8, 256)
 
 
@@ -363,52 +417,61 @@
 
 
 def body(charges, kernel_taps):
-    ry, rz, ry2, rz2, offsets0, basis1, basis2, up2, up1 = tables()
+    offsets0, basis1, basis2, up2, up1 = tables()
     taps = kernel_taps.reshape(3, 63)
     b16 = lambda x: jnp.asarray(x, BF)
-    before = shift(charges[22:], "gx", 1)
-    after = shift(charges[:10], "gx", -1)
-    l1, l2, s_up, s_down, s_two = call(
+    l1, l2, s_up, s_down, o_up, o_down = call(
         restrict_kernel,
-        [((18, 24, 128), F32), ((6, 16, 128), F32), ((288, 128), F32), ((288, 128), F32), ((56, 128), F32)],
-        [((18, 24, 256), F32), ((12, 16, 128), F32)], 0, 5, 10**8, 2 * 10**6, name="restrict",
-    )(charges, b16(ry), b16(rz), b16(ry2), b16(rz2))
+        [((18, 24, 128), F32), ((6, 16, 128), F32), ((288, 128), F32), ((288, 128), F32),
+         ((328, 256), F32), ((328, 256), F32)],
+        [((18, 24, 256), F32), ((12, 16, 128), F32)], 0, 1, 10**8, 2 * 10**6, name="restrict",
+    )(charges)
     x_left = shift(s_up, "gx", 1)
     x_right = shift(s_down, "gx", -1)
-    x_left2 = shift(s_two, "gx", 2)
-    x_right2 = shift(s_two, "gx", -2)
+    own_left = shift(o_up, "gy", 1)
+    own_right = shift(o_down, "gy", -1)
+    taps, l1 = lax.optimization_barrier((taps, l1))
     y0, y1, y2, z0h, z0l, z1h, z1l, z2h, z2l = call(
         matrices_kernel,
         [((96, 192), BF), ((96, 144), BF), ((96, 144), BF), ((768, 256), BF), ((768, 256), BF),
          ((384, 128), BF), ((384, 128), BF), ((384, 128), BF), ((384, 128), BF)],
         [], 1, 5, 10**8, 4 * 10**6, name="matrices",
     )(taps, jnp.asarray(offsets0), jnp.asarray(basis1), jnp.asarray(basis2), b16(up2))
-    l1x, l2x, t_up, t_down, t_up2, t_down2 = call(
+    x_left, x_right, y0 = lax.optimization_barrier((x_left, x_right, y0))
+    c_up, c_down = call(
+        face_x_kernel, [((360, 256), F32), ((360, 256), F32)], [], 0, 3, 10**6, 2 * 10**6, name="face_x",
+    )(charges, x_left, x_right)
+    before = shift(c_up, "gx", 1)
+    after = shift(c_down, "gx", -1)
+    y0, c_up, c_down = lax.optimization_barrier((y0, c_up, c_down))
+    inner, = call(
+        inner_kernel, [((32, 96, 256), F32)], [((32, 96, 256), F32)], 1, 5, 10**9, 6 * 10**6, name="inner",
+    )(taps, charges, own_left, own_right, y0)
+    before, after, inner = lax.optimization_barrier((before, after, inner))
+    l1x, l2x, f_up, f_down = call(
         gather_x_kernel,
-        [((38, 24, 128), F32), ((16, 16, 128), F32), ((632, 128), F32), ((632, 128), F32),
-         ((80, 128), F32), ((80, 128), F32)],
-        [], 0, 6, 10**6, 2 * 10**6, name="gather_x",
-    )(l1, l2, x_left, x_right, x_left2, x_right2)
-    f_up, f_down = call(
-        face_kernel, [((528, 256), F32), ((528, 256), F32)], [], 0, 3, 10**6, 3 * 10**6, name="faces",
-    )(charges, before, after)
+        [((38, 24, 128), F32), ((16, 16, 128), F32), ((528, 256), F32), ((528, 256), F32)],
+        [], 0, 6, 10**6, 5 * 10**6, name="gather_x",
+    )(before, after, l1, l2, x_left, x_right)
     left = shift(f_up, "gy", 1)
     right = shift(f_down, "gy", -1)
-    y_left = shift(t_up, "gy", 1)
-    y_right = shift(t_down, "gy", -1)
-    y_left2 = shift(t_up2, "gy", 2)
-    y_right2 = shift(t_down2, "gy", -2)
-    middle, = call(
-        upper_kernel, [((32, 32, 128), F32)],
+    t_up, t_down = call(
+        second_kernel, [((80, 128), F32), ((80, 128), F32)], [], 0, 2, 10**5, 10**6, name="second",
+    )(left, right)
+    left2 = shift(t_up, "gy", 1)
+    right2 = shift(t_down, "gy", -1)
+    y0, t_up, t_down = lax.optimization_barrier((y0, t_up, t_down))
+    direct, = call(
+        finest_kernel, [((32, 32, 256), F32)],
+        [((20, 96, 256), F32), ((256, 768), BF), ((256, 768), BF)],
+        1, 9, 2 * 10**9, 6 * 10**6, name="finest",
+    )(taps, before, after, left, right, y0, z0h, z0l, inner)
+    result, = call(
+        upper_kernel, [((32, 32, 256), F32)],
         [((38, 48, 128), F32), ((16, 48, 128), F32), ((38, 96, 128), F32), ((32, 96, 128), F32),
-         ((18, 96, 128), F32), ((11, 96, 128), F32), ((18, 32, 128), F32)],
-        1, 13, 4 * 10**8, 4 * 10**6, name="upper",
-    )(taps, l1x, l2x, y_left, y_right, y_left2, y_right2, y1, y2, z1h, z1l, z2h, z2l)
-    result, = call(
-        finest_kernel, [((32, 32, 256), F32)],
-        [((52, 96, 256), F32), ((256, 768), BF), ((256, 768), BF)],
-        1, 11, 2 * 10**9, 6 * 10**6, name="finest",
-    )(taps, charges, before, after, left, right, middle, y0, z0h, z0l, b16(up1))
+         ((18, 96, 128), F32), ((11, 96, 128), F32), ((18, 32, 128), F32), ((32, 32, 128), F32)],
+        1, 15, 4 * 10**8, 4 * 10**6, name="upper",
+    )(taps, l1x, l2x, left, right, left2, right2, y1, y2, z1h, z1l, z2h, z2l, b16(up1), direct)
     return result
 
 

time: 102 us -> 76.7 us (0.75)
  the two profiles are of different devices: /device:TPU:1 before, /device:TPU:216 now
where the time goes in v2:
time: 76.7 us; the launch traced here: 76.4 us
  Pallas kernels  25.9 us (34%)
  waiting for transfers between devices  24.8 us (32%)
  starting transfers between devices  18.2 us (24%)
  local copies, waits for them, and re-layouts  7.31 us (10%)
    ppermute x10, waiting for transfers between devices, shift(): return lax.ppermute(x, axis, [(i, (i + by) % n) for i in range(n)])  24.8 us
    ppermute x10, starting transfers between devices, shift(): return lax.ppermute(x, axis, [(i, (i + by) % n) for i in range(n)])  18.2 us
    pallas_call x1, Pallas kernels, body(): call(upper_kernel, [((32, 32, 256), F32)], [((38, 48, 128), F32), ((16, 4...  10.4 us
    unnamed x16, local copies, waits for them, and re-layouts  6.54 us
    pallas_call x1, Pallas kernels, body(): call(inner_kernel, [((32, 96, 256), F32)], [((32, 96, 256), F32)], 1, 5,...  5.98 us
    pallas_call x1, Pallas kernels, body(): call(finest_kernel, [((32, 32, 256), F32)], [((20, 96, 256), F32), ((256,...  5.18 us
    pallas_call x1, Pallas kernels, body(): call(matrices_kernel, [((96, 192), BF), ((96, 144), BF), ((96, 144), BF),...  3.05 us
  transfers between devices with their start and end apart: 10, of which 4 were waited for; matrix products, arithmetic and copies ran while one was open for 1% of the time, Pallas kernels for 19%

profile of v2, /device:TPU:216, one launch (start us, length us, event | category | flops | bytes accessed | tf_op | source)
XLA Modules:
  0.0 76.4 jit_solution(1532816894267473196)
XLA Ops:
  0.0 1.2 %copy-done = f32[32,32,256]{2,1,0:T(8,128)S(1)} copy-done((f32[32,32,256]{2,1,0:T(8,128)S(1)}, f32[32,32,256]{2,1,0:T(8,128)}, u32[]{:S(2)}) %copy-start) | copy-done | bytes 1048600
  1.2 1.0 %restrict.1 = (f32[18,24,128]{2,1,0:T(8,128)S(1)}, f32[6,16,128]{2,1,0:T(8,128)S(1)}, f32[288,128]{1,0:T(8,128)S(1)}, f32[288,128]{1,0:T(8,128)S(1)}, f32[328,256]{1,0:T(8,128)S(1)}, /*index=5*/f32[328,256]{1,0:T(8,128)S(1)}) custom-call(f32[32,32,256]{2,1,0:T(8,128)S(1)} %copy-done), custom_call_target="tpu_custom_call" | custom-call | flops 100000000 | bytes 2000000 | tf_op jit(solution)/shard_map/restrict/pallas_call | solution.py:423
  2.2 0.1 collective-permute-start
  2.3 2.9 %collective-permute-start.1 = (f32[288,128]{1,0:T(8,128)S(1)}, f32[288,128]{1,0:T(8,128)S(1)}, u32[]{:S(2)}, u32[]{:S(2)}) collective-permute-start(f32[288,128]{1,0:T(8,128)S(1)} %get-tuple-element.41), channel_id=1, source_target_pairs={{0,240},{16,0},{32,16},{48,32},{64,48},{80,64},{96,80},{112,96},{1... | collective-permute-start | bytes 442376 | tf_op jit(solution)/shard_map/ppermute | solution.py:416
  5.2 3.9 %collective-permute-start.5 = (f32[328,256]{1,0:T(8,128)S(1)}, f32[328,256]{1,0:T(8,128)S(1)}, u32[]{:S(2)}, u32[]{:S(2)}) collective-permute-start(f32[328,256]{1,0:T(8,128)S(1)} %get-tuple-element.48), channel_id=1, source_target_pairs={{0,15},{1,0},{2,1},{3,2},{4,3},{5,4},{6,5},{7,6},{8,7},{9,8},{10,9... | collective-permute-start | bytes 1007624 | tf_op jit(solution)/shard_map/ppermute | solution.py:416
  9.1 0.8 %reshape.3.taps = f32[3,63]{1,0:T(4,128)S(1)} reshape(f32[3,3,21]{2,1,0:T(4,128)} %param.8) | data formatting | bytes 1512 | tf_op jit(solution)/shard_map/reshape | solution.py:421
  9.9 1.1 %copy-done.3 = f32[21,32,144]{2,1,0:T(8,128)S(1)} copy-done((f32[21,32,144]{2,1,0:T(8,128)S(1)}, f32[21,32,144]{2,1,0:T(8,128)}, u32[]{:S(2)}) %copy-start.3) | copy-done | bytes 387096
  11.0 1.1 %copy-done.4 = f32[21,32,144]{2,1,0:T(8,128)S(1)} copy-done((f32[21,32,144]{2,1,0:T(8,128)S(1)}, f32[21,32,144]{2,1,0:T(8,128)}, u32[]{:S(2)}) %copy-start.4) | copy-done | bytes 387096
  12.1 0.8 copy-done.6
  12.8 0.7 copy-done.7
  13.6 3.1 %matrices.1 = (bf16[96,192]{1,0:T(8,128)(2,1)S(1)}, bf16[96,144]{1,0:T(8,128)(2,1)S(1)}, bf16[96,144]{1,0:T(8,128)(2,1)S(1)}, bf16[768,256]{1,0:T(8,128)(2,1)S(1...) custom-call(f32[3,63]{1,0:T(4,128)S(1)} %reshape.3.taps, ...), custom_call_target="tpu_custom_call" | custom-call | flops 100000000 | bytes 4000000 | tf_op jit(solution)/shard_map/matrices/pallas_call | solution.py:434
  16.7 3.5 %collective-permute-start.2 = (f32[360,256]{1,0:T(8,128)S(1)}, f32[360,256]{1,0:T(8,128)S(1)}, u32[]{:S(2)}, u32[]{:S(2)}) collective-permute-start(f32[360,256]{1,0:T(8,128)S(1)} %get-tuple-element.45), channel_id=1, source_target_pairs={{0,16},{16,32},{32,48},{48,64},{64,80},{80,96},{96,112},{112,128},... | collective-permute-start | bytes 1105928 | tf_op jit(solution)/shard_map/ppermute | solution.py:416
  20.2 1.0 %collective-permute-done.4.left = f32[328,256]{1,0:T(8,128)S(1)} collective-permute-done((f32[328,256]{1,0:T(8,128)S(1)}, f32[328,256]{1,0:T(8,128)S(1)}, u32[]{:S(2)}, u32[]{:S(2)}) %collective-permute-start.4) | collective-permute-done | bytes 335904 | tf_op jit(solution)/shard_map/ppermute | solution.py:416
  21.2 6.0 %inner.1.w = f32[32,96,256]{2,1,0:T(8,128)S(1)} custom-call(f32[3,63]{1,0:T(4,128)S(1)} %reshape.3.taps, f32[32,32,256]{2,1,0:T(8,128)S(1)} %copy-done.1, f32[328,256]{1,0:T(8,128)S(1)} %collective-permute-done.4.left, f32[328,256]{1,0:T(8,128)S(1)} %collective-permute-done.5.right, bf16[96,192]{1,0:T(8,128)(2,1)S(1)} %get-tuple-element.67.y0), custom_call_target="tpu_custom_call" | custom-call | flops 1000000000 | bytes 6000000 | tf_op jit(solution)/shard_map/inner/pallas_call | solution.py:447
  27.2 1.6 %copy-done.2 = f32[32,96,256]{2,1,0:T(8,128)} copy-done((f32[32,96,256]{2,1,0:T(8,128)}, f32[32,96,256]{2,1,0:T(8,128)S(1)}, u32[]{:S(2)}) %copy-start.2) | copy-done | bytes 3145752
  28.8 4.3 %collective-permute-done.2.before = f32[360,256]{1,0:T(8,128)S(1)} collective-permute-done((f32[360,256]{1,0:T(8,128)S(1)}, f32[360,256]{1,0:T(8,128)S(1)}, u32[]{:S(2)}, u32[]{:S(2)}) %collective-permute-start.2) | collective-permute-done | bytes 368672 | tf_op jit(solution)/shard_map/ppermute | solution.py:416
  33.1 6.8 %collective-permute-done.3.after = f32[360,256]{1,0:T(8,128)S(1)} collective-permute-done((f32[360,256]{1,0:T(8,128)S(1)}, f32[360,256]{1,0:T(8,128)S(1)}, u32[]{:S(2)}, u32[]{:S(2)}) %collective-permute-start.3) | collective-permute-done | bytes 368672 | tf_op jit(solution)/shard_map/ppermute | solution.py:416
  39.9 0.2 gather_x.1
  40.2 3.8 %collective-permute-start.7 = (f32[528,256]{1,0:T(8,128)S(1)}, f32[528,256]{1,0:T(8,128)S(1)}, u32[]{:S(2)}, u32[]{:S(2)}) collective-permute-start(f32[528,256]{1,0:T(8,128)S(1)} %get-tuple-element.58), channel_id=1, source_target_pairs={{0,15},{1,0},{2,1},{3,2},{4,3},{5,4},{6,5},{7,6},{8,7},{9,8},{10,9... | collective-permute-start | bytes 1622024 | tf_op jit(solution)/shard_map/ppermute | solution.py:416
  44.0 12.7 %collective-permute-done.6.left = f32[528,256]{1,0:T(8,128)S(1)} collective-permute-done((f32[528,256]{1,0:T(8,128)S(1)}, f32[528,256]{1,0:T(8,128)S(1)}, u32[]{:S(2)}, u32[]{:S(2)}) %collective-permute-start.6) | collective-permute-done | bytes 540704 | tf_op jit(solution)/shard_map/ppermute | solution.py:416
  56.8 0.1 collective-permute-start.8
  56.9 3.8 %collective-permute-start.9 = (f32[80,128]{1,0:T(8,128)S(1)}, f32[80,128]{1,0:T(8,128)S(1)}, u32[]{:S(2)}, u32[]{:S(2)}) collective-permute-start(f32[80,128]{1,0:T(8,128)S(1)} %get-tuple-element.60), channel_id=1, source_target_pairs={{0,15},{1,0},{2,1},{3,2},{4,3},{5,4},{6,5},{7,6},{8,7},{9,8},{10,9... | collective-permute-start | bytes 122888 | tf_op jit(solution)/shard_map/ppermute | solution.py:416
  60.7 5.2 %finest.1.direct = f32[32,32,256]{2,1,0:T(8,128)S(1)} custom-call(f32[3,63]{1,0:T(4,128)S(1)} %reshape.3.taps, f32[360,256]{1,0:T(8,128)S(1)} %collective-permute-done.2.before, f32[360,256]{1,0:T(8,128)S(1)} %collective-permute-done.3.after, f32[528,256]{1,0:T(8,128)S(1)} %collective-permute-done.6.left, f32[528,256]{1,0:T(8,128)S(1)} %collective-permute-done.7.right, ...), custom_call_target="tpu_custom_call" | custom-call | flops 2000000000 | bytes 6000000 | tf_op jit(solution)/shard_map/finest/pallas_call | solution.py:464
  66.0 10.4 %upper.1 = f32[32,32,256]{2,1,0:T(8,128)} custom-call(f32[3,63]{1,0:T(4,128)S(1)} %reshape.3.taps, f32[38,24,128]{2,1,0:T(8,128)S(1)} %get-tuple-element.55.l1x, f32[16,16,128]{2,1,0:T(8,128)S(1)} %get-tuple-element.56.l2x, f32[528,256]{1,0:T(8,128)S(1)} %collective-permute-done.6.left, f32[528,256]{1,0:T(8,128)S(1)} %collective-permute-done.7.right, ...), custom_call_target="tpu_custom_call" | custom-call | flops 400000000 | bytes 4000000 | tf_op jit(solution)/shard_map/upper/pallas_call | solution.py:469
  (21 shorter events, 0.2 us)
Async XLA Ops:
  0.0 1.2 %copy-start = (f32[32,32,256]{2,1,0:T(8,128)S(1)}, f32[32,32,256]{2,1,0:T(8,128)}, u32[]{:S(2)}) copy-start(f32[32,32,256]{2,1,0:T(8,128)} %c.5) | copy-start | bytes 3145732
  1.2 15.4 %copy-start.1 = (f32[32,32,256]{2,1,0:T(8,128)S(1)}, f32[32,32,256]{2,1,0:T(8,128)}, u32[]{:S(2)}) copy-start(f32[32,32,256]{2,1,0:T(8,128)} %c.5) | copy-start | bytes 3145732
  2.2 14.4 %collective-permute-start = (f32[288,128]{1,0:T(8,128)S(1)}, f32[288,128]{1,0:T(8,128)S(1)}, u32[]{:S(2)}, u32[]{:S(2)}) collective-permute-start(f32[288,128]{1,0:T(8,128)S(1)} %get-tuple-element.40), channel_id=1, source_target_pairs={{0,16},{16,32},{32,48},{48,64},{64,80},{80,96},{96,112},{112,128},... | collective-permute-start | bytes 442376 | tf_op jit(solution)/shard_map/ppermute | solution.py:416
  2.3 14.3 %collective-permute-start.1 = (f32[288,128]{1,0:T(8,128)S(1)}, f32[288,128]{1,0:T(8,128)S(1)}, u32[]{:S(2)}, u32[]{:S(2)}) collective-permute-start(f32[288,128]{1,0:T(8,128)S(1)} %get-tuple-element.41), channel_id=1, source_target_pairs={{0,240},{16,0},{32,16},{48,32},{64,48},{80,64},{96,80},{112,96},{1... | collective-permute-start | bytes 442376 | tf_op jit(solution)/shard_map/ppermute | solution.py:416
  5.2 15.9 %collective-permute-start.4 = (f32[328,256]{1,0:T(8,128)S(1)}, f32[328,256]{1,0:T(8,128)S(1)}, u32[]{:S(2)}, u32[]{:S(2)}) collective-permute-start(f32[328,256]{1,0:T(8,128)S(1)} %get-tuple-element.47), channel_id=1, source_target_pairs={{0,1},{1,2},{2,3},{3,4},{4,5},{5,6},{6,7},{7,8},{8,9},{9,10},{10,1... | collective-permute-start | bytes 1007624 | tf_op jit(solution)/shard_map/ppermute | solution.py:416
  5.2 15.9 %collective-permute-start.5 = (f32[328,256]{1,0:T(8,128)S(1)}, f32[328,256]{1,0:T(8,128)S(1)}, u32[]{:S(2)}, u32[]{:S(2)}) collective-permute-start(f32[328,256]{1,0:T(8,128)S(1)} %get-tuple-element.48), channel_id=1, source_target_pairs={{0,15},{1,0},{2,1},{3,2},{4,3},{5,4},{6,5},{7,6},{8,7},{9,8},{10,9... | collective-permute-start | bytes 1007624 | tf_op jit(solution)/shard_map/ppermute | solution.py:416
  9.9 1.1 %copy-start.3 = (f32[21,32,144]{2,1,0:T(8,128)S(1)}, f32[21,32,144]{2,1,0:T(8,128)}, u32[]{:S(2)}) copy-start(f32[21,32,144]{2,1,0:T(8,128)} %constant.12.clone.basis2) | copy-start | bytes 1161220
  11.0 1.1 %copy-start.4 = (f32[21,32,144]{2,1,0:T(8,128)S(1)}, f32[21,32,144]{2,1,0:T(8,128)}, u32[]{:S(2)}) copy-start(f32[21,32,144]{2,1,0:T(8,128)} %constant.11.clone.basis1) | copy-start | bytes 1161220
  12.1 0.8 copy-start.6
  12.8 0.7 copy-start.7
  16.7 16.4 %collective-permute-start.2 = (f32[360,256]{1,0:T(8,128)S(1)}, f32[360,256]{1,0:T(8,128)S(1)}, u32[]{:S(2)}, u32[]{:S(2)}) collective-permute-start(f32[360,256]{1,0:T(8,128)S(1)} %get-tuple-element.45), channel_id=1, source_target_pairs={{0,16},{16,32},{32,48},{48,64},{64,80},{80,96},{96,112},{112,128},... | collective-permute-start | bytes 1105928 | tf_op jit(solution)/shard_map/ppermute | solution.py:416
  20.2 19.7 %collective-permute-start.3 = (f32[360,256]{1,0:T(8,128)S(1)}, f32[360,256]{1,0:T(8,128)S(1)}, u32[]{:S(2)}, u32[]{:S(2)}) collective-permute-start(f32[360,256]{1,0:T(8,128)S(1)} %get-tuple-element.46), channel_id=1, source_target_pairs={{0,240},{16,0},{32,16},{48,32},{64,48},{80,64},{96,80},{112,96},{1... | collective-permute-start | bytes 1105928 | tf_op jit(solution)/shard_map/ppermute | solution.py:416
  27.2 1.6 %copy-start.2 = (f32[32,96,256]{2,1,0:T(8,128)}, f32[32,96,256]{2,1,0:T(8,128)S(1)}, u32[]{:S(2)}) copy-start(f32[32,96,256]{2,1,0:T(8,128)S(1)} %inner.1.w) | copy-start | bytes 9437188
  40.1 16.7 %collective-permute-start.6 = (f32[528,256]{1,0:T(8,128)S(1)}, f32[528,256]{1,0:T(8,128)S(1)}, u32[]{:S(2)}, u32[]{:S(2)}) collective-permute-start(f32[528,256]{1,0:T(8,128)S(1)} %get-tuple-element.57), channel_id=1, source_target_pairs={{0,1},{1,2},{2,3},{3,4},{4,5},{5,6},{6,7},{7,8},{8,9},{9,10},{10,1... | collective-permute-start | bytes 1622024 | tf_op jit(solution)/shard_map/ppermute | solution.py:416
  40.2 16.6 %collective-permute-start.7 = (f32[528,256]{1,0:T(8,128)S(1)}, f32[528,256]{1,0:T(8,128)S(1)}, u32[]{:S(2)}, u32[]{:S(2)}) collective-permute-start(f32[528,256]{1,0:T(8,128)S(1)} %get-tuple-element.58), channel_id=1, source_target_pairs={{0,15},{1,0},{2,1},{3,2},{4,3},{5,4},{6,5},{7,6},{8,7},{9,8},{10,9... | collective-permute-start | bytes 1622024 | tf_op jit(solution)/shard_map/ppermute | solution.py:416
  56.8 9.1 %collective-permute-start.8 = (f32[80,128]{1,0:T(8,128)S(1)}, f32[80,128]{1,0:T(8,128)S(1)}, u32[]{:S(2)}, u32[]{:S(2)}) collective-permute-start(f32[80,128]{1,0:T(8,128)S(1)} %get-tuple-element.59), channel_id=1, source_target_pairs={{0,1},{1,2},{2,3},{3,4},{4,5},{5,6},{6,7},{7,8},{8,9},{9,10},{10,1... | collective-permute-start | bytes 122888 | tf_op jit(solution)/shard_map/ppermute | solution.py:416
  56.9 9.0 %collective-permute-start.9 = (f32[80,128]{1,0:T(8,128)S(1)}, f32[80,128]{1,0:T(8,128)S(1)}, u32[]{:S(2)}, u32[]{:S(2)}) collective-permute-start(f32[80,128]{1,0:T(8,128)S(1)} %get-tuple-element.60), channel_id=1, source_target_pairs={{0,15},{1,0},{2,1},{3,2},{4,3},{5,4},{6,5},{7,6},{8,7},{9,8},{10,9... | collective-permute-start | bytes 122888 | tf_op jit(solution)/shard_map/ppermute | solution.py:416
  60.7 5.2 %copy-start.5 = (bf16[128,256]{1,0:T(8,128)(2,1)S(1)}, bf16[128,256]{1,0:T(8,128)(2,1)}, u32[]{:S(2)}) copy-start(bf16[128,256]{1,0:T(8,128)(2,1)} %constant.14.clone.up1) | copy-start | bytes 196612

commit v3 on v2

v3 whole, which is shorter than its diff:
```python
import jax
import jax.numpy as jnp
from jax import lax
from jax.experimental import pallas as pl
from jax.experimental.pallas import tpu as pltpu
from jax.sharding import PartitionSpec as P

SPLINE = (0.125, 0.5, 0.75, 0.5, 0.125)
RADIUS = 10
TAPS = 21
BF = jnp.bfloat16
F32 = jnp.float32
VMEM_LIMIT = 48 * 1024 * 1024


def halves(x):
    high = x.astype(BF)
    return high, (x - high.astype(F32)).astype(BF)


def dot(a, b):
    return jnp.dot(a, b, preferred_element_type=F32)


def spline_sum(read, center, low, high):
    total = None
    for k in range(-2, 3):
        if low <= 2 * center + k <= high:
            term = SPLINE[k + 2] * read(2 * center + k)
            total = term if total is None else total + term
    return total


def matrices_kernel(taps, y0, y1, y2, z0h, z0l, z1h, z1l, z2h, z2l, up1):
    def iota(shape, dim):
        return lax.broadcasted_iota(jnp.int32, shape, dim)

    def pick(level, member, offsets):
        table = jnp.zeros(offsets.shape, F32)
        for k in range(TAPS):
            table = jnp.where(offsets == k, taps[level, member, k], table)
        return table

    def cycle(level, member, length):
        offsets = (iota((length, length), 0) - iota((length, length), 1) + RADIUS) & (length - 1)
        return pick(level, member, offsets)

    def spread(lanes, width, pieces):
        cols = lanes
        for _ in range(2):
            cols = jnp.where(cols >= width, cols - width, cols)
        place = jnp.full(lanes.shape, -99, jnp.int32)
        for begin, end, position in pieces:
            place = jnp.where((cols >= begin) & (cols < end), cols - begin + position, place)
        return place

    def put(out, rows, table, width):
        high, low = halves(table)
        out[rows] = jnp.where(iota(table.shape, 1) < 2 * width, high.astype(F32), low.astype(F32)).astype(BF)

    def product(weights, table):
        high, low = halves(table)
        return dot(weights, high) + dot(weights, low)

    place0 = spread(iota((32, 192), 1), 64, ((0, 32, 0), (32, 42, -10), (48, 58, 32))) - iota((32, 192), 0) + RADIUS
    place1 = spread(iota((32, 144), 1), 48, ((0, 12, -11), (12, 30, -1), (30, 42, 15)))
    place1 = place1 - (iota((32, 144), 0) - 1) + RADIUS
    place2 = spread(iota((32, 144), 1), 48, ((0, 11, -1), (16, 27, -9), (27, 38, 7), (38, 43, -11), (43, 48, 15)))
    place2 = place2 - (iota((32, 144), 0) - 1) + RADIUS
    columns = iota((32, 32), 1) - 1
    lift1 = jnp.where(columns < 17, spline_of(iota((32, 32), 0) - 2 * columns), 0.0).astype(BF)
    lift2 = jnp.where(columns < 10, spline_of(iota((32, 32), 0) - 1 - 2 * columns), 0.0).astype(BF)
    lift2 = dot(lift1, lift2).astype(BF)
    up2 = cyclic_iota((64, 128), 0, 1, 128).astype(BF)
    up1[...] = cyclic_iota((128, 256), 0, 1, 256).astype(BF)
    for member in range(3):
        rows = pl.ds(32 * member, 32)
        put(y0, rows, pick(0, member, place0), 64)
        put(y1, rows, product(lift1, pick(1, member, place1)), 48)
        put(y2, rows, product(lift2, pick(2, member, place2)), 48)
        high, low = halves(cycle(0, member, 256))
        z0h[pl.ds(256 * member, 256)] = high
        z0l[pl.ds(256 * member, 256)] = low
        high, low = halves(cycle(1, member, 128))
        z1h[pl.ds(128 * member, 128)] = high
        z1l[pl.ds(128 * member, 128)] = low
        high, low = halves(cycle(2, member, 64))
        table = dot(high, up2) + dot(low, up2)
        high, low = halves(table)
        z2h[pl.ds(128 * member, 64)] = high
        z2l[pl.ds(128 * member, 64)] = low
        z2h[pl.ds(128 * member + 64, 64)] = jnp.zeros((64, 128), BF)
        z2l[pl.ds(128 * member + 64, 64)] = jnp.zeros((64, 128), BF)


def spline_iota(shape, offset, coarse_dim, fine_dim, keep=None):
    fine = lax.broadcasted_iota(jnp.int32, shape, fine_dim)
    coarse = lax.broadcasted_iota(jnp.int32, shape, coarse_dim)
    delta = fine - 2 * coarse + offset
    if keep is not None:
        delta = jnp.where(coarse < keep, delta, 99)
    return spline_of(delta)


def spline_of(delta):
    far = jnp.abs(delta)
    return jnp.where(far == 0, 0.75, jnp.where(far == 1, 0.5, jnp.where(far == 2, 0.125, 0.0)))


def cyclic_iota(shape, coarse_dim, fine_dim, fine_len):
    fine = lax.broadcasted_iota(jnp.int32, shape, fine_dim)
    coarse = lax.broadcasted_iota(jnp.int32, shape, coarse_dim)
    return spline_of(((fine - 2 * coarse + 2) & (fine_len - 1)) - 2)


def restrict_kernel(c, l1, l2, up1, down1, face_up, face_down, last, first, s1, s2):
    for r in range(10):
        last[pl.ds(32 * r, 32)] = c[22 + r]
        first[pl.ds(32 * r, 32)] = c[r]
    for i in range(32):
        face_up[pl.ds(10 * i, 10)] = c[i, 22:32]
        face_down[pl.ds(10 * i, 10)] = c[i, 0:10]
    face_up[pl.ds(320, 8)] = jnp.zeros((8, 256), F32)
    face_down[pl.ds(320, 8)] = jnp.zeros((8, 256), F32)
    ry = spline_iota((24, 32), 2, 0, 1, 18).astype(BF)
    for i in range(-1, 17):
        high, low = halves(spline_sum(lambda r: c[r], i, 0, 31))
        s1[i + 1] = dot(ry, high) + dot(ry, low)
    rz = cyclic_iota((256, 128), 1, 0, 256).astype(BF)
    high, low = halves(s1[...].reshape(18 * 24, 256))
    l1[...] = (dot(high, rz) + dot(low, rz)).reshape(18, 24, 128)
    ry2 = spline_iota((16, 24), 1, 0, 1, 11).astype(BF)
    for i in range(-1, 10):
        high, low = halves(spline_sum(lambda r: l1[r + 1], i, -1, 16))
        s2[i + 1] = dot(ry2, high) + dot(ry2, low)
    s2[11] = jnp.zeros((16, 128), F32)
    near = s2[pl.ds(0, 6)].reshape(96, 128)
    far = s2[pl.ds(6, 6)].reshape(96, 128)
    lanes = lax.broadcasted_iota(jnp.int32, (128, 128), 1)
    both = spline_of(((lax.broadcasted_iota(jnp.int32, (128, 128), 0) - 2 * (lanes & 63) + 2) & 127) - 2)
    total = jnp.zeros((96, 128), F32)
    for part, upper in ((near, False), (far, True)):
        weights = jnp.where((lanes >= 64) == upper, both, 0.0).astype(BF)
        high, low = halves(part)
        total = total + dot(high, weights) + dot(low, weights)
    total = total.reshape(6, 16, 128)
    l2[...] = total
    up1[pl.ds(64, 8)] = jnp.zeros((8, 128), F32)
    down1[pl.ds(64, 8)] = jnp.zeros((8, 128), F32)
    for j in range(6):
        up1[pl.ds(11 * j, 11)] = total[j, :11]
        down1[pl.ds(11 * j, 11)] = total[j, :11]
    for r in range(12):
        up1[pl.ds(72 + 18 * r, 18)] = l1[6 + r, :18]
        down1[pl.ds(72 + 18 * r, 18)] = l1[r, :18]


def paired(base, count, j):
    return (pl.ds(base + count * (j // 2), count), pl.ds(128 * (j % 2), 128))


def face_x_kernel(last, first, left, right, up, down):
    up[pl.ds(0, 320)] = last[...]
    down[pl.ds(0, 320)] = first[...]
    lower = lax.broadcasted_iota(jnp.int32, (11, 128), 1) < 64
    for p in range(3):
        even = 2 * p
        odd = min(even + 1, 4)
        a = left[pl.ds(11 * even, 11)]
        b = left[pl.ds(11 * odd, 11)]
        up[paired(320, 11, p)] = jnp.where(lower, pltpu.roll(a, 64, 1), b)
        a = right[pl.ds(11 * even, 11)]
        b = right[pl.ds(11 * odd, 11)]
        down[paired(320, 11, p)] = jnp.where(lower, a, pltpu.roll(b, 64, 1))


def gather_fine_kernel(l1, left, right, l1x, up, down):
    for i in range(38):
        if i < 12:
            l1x[i, :18] = left[pl.ds(72 + 18 * i, 18)]
            l1x[i, pl.ds(18, 6)] = jnp.zeros((6, 128), F32)
        elif i >= 26:
            l1x[i, :18] = right[pl.ds(72 + 18 * (i - 26), 18)]
            l1x[i, pl.ds(18, 6)] = jnp.zeros((6, 128), F32)
        if 10 <= i < 12 or 26 <= i < 28:
            l1x[i] = l1x[i] + l1[i - 10]
        elif 12 <= i < 26:
            l1x[i] = l1[i - 10]
    for i in range(38):
        up[pl.ds(12 * i, 12)] = l1x[i, 6:18]
        down[pl.ds(12 * i, 12)] = l1x[i, 0:12]


def gather_top_kernel(before, after, l2, left, right, l2x, up, down):
    for i in range(20):
        row = before[pl.ds(32 * i, 32)] if i < 10 else after[pl.ds(32 * (i - 10), 32)]
        up[pl.ds(10 * i, 10)] = row[22:32]
        down[pl.ds(10 * i, 10)] = row[0:10]
    up[pl.ds(200, 8)] = jnp.zeros((8, 256), F32)
    down[pl.ds(200, 8)] = jnp.zeros((8, 256), F32)
    lanes = lax.broadcasted_iota(jnp.int32, (11, 128), 1)
    lower = lanes < 64
    rolled = lambda x: pltpu.roll(x, 64, 1)
    for j in range(16):
        low = []
        high = []
        if j < 5:
            slab = before[paired(320, 11, j // 2)]
            low.append(slab if j % 2 == 0 else rolled(slab))
        if 2 <= j < 8:
            low.append(left[pl.ds(11 * (j - 2), 11)])
        if 8 <= j < 13:
            low.append(rolled(left[pl.ds(11 * (j - 8), 11)]))
        if j >= 10:
            low.append(l2[j - 10, :11])
        if j < 5:
            high.append(l2[j, :11])
        if 2 <= j < 8:
            high.append(rolled(right[pl.ds(11 * (j - 2), 11)]))
        if 8 <= j < 13:
            high.append(right[pl.ds(11 * (j - 8), 11)])
        if 10 <= j < 15:
            slab = after[paired(320, 11, (j - 10) // 2)]
            high.append(rolled(slab) if j % 2 == 0 else slab)
        row = jnp.where(lower, sum(low, jnp.zeros((11, 128), F32)), sum(high, jnp.zeros((11, 128), F32)))
        l2x[j, :11] = row
        l2x[j, pl.ds(11, 5)] = jnp.zeros((5, 128), F32)
        up[paired(208, 11, j)] = row
        down[paired(208, 11, j)] = row


def second_kernel(left, right, up, down):
    for j in range(16):
        rows, lanes = paired(208, 11, j)
        up[pl.ds(5 * j, 5)] = left[pl.ds(rows.start + 6, 5), lanes]
        down[pl.ds(5 * j, 5)] = right[pl.ds(rows.start, 5), lanes]


def correlate_x(taps, level, v, w, count, many):
    @pl.loop(0, 12)
    def _(g):
        member = g // 4
        rows = pl.ds(pl.multiple_of(8 * g, 8), 8)
        scale = [taps[level, member, k] for k in range(TAPS)]
        for base in range(0, count, many):
            sums = [None] * many
            for i in range(base, base + many + TAPS - 1):
                value = v[i, rows]
                for m in range(many):
                    k = i - base - m
                    if 0 <= k < TAPS:
                        term = scale[k] * value
                        sums[m] = term if sums[m] is None else sums[m] + term
            for m in range(many):
                w[base + m, rows] = sums[m]


def correlate_z(w, count, high_table, low_table):
    total = jnp.zeros((count * 32, 128), F32)
    for member in range(3):
        high, low = halves(w[:, pl.ds(32 * member, 32)].reshape(count * 32, 128))
        rows = pl.ds(128 * member, 128)
        total = total + dot(high, high_table[rows]) + dot(low, high_table[rows]) + dot(high, low_table[rows])
    return total.reshape(count, 32, 128)


def fine_level_kernel(taps, l1x, left, right, y1, z1h, z1l, mid, f1, v1, w1):
    for i in range(38):
        f1[i, pl.ds(0, 12)] = left[pl.ds(12 * i, 12)]
        f1[i, pl.ds(12, 18)] = l1x[i, :18]
        f1[i, pl.ds(30, 12)] = right[pl.ds(12 * i, 12)]
        f1[i, pl.ds(42, 6)] = jnp.zeros((6, 128), F32)

    @pl.loop(0, 38, unroll=2)
    def _(i):
        high, low = halves(f1[i])
        v1[i] = dot(y1[...], jnp.concatenate([high, low, high], 0))

    correlate_x(taps, 1, v1, w1, 18, 9)
    mid[...] = correlate_z(w1, 18, z1h, z1l)


def upper_kernel(taps, l2x, left, right, left2, right2, y2, z2h, z2l, up1, mid_in, direct, out,
                 f2, v2, w2, mid, fine):
    for j in range(16):
        f2[j, pl.ds(0, 16)] = l2x[j]
        f2[j, pl.ds(16, 11)] = left[paired(208, 11, j)]
        f2[j, pl.ds(27, 11)] = right[paired(208, 11, j)]
        f2[j, pl.ds(38, 5)] = left2[pl.ds(5 * j, 5)]
        f2[j, pl.ds(43, 5)] = right2[pl.ds(5 * j, 5)]

    @pl.loop(0, 16, unroll=2)
    def _(j):
        high, low = halves(f2[j])
        v = dot(y2[...], jnp.concatenate([high, low, high], 0))
        v2[j] = v
        v2[16 + j] = pltpu.roll(v, 64, 1)

    correlate_x(taps, 2, v2, w2, 11, 11)
    v2[pl.ds(0, 11), pl.ds(0, 32)] = correlate_z(w2, 11, z2h, z2l)
    top = lambda i: v2[i + 1, pl.ds(0, 32)]
    for a in range(-1, 9):
        if a >= 0:
            mid[2 * a + 1] = mid_in[2 * a + 1] + (0.75 * top(a) + 0.125 * (top(a - 1) + top(a + 1)))
        if a < 8:
            mid[2 * a + 2] = mid_in[2 * a + 2] + 0.5 * (top(a) + top(a + 1))
    for a in range(16):
        fine[2 * a] = 0.75 * mid[a + 1] + 0.125 * (mid[a] + mid[a + 2])
        fine[2 * a + 1] = 0.5 * (mid[a + 1] + mid[a + 2])
    for q in range(4):
        rows = pl.ds(8 * q, 8)
        high, low = halves(fine[rows].reshape(256, 128))
        out[rows] = direct[rows] + (dot(high, up1[...]) + dot(low, up1[...])).reshape(8, 32, 256)


def section(table, own, left, right, base, at):
    b = left[pl.ds(base, 48)][10 * at:10 * at + 16]
    a = right[pl.ds(base, 48)][10 * at:10 * at + 16]
    high, low = halves(jnp.concatenate([own, b, a], 0))
    return dot(table[...], jnp.concatenate([high, low, high], 0))


def inner_kernel(taps, c, left, right, y0, w, v):
    @pl.loop(0, 8)
    def _(q):
        base = pl.multiple_of(40 * q, 8)
        for at in range(4):
            i = 4 * q + at
            v[i] = section(y0, c[i], left, right, base, at)

    @pl.loop(0, 4)
    def _(g):
        for member in range(3):
            rows = pl.ds(pl.multiple_of(32 * member + 8 * g, 8), 8)
            scale = [taps[0, member, k] for k in range(TAPS)]
            for h in range(2):
                lanes = pl.ds(128 * h, 128)
                for base in range(0, 32, 8):
                    sums = [None] * 8
                    for i in range(max(base - RADIUS, 0), min(base + 8 + RADIUS, 32)):
                        value = v[i, rows, lanes]
                        for m in range(8):
                            k = i - base - m + RADIUS
                            if 0 <= k < TAPS:
                                term = scale[k] * value
                                sums[m] = term if sums[m] is None else sums[m] + term
                    for m in range(8):
                        w[base + m, rows, lanes] = sums[m]


def finest_kernel(taps, before, after, left, right, y0, z0h, z0l, w, out, v, wh, wl):
    for i in range(20):
        own = before[pl.ds(32 * i, 32)] if i < 10 else after[pl.ds(32 * (i - 10), 32)]
        b = left[pl.ds(10 * i, 16)]
        a = right[pl.ds(10 * i, 16)]
        high, low = halves(jnp.concatenate([own, b, a], 0))
        v[i] = dot(y0[...], jnp.concatenate([high, low, high], 0))

    @pl.loop(0, 4)
    def _(g):
        for member in range(3):
            rows = pl.ds(pl.multiple_of(32 * member + 8 * g, 8), 8)
            scale = [taps[0, member, k] for k in range(TAPS)]
            for h in range(2):
                lanes = pl.ds(128 * h, 128)
                for base in range(0, 32, 2):
                    sums = []
                    for m in (base, base + 1):
                        total = w[m, rows, lanes]
                        for r in range(10):
                            if r >= m:
                                total = total + scale[r - m] * v[r, rows, lanes]
                            if r <= m - 22:
                                total = total + scale[42 + r - m] * v[10 + r, rows, lanes]
                        sums.append(total)
                    high, low = halves(jnp.concatenate(sums, 0))
                    at = (pl.ds(8 * base, 16), pl.ds(256 * member + 128 * h, 128))
                    wh[at] = high
                    wl[at] = low
        cols = pl.ds(pl.multiple_of(8 * g, 8), 8)
        total = dot(wh[...], z0h[...]) + dot(wl[...], z0h[...]) + dot(wh[...], z0l[...])
        out[:, cols] = total.reshape(32, 8, 256)


def call(kernel, outs, scratch=(), scalars=0, count=0, flops=0, moved=0, name=None):
    vmem = pl.BlockSpec(memory_space=pltpu.VMEM)
    smem = pl.BlockSpec(memory_space=pltpu.SMEM)
    shapes = [jax.ShapeDtypeStruct(*o) for o in outs]
    return pl.pallas_call(
        kernel,
        out_shape=shapes,
        in_specs=[smem] * scalars + [vmem] * (count - scalars),
        out_specs=[vmem] * len(shapes),
        scratch_shapes=[pltpu.VMEM(*s) for s in scratch],
        compiler_params=pltpu.CompilerParams(vmem_limit_bytes=VMEM_LIMIT),
        cost_estimate=pl.CostEstimate(flops=flops, bytes_accessed=moved, transcendentals=0),
        name=name,
    )


def shift(x, axis, by):
    n = lax.axis_size(axis)
    return lax.ppermute(x, axis, [(i, (i + by) % n) for i in range(n)])


def body(charges, kernel_taps):
    taps = kernel_taps
    l1, l2, s_up, s_down, o_up, o_down, last, first = call(
        restrict_kernel,
        [((18, 24, 128), F32), ((6, 16, 128), F32), ((288, 128), F32), ((288, 128), F32),
         ((328, 256), F32), ((328, 256), F32), ((320, 256), F32), ((320, 256), F32)],
        [((18, 24, 256), F32), ((12, 16, 128), F32)], 0, 1, 10**8, 2 * 10**6, name="restrict",
    )(charges)
    x_left = shift(s_up, "gx", 1)
    x_right = shift(s_down, "gx", -1)
    own_left = shift(o_up, "gy", 1)
    own_right = shift(o_down, "gy", -1)
    taps, l1 = lax.optimization_barrier((taps, l1))
    y0, y1, y2, z0h, z0l, z1h, z1l, z2h, z2l, up1 = call(
        matrices_kernel,
        [((96, 192), BF), ((96, 144), BF), ((96, 144), BF), ((768, 256), BF), ((768, 256), BF),
         ((384, 128), BF), ((384, 128), BF), ((384, 128), BF), ((384, 128), BF), ((128, 256), BF)],
        [], 1, 1, 10**8, 4 * 10**6, name="matrices",
    )(taps)
    x_left, x_right, y0 = lax.optimization_barrier((x_left, x_right, y0))
    c_up, c_down = call(
        face_x_kernel, [((344, 256), F32), ((344, 256), F32)], [], 0, 4, 10**6, 2 * 10**6, name="face_x",
    )(last, first, x_left, x_right)
    before = shift(c_up, "gx", 1)
    after = shift(c_down, "gx", -1)
    x_left, x_right, c_up = lax.optimization_barrier((x_left, x_right, c_up))
    l1x, g_up, g_down = call(
        gather_fine_kernel, [((38, 24, 128), F32), ((456, 128), F32), ((456, 128), F32)],
        [], 0, 3, 10**6, 2 * 10**6, name="gather_fine",
    )(l1, x_left, x_right)
    fine_left = shift(g_up, "gy", 1)
    fine_right = shift(g_down, "gy", -1)
    y0, g_up, g_down = lax.optimization_barrier((y0, g_up, g_down))
    inner, = call(
        inner_kernel, [((32, 96, 256), F32)], [((32, 96, 256), F32)], 1, 5, 10**9, 6 * 10**6, name="inner",
    )(taps, charges, own_left, own_right, y0)
    before, after, inner, fine_left, fine_right = lax.optimization_barrier(
        (before, after, inner, fine_left, fine_right)
    )
    l2x, f_up, f_down = call(
        gather_top_kernel,
        [((16, 16, 128), F32), ((296, 256), F32), ((296, 256), F32)],
        [], 0, 5, 10**6, 5 * 10**6, name="gather_top",
    )(before, after, l2, x_left, x_right)
    left = shift(f_up, "gy", 1)
    right = shift(f_down, "gy", -1)
    l1x, f_up, f_down = lax.optimization_barrier((l1x, f_up, f_down))
    mid, = call(
        fine_level_kernel, [((18, 32, 128), F32)],
        [((38, 48, 128), F32), ((38, 96, 128), F32), ((18, 96, 128), F32)],
        1, 7, 4 * 10**8, 4 * 10**6, name="fine_level",
    )(taps, l1x, fine_left, fine_right, y1, z1h, z1l)
    left, right, mid = lax.optimization_barrier((left, right, mid))
    t_up, t_down = call(
        second_kernel, [((80, 128), F32), ((80, 128), F32)], [], 0, 2, 10**5, 10**6, name="second",
    )(left, right)
    left2 = shift(t_up, "gy", 1)
    right2 = shift(t_down, "gy", -1)
    y0, t_up, t_down = lax.optimization_barrier((y0, t_up, t_down))
    direct, = call(
        finest_kernel, [((32, 32, 256), F32)],
        [((20, 96, 256), F32), ((256, 768), BF), ((256, 768), BF)],
        1, 9, 2 * 10**9, 6 * 10**6, name="finest",
    )(taps, before, after, left, right, y0, z0h, z0l, inner)
    result, = call(
        upper_kernel, [((32, 32, 256), F32)],
        [((16, 48, 128), F32), ((32, 96, 128), F32), ((11, 96, 128), F32), ((18, 32, 128), F32),
         ((32, 32, 128), F32)],
        1, 12, 4 * 10**8, 4 * 10**6, name="upper",
    )(taps, l2x, left, right, left2, right2, y2, z2h, z2l, up1, mid, direct)
    return result


def solution(mesh):
    return jax.shard_map(
        body,
        mesh=mesh,
        in_specs=(P("gx", "gy", None), P()),
        out_specs=P("gx", "gy", None),
        check_vma=False,
    )
```

time: 76.7 us -> 71.5 us (0.932)
  the two profiles are of different devices: /device:TPU:216 before, /device:TPU:1 now
where the time goes in v3:
time: 71.5 us; the launch traced here: 70.3 us
  Pallas kernels  27 us (38%)
  waiting for transfers between devices  24.6 us (34%)
  starting transfers between devices  15.1 us (21%)
  local copies, waits for them, and re-layouts  3.56 us (5%)
    ppermute x12, waiting for transfers between devices, shift(): return lax.ppermute(x, axis, [(i, (i + by) % n) for i in range(n)])  24.6 us
    ppermute x12, starting transfers between devices, shift(): return lax.ppermute(x, axis, [(i, (i + by) % n) for i in range(n)])  15.1 us
    pallas_call x1, Pallas kernels, body(): call(inner_kernel, [((32, 96, 256), F32)], [((32, 96, 256), F32)], 1, 5,...  6.05 us
    pallas_call x1, Pallas kernels, body(): call(fine_level_kernel, [((18, 32, 128), F32)], [((38, 48, 128), F32), ((...  5.87 us
    pallas_call x1, Pallas kernels, body(): call(upper_kernel, [((32, 32, 256), F32)], [((16, 48, 128), F32), ((32, 9...  5.7 us
    pallas_call x1, Pallas kernels, body(): call(finest_kernel, [((32, 32, 256), F32)], [((20, 96, 256), F32), ((256,...  5.07 us
    unnamed x10, local copies, waits for them, and re-layouts  3.56 us
    pallas_call x1, Pallas kernels, body(): call(matrices_kernel, [((96, 192), BF), ((96, 144), BF), ((96, 144), BF),...  2.98 us
  transfers between devices with their start and end apart: 12, of which 5 were waited for; matrix products, arithmetic and copies ran while one was open for 0% of the time, Pallas kernels for 29%

profile of v3, /device:TPU:1, one launch (start us, length us, event | category | flops | bytes accessed | tf_op | source)
XLA Modules:
  0.0 70.3 jit_solution(2983240368585663116)
XLA Ops:
  0.0 1.2 %copy-done = f32[32,32,256]{2,1,0:T(8,128)S(1)} copy-done((f32[32,32,256]{2,1,0:T(8,128)S(1)}, f32[32,32,256]{2,1,0:T(8,128)}, u32[]{:S(2)}) %copy-start) | copy-done | bytes 1048600
  1.2 1.0 %restrict.1 = (f32[18,24,128]{2,1,0:T(8,128)S(1)}, f32[6,16,128]{2,1,0:T(8,128)S(1)}, f32[288,128]{1,0:T(8,128)S(1)}, f32[288,128]{1,0:T(8,128)S(1)}, f32[328,25...) custom-call(f32[32,32,256]{2,1,0:T(8,128)S(1)} %copy-done), custom_call_target="tpu_custom_call" | custom-call | flops 100000000 | bytes 2000000 | tf_op jit(solution)/shard_map/restrict/pallas_call | solution.py:408
  2.3 3.1 %collective-permute-start.4 = (f32[328,256]{1,0:T(8,128)S(1)}, f32[328,256]{1,0:T(8,128)S(1)}, u32[]{:S(2)}, u32[]{:S(2)}) collective-permute-start(f32[328,256]{1,0:T(8,128)S(1)} %get-tuple-element.62), channel_id=1, source_target_pairs={{0,1},{1,2},{2,3},{3,4},{4,5},{5,6},{6,7},{7,8},{8,9},{9,10},{10,1... | collective-permute-start | bytes 1007624 | tf_op jit(solution)/shard_map/ppermute | solution.py:403
  5.4 3.0 %collective-permute-start = (f32[288,128]{1,0:T(8,128)S(1)}, f32[288,128]{1,0:T(8,128)S(1)}, u32[]{:S(2)}, u32[]{:S(2)}) collective-permute-start(f32[288,128]{1,0:T(8,128)S(1)} %get-tuple-element.55), channel_id=1, source_target_pairs={{0,16},{16,32},{32,48},{48,64},{64,80},{80,96},{96,112},{112,128},... | collective-permute-start | bytes 442376 | tf_op jit(solution)/shard_map/ppermute | solution.py:403
  8.4 4.6 %collective-permute-start.1 = (f32[288,128]{1,0:T(8,128)S(1)}, f32[288,128]{1,0:T(8,128)S(1)}, u32[]{:S(2)}, u32[]{:S(2)}) collective-permute-start(f32[288,128]{1,0:T(8,128)S(1)} %get-tuple-element.56), channel_id=1, source_target_pairs={{0,240},{16,0},{32,16},{48,32},{64,48},{80,64},{96,80},{112,96},{1... | collective-permute-start | bytes 442376 | tf_op jit(solution)/shard_map/ppermute | solution.py:403
  13.0 0.7 copy-done.3
  13.6 3.0 %matrices.1 = (bf16[96,192]{1,0:T(8,128)(2,1)S(1)}, bf16[96,144]{1,0:T(8,128)(2,1)S(1)}, bf16[96,144]{1,0:T(8,128)(2,1)S(1)}, bf16[768,256]{1,0:T(8,128)(2,1)S(1...) custom-call(f32[3,3,21]{2,1,0:T(4,128)S(1)} %copy-done.3), custom_call_target="tpu_custom_call" | custom-call | flops 100000000 | bytes 4000000 | tf_op jit(solution)/shard_map/matrices/pallas_call | solution.py:419
  16.6 10.4 %collective-permute-done.left = f32[288,128]{1,0:T(8,128)S(1)} collective-permute-done((f32[288,128]{1,0:T(8,128)S(1)}, f32[288,128]{1,0:T(8,128)S(1)}, u32[]{:S(2)}, u32[]{:S(2)}) %collective-permute-start) | collective-permute-done | bytes 147488 | tf_op jit(solution)/shard_map/ppermute | solution.py:403
  27.1 0.1 face_x.1
  27.2 0.5 collective-permute-start.3
  27.6 2.0 %collective-permute-start.2 = (f32[344,256]{1,0:T(8,128)S(1)}, f32[344,256]{1,0:T(8,128)S(1)}, u32[]{:S(2)}, u32[]{:S(2)}) collective-permute-start(f32[344,256]{1,0:T(8,128)S(1)} %get-tuple-element.60), channel_id=1, source_target_pairs={{0,16},{16,32},{32,48},{48,64},{64,80},{80,96},{96,112},{112,128},... | collective-permute-start | bytes 1056776 | tf_op jit(solution)/shard_map/ppermute | solution.py:403
  29.8 0.5 collective-permute-start.7
  30.3 6.0 %inner.1.w = f32[32,96,256]{2,1,0:T(8,128)S(1)} custom-call(f32[3,3,21]{2,1,0:T(4,128)S(1)} %copy-done.3, f32[32,32,256]{2,1,0:T(8,128)S(1)} %copy-done.1, f32[328,256]{1,0:T(8,128)S(1)} %collective-permute-done.4.left, f32[328,256]{1,0:T(8,128)S(1)} %collective-permute-done.5.right, bf16[96,192]{1,0:T(8,128)(2,1)S(1)} %get-tuple-element.93.y0), custom_call_target="tpu_custom_call" | custom-call | flops 1000000000 | bytes 6000000 | tf_op jit(solution)/shard_map/inner/pallas_call | solution.py:439
  36.3 1.6 %copy-done.2 = f32[32,96,256]{2,1,0:T(8,128)} copy-done((f32[32,96,256]{2,1,0:T(8,128)}, f32[32,96,256]{2,1,0:T(8,128)S(1)}, u32[]{:S(2)}) %copy-start.2) | copy-done | bytes 3145752
  38.0 7.5 %collective-permute-done.6.left = f32[456,128]{1,0:T(8,128)S(1)} collective-permute-done((f32[456,128]{1,0:T(8,128)S(1)}, f32[456,128]{1,0:T(8,128)S(1)}, u32[]{:S(2)}, u32[]{:S(2)}) %collective-permute-start.6) | collective-permute-done | bytes 233504 | tf_op jit(solution)/shard_map/ppermute | solution.py:403
  45.5 0.2 collective-permute-done.7.right
  45.7 3.0 %collective-permute-done.2.before = f32[344,256]{1,0:T(8,128)S(1)} collective-permute-done((f32[344,256]{1,0:T(8,128)S(1)}, f32[344,256]{1,0:T(8,128)S(1)}, u32[]{:S(2)}, u32[]{:S(2)}) %collective-permute-start.2) | collective-permute-done | bytes 352288 | tf_op jit(solution)/shard_map/ppermute | solution.py:403
  48.7 0.1 gather_top.1
  48.9 0.5 collective-permute-start.9
  49.4 5.9 %fine_level.1.mid_in = f32[18,32,128]{2,1,0:T(8,128)S(1)} custom-call(f32[3,3,21]{2,1,0:T(4,128)S(1)} %copy-done.4, f32[38,24,128]{2,1,0:T(8,128)S(1)} %get-tuple-element.78.l1x, f32[456,128]{1,0:T(8,128)S(1)} %collective-permute-done.6.left, f32[456,128]{1,0:T(8,128)S(1)} %collective-permute-done.7.right, bf16[96,144]{1,0:T(8,128)(2,1)S(1)} %get-tuple-element.81.y1, ...), custom_call_target="tpu_custom_call" | custom-call | flops 400000000 | bytes 4000000 | tf_op jit(solution)/shard_map/fine_level/pallas_call | solution.py:453
  55.3 3.4 %collective-permute-done.9.right = f32[296,256]{1,0:T(8,128)S(1)} collective-permute-done((f32[296,256]{1,0:T(8,128)S(1)}, f32[296,256]{1,0:T(8,128)S(1)}, u32[]{:S(2)}, u32[]{:S(2)}) %collective-permute-start.9) | collective-permute-done | bytes 303136 | tf_op jit(solution)/shard_map/ppermute | solution.py:403
  58.8 0.7 %collective-permute-start.11 = (f32[80,128]{1,0:T(8,128)S(1)}, f32[80,128]{1,0:T(8,128)S(1)}, u32[]{:S(2)}, u32[]{:S(2)}) collective-permute-start(f32[80,128]{1,0:T(8,128)S(1)} %get-tuple-element.87), channel_id=1, source_target_pairs={{0,15},{1,0},{2,1},{3,2},{4,3},{5,4},{6,5},{7,6},{8,7},{9,8},{10,9... | collective-permute-start | bytes 122888 | tf_op jit(solution)/shard_map/ppermute | solution.py:403
  59.5 5.1 %finest.1.direct = f32[32,32,256]{2,1,0:T(8,128)S(1)} custom-call(f32[3,3,21]{2,1,0:T(4,128)S(1)} %copy-done.4, f32[344,256]{1,0:T(8,128)S(1)} %collective-permute-done.2.before, f32[344,256]{1,0:T(8,128)S(1)} %collective-permute-done.3.after, f32[296,256]{1,0:T(8,128)S(1)} %collective-permute-done.8.left, f32[296,256]{1,0:T(8,128)S(1)} %collective-permute-done.9.right, ...), custom_call_target="tpu_custom_call" | custom-call | flops 2000000000 | bytes 6000000 | tf_op jit(solution)/shard_map/finest/pallas_call | solution.py:465
  64.6 5.7 %upper.1 = f32[32,32,256]{2,1,0:T(8,128)} custom-call(f32[3,3,21]{2,1,0:T(4,128)S(1)} %copy-done.4, f32[16,16,128]{2,1,0:T(8,128)S(1)} %get-tuple-element.74.l2x, f32[296,256]{1,0:T(8,128)S(1)} %collective-permute-done.8.left, f32[296,256]{1,0:T(8,128)S(1)} %collective-permute-done.9.right, f32[80,128]{1,0:T(8,128)S(1)} %collective-permute-done.10.left2, ...), custom_call_target="tpu_custom_call" | custom-call | flops 400000000 | bytes 4000000 | tf_op jit(solution)/shard_map/upper/pallas_call | solution.py:470
  (20 shorter events, 0.4 us)
Async XLA Ops:
  0.0 1.2 %copy-start = (f32[32,32,256]{2,1,0:T(8,128)S(1)}, f32[32,32,256]{2,1,0:T(8,128)}, u32[]{:S(2)}) copy-start(f32[32,32,256]{2,1,0:T(8,128)} %c.3) | copy-start | bytes 3145732
  1.2 29.1 %copy-start.1 = (f32[32,32,256]{2,1,0:T(8,128)S(1)}, f32[32,32,256]{2,1,0:T(8,128)}, u32[]{:S(2)}) copy-start(f32[32,32,256]{2,1,0:T(8,128)} %c.3) | copy-start | bytes 3145732
  2.3 27.5 %collective-permute-start.4 = (f32[328,256]{1,0:T(8,128)S(1)}, f32[328,256]{1,0:T(8,128)S(1)}, u32[]{:S(2)}, u32[]{:S(2)}) collective-permute-start(f32[328,256]{1,0:T(8,128)S(1)} %get-tuple-element.62), channel_id=1, source_target_pairs={{0,1},{1,2},{2,3},{3,4},{4,5},{5,6},{6,7},{7,8},{8,9},{9,10},{10,1... | collective-permute-start | bytes 1007624 | tf_op jit(solution)/shard_map/ppermute | solution.py:403
  5.4 21.7 %collective-permute-start = (f32[288,128]{1,0:T(8,128)S(1)}, f32[288,128]{1,0:T(8,128)S(1)}, u32[]{:S(2)}, u32[]{:S(2)}) collective-permute-start(f32[288,128]{1,0:T(8,128)S(1)} %get-tuple-element.55), channel_id=1, source_target_pairs={{0,16},{16,32},{32,48},{48,64},{64,80},{80,96},{96,112},{112,128},... | collective-permute-start | bytes 442376 | tf_op jit(solution)/shard_map/ppermute | solution.py:403
  8.4 18.7 %collective-permute-start.1 = (f32[288,128]{1,0:T(8,128)S(1)}, f32[288,128]{1,0:T(8,128)S(1)}, u32[]{:S(2)}, u32[]{:S(2)}) collective-permute-start(f32[288,128]{1,0:T(8,128)S(1)} %get-tuple-element.56), channel_id=1, source_target_pairs={{0,240},{16,0},{32,16},{48,32},{64,48},{80,64},{96,80},{112,96},{1... | collective-permute-start | bytes 442376 | tf_op jit(solution)/shard_map/ppermute | solution.py:403
  12.9 17.3 %collective-permute-start.5 = (f32[328,256]{1,0:T(8,128)S(1)}, f32[328,256]{1,0:T(8,128)S(1)}, u32[]{:S(2)}, u32[]{:S(2)}) collective-permute-start(f32[328,256]{1,0:T(8,128)S(1)} %get-tuple-element.63), channel_id=1, source_target_pairs={{0,15},{1,0},{2,1},{3,2},{4,3},{5,4},{6,5},{7,6},{8,7},{9,8},{10,9... | collective-permute-start | bytes 1007624 | tf_op jit(solution)/shard_map/ppermute | solution.py:403
  13.0 0.7 copy-start.3
  27.2 18.6 %collective-permute-start.3 = (f32[344,256]{1,0:T(8,128)S(1)}, f32[344,256]{1,0:T(8,128)S(1)}, u32[]{:S(2)}, u32[]{:S(2)}) collective-permute-start(f32[344,256]{1,0:T(8,128)S(1)} %get-tuple-element.61), channel_id=1, source_target_pairs={{0,240},{16,0},{32,16},{48,32},{64,48},{80,64},{96,80},{112,96},{1... | collective-permute-start | bytes 1056776 | tf_op jit(solution)/shard_map/ppermute | solution.py:403
  27.6 21.8 %copy-start.4 = (f32[3,3,21]{2,1,0:T(4,128)S(1)}, f32[3,3,21]{2,1,0:T(4,128)}, u32[]{:S(2)}) copy-start(f32[3,3,21]{2,1,0:T(4,128)} %taps.4) | copy-start | bytes 2272
  27.6 21.1 %collective-permute-start.2 = (f32[344,256]{1,0:T(8,128)S(1)}, f32[344,256]{1,0:T(8,128)S(1)}, u32[]{:S(2)}, u32[]{:S(2)}) collective-permute-start(f32[344,256]{1,0:T(8,128)S(1)} %get-tuple-element.60), channel_id=1, source_target_pairs={{0,16},{16,32},{32,48},{48,64},{64,80},{80,96},{96,112},{112,128},... | collective-permute-start | bytes 1056776 | tf_op jit(solution)/shard_map/ppermute | solution.py:403
  29.7 15.8 %collective-permute-start.6 = (f32[456,128]{1,0:T(8,128)S(1)}, f32[456,128]{1,0:T(8,128)S(1)}, u32[]{:S(2)}, u32[]{:S(2)}) collective-permute-start(f32[456,128]{1,0:T(8,128)S(1)} %get-tuple-element.68), channel_id=1, source_target_pairs={{0,1},{1,2},{2,3},{3,4},{4,5},{5,6},{6,7},{7,8},{8,9},{9,10},{10,1... | collective-permute-start | bytes 700424 | tf_op jit(solution)/shard_map/ppermute | solution.py:403
  29.8 15.9 %collective-permute-start.7 = (f32[456,128]{1,0:T(8,128)S(1)}, f32[456,128]{1,0:T(8,128)S(1)}, u32[]{:S(2)}, u32[]{:S(2)}) collective-permute-start(f32[456,128]{1,0:T(8,128)S(1)} %get-tuple-element.69), channel_id=1, source_target_pairs={{0,15},{1,0},{2,1},{3,2},{4,3},{5,4},{6,5},{7,6},{8,7},{9,8},{10,9... | collective-permute-start | bytes 700424 | tf_op jit(solution)/shard_map/ppermute | solution.py:403
  36.3 1.6 %copy-start.2 = (f32[32,96,256]{2,1,0:T(8,128)}, f32[32,96,256]{2,1,0:T(8,128)S(1)}, u32[]{:S(2)}) copy-start(f32[32,96,256]{2,1,0:T(8,128)S(1)} %inner.1.w) | copy-start | bytes 9437188
  48.9 6.5 %collective-permute-start.8 = (f32[296,256]{1,0:T(8,128)S(1)}, f32[296,256]{1,0:T(8,128)S(1)}, u32[]{:S(2)}, u32[]{:S(2)}) collective-permute-start(f32[296,256]{1,0:T(8,128)S(1)} %get-tuple-element.75), channel_id=1, source_target_pairs={{0,1},{1,2},{2,3},{3,4},{4,5},{5,6},{6,7},{7,8},{8,9},{9,10},{10,1... | collective-permute-start | bytes 909320 | tf_op jit(solution)/shard_map/ppermute | solution.py:403
  48.9 9.7 %collective-permute-start.9 = (f32[296,256]{1,0:T(8,128)S(1)}, f32[296,256]{1,0:T(8,128)S(1)}, u32[]{:S(2)}, u32[]{:S(2)}) collective-permute-start(f32[296,256]{1,0:T(8,128)S(1)} %get-tuple-element.76), channel_id=1, source_target_pairs={{0,15},{1,0},{2,1},{3,2},{4,3},{5,4},{6,5},{7,6},{8,7},{9,8},{10,9... | collective-permute-start | bytes 909320 | tf_op jit(solution)/shard_map/ppermute | solution.py:403
  58.7 5.9 %collective-permute-start.10 = (f32[80,128]{1,0:T(8,128)S(1)}, f32[80,128]{1,0:T(8,128)S(1)}, u32[]{:S(2)}, u32[]{:S(2)}) collective-permute-start(f32[80,128]{1,0:T(8,128)S(1)} %get-tuple-element.86), channel_id=1, source_target_pairs={{0,1},{1,2},{2,3},{3,4},{4,5},{5,6},{6,7},{7,8},{8,9},{9,10},{10,1... | collective-permute-start | bytes 122888 | tf_op jit(solution)/shard_map/ppermute | solution.py:403
  58.8 5.8 %collective-permute-start.11 = (f32[80,128]{1,0:T(8,128)S(1)}, f32[80,128]{1,0:T(8,128)S(1)}, u32[]{:S(2)}, u32[]{:S(2)}) collective-permute-start(f32[80,128]{1,0:T(8,128)S(1)} %get-tuple-element.87), channel_id=1, source_target_pairs={{0,15},{1,0},{2,1},{3,2},{4,3},{5,4},{6,5},{7,6},{8,7},{9,8},{10,9... | collective-permute-start | bytes 122888 | tf_op jit(solution)/shard_map/ppermute | solution.py:403

commit v4 on v3

--- a/solution.py
+++ b/solution.py
@@ -11,6 +11,7 @@
 BF = jnp.bfloat16
 F32 = jnp.float32
 VMEM_LIMIT = 48 * 1024 * 1024
+HINT = 2 * 10**10
 
 
 def halves(x):
@@ -31,7 +32,7 @@
     return total
 
 
-def matrices_kernel(taps, y0, y1, y2, z0h, z0l, z1h, z1l, z2h, z2l, up1):
+def matrices_kernel(taps, y0, y1, y2, z0h, z0l, z1, z2, up1):
     def iota(shape, dim):
         return lax.broadcasted_iota(jnp.int32, shape, dim)
 
@@ -57,6 +58,17 @@
     def put(out, rows, table, width):
         high, low = halves(table)
         out[rows] = jnp.where(iota(table.shape, 1) < 2 * width, high.astype(F32), low.astype(F32)).astype(BF)
+
+    def block(out, base, table, count):
+        high, low = halves(table)
+        zero = jnp.zeros((128, 128), BF)
+        if count < 128:
+            for at in (base, base + 128):
+                out[pl.ds(at + count, 128 - count)] = jnp.zeros((128 - count, 256), BF)
+        out[pl.ds(base, count), pl.ds(0, 128)] = high
+        out[pl.ds(base, count), pl.ds(128, 128)] = low
+        out[pl.ds(base + 128, count), pl.ds(0, 128)] = high
+        out[pl.ds(base + 128, count), pl.ds(128, 128)] = zero[:count]
 
     def product(weights, table):
         high, low = halves(table)
@@ -72,7 +84,8 @@
     lift2 = jnp.where(columns < 10, spline_of(iota((32, 32), 0) - 1 - 2 * columns), 0.0).astype(BF)
     lift2 = dot(lift1, lift2).astype(BF)
     up2 = cyclic_iota((64, 128), 0, 1, 128).astype(BF)
-    up1[...] = cyclic_iota((128, 256), 0, 1, 256).astype(BF)
+    up1[pl.ds(0, 128)] = cyclic_iota((128, 256), 0, 1, 256).astype(BF)
+    up1[pl.ds(128, 128)] = cyclic_iota((128, 256), 0, 1, 256).astype(BF)
     for member in range(3):
         rows = pl.ds(32 * member, 32)
         put(y0, rows, pick(0, member, place0), 64)
@@ -81,16 +94,9 @@
         high, low = halves(cycle(0, member, 256))
         z0h[pl.ds(256 * member, 256)] = high
         z0l[pl.ds(256 * member, 256)] = low
-        high, low = halves(cycle(1, member, 128))
-        z1h[pl.ds(128 * member, 128)] = high
-        z1l[pl.ds(128 * member, 128)] = low
+        block(z1, 256 * member, cycle(1, member, 128), 128)
         high, low = halves(cycle(2, member, 64))
-        table = dot(high, up2) + dot(low, up2)
-        high, low = halves(table)
-        z2h[pl.ds(128 * member, 64)] = high
-        z2l[pl.ds(128 * member, 64)] = low
-        z2h[pl.ds(128 * member + 64, 64)] = jnp.zeros((64, 128), BF)
-        z2l[pl.ds(128 * member + 64, 64)] = jnp.zeros((64, 128), BF)
+        block(z2, 256 * member, dot(high, up2) + dot(low, up2), 64)
 
 
 def spline_iota(shape, offset, coarse_dim, fine_dim, keep=None):
@@ -113,15 +119,15 @@
     return spline_of(((fine - 2 * coarse + 2) & (fine_len - 1)) - 2)
 
 
-def restrict_kernel(c, l1, l2, up1, down1, face_up, face_down, last, first, s1, s2):
-    for r in range(10):
-        last[pl.ds(32 * r, 32)] = c[22 + r]
-        first[pl.ds(32 * r, 32)] = c[r]
+def restrict_kernel(c, l1, l2, up1, down1, last, first, face_up, face_down, s1, s2):
     for i in range(32):
         face_up[pl.ds(10 * i, 10)] = c[i, 22:32]
         face_down[pl.ds(10 * i, 10)] = c[i, 0:10]
     face_up[pl.ds(320, 8)] = jnp.zeros((8, 256), F32)
     face_down[pl.ds(320, 8)] = jnp.zeros((8, 256), F32)
+    for r in range(10):
+        last[pl.ds(32 * r, 32)] = c[22 + r]
+        first[pl.ds(32 * r, 32)] = c[r]
     ry = spline_iota((24, 32), 2, 0, 1, 18).astype(BF)
     for i in range(-1, 17):
         high, low = halves(spline_sum(lambda r: c[r], i, 0, 31))
@@ -159,22 +165,21 @@
     return (pl.ds(base + count * (j // 2), count), pl.ds(128 * (j % 2), 128))
 
 
-def face_x_kernel(last, first, left, right, up, down):
-    up[pl.ds(0, 320)] = last[...]
-    down[pl.ds(0, 320)] = first[...]
+def forward_kernel(left, right, up, down):
     lower = lax.broadcasted_iota(jnp.int32, (11, 128), 1) < 64
     for p in range(3):
         even = 2 * p
         odd = min(even + 1, 4)
+        rows = pl.ds(11 * p, 11)
         a = left[pl.ds(11 * even, 11)]
         b = left[pl.ds(11 * odd, 11)]
-        up[paired(320, 11, p)] = jnp.where(lower, pltpu.roll(a, 64, 1), b)
+        up[rows] = jnp.where(lower, pltpu.roll(a, 64, 1), b)
         a = right[pl.ds(11 * even, 11)]
         b = right[pl.ds(11 * odd, 11)]
-        down[paired(320, 11, p)] = jnp.where(lower, a, pltpu.roll(b, 64, 1))
-
-
-def gather_fine_kernel(l1, left, right, l1x, up, down):
+        down[rows] = jnp.where(lower, a, pltpu.roll(b, 64, 1))
+
+
+def gather_kernel(l1, l2, left, right, left2, right2, l1x, l2x, up, down):
     for i in range(38):
         if i < 12:
             l1x[i, :18] = left[pl.ds(72 + 18 * i, 18)]
@@ -187,17 +192,8 @@
         elif 12 <= i < 26:
             l1x[i] = l1[i - 10]
     for i in range(38):
-        up[pl.ds(12 * i, 12)] = l1x[i, 6:18]
-        down[pl.ds(12 * i, 12)] = l1x[i, 0:12]
-
-
-def gather_top_kernel(before, after, l2, left, right, l2x, up, down):
-    for i in range(20):
-        row = before[pl.ds(32 * i, 32)] if i < 10 else after[pl.ds(32 * (i - 10), 32)]
-        up[pl.ds(10 * i, 10)] = row[22:32]
-        down[pl.ds(10 * i, 10)] = row[0:10]
-    up[pl.ds(200, 8)] = jnp.zeros((8, 256), F32)
-    down[pl.ds(200, 8)] = jnp.zeros((8, 256), F32)
+        up[paired(0, 12, i)] = l1x[i, 6:18]
+        down[paired(0, 12, i)] = l1x[i, 0:12]
     lanes = lax.broadcasted_iota(jnp.int32, (11, 128), 1)
     lower = lanes < 64
     rolled = lambda x: pltpu.roll(x, 64, 1)
@@ -205,7 +201,7 @@
         low = []
         high = []
         if j < 5:
-            slab = before[paired(320, 11, j // 2)]
+            slab = left2[pl.ds(11 * (j // 2), 11)]
             low.append(slab if j % 2 == 0 else rolled(slab))
         if 2 <= j < 8:
             low.append(left[pl.ds(11 * (j - 2), 11)])
@@ -220,18 +216,27 @@
         if 8 <= j < 13:
             high.append(right[pl.ds(11 * (j - 8), 11)])
         if 10 <= j < 15:
-            slab = after[paired(320, 11, (j - 10) // 2)]
+            slab = right2[pl.ds(11 * ((j - 10) // 2), 11)]
             high.append(rolled(slab) if j % 2 == 0 else slab)
         row = jnp.where(lower, sum(low, jnp.zeros((11, 128), F32)), sum(high, jnp.zeros((11, 128), F32)))
         l2x[j, :11] = row
         l2x[j, pl.ds(11, 5)] = jnp.zeros((5, 128), F32)
-        up[paired(208, 11, j)] = row
-        down[paired(208, 11, j)] = row
+        up[paired(228, 11, j)] = row
+        down[paired(228, 11, j)] = row
+
+
+def corner_kernel(before, after, up, down):
+    for i in range(20):
+        row = before[pl.ds(32 * i, 32)] if i < 10 else after[pl.ds(32 * (i - 10), 32)]
+        up[pl.ds(10 * i, 10)] = row[22:32]
+        down[pl.ds(10 * i, 10)] = row[0:10]
+    up[pl.ds(200, 8)] = jnp.zeros((8, 256), F32)
+    down[pl.ds(200, 8)] = jnp.zeros((8, 256), F32)
 
 
 def second_kernel(left, right, up, down):
     for j in range(16):
-        rows, lanes = paired(208, 11, j)
+        rows, lanes = paired(228, 11, j)
         up[pl.ds(5 * j, 5)] = left[pl.ds(rows.start + 6, 5), lanes]
         down[pl.ds(5 * j, 5)] = right[pl.ds(rows.start, 5), lanes]
 
@@ -255,41 +260,40 @@
                 w[base + m, rows] = sums[m]
 
 
-def correlate_z(w, count, high_table, low_table):
-    total = jnp.zeros((count * 32, 128), F32)
+def correlate_z(w, count, table):
+    total = jnp.zeros((count * 32, 256), F32)
     for member in range(3):
         high, low = halves(w[:, pl.ds(32 * member, 32)].reshape(count * 32, 128))
-        rows = pl.ds(128 * member, 128)
-        total = total + dot(high, high_table[rows]) + dot(low, high_table[rows]) + dot(high, low_table[rows])
-    return total.reshape(count, 32, 128)
-
-
-def fine_level_kernel(taps, l1x, left, right, y1, z1h, z1l, mid, f1, v1, w1):
+        total = total + dot(jnp.concatenate([high, low], 1), table[pl.ds(256 * member, 256)])
+    return (total[:, :128] + total[:, 128:]).reshape(count, 32, 128)
+
+
+def fine_level_kernel(taps, l1x, left, right, y1, z1, mid, f1, v1, w1):
     for i in range(38):
-        f1[i, pl.ds(0, 12)] = left[pl.ds(12 * i, 12)]
+        f1[i, pl.ds(0, 12)] = left[paired(0, 12, i)]
         f1[i, pl.ds(12, 18)] = l1x[i, :18]
-        f1[i, pl.ds(30, 12)] = right[pl.ds(12 * i, 12)]
+        f1[i, pl.ds(30, 12)] = right[paired(0, 12, i)]
         f1[i, pl.ds(42, 6)] = jnp.zeros((6, 128), F32)
 
-    @pl.loop(0, 38, unroll=2)
+    @pl.loop(0, 38, unroll=19)
     def _(i):
         high, low = halves(f1[i])
         v1[i] = dot(y1[...], jnp.concatenate([high, low, high], 0))
 
     correlate_x(taps, 1, v1, w1, 18, 9)
-    mid[...] = correlate_z(w1, 18, z1h, z1l)
-
-
-def upper_kernel(taps, l2x, left, right, left2, right2, y2, z2h, z2l, up1, mid_in, direct, out,
+    mid[...] = correlate_z(w1, 18, z1)
+
+
+def upper_kernel(taps, l2x, left, right, left2, right2, y2, z2, up1, mid_in, direct, out,
                  f2, v2, w2, mid, fine):
     for j in range(16):
         f2[j, pl.ds(0, 16)] = l2x[j]
-        f2[j, pl.ds(16, 11)] = left[paired(208, 11, j)]
-        f2[j, pl.ds(27, 11)] = right[paired(208, 11, j)]
+        f2[j, pl.ds(16, 11)] = left[paired(228, 11, j)]
+        f2[j, pl.ds(27, 11)] = right[paired(228, 11, j)]
         f2[j, pl.ds(38, 5)] = left2[pl.ds(5 * j, 5)]
         f2[j, pl.ds(43, 5)] = right2[pl.ds(5 * j, 5)]
 
-    @pl.loop(0, 16, unroll=2)
+    @pl.loop(0, 16, unroll=16)
     def _(j):
         high, low = halves(f2[j])
         v = dot(y2[...], jnp.concatenate([high, low, high], 0))
@@ -297,7 +301,7 @@
         v2[16 + j] = pltpu.roll(v, 64, 1)
 
     correlate_x(taps, 2, v2, w2, 11, 11)
-    v2[pl.ds(0, 11), pl.ds(0, 32)] = correlate_z(w2, 11, z2h, z2l)
+    v2[pl.ds(0, 11), pl.ds(0, 32)] = correlate_z(w2, 11, z2)
     top = lambda i: v2[i + 1, pl.ds(0, 32)]
     for a in range(-1, 9):
         if a >= 0:
@@ -310,7 +314,7 @@
     for q in range(4):
         rows = pl.ds(8 * q, 8)
         high, low = halves(fine[rows].reshape(256, 128))
-        out[rows] = direct[rows] + (dot(high, up1[...]) + dot(low, up1[...])).reshape(8, 32, 256)
+        out[rows] = direct[rows] + dot(jnp.concatenate([high, low], 1), up1[...]).reshape(8, 32, 256)
 
 
 def section(table, own, left, right, base, at):
@@ -320,8 +324,8 @@
     return dot(table[...], jnp.concatenate([high, low, high], 0))
 
 
-def inner_kernel(taps, c, left, right, y0, w, v):
-    @pl.loop(0, 8)
+def inner_kernel(taps, c, left, right, y0, z0h, z0l, out, v, wh, wl):
+    @pl.loop(0, 8, unroll=4)
     def _(q):
         base = pl.multiple_of(40 * q, 8)
         for at in range(4):
@@ -344,11 +348,17 @@
                             if 0 <= k < TAPS:
                                 term = scale[k] * value
                                 sums[m] = term if sums[m] is None else sums[m] + term
-                    for m in range(8):
-                        w[base + m, rows, lanes] = sums[m]
-
-
-def finest_kernel(taps, before, after, left, right, y0, z0h, z0l, w, out, v, wh, wl):
+                    for m in range(0, 8, 2):
+                        high, low = halves(jnp.concatenate([sums[m], sums[m + 1]], 0))
+                        at = (pl.ds(8 * (base + m), 16), pl.ds(256 * member + 128 * h, 128))
+                        wh[at] = high
+                        wl[at] = low
+        cols = pl.ds(pl.multiple_of(8 * g, 8), 8)
+        total = dot(wh[...], z0h[...]) + dot(wl[...], z0h[...]) + dot(wh[...], z0l[...])
+        out[:, cols] = total.reshape(32, 8, 256)
+
+
+def finest_kernel(taps, before, after, left, right, y0, z0h, z0l, inner, out, v, wh, wl):
     for i in range(20):
         own = before[pl.ds(32 * i, 32)] if i < 10 else after[pl.ds(32 * (i - 10), 32)]
         b = left[pl.ds(10 * i, 16)]
@@ -363,23 +373,27 @@
             scale = [taps[0, member, k] for k in range(TAPS)]
             for h in range(2):
                 lanes = pl.ds(128 * h, 128)
-                for base in range(0, 32, 2):
-                    sums = []
-                    for m in (base, base + 1):
-                        total = w[m, rows, lanes]
-                        for r in range(10):
-                            if r >= m:
-                                total = total + scale[r - m] * v[r, rows, lanes]
-                            if r <= m - 22:
-                                total = total + scale[42 + r - m] * v[10 + r, rows, lanes]
-                        sums.append(total)
-                    high, low = halves(jnp.concatenate(sums, 0))
-                    at = (pl.ds(8 * base, 16), pl.ds(256 * member + 128 * h, 128))
+                sums = [None] * 20
+                for r in range(20):
+                    value = v[r, rows, lanes]
+                    for m in range(10):
+                        k = r - m if r < 10 else 20 + r - 10 - m
+                        at = m if r < 10 else 10 + m
+                        if r < 10 and m > r or r >= 10 and m < r - 10:
+                            continue
+                        term = scale[k] * value
+                        sums[at] = term if sums[at] is None else sums[at] + term
+                for m in range(0, 20, 2):
+                    high, low = halves(jnp.concatenate([sums[m], sums[m + 1]], 0))
+                    at = (pl.ds(8 * m, 16), pl.ds(256 * member + 128 * h, 128))
                     wh[at] = high
                     wl[at] = low
         cols = pl.ds(pl.multiple_of(8 * g, 8), 8)
         total = dot(wh[...], z0h[...]) + dot(wl[...], z0h[...]) + dot(wh[...], z0l[...])
-        out[:, cols] = total.reshape(32, 8, 256)
+        total = total.reshape(20, 8, 256)
+        out[pl.ds(0, 10), cols] = inner[pl.ds(0, 10), cols] + total[:10]
+        out[pl.ds(10, 12), cols] = inner[pl.ds(10, 12), cols]
+        out[pl.ds(22, 10), cols] = inner[pl.ds(22, 10), cols] + total[10:]
 
 
 def call(kernel, outs, scratch=(), scalars=0, count=0, flops=0, moved=0, name=None):
@@ -405,10 +419,10 @@
 
 def body(charges, kernel_taps):
     taps = kernel_taps
-    l1, l2, s_up, s_down, o_up, o_down, last, first = call(
+    l1, l2, s_up, s_down, last, first, o_up, o_down = call(
         restrict_kernel,
         [((18, 24, 128), F32), ((6, 16, 128), F32), ((288, 128), F32), ((288, 128), F32),
-         ((328, 256), F32), ((328, 256), F32), ((320, 256), F32), ((320, 256), F32)],
+         ((320, 256), F32), ((320, 256), F32), ((328, 256), F32), ((328, 256), F32)],
         [((18, 24, 256), F32), ((12, 16, 128), F32)], 0, 1, 10**8, 2 * 10**6, name="restrict",
     )(charges)
     x_left = shift(s_up, "gx", 1)
@@ -416,63 +430,64 @@
     own_left = shift(o_up, "gy", 1)
     own_right = shift(o_down, "gy", -1)
     taps, l1 = lax.optimization_barrier((taps, l1))
-    y0, y1, y2, z0h, z0l, z1h, z1l, z2h, z2l, up1 = call(
+    y0, y1, y2, z0h, z0l, z1, z2, up1 = call(
         matrices_kernel,
         [((96, 192), BF), ((96, 144), BF), ((96, 144), BF), ((768, 256), BF), ((768, 256), BF),
-         ((384, 128), BF), ((384, 128), BF), ((384, 128), BF), ((384, 128), BF), ((128, 256), BF)],
+         ((768, 256), BF), ((768, 256), BF), ((256, 256), BF)],
         [], 1, 1, 10**8, 4 * 10**6, name="matrices",
     )(taps)
     x_left, x_right, y0 = lax.optimization_barrier((x_left, x_right, y0))
     c_up, c_down = call(
-        face_x_kernel, [((344, 256), F32), ((344, 256), F32)], [], 0, 4, 10**6, 2 * 10**6, name="face_x",
-    )(last, first, x_left, x_right)
-    before = shift(c_up, "gx", 1)
-    after = shift(c_down, "gx", -1)
-    x_left, x_right, c_up = lax.optimization_barrier((x_left, x_right, c_up))
-    l1x, g_up, g_down = call(
-        gather_fine_kernel, [((38, 24, 128), F32), ((456, 128), F32), ((456, 128), F32)],
-        [], 0, 3, 10**6, 2 * 10**6, name="gather_fine",
-    )(l1, x_left, x_right)
-    fine_left = shift(g_up, "gy", 1)
-    fine_right = shift(g_down, "gy", -1)
+        forward_kernel, [((40, 128), F32), ((40, 128), F32)], [], 0, 2, HINT, 0, name="forward",
+    )(x_left, x_right)
+    x_left2 = shift(c_up, "gx", 1)
+    x_right2 = shift(c_down, "gx", -1)
+
+    l1x, l2x, g_up, g_down = call(
+        gather_kernel,
+        [((38, 24, 128), F32), ((16, 16, 128), F32), ((316, 256), F32), ((316, 256), F32)],
+        [], 0, 6, 0, 0, name="gather",
+    )(l1, l2, x_left, x_right, x_left2, x_right2)
+    left = shift(g_up, "gy", 1)
+    right = shift(g_down, "gy", -1)
+    last, first, g_up, g_down = lax.optimization_barrier((last, first, g_up, g_down))
+    before = shift(last, "gx", 1)
+    after = shift(first, "gx", -1)
     y0, g_up, g_down = lax.optimization_barrier((y0, g_up, g_down))
     inner, = call(
-        inner_kernel, [((32, 96, 256), F32)], [((32, 96, 256), F32)], 1, 5, 10**9, 6 * 10**6, name="inner",
-    )(taps, charges, own_left, own_right, y0)
-    before, after, inner, fine_left, fine_right = lax.optimization_barrier(
-        (before, after, inner, fine_left, fine_right)
-    )
-    l2x, f_up, f_down = call(
-        gather_top_kernel,
-        [((16, 16, 128), F32), ((296, 256), F32), ((296, 256), F32)],
-        [], 0, 5, 10**6, 5 * 10**6, name="gather_top",
-    )(before, after, l2, x_left, x_right)
-    left = shift(f_up, "gy", 1)
-    right = shift(f_down, "gy", -1)
-    l1x, f_up, f_down = lax.optimization_barrier((l1x, f_up, f_down))
-    mid, = call(
-        fine_level_kernel, [((18, 32, 128), F32)],
-        [((38, 48, 128), F32), ((38, 96, 128), F32), ((18, 96, 128), F32)],
-        1, 7, 4 * 10**8, 4 * 10**6, name="fine_level",
-    )(taps, l1x, fine_left, fine_right, y1, z1h, z1l)
-    left, right, mid = lax.optimization_barrier((left, right, mid))
+        inner_kernel, [((32, 32, 256), F32)],
+        [((32, 96, 256), F32), ((256, 768), BF), ((256, 768), BF)], 1, 7, 2 * 10**9, 6 * 10**6, name="inner",
+    )(taps, charges, own_left, own_right, y0, z0h, z0l)
+    left, right, inner = lax.optimization_barrier((left, right, inner))
     t_up, t_down = call(
         second_kernel, [((80, 128), F32), ((80, 128), F32)], [], 0, 2, 10**5, 10**6, name="second",
     )(left, right)
     left2 = shift(t_up, "gy", 1)
     right2 = shift(t_down, "gy", -1)
-    y0, t_up, t_down = lax.optimization_barrier((y0, t_up, t_down))
-    direct, = call(
-        finest_kernel, [((32, 32, 256), F32)],
-        [((20, 96, 256), F32), ((256, 768), BF), ((256, 768), BF)],
-        1, 9, 2 * 10**9, 6 * 10**6, name="finest",
-    )(taps, before, after, left, right, y0, z0h, z0l, inner)
-    result, = call(
+    before, after, t_up, t_down = lax.optimization_barrier((before, after, t_up, t_down))
+    f_up, f_down = call(
+        corner_kernel, [((208, 256), F32), ((208, 256), F32)], [], 0, 2, 10**6, 10**6, name="corner",
+    )(before, after)
+    corner_left = shift(f_up, "gy", 1)
+    corner_right = shift(f_down, "gy", -1)
+    l1x, f_up, f_down = lax.optimization_barrier((l1x, f_up, f_down))
+    mid, = call(
+        fine_level_kernel, [((18, 32, 128), F32)],
+        [((38, 48, 128), F32), ((38, 96, 128), F32), ((18, 96, 128), F32)],
+        1, 6, 4 * 10**8, 4 * 10**6, name="fine_level",
+    )(taps, l1x, left, right, y1, z1)
+    partial, = call(
         upper_kernel, [((32, 32, 256), F32)],
         [((16, 48, 128), F32), ((32, 96, 128), F32), ((11, 96, 128), F32), ((18, 32, 128), F32),
          ((32, 32, 128), F32)],
-        1, 12, 4 * 10**8, 4 * 10**6, name="upper",
-    )(taps, l2x, left, right, left2, right2, y2, z2h, z2l, up1, mid, direct)
+        1, 11, 4 * 10**8, 4 * 10**6, name="upper",
+    )(taps, l2x, left, right, left2, right2, y2, z2, up1, mid, inner)
+    corner_left, corner_right, partial = lax.optimization_barrier((corner_left, corner_right, partial))
+    result, = call(
+        finest_kernel, [((32, 32, 256), F32)],
+        [((20, 96, 256), F32), ((160, 768), BF), ((160, 768), BF)],
+        1, 9, 2 * 10**9, 6 * 10**6, name="finest",
+    )(taps, before, after, corner_left, corner_right, y0, z0h, z0l, partial)
     return result
 
 

time: 71.5 us -> 69.3 us (0.969)
  starting transfers between devices: 15.1 us -> 31.9 us
  waiting for transfers between devices: 24.6 us -> 12.8 us
  Pallas kernels: 27 us -> 22.1 us
  local copies, waits for them, and re-layouts: 3.56 us -> 1.23 us
    ppermute x12 -> x14, starting transfers between devices: 15.1 us -> 31.9 us  [shift(): return lax.ppermute(x, axis, [(i, (i + by) % n) for i in range(n)])]
    ppermute x12 -> x14, waiting for transfers between devices: 24.6 us -> 12.8 us  [shift(): return lax.ppermute(x, axis, [(i, (i + by) % n) for i in range(n)])]
    pallas_call x1, Pallas kernels: 5.7 us -> 2.82 us  [body(): call(upper_kernel, [((32, 32, 256), F32)], [((16, 48, 128), F32), ((32, 9...]
    pallas_call x1, Pallas kernels: 5.87 us -> 3.37 us  [body(): call(fine_level_kernel, [((18, 32, 128), F32)], [((38, 48, 128), F32), ((...]
    unnamed x10 -> x6, local copies, waits for them, and re-layouts: 3.56 us -> 1.23 us
  transfers between devices with their start and end apart: 12 -> 14, of which waited for: 5 -> 4; matrix products, arithmetic and copies ran while one was open for 0% -> 0% of each run, Pallas kernels for 29% -> 25%
where the time goes in v4:
time: 69.3 us; the launch traced here: 68.2 us
  starting transfers between devices  31.9 us (46%)
  Pallas kernels  22.1 us (32%)
  waiting for transfers between devices  12.8 us (18%)
  local copies, waits for them, and re-layouts  1.23 us (2%)
    ppermute x14, starting transfers between devices, shift(): return lax.ppermute(x, axis, [(i, (i + by) % n) for i in range(n)])  31.9 us
    ppermute x14, waiting for transfers between devices, shift(): return lax.ppermute(x, axis, [(i, (i + by) % n) for i in range(n)])  12.8 us
    pallas_call x1, Pallas kernels, body(): call(inner_kernel, [((32, 32, 256), F32)], [((32, 96, 256), F32), ((256,...  7.28 us
    pallas_call x1, Pallas kernels, body(): call(finest_kernel, [((32, 32, 256), F32)], [((20, 96, 256), F32), ((160,...  4.24 us
    pallas_call x1, Pallas kernels, body(): call(fine_level_kernel, [((18, 32, 128), F32)], [((38, 48, 128), F32), ((...  3.37 us
    pallas_call x1, Pallas kernels, body(): call(matrices_kernel, [((96, 192), BF), ((96, 144), BF), ((96, 144), BF),...  3.02 us
    pallas_call x1, Pallas kernels, body(): call(upper_kernel, [((32, 32, 256), F32)], [((16, 48, 128), F32), ((32, 9...  2.82 us
  transfers between devices with their start and end apart: 14, of which 4 were waited for; matrix products, arithmetic and copies ran while one was open for 0% of the time, Pallas kernels for 25%

profile of v4, /device:TPU:1, one launch (start us, length us, event | category | flops | bytes accessed | tf_op | source)
XLA Modules:
  0.0 68.2 jit_solution(1776349881335790193)
XLA Ops:
  0.0 1.2 %copy-done = f32[32,32,256]{2,1,0:T(8,128)S(1)} copy-done((f32[32,32,256]{2,1,0:T(8,128)S(1)}, f32[32,32,256]{2,1,0:T(8,128)}, u32[]{:S(2)}) %copy-start) | copy-done | bytes 1048600
  1.2 1.0 %restrict.1 = (f32[18,24,128]{2,1,0:T(8,128)S(1)}, f32[6,16,128]{2,1,0:T(8,128)S(1)}, f32[288,128]{1,0:T(8,128)S(1)}, f32[288,128]{1,0:T(8,128)S(1)}, f32[320,25...) custom-call(f32[32,32,256]{2,1,0:T(8,128)S(1)} %copy-done), custom_call_target="tpu_custom_call" | custom-call | flops 100000000 | bytes 2000000 | tf_op jit(solution)/shard_map/restrict/pallas_call | solution.py:422
  2.3 3.9 %collective-permute-start = (f32[288,128]{1,0:T(8,128)S(1)}, f32[288,128]{1,0:T(8,128)S(1)}, u32[]{:S(2)}, u32[]{:S(2)}) collective-permute-start(f32[288,128]{1,0:T(8,128)S(1)} %get-tuple-element.53), channel_id=1, source_target_pairs={{0,16},{16,32},{32,48},{48,64},{64,80},{80,96},{96,112},{112,128},... | collective-permute-start | bytes 442376 | tf_op jit(solution)/shard_map/ppermute | solution.py:417
  6.2 5.6 %collective-permute-start.1 = (f32[288,128]{1,0:T(8,128)S(1)}, f32[288,128]{1,0:T(8,128)S(1)}, u32[]{:S(2)}, u32[]{:S(2)}) collective-permute-start(f32[288,128]{1,0:T(8,128)S(1)} %get-tuple-element.54), channel_id=1, source_target_pairs={{0,240},{16,0},{32,16},{48,32},{64,48},{80,64},{96,80},{112,96},{1... | collective-permute-start | bytes 442376 | tf_op jit(solution)/shard_map/ppermute | solution.py:417
  11.7 1.6 %collective-permute-start.8 = (f32[328,256]{1,0:T(8,128)S(1)}, f32[328,256]{1,0:T(8,128)S(1)}, u32[]{:S(2)}, u32[]{:S(2)}) collective-permute-start(f32[328,256]{1,0:T(8,128)S(1)} %get-tuple-element.64), channel_id=1, source_target_pairs={{0,1},{1,2},{2,3},{3,4},{4,5},{5,6},{6,7},{7,8},{8,9},{9,10},{10,1... | collective-permute-start | bytes 1007624 | tf_op jit(solution)/shard_map/ppermute | solution.py:417
  13.3 3.0 %matrices.1 = (bf16[96,192]{1,0:T(8,128)(2,1)S(1)}, bf16[96,144]{1,0:T(8,128)(2,1)S(1)}, bf16[96,144]{1,0:T(8,128)(2,1)S(1)}, bf16[768,256]{1,0:T(8,128)(2,1)S(1...) custom-call(f32[3,3,21]{2,1,0:T(4,128)S(1)} %copy-done.2), custom_call_target="tpu_custom_call" | custom-call | flops 100000000 | bytes 4000000 | tf_op jit(solution)/shard_map/matrices/pallas_call | solution.py:433
  16.4 1.0 %collective-permute-done.1.right = f32[288,128]{1,0:T(8,128)S(1)} collective-permute-done((f32[288,128]{1,0:T(8,128)S(1)}, f32[288,128]{1,0:T(8,128)S(1)}, u32[]{:S(2)}, u32[]{:S(2)}) %collective-permute-start.1) | collective-permute-done | bytes 147488 | tf_op jit(solution)/shard_map/ppermute | solution.py:417
  17.5 3.3 %collective-permute-start.2 = (f32[40,128]{1,0:T(8,128)S(1)}, f32[40,128]{1,0:T(8,128)S(1)}, u32[]{:S(2)}, u32[]{:S(2)}) collective-permute-start(f32[40,128]{1,0:T(8,128)S(1)} %get-tuple-element.58), channel_id=1, source_target_pairs={{0,16},{16,32},{32,48},{48,64},{64,80},{80,96},{96,112},{112,128},... | collective-permute-start | bytes 61448 | tf_op jit(solution)/shard_map/ppermute | solution.py:417
  20.7 2.5 %collective-permute-start.3 = (f32[40,128]{1,0:T(8,128)S(1)}, f32[40,128]{1,0:T(8,128)S(1)}, u32[]{:S(2)}, u32[]{:S(2)}) collective-permute-start(f32[40,128]{1,0:T(8,128)S(1)} %get-tuple-element.59), channel_id=1, source_target_pairs={{0,240},{16,0},{32,16},{48,32},{64,48},{80,64},{96,80},{112,96},{1... | collective-permute-start | bytes 61448 | tf_op jit(solution)/shard_map/ppermute | solution.py:417
  23.2 2.3 %collective-permute-done.2.left2 = f32[40,128]{1,0:T(8,128)S(1)} collective-permute-done((f32[40,128]{1,0:T(8,128)S(1)}, f32[40,128]{1,0:T(8,128)S(1)}, u32[]{:S(2)}, u32[]{:S(2)}) %collective-permute-start.2) | collective-permute-done | bytes 20512 | tf_op jit(solution)/shard_map/ppermute | solution.py:417
  25.5 0.2 gather.1
  25.7 0.7 collective-permute-start.4
  26.3 5.1 %collective-permute-start.5 = (f32[320,256]{1,0:T(8,128)S(1)}, f32[320,256]{1,0:T(8,128)S(1)}, u32[]{:S(2)}, u32[]{:S(2)}) collective-permute-start(f32[320,256]{1,0:T(8,128)S(1)} %get-tuple-element.63), channel_id=1, source_target_pairs={{0,240},{16,0},{32,16},{48,32},{64,48},{80,64},{96,80},{112,96},{1... | collective-permute-start | bytes 983048 | tf_op jit(solution)/shard_map/ppermute | solution.py:417
  31.4 4.0 %collective-permute-start.6 = (f32[316,256]{1,0:T(8,128)S(1)}, f32[316,256]{1,0:T(8,128)S(1)}, u32[]{:S(2)}, u32[]{:S(2)}) collective-permute-start(f32[316,256]{1,0:T(8,128)S(1)} %get-tuple-element.60), channel_id=1, source_target_pairs={{0,1},{1,2},{2,3},{3,4},{4,5},{5,6},{6,7},{7,8},{8,9},{9,10},{10,1... | collective-permute-start | bytes 970760 | tf_op jit(solution)/shard_map/ppermute | solution.py:417
  35.5 7.3 %inner.1.direct = f32[32,32,256]{2,1,0:T(8,128)S(1)} custom-call(f32[3,3,21]{2,1,0:T(4,128)S(1)} %copy-done.2, f32[32,32,256]{2,1,0:T(8,128)S(1)} %copy-done.1, f32[328,256]{1,0:T(8,128)S(1)} %collective-permute-done.8.left, f32[328,256]{1,0:T(8,128)S(1)} %collective-permute-done.9.right, bf16[96,192]{1,0:T(8,128)(2,1)S(1)} %get-tuple-element.66.y0, ...), custom_call_target="tpu_custom_call" | custom-call | flops 2000000000 | bytes 6000000 | tf_op jit(solution)/shard_map/inner/pallas_call | solution.py:457
  42.8 4.6 %collective-permute-done.6.left = f32[316,256]{1,0:T(8,128)S(1)} collective-permute-done((f32[316,256]{1,0:T(8,128)S(1)}, f32[316,256]{1,0:T(8,128)S(1)}, u32[]{:S(2)}, u32[]{:S(2)}) %collective-permute-start.6) | collective-permute-done | bytes 323616 | tf_op jit(solution)/shard_map/ppermute | solution.py:417
  47.3 4.9 %collective-permute-done.7.right = f32[316,256]{1,0:T(8,128)S(1)} collective-permute-done((f32[316,256]{1,0:T(8,128)S(1)}, f32[316,256]{1,0:T(8,128)S(1)}, u32[]{:S(2)}, u32[]{:S(2)}) %collective-permute-start.7) | collective-permute-done | bytes 323616 | tf_op jit(solution)/shard_map/ppermute | solution.py:417
  52.4 0.1 collective-permute-start.10
  52.5 1.5 %collective-permute-start.11 = (f32[208,256]{1,0:T(8,128)S(1)}, f32[208,256]{1,0:T(8,128)S(1)}, u32[]{:S(2)}, u32[]{:S(2)}) collective-permute-start(f32[208,256]{1,0:T(8,128)S(1)} %get-tuple-element.76), channel_id=1, source_target_pairs={{0,15},{1,0},{2,1},{3,2},{4,3},{5,4},{6,5},{7,6},{8,7},{9,8},{10,9... | collective-permute-start | bytes 638984 | tf_op jit(solution)/shard_map/ppermute | solution.py:417
  53.9 0.4 collective-permute-start.12
  54.3 3.4 %collective-permute-start.13 = (f32[80,128]{1,0:T(8,128)S(1)}, f32[80,128]{1,0:T(8,128)S(1)}, u32[]{:S(2)}, u32[]{:S(2)}) collective-permute-start(f32[80,128]{1,0:T(8,128)S(1)} %get-tuple-element.72), channel_id=1, source_target_pairs={{0,15},{1,0},{2,1},{3,2},{4,3},{5,4},{6,5},{7,6},{8,7},{9,8},{10,9... | collective-permute-start | bytes 122888 | tf_op jit(solution)/shard_map/ppermute | solution.py:417
  57.7 3.4 %fine_level.1.mid_in = f32[18,32,128]{2,1,0:T(8,128)S(1)} custom-call(f32[3,3,21]{2,1,0:T(4,128)S(1)} %copy-done.2, f32[38,24,128]{2,1,0:T(8,128)S(1)} %get-tuple-element.82.l1x, f32[316,256]{1,0:T(8,128)S(1)} %collective-permute-done.6.left, f32[316,256]{1,0:T(8,128)S(1)} %collective-permute-done.7.right, bf16[96,144]{1,0:T(8,128)(2,1)S(1)} %get-tuple-element.83.y1, ...), custom_call_target="tpu_custom_call" | custom-call | flops 400000000 | bytes 4000000 | tf_op jit(solution)/shard_map/fine_level/pallas_call | solution.py:474
  61.1 2.8 %upper.1.inner = f32[32,32,256]{2,1,0:T(8,128)S(1)} custom-call(f32[3,3,21]{2,1,0:T(4,128)S(1)} %copy-done.2, f32[16,16,128]{2,1,0:T(8,128)S(1)} %get-tuple-element.77.l2x, f32[316,256]{1,0:T(8,128)S(1)} %collective-permute-done.6.left, f32[316,256]{1,0:T(8,128)S(1)} %collective-permute-done.7.right, f32[80,128]{1,0:T(8,128)S(1)} %collective-permute-done.12.left2, ...), custom_call_target="tpu_custom_call" | custom-call | flops 400000000 | bytes 4000000 | tf_op jit(solution)/shard_map/upper/pallas_call | solution.py:479
  63.9 4.2 %finest.1 = f32[32,32,256]{2,1,0:T(8,128)} custom-call(f32[3,3,21]{2,1,0:T(4,128)S(1)} %copy-done.2, f32[320,256]{1,0:T(8,128)S(1)} %collective-permute-done.4.before, f32[320,256]{1,0:T(8,128)S(1)} %collective-permute-done.5.after, f32[208,256]{1,0:T(8,128)S(1)} %collective-permute-done.10.left, f32[208,256]{1,0:T(8,128)S(1)} %collective-permute-done.11.right, ...), custom_call_target="tpu_custom_call" | custom-call | flops 2000000000 | bytes 6000000 | tf_op jit(solution)/shard_map/finest/pallas_call | solution.py:486
  (20 shorter events, 0.2 us)
Async XLA Ops:
  0.0 1.2 %copy-start = (f32[32,32,256]{2,1,0:T(8,128)S(1)}, f32[32,32,256]{2,1,0:T(8,128)}, u32[]{:S(2)}) copy-start(f32[32,32,256]{2,1,0:T(8,128)} %c.3) | copy-start | bytes 3145732
  2.3 11.1 %copy-start.2 = (f32[3,3,21]{2,1,0:T(4,128)S(1)}, f32[3,3,21]{2,1,0:T(4,128)}, u32[]{:S(2)}) copy-start(f32[3,3,21]{2,1,0:T(4,128)} %taps.4) | copy-start | bytes 2272
  2.3 14.1 %collective-permute-start = (f32[288,128]{1,0:T(8,128)S(1)}, f32[288,128]{1,0:T(8,128)S(1)}, u32[]{:S(2)}, u32[]{:S(2)}) collective-permute-start(f32[288,128]{1,0:T(8,128)S(1)} %get-tuple-element.53), channel_id=1, source_target_pairs={{0,16},{16,32},{32,48},{48,64},{64,80},{80,96},{96,112},{112,128},... | collective-permute-start | bytes 442376 | tf_op jit(solution)/shard_map/ppermute | solution.py:417
  6.2 11.2 %collective-permute-start.1 = (f32[288,128]{1,0:T(8,128)S(1)}, f32[288,128]{1,0:T(8,128)S(1)}, u32[]{:S(2)}, u32[]{:S(2)}) collective-permute-start(f32[288,128]{1,0:T(8,128)S(1)} %get-tuple-element.54), channel_id=1, source_target_pairs={{0,240},{16,0},{32,16},{48,32},{64,48},{80,64},{96,80},{112,96},{1... | collective-permute-start | bytes 442376 | tf_op jit(solution)/shard_map/ppermute | solution.py:417
  11.7 23.7 %collective-permute-start.8 = (f32[328,256]{1,0:T(8,128)S(1)}, f32[328,256]{1,0:T(8,128)S(1)}, u32[]{:S(2)}, u32[]{:S(2)}) collective-permute-start(f32[328,256]{1,0:T(8,128)S(1)} %get-tuple-element.64), channel_id=1, source_target_pairs={{0,1},{1,2},{2,3},{3,4},{4,5},{5,6},{6,7},{7,8},{8,9},{9,10},{10,1... | collective-permute-start | bytes 1007624 | tf_op jit(solution)/shard_map/ppermute | solution.py:417
  13.3 22.1 %collective-permute-start.9 = (f32[328,256]{1,0:T(8,128)S(1)}, f32[328,256]{1,0:T(8,128)S(1)}, u32[]{:S(2)}, u32[]{:S(2)}) collective-permute-start(f32[328,256]{1,0:T(8,128)S(1)} %get-tuple-element.65), channel_id=1, source_target_pairs={{0,15},{1,0},{2,1},{3,2},{4,3},{5,4},{6,5},{7,6},{8,7},{9,8},{10,9... | collective-permute-start | bytes 1007624 | tf_op jit(solution)/shard_map/ppermute | solution.py:417
  17.4 18.1 %copy-start.1 = (f32[32,32,256]{2,1,0:T(8,128)S(1)}, f32[32,32,256]{2,1,0:T(8,128)}, u32[]{:S(2)}) copy-start(f32[32,32,256]{2,1,0:T(8,128)} %c.3) | copy-start | bytes 3145732
  17.5 8.0 %collective-permute-start.2 = (f32[40,128]{1,0:T(8,128)S(1)}, f32[40,128]{1,0:T(8,128)S(1)}, u32[]{:S(2)}, u32[]{:S(2)}) collective-permute-start(f32[40,128]{1,0:T(8,128)S(1)} %get-tuple-element.58), channel_id=1, source_target_pairs={{0,16},{16,32},{32,48},{48,64},{64,80},{80,96},{96,112},{112,128},... | collective-permute-start | bytes 61448 | tf_op jit(solution)/shard_map/ppermute | solution.py:417
  20.7 4.8 %collective-permute-start.3 = (f32[40,128]{1,0:T(8,128)S(1)}, f32[40,128]{1,0:T(8,128)S(1)}, u32[]{:S(2)}, u32[]{:S(2)}) collective-permute-start(f32[40,128]{1,0:T(8,128)S(1)} %get-tuple-element.59), channel_id=1, source_target_pairs={{0,240},{16,0},{32,16},{48,32},{64,48},{80,64},{96,80},{112,96},{1... | collective-permute-start | bytes 61448 | tf_op jit(solution)/shard_map/ppermute | solution.py:417
  25.7 26.6 %collective-permute-start.4 = (f32[320,256]{1,0:T(8,128)S(1)}, f32[320,256]{1,0:T(8,128)S(1)}, u32[]{:S(2)}, u32[]{:S(2)}) collective-permute-start(f32[320,256]{1,0:T(8,128)S(1)} %get-tuple-element.62), channel_id=1, source_target_pairs={{0,16},{16,32},{32,48},{48,64},{64,80},{80,96},{96,112},{112,128},... | collective-permute-start | bytes 983048 | tf_op jit(solution)/shard_map/ppermute | solution.py:417
  26.3 26.0 %collective-permute-start.5 = (f32[320,256]{1,0:T(8,128)S(1)}, f32[320,256]{1,0:T(8,128)S(1)}, u32[]{:S(2)}, u32[]{:S(2)}) collective-permute-start(f32[320,256]{1,0:T(8,128)S(1)} %get-tuple-element.63), channel_id=1, source_target_pairs={{0,240},{16,0},{32,16},{48,32},{64,48},{80,64},{96,80},{112,96},{1... | collective-permute-start | bytes 983048 | tf_op jit(solution)/shard_map/ppermute | solution.py:417
  31.4 15.9 %collective-permute-start.6 = (f32[316,256]{1,0:T(8,128)S(1)}, f32[316,256]{1,0:T(8,128)S(1)}, u32[]{:S(2)}, u32[]{:S(2)}) collective-permute-start(f32[316,256]{1,0:T(8,128)S(1)} %get-tuple-element.60), channel_id=1, source_target_pairs={{0,1},{1,2},{2,3},{3,4},{4,5},{5,6},{6,7},{7,8},{8,9},{9,10},{10,1... | collective-permute-start | bytes 970760 | tf_op jit(solution)/shard_map/ppermute | solution.py:417
  35.4 16.8 %collective-permute-start.7 = (f32[316,256]{1,0:T(8,128)S(1)}, f32[316,256]{1,0:T(8,128)S(1)}, u32[]{:S(2)}, u32[]{:S(2)}) collective-permute-start(f32[316,256]{1,0:T(8,128)S(1)} %get-tuple-element.61), channel_id=1, source_target_pairs={{0,15},{1,0},{2,1},{3,2},{4,3},{5,4},{6,5},{7,6},{8,7},{9,8},{10,9... | collective-permute-start | bytes 970760 | tf_op jit(solution)/shard_map/ppermute | solution.py:417
  52.4 11.6 %collective-permute-start.10 = (f32[208,256]{1,0:T(8,128)S(1)}, f32[208,256]{1,0:T(8,128)S(1)}, u32[]{:S(2)}, u32[]{:S(2)}) collective-permute-start(f32[208,256]{1,0:T(8,128)S(1)} %get-tuple-element.75), channel_id=1, source_target_pairs={{0,1},{1,2},{2,3},{3,4},{4,5},{5,6},{6,7},{7,8},{8,9},{9,10},{10,1... | collective-permute-start | bytes 638984 | tf_op jit(solution)/shard_map/ppermute | solution.py:417
  52.5 11.5 %collective-permute-start.11 = (f32[208,256]{1,0:T(8,128)S(1)}, f32[208,256]{1,0:T(8,128)S(1)}, u32[]{:S(2)}, u32[]{:S(2)}) collective-permute-start(f32[208,256]{1,0:T(8,128)S(1)} %get-tuple-element.76), channel_id=1, source_target_pairs={{0,15},{1,0},{2,1},{3,2},{4,3},{5,4},{6,5},{7,6},{8,7},{9,8},{10,9... | collective-permute-start | bytes 638984 | tf_op jit(solution)/shard_map/ppermute | solution.py:417
  53.9 7.1 %collective-permute-start.12 = (f32[80,128]{1,0:T(8,128)S(1)}, f32[80,128]{1,0:T(8,128)S(1)}, u32[]{:S(2)}, u32[]{:S(2)}) collective-permute-start(f32[80,128]{1,0:T(8,128)S(1)} %get-tuple-element.71), channel_id=1, source_target_pairs={{0,1},{1,2},{2,3},{3,4},{4,5},{5,6},{6,7},{7,8},{8,9},{9,10},{10,1... | collective-permute-start | bytes 122888 | tf_op jit(solution)/shard_map/ppermute | solution.py:417
  54.3 6.8 %collective-permute-start.13 = (f32[80,128]{1,0:T(8,128)S(1)}, f32[80,128]{1,0:T(8,128)S(1)}, u32[]{:S(2)}, u32[]{:S(2)}) collective-permute-start(f32[80,128]{1,0:T(8,128)S(1)} %get-tuple-element.72), channel_id=1, source_target_pairs={{0,15},{1,0},{2,1},{3,2},{4,3},{5,4},{6,5},{7,6},{8,7},{9,8},{10,9... | collective-permute-start | bytes 122888 | tf_op jit(solution)/shard_map/ppermute | solution.py:417

commit v5 on v4

--- a/solution.py
+++ b/solution.py
@@ -11,7 +11,6 @@
 BF = jnp.bfloat16
 F32 = jnp.float32
 VMEM_LIMIT = 48 * 1024 * 1024
-HINT = 2 * 10**10
 
 
 def halves(x):
@@ -120,6 +119,10 @@
 
 
 def restrict_kernel(c, l1, l2, up1, down1, last, first, face_up, face_down, s1, s2):
+    ry = spline_iota((24, 32), 2, 0, 1, 18).astype(BF)
+    for i in range(-1, 17):
+        high, low = halves(spline_sum(lambda r: c[r], i, 0, 31))
+        s1[i + 1] = dot(ry, high) + dot(ry, low)
     for i in range(32):
         face_up[pl.ds(10 * i, 10)] = c[i, 22:32]
         face_down[pl.ds(10 * i, 10)] = c[i, 0:10]
@@ -128,10 +131,6 @@
     for r in range(10):
         last[pl.ds(32 * r, 32)] = c[22 + r]
         first[pl.ds(32 * r, 32)] = c[r]
-    ry = spline_iota((24, 32), 2, 0, 1, 18).astype(BF)
-    for i in range(-1, 17):
-        high, low = halves(spline_sum(lambda r: c[r], i, 0, 31))
-        s1[i + 1] = dot(ry, high) + dot(ry, low)
     rz = cyclic_iota((256, 128), 1, 0, 256).astype(BF)
     high, low = halves(s1[...].reshape(18 * 24, 256))
     l1[...] = (dot(high, rz) + dot(low, rz)).reshape(18, 24, 128)
@@ -165,21 +164,22 @@
     return (pl.ds(base + count * (j // 2), count), pl.ds(128 * (j % 2), 128))
 
 
-def forward_kernel(left, right, up, down):
+def face_x_kernel(last, first, left, right, up, down):
+    up[pl.ds(0, 320)] = last[...]
+    down[pl.ds(0, 320)] = first[...]
     lower = lax.broadcasted_iota(jnp.int32, (11, 128), 1) < 64
     for p in range(3):
         even = 2 * p
         odd = min(even + 1, 4)
-        rows = pl.ds(11 * p, 11)
         a = left[pl.ds(11 * even, 11)]
         b = left[pl.ds(11 * odd, 11)]
-        up[rows] = jnp.where(lower, pltpu.roll(a, 64, 1), b)
+        up[paired(320, 11, p)] = jnp.where(lower, pltpu.roll(a, 64, 1), b)
         a = right[pl.ds(11 * even, 11)]
         b = right[pl.ds(11 * odd, 11)]
-        down[rows] = jnp.where(lower, a, pltpu.roll(b, 64, 1))
-
-
-def gather_kernel(l1, l2, left, right, left2, right2, l1x, l2x, up, down):
+        down[paired(320, 11, p)] = jnp.where(lower, a, pltpu.roll(b, 64, 1))
+
+
+def gather_fine_kernel(l1, left, right, l1x, up, down):
     for i in range(38):
         if i < 12:
             l1x[i, :18] = left[pl.ds(72 + 18 * i, 18)]
@@ -192,8 +192,17 @@
         elif 12 <= i < 26:
             l1x[i] = l1[i - 10]
     for i in range(38):
-        up[paired(0, 12, i)] = l1x[i, 6:18]
-        down[paired(0, 12, i)] = l1x[i, 0:12]
+        up[pl.ds(12 * i, 12)] = l1x[i, 6:18]
+        down[pl.ds(12 * i, 12)] = l1x[i, 0:12]
+
+
+def gather_top_kernel(before, after, l2, left, right, l2x, up, down, up2, down2):
+    for i in range(20):
+        row = before[pl.ds(32 * i, 32)] if i < 10 else after[pl.ds(32 * (i - 10), 32)]
+        up[pl.ds(10 * i, 10)] = row[22:32]
+        down[pl.ds(10 * i, 10)] = row[0:10]
+    up[pl.ds(200, 8)] = jnp.zeros((8, 256), F32)
+    down[pl.ds(200, 8)] = jnp.zeros((8, 256), F32)
     lanes = lax.broadcasted_iota(jnp.int32, (11, 128), 1)
     lower = lanes < 64
     rolled = lambda x: pltpu.roll(x, 64, 1)
@@ -201,7 +210,7 @@
         low = []
         high = []
         if j < 5:
-            slab = left2[pl.ds(11 * (j // 2), 11)]
+            slab = before[paired(320, 11, j // 2)]
             low.append(slab if j % 2 == 0 else rolled(slab))
         if 2 <= j < 8:
             low.append(left[pl.ds(11 * (j - 2), 11)])
@@ -216,29 +225,15 @@
         if 8 <= j < 13:
             high.append(right[pl.ds(11 * (j - 8), 11)])
         if 10 <= j < 15:
-            slab = right2[pl.ds(11 * ((j - 10) // 2), 11)]
+            slab = after[paired(320, 11, (j - 10) // 2)]
             high.append(rolled(slab) if j % 2 == 0 else slab)
         row = jnp.where(lower, sum(low, jnp.zeros((11, 128), F32)), sum(high, jnp.zeros((11, 128), F32)))
         l2x[j, :11] = row
         l2x[j, pl.ds(11, 5)] = jnp.zeros((5, 128), F32)
-        up[paired(228, 11, j)] = row
-        down[paired(228, 11, j)] = row
-
-
-def corner_kernel(before, after, up, down):
-    for i in range(20):
-        row = before[pl.ds(32 * i, 32)] if i < 10 else after[pl.ds(32 * (i - 10), 32)]
-        up[pl.ds(10 * i, 10)] = row[22:32]
-        down[pl.ds(10 * i, 10)] = row[0:10]
-    up[pl.ds(200, 8)] = jnp.zeros((8, 256), F32)
-    down[pl.ds(200, 8)] = jnp.zeros((8, 256), F32)
-
-
-def second_kernel(left, right, up, down):
-    for j in range(16):
-        rows, lanes = paired(228, 11, j)
-        up[pl.ds(5 * j, 5)] = left[pl.ds(rows.start + 6, 5), lanes]
-        down[pl.ds(5 * j, 5)] = right[pl.ds(rows.start, 5), lanes]
+        up[paired(208, 11, j)] = row
+        down[paired(208, 11, j)] = row
+        up2[pl.ds(5 * j, 5)] = row[6:11]
+        down2[pl.ds(5 * j, 5)] = row[0:5]
 
 
 def correlate_x(taps, level, v, w, count, many):
@@ -270,9 +265,9 @@
 
 def fine_level_kernel(taps, l1x, left, right, y1, z1, mid, f1, v1, w1):
     for i in range(38):
-        f1[i, pl.ds(0, 12)] = left[paired(0, 12, i)]
+        f1[i, pl.ds(0, 12)] = left[pl.ds(12 * i, 12)]
         f1[i, pl.ds(12, 18)] = l1x[i, :18]
-        f1[i, pl.ds(30, 12)] = right[paired(0, 12, i)]
+        f1[i, pl.ds(30, 12)] = right[pl.ds(12 * i, 12)]
         f1[i, pl.ds(42, 6)] = jnp.zeros((6, 128), F32)
 
     @pl.loop(0, 38, unroll=19)
@@ -285,11 +280,11 @@
 
 
 def upper_kernel(taps, l2x, left, right, left2, right2, y2, z2, up1, mid_in, direct, out,
-                 f2, v2, w2, mid, fine):
+                 f2, v2, w2, mid, fine, done, sems):
     for j in range(16):
         f2[j, pl.ds(0, 16)] = l2x[j]
-        f2[j, pl.ds(16, 11)] = left[paired(228, 11, j)]
-        f2[j, pl.ds(27, 11)] = right[paired(228, 11, j)]
+        f2[j, pl.ds(16, 11)] = left[paired(208, 11, j)]
+        f2[j, pl.ds(27, 11)] = right[paired(208, 11, j)]
         f2[j, pl.ds(38, 5)] = left2[pl.ds(5 * j, 5)]
         f2[j, pl.ds(43, 5)] = right2[pl.ds(5 * j, 5)]
 
@@ -311,10 +306,15 @@
     for a in range(16):
         fine[2 * a] = 0.75 * mid[a + 1] + 0.125 * (mid[a] + mid[a + 2])
         fine[2 * a + 1] = 0.5 * (mid[a + 1] + mid[a + 2])
+    copies = []
     for q in range(4):
         rows = pl.ds(8 * q, 8)
         high, low = halves(fine[rows].reshape(256, 128))
-        out[rows] = direct[rows] + dot(jnp.concatenate([high, low], 1), up1[...]).reshape(8, 32, 256)
+        done[rows] = direct[rows] + dot(jnp.concatenate([high, low], 1), up1[...]).reshape(8, 32, 256)
+        copies.append(pltpu.make_async_copy(done.at[rows], out.at[rows], sems.at[q]))
+        copies[q].start()
+    for copy in copies:
+        copy.wait()
 
 
 def section(table, own, left, right, base, at):
@@ -396,16 +396,17 @@
         out[pl.ds(22, 10), cols] = inner[pl.ds(22, 10), cols] + total[10:]
 
 
-def call(kernel, outs, scratch=(), scalars=0, count=0, flops=0, moved=0, name=None):
+def call(kernel, outs, scratch=(), scalars=0, count=0, flops=0, moved=0, name=None, sems=0, far=False):
     vmem = pl.BlockSpec(memory_space=pltpu.VMEM)
     smem = pl.BlockSpec(memory_space=pltpu.SMEM)
+    hbm = pl.BlockSpec(memory_space=pltpu.HBM)
     shapes = [jax.ShapeDtypeStruct(*o) for o in outs]
     return pl.pallas_call(
         kernel,
         out_shape=shapes,
         in_specs=[smem] * scalars + [vmem] * (count - scalars),
-        out_specs=[vmem] * len(shapes),
-        scratch_shapes=[pltpu.VMEM(*s) for s in scratch],
+        out_specs=[hbm if far else vmem] * len(shapes),
+        scratch_shapes=[pltpu.VMEM(*s) for s in scratch] + [pltpu.SemaphoreType.DMA((sems,))] * (sems > 0),
         compiler_params=pltpu.CompilerParams(vmem_limit_bytes=VMEM_LIMIT),
         cost_estimate=pl.CostEstimate(flops=flops, bytes_accessed=moved, transcendentals=0),
         name=name,
@@ -427,8 +428,6 @@
     )(charges)
     x_left = shift(s_up, "gx", 1)
     x_right = shift(s_down, "gx", -1)
-    own_left = shift(o_up, "gy", 1)
-    own_right = shift(o_down, "gy", -1)
     taps, l1 = lax.optimization_barrier((taps, l1))
     y0, y1, y2, z0h, z0l, z1, z2, up1 = call(
         matrices_kernel,
@@ -436,58 +435,56 @@
          ((768, 256), BF), ((768, 256), BF), ((256, 256), BF)],
         [], 1, 1, 10**8, 4 * 10**6, name="matrices",
     )(taps)
+    own_left = shift(o_up, "gy", 1)
+    own_right = shift(o_down, "gy", -1)
     x_left, x_right, y0 = lax.optimization_barrier((x_left, x_right, y0))
     c_up, c_down = call(
-        forward_kernel, [((40, 128), F32), ((40, 128), F32)], [], 0, 2, HINT, 0, name="forward",
-    )(x_left, x_right)
-    x_left2 = shift(c_up, "gx", 1)
-    x_right2 = shift(c_down, "gx", -1)
-
-    l1x, l2x, g_up, g_down = call(
-        gather_kernel,
-        [((38, 24, 128), F32), ((16, 16, 128), F32), ((316, 256), F32), ((316, 256), F32)],
-        [], 0, 6, 0, 0, name="gather",
-    )(l1, l2, x_left, x_right, x_left2, x_right2)
-    left = shift(g_up, "gy", 1)
-    right = shift(g_down, "gy", -1)
-    last, first, g_up, g_down = lax.optimization_barrier((last, first, g_up, g_down))
-    before = shift(last, "gx", 1)
-    after = shift(first, "gx", -1)
+        face_x_kernel, [((344, 256), F32), ((344, 256), F32)], [], 0, 4, 2 * 10**10, 2 * 10**6, name="face_x",
+    )(last, first, x_left, x_right)
+    before = shift(c_up, "gx", 1)
+    after = shift(c_down, "gx", -1)
+    x_left, x_right, c_up = lax.optimization_barrier((x_left, x_right, c_up))
+    l1x, g_up, g_down = call(
+        gather_fine_kernel, [((38, 24, 128), F32), ((456, 128), F32), ((456, 128), F32)],
+        [], 0, 3, 2 * 10**10, 2 * 10**6, name="gather_fine",
+    )(l1, x_left, x_right)
+    fine_left = shift(g_up, "gy", 1)
+    fine_right = shift(g_down, "gy", -1)
     y0, g_up, g_down = lax.optimization_barrier((y0, g_up, g_down))
     inner, = call(
         inner_kernel, [((32, 32, 256), F32)],
         [((32, 96, 256), F32), ((256, 768), BF), ((256, 768), BF)], 1, 7, 2 * 10**9, 6 * 10**6, name="inner",
     )(taps, charges, own_left, own_right, y0, z0h, z0l)
-    left, right, inner = lax.optimization_barrier((left, right, inner))
-    t_up, t_down = call(
-        second_kernel, [((80, 128), F32), ((80, 128), F32)], [], 0, 2, 10**5, 10**6, name="second",
-    )(left, right)
-    left2 = shift(t_up, "gy", 1)
-    right2 = shift(t_down, "gy", -1)
-    before, after, t_up, t_down = lax.optimization_barrier((before, after, t_up, t_down))
-    f_up, f_down = call(
-        corner_kernel, [((208, 256), F32), ((208, 256), F32)], [], 0, 2, 10**6, 10**6, name="corner",
-    )(before, after)
-    corner_left = shift(f_up, "gy", 1)
-    corner_right = shift(f_down, "gy", -1)
+    before, after, inner, fine_left, fine_right = lax.optimization_barrier(
+        (before, after, inner, fine_left, fine_right)
+    )
+    l2x, f_up, f_down, t_up, t_down = call(
+        gather_top_kernel,
+        [((16, 16, 128), F32), ((296, 256), F32), ((296, 256), F32), ((80, 128), F32), ((80, 128), F32)],
+        [], 0, 5, 10**6, 5 * 10**6, name="gather_top",
+    )(before, after, l2, x_left, x_right)
+    left = shift(f_up, "gy", 1)
+    right = shift(f_down, "gy", -1)
+    left2 = shift(t_up, "gy", 2)
+    right2 = shift(t_down, "gy", -2)
     l1x, f_up, f_down = lax.optimization_barrier((l1x, f_up, f_down))
     mid, = call(
         fine_level_kernel, [((18, 32, 128), F32)],
         [((38, 48, 128), F32), ((38, 96, 128), F32), ((18, 96, 128), F32)],
         1, 6, 4 * 10**8, 4 * 10**6, name="fine_level",
-    )(taps, l1x, left, right, y1, z1)
-    partial, = call(
-        upper_kernel, [((32, 32, 256), F32)],
-        [((16, 48, 128), F32), ((32, 96, 128), F32), ((11, 96, 128), F32), ((18, 32, 128), F32),
-         ((32, 32, 128), F32)],
-        1, 11, 4 * 10**8, 4 * 10**6, name="upper",
-    )(taps, l2x, left, right, left2, right2, y2, z2, up1, mid, inner)
-    corner_left, corner_right, partial = lax.optimization_barrier((corner_left, corner_right, partial))
-    result, = call(
+    )(taps, l1x, fine_left, fine_right, y1, z1)
+    left, right, mid = lax.optimization_barrier((left, right, mid))
+    direct, = call(
         finest_kernel, [((32, 32, 256), F32)],
         [((20, 96, 256), F32), ((160, 768), BF), ((160, 768), BF)],
         1, 9, 2 * 10**9, 6 * 10**6, name="finest",
-    )(taps, before, after, corner_left, corner_right, y0, z0h, z0l, partial)
+    )(taps, before, after, left, right, y0, z0h, z0l, inner)
+    result, = call(
+        upper_kernel, [((32, 32, 256), F32)],
+        [((16, 48, 128), F32), ((32, 96, 128), F32), ((11, 96, 128), F32), ((18, 32, 128), F32),
+         ((32, 32, 128), F32), ((32, 32, 256), F32)],
+        1, 11, 4 * 10**8, 4 * 10**6, name="upper", sems=4, far=True,
+    )(taps, l2x, left, right, left2, right2, y2, z2, up1, mid, direct)
     return result
 
 

time: 69.3 us -> 64.5 us (0.931)
  waiting for transfers between devices: 12.8 us -> 5.68 us
  starting transfers between devices: 31.9 us -> 35 us
    ppermute x14 -> x12, waiting for transfers between devices: 12.8 us -> 5.68 us  [shift(): return lax.ppermute(x, axis, [(i, (i + by) % n) for i in range(n)])]
    ppermute x14 -> x12, starting transfers between devices: 31.9 us -> 35 us  [shift(): return lax.ppermute(x, axis, [(i, (i + by) % n) for i in range(n)])]
    pallas_call x1, Pallas kernels: 4.24 us -> 3.29 us  [body(): call(finest_kernel, [((32, 32, 256), F32)], [((20, 96, 256), F32), ((160,...]
    pallas_call x1, Pallas kernels: 2.82 us -> 3.61 us  [body(): call(upper_kernel, [((32, 32, 256), F32)], [((16, 48, 128), F32), ((32, 9...]
  transfers between devices with their start and end apart: 14 -> 12, of which waited for: 4 -> 3; matrix products, arithmetic and copies ran while one was open for 0% -> 0% of each run, Pallas kernels for 25% -> 27%
where the time goes in v5:
time: 64.5 us; the launch traced here: 64.1 us
  starting transfers between devices  35 us (54%)
  Pallas kernels  21.8 us (34%)
  waiting for transfers between devices  5.68 us (9%)
  local copies, waits for them, and re-layouts  1.23 us (2%)
    ppermute x12, starting transfers between devices, shift(): return lax.ppermute(x, axis, [(i, (i + by) % n) for i in range(n)])  35 us
    pallas_call x1, Pallas kernels, body(): call(inner_kernel, [((32, 32, 256), F32)], [((32, 96, 256), F32), ((256,...  7.25 us
    ppermute x12, waiting for transfers between devices, shift(): return lax.ppermute(x, axis, [(i, (i + by) % n) for i in range(n)])  5.68 us
    pallas_call x1, Pallas kernels, body(): call(upper_kernel, [((32, 32, 256), F32)], [((16, 48, 128), F32), ((32, 9...  3.61 us
    pallas_call x1, Pallas kernels, body(): call(fine_level_kernel, [((18, 32, 128), F32)], [((38, 48, 128), F32), ((...  3.38 us
    pallas_call x1, Pallas kernels, body(): call(finest_kernel, [((32, 32, 256), F32)], [((20, 96, 256), F32), ((160,...  3.29 us
    pallas_call x1, Pallas kernels, body(): call(matrices_kernel, [((96, 192), BF), ((96, 144), BF), ((96, 144), BF),...  3.02 us
  transfers between devices with their start and end apart: 12, of which 3 were waited for; matrix products, arithmetic and copies ran while one was open for 0% of the time, Pallas kernels for 27%

profile of v5, /device:TPU:1, one launch (start us, length us, event | category | flops | bytes accessed | tf_op | source)
XLA Modules:
  0.0 64.1 jit_solution(7014128640708067679)
XLA Ops:
  0.0 1.2 %copy-done = f32[32,32,256]{2,1,0:T(8,128)S(1)} copy-done((f32[32,32,256]{2,1,0:T(8,128)S(1)}, f32[32,32,256]{2,1,0:T(8,128)}, u32[]{:S(2)}) %copy-start) | copy-done | bytes 1048600
  1.2 1.0 %restrict.1 = (f32[18,24,128]{2,1,0:T(8,128)S(1)}, f32[6,16,128]{2,1,0:T(8,128)S(1)}, f32[288,128]{1,0:T(8,128)S(1)}, f32[288,128]{1,0:T(8,128)S(1)}, f32[320,25...) custom-call(f32[32,32,256]{2,1,0:T(8,128)S(1)} %copy-done), custom_call_target="tpu_custom_call" | custom-call | flops 100000000 | bytes 2000000 | tf_op jit(solution)/shard_map/restrict/pallas_call | solution.py:423
  2.2 0.0 copy-start.2
  2.3 3.9 %collective-permute-start = (f32[288,128]{1,0:T(8,128)S(1)}, f32[288,128]{1,0:T(8,128)S(1)}, u32[]{:S(2)}, u32[]{:S(2)}) collective-permute-start(f32[288,128]{1,0:T(8,128)S(1)} %get-tuple-element.52), channel_id=1, source_target_pairs={{0,16},{16,32},{32,48},{48,64},{64,80},{80,96},{96,112},{112,128},... | collective-permute-start | bytes 442376 | tf_op jit(solution)/shard_map/ppermute | solution.py:418
  6.2 5.6 %collective-permute-start.1 = (f32[288,128]{1,0:T(8,128)S(1)}, f32[288,128]{1,0:T(8,128)S(1)}, u32[]{:S(2)}, u32[]{:S(2)}) collective-permute-start(f32[288,128]{1,0:T(8,128)S(1)} %get-tuple-element.53), channel_id=1, source_target_pairs={{0,240},{16,0},{32,16},{48,32},{64,48},{80,64},{96,80},{112,96},{1... | collective-permute-start | bytes 442376 | tf_op jit(solution)/shard_map/ppermute | solution.py:418
  11.7 1.6 %collective-permute-start.4 = (f32[328,256]{1,0:T(8,128)S(1)}, f32[328,256]{1,0:T(8,128)S(1)}, u32[]{:S(2)}, u32[]{:S(2)}) collective-permute-start(f32[328,256]{1,0:T(8,128)S(1)} %get-tuple-element.59), channel_id=1, source_target_pairs={{0,1},{1,2},{2,3},{3,4},{4,5},{5,6},{6,7},{7,8},{8,9},{9,10},{10,1... | collective-permute-start | bytes 1007624 | tf_op jit(solution)/shard_map/ppermute | solution.py:418
  13.3 3.0 %matrices.1 = (bf16[96,192]{1,0:T(8,128)(2,1)S(1)}, bf16[96,144]{1,0:T(8,128)(2,1)S(1)}, bf16[96,144]{1,0:T(8,128)(2,1)S(1)}, bf16[768,256]{1,0:T(8,128)(2,1)S(1...) custom-call(f32[3,3,21]{2,1,0:T(4,128)S(1)} %copy-done.2), custom_call_target="tpu_custom_call" | custom-call | flops 100000000 | bytes 4000000 | tf_op jit(solution)/shard_map/matrices/pallas_call | solution.py:432
  16.3 1.0 %collective-permute-done.1.right = f32[288,128]{1,0:T(8,128)S(1)} collective-permute-done((f32[288,128]{1,0:T(8,128)S(1)}, f32[288,128]{1,0:T(8,128)S(1)}, u32[]{:S(2)}, u32[]{:S(2)}) %collective-permute-start.1) | collective-permute-done | bytes 147488 | tf_op jit(solution)/shard_map/ppermute | solution.py:418
  17.3 0.1 face_x.1
  17.4 3.3 %collective-permute-start.2 = (f32[344,256]{1,0:T(8,128)S(1)}, f32[344,256]{1,0:T(8,128)S(1)}, u32[]{:S(2)}, u32[]{:S(2)}) collective-permute-start(f32[344,256]{1,0:T(8,128)S(1)} %get-tuple-element.57), channel_id=1, source_target_pairs={{0,16},{16,32},{32,48},{48,64},{64,80},{80,96},{96,112},{112,128},... | collective-permute-start | bytes 1056776 | tf_op jit(solution)/shard_map/ppermute | solution.py:418
  20.7 2.5 %collective-permute-start.3 = (f32[344,256]{1,0:T(8,128)S(1)}, f32[344,256]{1,0:T(8,128)S(1)}, u32[]{:S(2)}, u32[]{:S(2)}) collective-permute-start(f32[344,256]{1,0:T(8,128)S(1)} %get-tuple-element.58), channel_id=1, source_target_pairs={{0,240},{16,0},{32,16},{48,32},{64,48},{80,64},{96,80},{112,96},{1... | collective-permute-start | bytes 1056776 | tf_op jit(solution)/shard_map/ppermute | solution.py:418
  23.2 0.1 gather_fine.1
  23.3 3.9 %collective-permute-start.6 = (f32[456,128]{1,0:T(8,128)S(1)}, f32[456,128]{1,0:T(8,128)S(1)}, u32[]{:S(2)}, u32[]{:S(2)}) collective-permute-start(f32[456,128]{1,0:T(8,128)S(1)} %get-tuple-element.65), channel_id=1, source_target_pairs={{0,1},{1,2},{2,3},{3,4},{4,5},{5,6},{6,7},{7,8},{8,9},{9,10},{10,1... | collective-permute-start | bytes 700424 | tf_op jit(solution)/shard_map/ppermute | solution.py:418
  27.2 8.7 %collective-permute-start.7 = (f32[456,128]{1,0:T(8,128)S(1)}, f32[456,128]{1,0:T(8,128)S(1)}, u32[]{:S(2)}, u32[]{:S(2)}) collective-permute-start(f32[456,128]{1,0:T(8,128)S(1)} %get-tuple-element.66), channel_id=1, source_target_pairs={{0,15},{1,0},{2,1},{3,2},{4,3},{5,4},{6,5},{7,6},{8,7},{9,8},{10,9... | collective-permute-start | bytes 700424 | tf_op jit(solution)/shard_map/ppermute | solution.py:418
  35.9 7.2 %inner.1 = f32[32,32,256]{2,1,0:T(8,128)S(1)} custom-call(f32[3,3,21]{2,1,0:T(4,128)S(1)} %copy-done.2, f32[32,32,256]{2,1,0:T(8,128)S(1)} %copy-done.1, f32[328,256]{1,0:T(8,128)S(1)} %collective-permute-done.4.left, f32[328,256]{1,0:T(8,128)S(1)} %collective-permute-done.5.right, bf16[96,192]{1,0:T(8,128)(2,1)S(1)} %get-tuple-element.67.y0, ...), custom_call_target="tpu_custom_call" | custom-call | flops 2000000000 | bytes 6000000 | tf_op jit(solution)/shard_map/inner/pallas_call | solution.py:454
  43.2 3.6 %collective-permute-done.7.right = f32[456,128]{1,0:T(8,128)S(1)} collective-permute-done((f32[456,128]{1,0:T(8,128)S(1)}, f32[456,128]{1,0:T(8,128)S(1)}, u32[]{:S(2)}, u32[]{:S(2)}) %collective-permute-start.7) | collective-permute-done | bytes 233504 | tf_op jit(solution)/shard_map/ppermute | solution.py:418
  46.8 0.1 gather_top.1
  46.9 0.3 collective-permute-start.8
  47.2 1.8 %collective-permute-start.9 = (f32[296,256]{1,0:T(8,128)S(1)}, f32[296,256]{1,0:T(8,128)S(1)}, u32[]{:S(2)}, u32[]{:S(2)}) collective-permute-start(f32[296,256]{1,0:T(8,128)S(1)} %get-tuple-element.75), channel_id=1, source_target_pairs={{0,15},{1,0},{2,1},{3,2},{4,3},{5,4},{6,5},{7,6},{8,7},{9,8},{10,9... | collective-permute-start | bytes 909320 | tf_op jit(solution)/shard_map/ppermute | solution.py:418
  49.0 3.6 %collective-permute-start.11 = (f32[80,128]{1,0:T(8,128)S(1)}, f32[80,128]{1,0:T(8,128)S(1)}, u32[]{:S(2)}, u32[]{:S(2)}) collective-permute-start(f32[80,128]{1,0:T(8,128)S(1)} %get-tuple-element.85), channel_id=1, source_target_pairs={{0,14},{1,15},{2,0},{3,1},{4,2},{5,3},{6,4},{7,5},{8,6},{9,7},{10,... | collective-permute-start | bytes 122888 | tf_op jit(solution)/shard_map/ppermute | solution.py:418
  52.5 3.4 %fine_level.1.mid_in = f32[18,32,128]{2,1,0:T(8,128)S(1)} custom-call(f32[3,3,21]{2,1,0:T(4,128)S(1)} %copy-done.2, f32[38,24,128]{2,1,0:T(8,128)S(1)} %get-tuple-element.77.l1x, f32[456,128]{1,0:T(8,128)S(1)} %collective-permute-done.6.left, f32[456,128]{1,0:T(8,128)S(1)} %collective-permute-done.7.right, bf16[96,144]{1,0:T(8,128)(2,1)S(1)} %get-tuple-element.80.y1, ...), custom_call_target="tpu_custom_call" | custom-call | flops 400000000 | bytes 4000000 | tf_op jit(solution)/shard_map/fine_level/pallas_call | solution.py:471
  55.9 1.1 %collective-permute-done.9.right = f32[296,256]{1,0:T(8,128)S(1)} collective-permute-done((f32[296,256]{1,0:T(8,128)S(1)}, f32[296,256]{1,0:T(8,128)S(1)}, u32[]{:S(2)}, u32[]{:S(2)}) %collective-permute-start.9) | collective-permute-done | bytes 303136 | tf_op jit(solution)/shard_map/ppermute | solution.py:418
  57.0 3.3 %finest.1.direct = f32[32,32,256]{2,1,0:T(8,128)S(1)} custom-call(f32[3,3,21]{2,1,0:T(4,128)S(1)} %copy-done.2, f32[344,256]{1,0:T(8,128)S(1)} %collective-permute-done.2.before, f32[344,256]{1,0:T(8,128)S(1)} %collective-permute-done.3.after, f32[296,256]{1,0:T(8,128)S(1)} %collective-permute-done.8.left, f32[296,256]{1,0:T(8,128)S(1)} %collective-permute-done.9.right, ...), custom_call_target="tpu_custom_call" | custom-call | flops 2000000000 | bytes 6000000 | tf_op jit(solution)/shard_map/finest/pallas_call | solution.py:477
  60.3 3.6 %upper.1 = f32[32,32,256]{2,1,0:T(8,128)} custom-call(f32[3,3,21]{2,1,0:T(4,128)S(1)} %copy-done.2, f32[16,16,128]{2,1,0:T(8,128)S(1)} %get-tuple-element.73.l2x, f32[296,256]{1,0:T(8,128)S(1)} %collective-permute-done.8.left, f32[296,256]{1,0:T(8,128)S(1)} %collective-permute-done.9.right, f32[80,128]{1,0:T(8,128)S(1)} %collective-permute-done.10.left2, ...), custom_call_target="tpu_custom_call" | custom-call | flops 400000000 | bytes 4000000 | tf_op jit(solution)/shard_map/upper/pallas_call | solution.py:482
  (15 shorter events, 0.0 us)
Async XLA Ops:
  0.0 1.2 %copy-start = (f32[32,32,256]{2,1,0:T(8,128)S(1)}, f32[32,32,256]{2,1,0:T(8,128)}, u32[]{:S(2)}) copy-start(f32[32,32,256]{2,1,0:T(8,128)} %c.3) | copy-start | bytes 3145732
  2.2 11.1 %copy-start.2 = (f32[3,3,21]{2,1,0:T(4,128)S(1)}, f32[3,3,21]{2,1,0:T(4,128)}, u32[]{:S(2)}) copy-start(f32[3,3,21]{2,1,0:T(4,128)} %taps.4) | copy-start | bytes 2272
  2.3 14.1 %collective-permute-start = (f32[288,128]{1,0:T(8,128)S(1)}, f32[288,128]{1,0:T(8,128)S(1)}, u32[]{:S(2)}, u32[]{:S(2)}) collective-permute-start(f32[288,128]{1,0:T(8,128)S(1)} %get-tuple-element.52), channel_id=1, source_target_pairs={{0,16},{16,32},{32,48},{48,64},{64,80},{80,96},{96,112},{112,128},... | collective-permute-start | bytes 442376 | tf_op jit(solution)/shard_map/ppermute | solution.py:418
  6.2 11.2 %collective-permute-start.1 = (f32[288,128]{1,0:T(8,128)S(1)}, f32[288,128]{1,0:T(8,128)S(1)}, u32[]{:S(2)}, u32[]{:S(2)}) collective-permute-start(f32[288,128]{1,0:T(8,128)S(1)} %get-tuple-element.53), channel_id=1, source_target_pairs={{0,240},{16,0},{32,16},{48,32},{64,48},{80,64},{96,80},{112,96},{1... | collective-permute-start | bytes 442376 | tf_op jit(solution)/shard_map/ppermute | solution.py:418
  11.7 15.5 %collective-permute-start.4 = (f32[328,256]{1,0:T(8,128)S(1)}, f32[328,256]{1,0:T(8,128)S(1)}, u32[]{:S(2)}, u32[]{:S(2)}) collective-permute-start(f32[328,256]{1,0:T(8,128)S(1)} %get-tuple-element.59), channel_id=1, source_target_pairs={{0,1},{1,2},{2,3},{3,4},{4,5},{5,6},{6,7},{7,8},{8,9},{9,10},{10,1... | collective-permute-start | bytes 1007624 | tf_op jit(solution)/shard_map/ppermute | solution.py:418
  13.3 22.6 %collective-permute-start.5 = (f32[328,256]{1,0:T(8,128)S(1)}, f32[328,256]{1,0:T(8,128)S(1)}, u32[]{:S(2)}, u32[]{:S(2)}) collective-permute-start(f32[328,256]{1,0:T(8,128)S(1)} %get-tuple-element.60), channel_id=1, source_target_pairs={{0,15},{1,0},{2,1},{3,2},{4,3},{5,4},{6,5},{7,6},{8,7},{9,8},{10,9... | collective-permute-start | bytes 1007624 | tf_op jit(solution)/shard_map/ppermute | solution.py:418
  17.4 29.4 %collective-permute-start.2 = (f32[344,256]{1,0:T(8,128)S(1)}, f32[344,256]{1,0:T(8,128)S(1)}, u32[]{:S(2)}, u32[]{:S(2)}) collective-permute-start(f32[344,256]{1,0:T(8,128)S(1)} %get-tuple-element.57), channel_id=1, source_target_pairs={{0,16},{16,32},{32,48},{48,64},{64,80},{80,96},{96,112},{112,128},... | collective-permute-start | bytes 1056776 | tf_op jit(solution)/shard_map/ppermute | solution.py:418
  20.7 15.2 %copy-start.1 = (f32[32,32,256]{2,1,0:T(8,128)S(1)}, f32[32,32,256]{2,1,0:T(8,128)}, u32[]{:S(2)}) copy-start(f32[32,32,256]{2,1,0:T(8,128)} %c.3) | copy-start | bytes 3145732
  20.7 26.1 %collective-permute-start.3 = (f32[344,256]{1,0:T(8,128)S(1)}, f32[344,256]{1,0:T(8,128)S(1)}, u32[]{:S(2)}, u32[]{:S(2)}) collective-permute-start(f32[344,256]{1,0:T(8,128)S(1)} %get-tuple-element.58), channel_id=1, source_target_pairs={{0,240},{16,0},{32,16},{48,32},{64,48},{80,64},{96,80},{112,96},{1... | collective-permute-start | bytes 1056776 | tf_op jit(solution)/shard_map/ppermute | solution.py:418
  23.3 19.9 %collective-permute-start.6 = (f32[456,128]{1,0:T(8,128)S(1)}, f32[456,128]{1,0:T(8,128)S(1)}, u32[]{:S(2)}, u32[]{:S(2)}) collective-permute-start(f32[456,128]{1,0:T(8,128)S(1)} %get-tuple-element.65), channel_id=1, source_target_pairs={{0,1},{1,2},{2,3},{3,4},{4,5},{5,6},{6,7},{7,8},{8,9},{9,10},{10,1... | collective-permute-start | bytes 700424 | tf_op jit(solution)/shard_map/ppermute | solution.py:418
  27.2 19.6 %collective-permute-start.7 = (f32[456,128]{1,0:T(8,128)S(1)}, f32[456,128]{1,0:T(8,128)S(1)}, u32[]{:S(2)}, u32[]{:S(2)}) collective-permute-start(f32[456,128]{1,0:T(8,128)S(1)} %get-tuple-element.66), channel_id=1, source_target_pairs={{0,15},{1,0},{2,1},{3,2},{4,3},{5,4},{6,5},{7,6},{8,7},{9,8},{10,9... | collective-permute-start | bytes 700424 | tf_op jit(solution)/shard_map/ppermute | solution.py:418
  46.9 9.0 %collective-permute-start.8 = (f32[296,256]{1,0:T(8,128)S(1)}, f32[296,256]{1,0:T(8,128)S(1)}, u32[]{:S(2)}, u32[]{:S(2)}) collective-permute-start(f32[296,256]{1,0:T(8,128)S(1)} %get-tuple-element.74), channel_id=1, source_target_pairs={{0,1},{1,2},{2,3},{3,4},{4,5},{5,6},{6,7},{7,8},{8,9},{9,10},{10,1... | collective-permute-start | bytes 909320 | tf_op jit(solution)/shard_map/ppermute | solution.py:418
  47.2 9.8 %collective-permute-start.9 = (f32[296,256]{1,0:T(8,128)S(1)}, f32[296,256]{1,0:T(8,128)S(1)}, u32[]{:S(2)}, u32[]{:S(2)}) collective-permute-start(f32[296,256]{1,0:T(8,128)S(1)} %get-tuple-element.75), channel_id=1, source_target_pairs={{0,15},{1,0},{2,1},{3,2},{4,3},{5,4},{6,5},{7,6},{8,7},{9,8},{10,9... | collective-permute-start | bytes 909320 | tf_op jit(solution)/shard_map/ppermute | solution.py:418
  49.0 11.3 %collective-permute-start.10 = (f32[80,128]{1,0:T(8,128)S(1)}, f32[80,128]{1,0:T(8,128)S(1)}, u32[]{:S(2)}, u32[]{:S(2)}) collective-permute-start(f32[80,128]{1,0:T(8,128)S(1)} %get-tuple-element.84), channel_id=1, source_target_pairs={{0,2},{1,3},{2,4},{3,5},{4,6},{5,7},{6,8},{7,9},{8,10},{9,11},{10,... | collective-permute-start | bytes 122888 | tf_op jit(solution)/shard_map/ppermute | solution.py:418
  49.0 11.3 %collective-permute-start.11 = (f32[80,128]{1,0:T(8,128)S(1)}, f32[80,128]{1,0:T(8,128)S(1)}, u32[]{:S(2)}, u32[]{:S(2)}) collective-permute-start(f32[80,128]{1,0:T(8,128)S(1)} %get-tuple-element.85), channel_id=1, source_target_pairs={{0,14},{1,15},{2,0},{3,1},{4,2},{5,3},{6,4},{7,5},{8,6},{9,7},{10,... | collective-permute-start | bytes 122888 | tf_op jit(solution)/shard_map/ppermute | solution.py:418

commit v6 on v4

--- a/solution.py
+++ b/solution.py
@@ -179,7 +179,7 @@
         down[rows] = jnp.where(lower, a, pltpu.roll(b, 64, 1))
 
 
-def gather_kernel(l1, l2, left, right, left2, right2, l1x, l2x, up, down):
+def gather_kernel(l1, l2, left, right, left2, right2, l1x, l2x, up, down, up2, down2):
     for i in range(38):
         if i < 12:
             l1x[i, :18] = left[pl.ds(72 + 18 * i, 18)]
@@ -223,6 +223,8 @@
         l2x[j, pl.ds(11, 5)] = jnp.zeros((5, 128), F32)
         up[paired(228, 11, j)] = row
         down[paired(228, 11, j)] = row
+        up2[pl.ds(5 * j, 5)] = row[6:11]
+        down2[pl.ds(5 * j, 5)] = row[0:5]
 
 
 def corner_kernel(before, after, up, down):
@@ -232,13 +234,6 @@
         down[pl.ds(10 * i, 10)] = row[0:10]
     up[pl.ds(200, 8)] = jnp.zeros((8, 256), F32)
     down[pl.ds(200, 8)] = jnp.zeros((8, 256), F32)
-
-
-def second_kernel(left, right, up, down):
-    for j in range(16):
-        rows, lanes = paired(228, 11, j)
-        up[pl.ds(5 * j, 5)] = left[pl.ds(rows.start + 6, 5), lanes]
-        down[pl.ds(5 * j, 5)] = right[pl.ds(rows.start, 5), lanes]
 
 
 def correlate_x(taps, level, v, w, count, many):
@@ -358,7 +353,7 @@
         out[:, cols] = total.reshape(32, 8, 256)
 
 
-def finest_kernel(taps, before, after, left, right, y0, z0h, z0l, inner, out, v, wh, wl):
+def finest_kernel(taps, before, after, left, right, y0, z0h, z0l, inner, out, v, wh, wl, done, sems):
     for i in range(20):
         own = before[pl.ds(32 * i, 32)] if i < 10 else after[pl.ds(32 * (i - 10), 32)]
         b = left[pl.ds(10 * i, 16)]
@@ -391,21 +386,27 @@
         cols = pl.ds(pl.multiple_of(8 * g, 8), 8)
         total = dot(wh[...], z0h[...]) + dot(wl[...], z0h[...]) + dot(wh[...], z0l[...])
         total = total.reshape(20, 8, 256)
-        out[pl.ds(0, 10), cols] = inner[pl.ds(0, 10), cols] + total[:10]
-        out[pl.ds(10, 12), cols] = inner[pl.ds(10, 12), cols]
-        out[pl.ds(22, 10), cols] = inner[pl.ds(22, 10), cols] + total[10:]
-
-
-def call(kernel, outs, scratch=(), scalars=0, count=0, flops=0, moved=0, name=None):
+        done[pl.ds(0, 10), cols] = inner[pl.ds(0, 10), cols] + total[:10]
+        done[pl.ds(10, 12), cols] = inner[pl.ds(10, 12), cols]
+        done[pl.ds(22, 10), cols] = inner[pl.ds(22, 10), cols] + total[10:]
+        pltpu.make_async_copy(done.at[:, cols], out.at[:, cols], sems.at[g]).start()
+
+    for g in range(4):
+        cols = pl.ds(8 * g, 8)
+        pltpu.make_async_copy(done.at[:, cols], out.at[:, cols], sems.at[g]).wait()
+
+
+def call(kernel, outs, scratch=(), scalars=0, count=0, flops=0, moved=0, name=None, sems=0, far=False):
     vmem = pl.BlockSpec(memory_space=pltpu.VMEM)
     smem = pl.BlockSpec(memory_space=pltpu.SMEM)
+    hbm = pl.BlockSpec(memory_space=pltpu.HBM)
     shapes = [jax.ShapeDtypeStruct(*o) for o in outs]
     return pl.pallas_call(
         kernel,
         out_shape=shapes,
         in_specs=[smem] * scalars + [vmem] * (count - scalars),
-        out_specs=[vmem] * len(shapes),
-        scratch_shapes=[pltpu.VMEM(*s) for s in scratch],
+        out_specs=[hbm if far else vmem] * len(shapes),
+        scratch_shapes=[pltpu.VMEM(*s) for s in scratch] + [pltpu.SemaphoreType.DMA((sems,))] * (sems > 0),
         compiler_params=pltpu.CompilerParams(vmem_limit_bytes=VMEM_LIMIT),
         cost_estimate=pl.CostEstimate(flops=flops, bytes_accessed=moved, transcendentals=0),
         name=name,
@@ -442,29 +443,25 @@
     )(x_left, x_right)
     x_left2 = shift(c_up, "gx", 1)
     x_right2 = shift(c_down, "gx", -1)
-
-    l1x, l2x, g_up, g_down = call(
+    last, first, c_up, c_down = lax.optimization_barrier((last, first, c_up, c_down))
+    before = shift(last, "gx", 1)
+    after = shift(first, "gx", -1)
+    l1x, l2x, g_up, g_down, t_up, t_down = call(
         gather_kernel,
-        [((38, 24, 128), F32), ((16, 16, 128), F32), ((316, 256), F32), ((316, 256), F32)],
+        [((38, 24, 128), F32), ((16, 16, 128), F32), ((316, 256), F32), ((316, 256), F32),
+         ((80, 128), F32), ((80, 128), F32)],
         [], 0, 6, 0, 0, name="gather",
     )(l1, l2, x_left, x_right, x_left2, x_right2)
     left = shift(g_up, "gy", 1)
     right = shift(g_down, "gy", -1)
-    last, first, g_up, g_down = lax.optimization_barrier((last, first, g_up, g_down))
-    before = shift(last, "gx", 1)
-    after = shift(first, "gx", -1)
+    left2 = shift(t_up, "gy", 2)
+    right2 = shift(t_down, "gy", -2)
     y0, g_up, g_down = lax.optimization_barrier((y0, g_up, g_down))
     inner, = call(
         inner_kernel, [((32, 32, 256), F32)],
-        [((32, 96, 256), F32), ((256, 768), BF), ((256, 768), BF)], 1, 7, 2 * 10**9, 6 * 10**6, name="inner",
+        [((32, 96, 256), F32), ((256, 768), BF), ((256, 768), BF)], 1, 7, 3 * 10**9, 6 * 10**6, name="inner",
     )(taps, charges, own_left, own_right, y0, z0h, z0l)
-    left, right, inner = lax.optimization_barrier((left, right, inner))
-    t_up, t_down = call(
-        second_kernel, [((80, 128), F32), ((80, 128), F32)], [], 0, 2, 10**5, 10**6, name="second",
-    )(left, right)
-    left2 = shift(t_up, "gy", 1)
-    right2 = shift(t_down, "gy", -1)
-    before, after, t_up, t_down = lax.optimization_barrier((before, after, t_up, t_down))
+    before, after, left2, right2, inner = lax.optimization_barrier((before, after, left2, right2, inner))
     f_up, f_down = call(
         corner_kernel, [((208, 256), F32), ((208, 256), F32)], [], 0, 2, 10**6, 10**6, name="corner",
     )(before, after)
@@ -485,8 +482,8 @@
     corner_left, corner_right, partial = lax.optimization_barrier((corner_left, corner_right, partial))
     result, = call(
         finest_kernel, [((32, 32, 256), F32)],
-        [((20, 96, 256), F32), ((160, 768), BF), ((160, 768), BF)],
-        1, 9, 2 * 10**9, 6 * 10**6, name="finest",
+        [((20, 96, 256), F32), ((160, 768), BF), ((160, 768), BF), ((32, 32, 256), F32)],
+        1, 9, 2 * 10**9, 6 * 10**6, name="finest", sems=4, far=True,
     )(taps, before, after, corner_left, corner_right, y0, z0h, z0l, partial)
     return result
 

time: 69.3 us -> 71.9 us (1.038); the launches traced: 68.2 us -> 71.7 us
  waiting for transfers between devices: 12.8 us -> 18.4 us
  starting transfers between devices: 31.9 us -> 30.1 us
    ppermute x14, waiting for transfers between devices: 12.8 us -> 18.4 us  [shift(): return lax.ppermute(x, axis, [(i, (i + by) % n) for i in range(n)])]
    ppermute x14, starting transfers between devices: 31.9 us -> 30.1 us  [shift(): return lax.ppermute(x, axis, [(i, (i + by) % n) for i in range(n)])]
  transfers between devices with their start and end apart: 14 -> 14, of which waited for: 4 -> 3; matrix products, arithmetic and copies ran while one was open for 0% -> 0% of each run, Pallas kernels for 25% -> 23%
where the time goes in v6:
time: 71.9 us; the launch traced here: 71.7 us
  starting transfers between devices  30.1 us (42%)
  Pallas kernels  21.7 us (30%)
  waiting for transfers between devices  18.4 us (26%)
  local copies, waits for them, and re-layouts  1.23 us (2%)
    ppermute x14, starting transfers between devices, shift(): return lax.ppermute(x, axis, [(i, (i + by) % n) for i in range(n)])  30.1 us
    ppermute x14, waiting for transfers between devices, shift(): return lax.ppermute(x, axis, [(i, (i + by) % n) for i in range(n)])  18.4 us
    pallas_call x1, Pallas kernels, body(): call(inner_kernel, [((32, 32, 256), F32)], [((32, 96, 256), F32), ((256,...  7.18 us
    pallas_call x1, Pallas kernels, body(): call(finest_kernel, [((32, 32, 256), F32)], [((20, 96, 256), F32), ((160,...  3.99 us
    pallas_call x1, Pallas kernels, body(): call(fine_level_kernel, [((18, 32, 128), F32)], [((38, 48, 128), F32), ((...  3.37 us
    pallas_call x1, Pallas kernels, body(): call(matrices_kernel, [((96, 192), BF), ((96, 144), BF), ((96, 144), BF),...  3.02 us
    pallas_call x1, Pallas kernels, body(): call(upper_kernel, [((32, 32, 256), F32)], [((16, 48, 128), F32), ((32, 9...  2.81 us
  transfers between devices with their start and end apart: 14, of which 3 were waited for; matrix products, arithmetic and copies ran while one was open for 0% of the time, Pallas kernels for 23%

profile of v6, /device:TPU:1, one launch (start us, length us, event | category | flops | bytes accessed | tf_op | source)
XLA Modules:
  0.0 71.7 jit_solution(11454181705460940777)
XLA Ops:
  0.0 1.2 %copy-done = f32[32,32,256]{2,1,0:T(8,128)S(1)} copy-done((f32[32,32,256]{2,1,0:T(8,128)S(1)}, f32[32,32,256]{2,1,0:T(8,128)}, u32[]{:S(2)}) %copy-start) | copy-done | bytes 1048600
  1.2 1.0 %restrict.1 = (f32[18,24,128]{2,1,0:T(8,128)S(1)}, f32[6,16,128]{2,1,0:T(8,128)S(1)}, f32[288,128]{1,0:T(8,128)S(1)}, f32[288,128]{1,0:T(8,128)S(1)}, f32[320,25...) custom-call(f32[32,32,256]{2,1,0:T(8,128)S(1)} %copy-done), custom_call_target="tpu_custom_call" | custom-call | flops 100000000 | bytes 2000000 | tf_op jit(solution)/shard_map/restrict/pallas_call | solution.py:423
  2.3 0.0 copy-start.2
  2.3 3.9 %collective-permute-start = (f32[288,128]{1,0:T(8,128)S(1)}, f32[288,128]{1,0:T(8,128)S(1)}, u32[]{:S(2)}, u32[]{:S(2)}) collective-permute-start(f32[288,128]{1,0:T(8,128)S(1)} %get-tuple-element.52), channel_id=1, source_target_pairs={{0,16},{16,32},{32,48},{48,64},{64,80},{80,96},{96,112},{112,128},... | collective-permute-start | bytes 442376 | tf_op jit(solution)/shard_map/ppermute | solution.py:418
  6.2 5.6 %collective-permute-start.1 = (f32[288,128]{1,0:T(8,128)S(1)}, f32[288,128]{1,0:T(8,128)S(1)}, u32[]{:S(2)}, u32[]{:S(2)}) collective-permute-start(f32[288,128]{1,0:T(8,128)S(1)} %get-tuple-element.53), channel_id=1, source_target_pairs={{0,240},{16,0},{32,16},{48,32},{64,48},{80,64},{96,80},{112,96},{1... | collective-permute-start | bytes 442376 | tf_op jit(solution)/shard_map/ppermute | solution.py:418
  11.7 1.6 %collective-permute-start.8 = (f32[328,256]{1,0:T(8,128)S(1)}, f32[328,256]{1,0:T(8,128)S(1)}, u32[]{:S(2)}, u32[]{:S(2)}) collective-permute-start(f32[328,256]{1,0:T(8,128)S(1)} %get-tuple-element.65), channel_id=1, source_target_pairs={{0,1},{1,2},{2,3},{3,4},{4,5},{5,6},{6,7},{7,8},{8,9},{9,10},{10,1... | collective-permute-start | bytes 1007624 | tf_op jit(solution)/shard_map/ppermute | solution.py:418
  13.3 3.0 %matrices.1 = (bf16[96,192]{1,0:T(8,128)(2,1)S(1)}, bf16[96,144]{1,0:T(8,128)(2,1)S(1)}, bf16[96,144]{1,0:T(8,128)(2,1)S(1)}, bf16[768,256]{1,0:T(8,128)(2,1)S(1...) custom-call(f32[3,3,21]{2,1,0:T(4,128)S(1)} %copy-done.2), custom_call_target="tpu_custom_call" | custom-call | flops 100000000 | bytes 4000000 | tf_op jit(solution)/shard_map/matrices/pallas_call | solution.py:434
  16.4 1.0 %collective-permute-done.1.right = f32[288,128]{1,0:T(8,128)S(1)} collective-permute-done((f32[288,128]{1,0:T(8,128)S(1)}, f32[288,128]{1,0:T(8,128)S(1)}, u32[]{:S(2)}, u32[]{:S(2)}) %collective-permute-start.1) | collective-permute-done | bytes 147488 | tf_op jit(solution)/shard_map/ppermute | solution.py:418
  17.4 0.1 forward.1
  17.5 3.3 %collective-permute-start.4 = (f32[40,128]{1,0:T(8,128)S(1)}, f32[40,128]{1,0:T(8,128)S(1)}, u32[]{:S(2)}, u32[]{:S(2)}) collective-permute-start(f32[40,128]{1,0:T(8,128)S(1)} %get-tuple-element.57), channel_id=1, source_target_pairs={{0,16},{16,32},{32,48},{48,64},{64,80},{80,96},{96,112},{112,128},... | collective-permute-start | bytes 61448 | tf_op jit(solution)/shard_map/ppermute | solution.py:418
  20.7 2.5 %collective-permute-start.5 = (f32[40,128]{1,0:T(8,128)S(1)}, f32[40,128]{1,0:T(8,128)S(1)}, u32[]{:S(2)}, u32[]{:S(2)}) collective-permute-start(f32[40,128]{1,0:T(8,128)S(1)} %get-tuple-element.58), channel_id=1, source_target_pairs={{0,240},{16,0},{32,16},{48,32},{64,48},{80,64},{96,80},{112,96},{1... | collective-permute-start | bytes 61448 | tf_op jit(solution)/shard_map/ppermute | solution.py:418
  23.2 2.3 %collective-permute-done.4.left2 = f32[40,128]{1,0:T(8,128)S(1)} collective-permute-done((f32[40,128]{1,0:T(8,128)S(1)}, f32[40,128]{1,0:T(8,128)S(1)}, u32[]{:S(2)}, u32[]{:S(2)}) %collective-permute-start.4) | collective-permute-done | bytes 20512 | tf_op jit(solution)/shard_map/ppermute | solution.py:418
  25.5 3.4 %collective-permute-start.3 = (f32[320,256]{1,0:T(8,128)S(1)}, f32[320,256]{1,0:T(8,128)S(1)}, u32[]{:S(2)}, u32[]{:S(2)}) collective-permute-start(f32[320,256]{1,0:T(8,128)S(1)} %get-tuple-element.60), channel_id=1, source_target_pairs={{0,240},{16,0},{32,16},{48,32},{64,48},{80,64},{96,80},{112,96},{1... | collective-permute-start | bytes 983048 | tf_op jit(solution)/shard_map/ppermute | solution.py:418
  28.9 0.2 gather.1
  29.1 2.1 %collective-permute-start.6 = (f32[80,128]{1,0:T(8,128)S(1)}, f32[80,128]{1,0:T(8,128)S(1)}, u32[]{:S(2)}, u32[]{:S(2)}) collective-permute-start(f32[80,128]{1,0:T(8,128)S(1)} %get-tuple-element.63), channel_id=1, source_target_pairs={{0,2},{1,3},{2,4},{3,5},{4,6},{5,7},{6,8},{7,9},{8,10},{9,11},{10,... | collective-permute-start | bytes 122888 | tf_op jit(solution)/shard_map/ppermute | solution.py:418
  31.2 15.1 %collective-permute-done.6.left2 = f32[80,128]{1,0:T(8,128)S(1)} collective-permute-done((f32[80,128]{1,0:T(8,128)S(1)}, f32[80,128]{1,0:T(8,128)S(1)}, u32[]{:S(2)}, u32[]{:S(2)}) %collective-permute-start.6) | collective-permute-done | bytes 40992 | tf_op jit(solution)/shard_map/ppermute | solution.py:418
  46.3 2.2 %collective-permute-start.13 = (f32[316,256]{1,0:T(8,128)S(1)}, f32[316,256]{1,0:T(8,128)S(1)}, u32[]{:S(2)}, u32[]{:S(2)}) collective-permute-start(f32[316,256]{1,0:T(8,128)S(1)} %get-tuple-element.69), channel_id=1, source_target_pairs={{0,15},{1,0},{2,1},{3,2},{4,3},{5,4},{6,5},{7,6},{8,7},{9,8},{10,9... | collective-permute-start | bytes 970760 | tf_op jit(solution)/shard_map/ppermute | solution.py:418
  48.5 3.7 %collective-permute-start.7 = (f32[80,128]{1,0:T(8,128)S(1)}, f32[80,128]{1,0:T(8,128)S(1)}, u32[]{:S(2)}, u32[]{:S(2)}) collective-permute-start(f32[80,128]{1,0:T(8,128)S(1)} %get-tuple-element.64), channel_id=1, source_target_pairs={{0,14},{1,15},{2,0},{3,1},{4,2},{5,3},{6,4},{7,5},{8,6},{9,7},{10,... | collective-permute-start | bytes 122888 | tf_op jit(solution)/shard_map/ppermute | solution.py:418
  52.2 7.2 %inner.1.direct = f32[32,32,256]{2,1,0:T(8,128)S(1)} custom-call(f32[3,3,21]{2,1,0:T(4,128)S(1)} %copy-done.2, f32[32,32,256]{2,1,0:T(8,128)S(1)} %copy-done.1, f32[328,256]{1,0:T(8,128)S(1)} %collective-permute-done.8.left, f32[328,256]{1,0:T(8,128)S(1)} %collective-permute-done.9.right, bf16[96,192]{1,0:T(8,128)(2,1)S(1)} %get-tuple-element.70.y0, ...), custom_call_target="tpu_custom_call" | custom-call | flops 3000000000 | bytes 6000000 | tf_op jit(solution)/shard_map/inner/pallas_call | solution.py:460
  59.5 0.1 corner.1
  59.5 1.8 %collective-permute-start.10 = (f32[208,256]{1,0:T(8,128)S(1)}, f32[208,256]{1,0:T(8,128)S(1)}, u32[]{:S(2)}, u32[]{:S(2)}) collective-permute-start(f32[208,256]{1,0:T(8,128)S(1)} %get-tuple-element.75), channel_id=1, source_target_pairs={{0,1},{1,2},{2,3},{3,4},{4,5},{5,6},{6,7},{7,8},{8,9},{9,10},{10,1... | collective-permute-start | bytes 638984 | tf_op jit(solution)/shard_map/ppermute | solution.py:418
  61.4 3.4 %fine_level.1.mid_in = f32[18,32,128]{2,1,0:T(8,128)S(1)} custom-call(f32[3,3,21]{2,1,0:T(4,128)S(1)} %copy-done.2, f32[38,24,128]{2,1,0:T(8,128)S(1)} %get-tuple-element.84.l1x, f32[316,256]{1,0:T(8,128)S(1)} %collective-permute-done.12.left, f32[316,256]{1,0:T(8,128)S(1)} %collective-permute-done.13.right, bf16[96,144]{1,0:T(8,128)(2,1)S(1)} %get-tuple-element.85.y1, ...), custom_call_target="tpu_custom_call" | custom-call | flops 400000000 | bytes 4000000 | tf_op jit(solution)/shard_map/fine_level/pallas_call | solution.py:471
  64.7 2.8 %upper.1.inner = f32[32,32,256]{2,1,0:T(8,128)S(1)} custom-call(f32[3,3,21]{2,1,0:T(4,128)S(1)} %copy-done.2, f32[16,16,128]{2,1,0:T(8,128)S(1)} %get-tuple-element.77.l2x, f32[316,256]{1,0:T(8,128)S(1)} %collective-permute-done.12.left, f32[316,256]{1,0:T(8,128)S(1)} %collective-permute-done.13.right, f32[80,128]{1,0:T(8,128)S(1)} %collective-permute-done.6.left2, ...), custom_call_target="tpu_custom_call" | custom-call | flops 400000000 | bytes 4000000 | tf_op jit(solution)/shard_map/upper/pallas_call | solution.py:476
  67.6 4.0 %finest.1 = f32[32,32,256]{2,1,0:T(8,128)} custom-call(f32[3,3,21]{2,1,0:T(4,128)S(1)} %copy-done.2, f32[320,256]{1,0:T(8,128)S(1)} %collective-permute-done.2.before, f32[320,256]{1,0:T(8,128)S(1)} %collective-permute-done.3.after, f32[208,256]{1,0:T(8,128)S(1)} %collective-permute-done.10.left, f32[208,256]{1,0:T(8,128)S(1)} %collective-permute-done.11.right, ...), custom_call_target="tpu_custom_call" | custom-call | flops 2000000000 | bytes 6000000 | tf_op jit(solution)/shard_map/finest/pallas_call | solution.py:483
  (19 shorter events, 0.0 us)
Async XLA Ops:
  0.0 1.2 %copy-start = (f32[32,32,256]{2,1,0:T(8,128)S(1)}, f32[32,32,256]{2,1,0:T(8,128)}, u32[]{:S(2)}) copy-start(f32[32,32,256]{2,1,0:T(8,128)} %c.3) | copy-start | bytes 3145732
  2.3 11.1 %copy-start.2 = (f32[3,3,21]{2,1,0:T(4,128)S(1)}, f32[3,3,21]{2,1,0:T(4,128)}, u32[]{:S(2)}) copy-start(f32[3,3,21]{2,1,0:T(4,128)} %taps.4) | copy-start | bytes 2272
  2.3 14.1 %collective-permute-start = (f32[288,128]{1,0:T(8,128)S(1)}, f32[288,128]{1,0:T(8,128)S(1)}, u32[]{:S(2)}, u32[]{:S(2)}) collective-permute-start(f32[288,128]{1,0:T(8,128)S(1)} %get-tuple-element.52), channel_id=1, source_target_pairs={{0,16},{16,32},{32,48},{48,64},{64,80},{80,96},{96,112},{112,128},... | collective-permute-start | bytes 442376 | tf_op jit(solution)/shard_map/ppermute | solution.py:418
  6.2 11.2 %collective-permute-start.1 = (f32[288,128]{1,0:T(8,128)S(1)}, f32[288,128]{1,0:T(8,128)S(1)}, u32[]{:S(2)}, u32[]{:S(2)}) collective-permute-start(f32[288,128]{1,0:T(8,128)S(1)} %get-tuple-element.53), channel_id=1, source_target_pairs={{0,240},{16,0},{32,16},{48,32},{64,48},{80,64},{96,80},{112,96},{1... | collective-permute-start | bytes 442376 | tf_op jit(solution)/shard_map/ppermute | solution.py:418
  11.7 34.6 %collective-permute-start.8 = (f32[328,256]{1,0:T(8,128)S(1)}, f32[328,256]{1,0:T(8,128)S(1)}, u32[]{:S(2)}, u32[]{:S(2)}) collective-permute-start(f32[328,256]{1,0:T(8,128)S(1)} %get-tuple-element.65), channel_id=1, source_target_pairs={{0,1},{1,2},{2,3},{3,4},{4,5},{5,6},{6,7},{7,8},{8,9},{9,10},{10,1... | collective-permute-start | bytes 1007624 | tf_op jit(solution)/shard_map/ppermute | solution.py:418
  13.3 35.2 %collective-permute-start.9 = (f32[328,256]{1,0:T(8,128)S(1)}, f32[328,256]{1,0:T(8,128)S(1)}, u32[]{:S(2)}, u32[]{:S(2)}) collective-permute-start(f32[328,256]{1,0:T(8,128)S(1)} %get-tuple-element.66), channel_id=1, source_target_pairs={{0,15},{1,0},{2,1},{3,2},{4,3},{5,4},{6,5},{7,6},{8,7},{9,8},{10,9... | collective-permute-start | bytes 1007624 | tf_op jit(solution)/shard_map/ppermute | solution.py:418
  17.4 34.9 %copy-start.1 = (f32[32,32,256]{2,1,0:T(8,128)S(1)}, f32[32,32,256]{2,1,0:T(8,128)}, u32[]{:S(2)}) copy-start(f32[32,32,256]{2,1,0:T(8,128)} %c.3) | copy-start | bytes 3145732
  17.5 8.0 %collective-permute-start.4 = (f32[40,128]{1,0:T(8,128)S(1)}, f32[40,128]{1,0:T(8,128)S(1)}, u32[]{:S(2)}, u32[]{:S(2)}) collective-permute-start(f32[40,128]{1,0:T(8,128)S(1)} %get-tuple-element.57), channel_id=1, source_target_pairs={{0,16},{16,32},{32,48},{48,64},{64,80},{80,96},{96,112},{112,128},... | collective-permute-start | bytes 61448 | tf_op jit(solution)/shard_map/ppermute | solution.py:418
  20.7 8.2 %collective-permute-start.5 = (f32[40,128]{1,0:T(8,128)S(1)}, f32[40,128]{1,0:T(8,128)S(1)}, u32[]{:S(2)}, u32[]{:S(2)}) collective-permute-start(f32[40,128]{1,0:T(8,128)S(1)} %get-tuple-element.58), channel_id=1, source_target_pairs={{0,240},{16,0},{32,16},{48,32},{64,48},{80,64},{96,80},{112,96},{1... | collective-permute-start | bytes 61448 | tf_op jit(solution)/shard_map/ppermute | solution.py:418
  23.2 36.2 %collective-permute-start.2 = (f32[320,256]{1,0:T(8,128)S(1)}, f32[320,256]{1,0:T(8,128)S(1)}, u32[]{:S(2)}, u32[]{:S(2)}) collective-permute-start(f32[320,256]{1,0:T(8,128)S(1)} %get-tuple-element.59), channel_id=1, source_target_pairs={{0,16},{16,32},{32,48},{48,64},{64,80},{80,96},{96,112},{112,128},... | collective-permute-start | bytes 983048 | tf_op jit(solution)/shard_map/ppermute | solution.py:418
  25.5 34.0 %collective-permute-start.3 = (f32[320,256]{1,0:T(8,128)S(1)}, f32[320,256]{1,0:T(8,128)S(1)}, u32[]{:S(2)}, u32[]{:S(2)}) collective-permute-start(f32[320,256]{1,0:T(8,128)S(1)} %get-tuple-element.60), channel_id=1, source_target_pairs={{0,240},{16,0},{32,16},{48,32},{64,48},{80,64},{96,80},{112,96},{1... | collective-permute-start | bytes 983048 | tf_op jit(solution)/shard_map/ppermute | solution.py:418
  29.1 17.2 %collective-permute-start.6 = (f32[80,128]{1,0:T(8,128)S(1)}, f32[80,128]{1,0:T(8,128)S(1)}, u32[]{:S(2)}, u32[]{:S(2)}) collective-permute-start(f32[80,128]{1,0:T(8,128)S(1)} %get-tuple-element.63), channel_id=1, source_target_pairs={{0,2},{1,3},{2,4},{3,5},{4,6},{5,7},{6,8},{7,9},{8,10},{9,11},{10,... | collective-permute-start | bytes 122888 | tf_op jit(solution)/shard_map/ppermute | solution.py:418
  46.3 15.1 %collective-permute-start.12 = (f32[316,256]{1,0:T(8,128)S(1)}, f32[316,256]{1,0:T(8,128)S(1)}, u32[]{:S(2)}, u32[]{:S(2)}) collective-permute-start(f32[316,256]{1,0:T(8,128)S(1)} %get-tuple-element.68), channel_id=1, source_target_pairs={{0,1},{1,2},{2,3},{3,4},{4,5},{5,6},{6,7},{7,8},{8,9},{9,10},{10,1... | collective-permute-start | bytes 970760 | tf_op jit(solution)/shard_map/ppermute | solution.py:418
  46.3 15.0 %collective-permute-start.13 = (f32[316,256]{1,0:T(8,128)S(1)}, f32[316,256]{1,0:T(8,128)S(1)}, u32[]{:S(2)}, u32[]{:S(2)}) collective-permute-start(f32[316,256]{1,0:T(8,128)S(1)} %get-tuple-element.69), channel_id=1, source_target_pairs={{0,15},{1,0},{2,1},{3,2},{4,3},{5,4},{6,5},{7,6},{8,7},{9,8},{10,9... | collective-permute-start | bytes 970760 | tf_op jit(solution)/shard_map/ppermute | solution.py:418
  48.5 10.9 %collective-permute-start.7 = (f32[80,128]{1,0:T(8,128)S(1)}, f32[80,128]{1,0:T(8,128)S(1)}, u32[]{:S(2)}, u32[]{:S(2)}) collective-permute-start(f32[80,128]{1,0:T(8,128)S(1)} %get-tuple-element.64), channel_id=1, source_target_pairs={{0,14},{1,15},{2,0},{3,1},{4,2},{5,3},{6,4},{7,5},{8,6},{9,7},{10,... | collective-permute-start | bytes 122888 | tf_op jit(solution)/shard_map/ppermute | solution.py:418
  59.5 8.1 %collective-permute-start.10 = (f32[208,256]{1,0:T(8,128)S(1)}, f32[208,256]{1,0:T(8,128)S(1)}, u32[]{:S(2)}, u32[]{:S(2)}) collective-permute-start(f32[208,256]{1,0:T(8,128)S(1)} %get-tuple-element.75), channel_id=1, source_target_pairs={{0,1},{1,2},{2,3},{3,4},{4,5},{5,6},{6,7},{7,8},{8,9},{9,10},{10,1... | collective-permute-start | bytes 638984 | tf_op jit(solution)/shard_map/ppermute | solution.py:418
  61.4 6.2 %collective-permute-start.11 = (f32[208,256]{1,0:T(8,128)S(1)}, f32[208,256]{1,0:T(8,128)S(1)}, u32[]{:S(2)}, u32[]{:S(2)}) collective-permute-start(f32[208,256]{1,0:T(8,128)S(1)} %get-tuple-element.76), channel_id=1, source_target_pairs={{0,15},{1,0},{2,1},{3,2},{4,3},{5,4},{6,5},{7,6},{8,7},{9,8},{10,9... | collective-permute-start | bytes 638984 | tf_op jit(solution)/shard_map/ppermute | solution.py:418

commit v7 on v5

--- a/solution.py
+++ b/solution.py
@@ -279,7 +279,7 @@
     mid[...] = correlate_z(w1, 18, z1)
 
 
-def upper_kernel(taps, l2x, left, right, left2, right2, y2, z2, up1, mid_in, direct, out,
+def upper_part(taps, l2x, left, right, left2, right2, y2, z2, up1, mid_in, direct, out,
                  f2, v2, w2, mid, fine, done, sems):
     for j in range(16):
         f2[j, pl.ds(0, 16)] = l2x[j]
@@ -358,7 +358,7 @@
         out[:, cols] = total.reshape(32, 8, 256)
 
 
-def finest_kernel(taps, before, after, left, right, y0, z0h, z0l, inner, out, v, wh, wl):
+def finest_part(taps, before, after, left, right, y0, z0h, z0l, inner, out, v, wh, wl):
     for i in range(20):
         own = before[pl.ds(32 * i, 32)] if i < 10 else after[pl.ds(32 * (i - 10), 32)]
         b = left[pl.ds(10 * i, 16)]
@@ -385,15 +385,24 @@
                         sums[at] = term if sums[at] is None else sums[at] + term
                 for m in range(0, 20, 2):
                     high, low = halves(jnp.concatenate([sums[m], sums[m + 1]], 0))
-                    at = (pl.ds(8 * m, 16), pl.ds(256 * member + 128 * h, 128))
+                    at = (pl.ds(pl.multiple_of(160 * g, 32) + 8 * m, 16), pl.ds(256 * member + 128 * h, 128))
                     wh[at] = high
                     wl[at] = low
-        cols = pl.ds(pl.multiple_of(8 * g, 8), 8)
-        total = dot(wh[...], z0h[...]) + dot(wl[...], z0h[...]) + dot(wh[...], z0l[...])
-        total = total.reshape(20, 8, 256)
-        out[pl.ds(0, 10), cols] = inner[pl.ds(0, 10), cols] + total[:10]
+
+    total = dot(wh[...], z0h[...]) + dot(wl[...], z0h[...]) + dot(wh[...], z0l[...])
+    for g in range(4):
+        cols = pl.ds(8 * g, 8)
+        piece = total[160 * g:160 * g + 160].reshape(20, 8, 256)
+        out[pl.ds(0, 10), cols] = inner[pl.ds(0, 10), cols] + piece[:10]
         out[pl.ds(10, 12), cols] = inner[pl.ds(10, 12), cols]
-        out[pl.ds(22, 10), cols] = inner[pl.ds(22, 10), cols] + total[10:]
+        out[pl.ds(22, 10), cols] = inner[pl.ds(22, 10), cols] + piece[10:]
+
+
+def last_kernel(taps, before, after, left, right, y0, z0h, z0l, inner, l2x, left2, right2, y2, z2, up1, mid_in,
+                out, v, wh, wl, direct, f2, v2, w2, mid, fine, done, sems):
+    finest_part(taps, before, after, left, right, y0, z0h, z0l, inner, direct, v, wh, wl)
+    upper_part(taps, l2x, left, right, left2, right2, y2, z2, up1, mid_in, direct, out,
+               f2, v2, w2, mid, fine, done, sems)
 
 
 def call(kernel, outs, scratch=(), scalars=0, count=0, flops=0, moved=0, name=None, sems=0, far=False):
@@ -474,17 +483,13 @@
         1, 6, 4 * 10**8, 4 * 10**6, name="fine_level",
     )(taps, l1x, fine_left, fine_right, y1, z1)
     left, right, mid = lax.optimization_barrier((left, right, mid))
-    direct, = call(
-        finest_kernel, [((32, 32, 256), F32)],
-        [((20, 96, 256), F32), ((160, 768), BF), ((160, 768), BF)],
-        1, 9, 2 * 10**9, 6 * 10**6, name="finest",
-    )(taps, before, after, left, right, y0, z0h, z0l, inner)
     result, = call(
-        upper_kernel, [((32, 32, 256), F32)],
-        [((16, 48, 128), F32), ((32, 96, 128), F32), ((11, 96, 128), F32), ((18, 32, 128), F32),
+        last_kernel, [((32, 32, 256), F32)],
+        [((20, 96, 256), F32), ((640, 768), BF), ((640, 768), BF), ((32, 32, 256), F32),
+         ((16, 48, 128), F32), ((32, 96, 128), F32), ((11, 96, 128), F32), ((18, 32, 128), F32),
          ((32, 32, 128), F32), ((32, 32, 256), F32)],
-        1, 11, 4 * 10**8, 4 * 10**6, name="upper", sems=4, far=True,
-    )(taps, l2x, left, right, left2, right2, y2, z2, up1, mid, direct)
+        1, 16, 2 * 10**9, 6 * 10**6, name="last", sems=4, far=True,
+    )(taps, before, after, left, right, y0, z0h, z0l, inner, l2x, left2, right2, y2, z2, up1, mid)
     return result
 
 

time: 64.5 us -> 66.3 us (1.028)
  waiting for transfers between devices: 5.68 us -> 8.64 us
  Pallas kernels: 21.8 us -> 21 us
    ppermute x12, waiting for transfers between devices: 5.68 us -> 8.64 us  [shift(): return lax.ppermute(x, axis, [(i, (i + by) % n) for i in range(n)])]
    pallas_call x2 -> x1, Pallas kernels: 6.89 us -> 6.08 us  [body(): call(last_kernel, [((32, 32, 256), F32)], [((20, 96, 256), F32), ((640, 7...]
  transfers between devices with their start and end apart: 12 -> 12, of which waited for: 3 -> 4; matrix products, arithmetic and copies ran while one was open for 0% -> 0% of each run, Pallas kernels for 27% -> 21%
where the time goes in v7:
time: 66.3 us; the launch traced here: 66.2 us
  starting transfers between devices  35.1 us (53%)
  Pallas kernels  21 us (32%)
  waiting for transfers between devices  8.64 us (13%)
  local copies, waits for them, and re-layouts  1.23 us (2%)
    ppermute x12, starting transfers between devices, shift(): return lax.ppermute(x, axis, [(i, (i + by) % n) for i in range(n)])  35.1 us
    ppermute x12, waiting for transfers between devices, shift(): return lax.ppermute(x, axis, [(i, (i + by) % n) for i in range(n)])  8.64 us
    pallas_call x1, Pallas kernels, body(): call(inner_kernel, [((32, 32, 256), F32)], [((32, 96, 256), F32), ((256,...  7.23 us
    pallas_call x1, Pallas kernels, body(): call(last_kernel, [((32, 32, 256), F32)], [((20, 96, 256), F32), ((640, 7...  6.08 us
    pallas_call x1, Pallas kernels, body(): call(fine_level_kernel, [((18, 32, 128), F32)], [((38, 48, 128), F32), ((...  3.38 us
    pallas_call x1, Pallas kernels, body(): call(matrices_kernel, [((96, 192), BF), ((96, 144), BF), ((96, 144), BF),...  3.02 us
  transfers between devices with their start and end apart: 12, of which 4 were waited for; matrix products, arithmetic and copies ran while one was open for 0% of the time, Pallas kernels for 21%

profile of v7, /device:TPU:1, one launch (start us, length us, event | category | flops | bytes accessed | tf_op | source)
XLA Modules:
  0.0 66.2 jit_solution(11049128636780889799)
XLA Ops:
  0.0 1.2 %copy-done = f32[32,32,256]{2,1,0:T(8,128)S(1)} copy-done((f32[32,32,256]{2,1,0:T(8,128)S(1)}, f32[32,32,256]{2,1,0:T(8,128)}, u32[]{:S(2)}) %copy-start) | copy-done | bytes 1048600
  1.2 1.0 %restrict.1 = (f32[18,24,128]{2,1,0:T(8,128)S(1)}, f32[6,16,128]{2,1,0:T(8,128)S(1)}, f32[288,128]{1,0:T(8,128)S(1)}, f32[288,128]{1,0:T(8,128)S(1)}, f32[320,25...) custom-call(f32[32,32,256]{2,1,0:T(8,128)S(1)} %copy-done), custom_call_target="tpu_custom_call" | custom-call | flops 100000000 | bytes 2000000 | tf_op jit(solution)/shard_map/restrict/pallas_call | solution.py:432
  2.2 0.0 copy-start.2
  2.3 3.9 %collective-permute-start = (f32[288,128]{1,0:T(8,128)S(1)}, f32[288,128]{1,0:T(8,128)S(1)}, u32[]{:S(2)}, u32[]{:S(2)}) collective-permute-start(f32[288,128]{1,0:T(8,128)S(1)} %get-tuple-element.52), channel_id=1, source_target_pairs={{0,16},{16,32},{32,48},{48,64},{64,80},{80,96},{96,112},{112,128},... | collective-permute-start | bytes 442376 | tf_op jit(solution)/shard_map/ppermute | solution.py:427
  6.2 5.6 %collective-permute-start.1 = (f32[288,128]{1,0:T(8,128)S(1)}, f32[288,128]{1,0:T(8,128)S(1)}, u32[]{:S(2)}, u32[]{:S(2)}) collective-permute-start(f32[288,128]{1,0:T(8,128)S(1)} %get-tuple-element.53), channel_id=1, source_target_pairs={{0,240},{16,0},{32,16},{48,32},{64,48},{80,64},{96,80},{112,96},{1... | collective-permute-start | bytes 442376 | tf_op jit(solution)/shard_map/ppermute | solution.py:427
  11.7 1.6 %collective-permute-start.4 = (f32[328,256]{1,0:T(8,128)S(1)}, f32[328,256]{1,0:T(8,128)S(1)}, u32[]{:S(2)}, u32[]{:S(2)}) collective-permute-start(f32[328,256]{1,0:T(8,128)S(1)} %get-tuple-element.59), channel_id=1, source_target_pairs={{0,1},{1,2},{2,3},{3,4},{4,5},{5,6},{6,7},{7,8},{8,9},{9,10},{10,1... | collective-permute-start | bytes 1007624 | tf_op jit(solution)/shard_map/ppermute | solution.py:427
  13.3 3.0 %matrices.1 = (bf16[96,192]{1,0:T(8,128)(2,1)S(1)}, bf16[96,144]{1,0:T(8,128)(2,1)S(1)}, bf16[96,144]{1,0:T(8,128)(2,1)S(1)}, bf16[768,256]{1,0:T(8,128)(2,1)S(1...) custom-call(f32[3,3,21]{2,1,0:T(4,128)S(1)} %copy-done.2), custom_call_target="tpu_custom_call" | custom-call | flops 100000000 | bytes 4000000 | tf_op jit(solution)/shard_map/matrices/pallas_call | solution.py:441
  16.3 1.0 %collective-permute-done.1.right = f32[288,128]{1,0:T(8,128)S(1)} collective-permute-done((f32[288,128]{1,0:T(8,128)S(1)}, f32[288,128]{1,0:T(8,128)S(1)}, u32[]{:S(2)}, u32[]{:S(2)}) %collective-permute-start.1) | collective-permute-done | bytes 147488 | tf_op jit(solution)/shard_map/ppermute | solution.py:427
  17.3 0.1 face_x.1
  17.4 3.3 %collective-permute-start.2 = (f32[344,256]{1,0:T(8,128)S(1)}, f32[344,256]{1,0:T(8,128)S(1)}, u32[]{:S(2)}, u32[]{:S(2)}) collective-permute-start(f32[344,256]{1,0:T(8,128)S(1)} %get-tuple-element.57), channel_id=1, source_target_pairs={{0,16},{16,32},{32,48},{48,64},{64,80},{80,96},{96,112},{112,128},... | collective-permute-start | bytes 1056776 | tf_op jit(solution)/shard_map/ppermute | solution.py:427
  20.7 2.5 %collective-permute-start.3 = (f32[344,256]{1,0:T(8,128)S(1)}, f32[344,256]{1,0:T(8,128)S(1)}, u32[]{:S(2)}, u32[]{:S(2)}) collective-permute-start(f32[344,256]{1,0:T(8,128)S(1)} %get-tuple-element.58), channel_id=1, source_target_pairs={{0,240},{16,0},{32,16},{48,32},{64,48},{80,64},{96,80},{112,96},{1... | collective-permute-start | bytes 1056776 | tf_op jit(solution)/shard_map/ppermute | solution.py:427
  23.2 0.1 gather_fine.1
  23.3 3.9 %collective-permute-start.6 = (f32[456,128]{1,0:T(8,128)S(1)}, f32[456,128]{1,0:T(8,128)S(1)}, u32[]{:S(2)}, u32[]{:S(2)}) collective-permute-start(f32[456,128]{1,0:T(8,128)S(1)} %get-tuple-element.65), channel_id=1, source_target_pairs={{0,1},{1,2},{2,3},{3,4},{4,5},{5,6},{6,7},{7,8},{8,9},{9,10},{10,1... | collective-permute-start | bytes 700424 | tf_op jit(solution)/shard_map/ppermute | solution.py:427
  27.2 8.7 %collective-permute-start.7 = (f32[456,128]{1,0:T(8,128)S(1)}, f32[456,128]{1,0:T(8,128)S(1)}, u32[]{:S(2)}, u32[]{:S(2)}) collective-permute-start(f32[456,128]{1,0:T(8,128)S(1)} %get-tuple-element.66), channel_id=1, source_target_pairs={{0,15},{1,0},{2,1},{3,2},{4,3},{5,4},{6,5},{7,6},{8,7},{9,8},{10,9... | collective-permute-start | bytes 700424 | tf_op jit(solution)/shard_map/ppermute | solution.py:427
  35.9 7.2 %inner.1 = f32[32,32,256]{2,1,0:T(8,128)S(1)} custom-call(f32[3,3,21]{2,1,0:T(4,128)S(1)} %copy-done.2, f32[32,32,256]{2,1,0:T(8,128)S(1)} %copy-done.1, f32[328,256]{1,0:T(8,128)S(1)} %collective-permute-done.4.left, f32[328,256]{1,0:T(8,128)S(1)} %collective-permute-done.5.right, bf16[96,192]{1,0:T(8,128)(2,1)S(1)} %get-tuple-element.67.y0, ...), custom_call_target="tpu_custom_call" | custom-call | flops 2000000000 | bytes 6000000 | tf_op jit(solution)/shard_map/inner/pallas_call | solution.py:463
  43.2 3.6 %collective-permute-done.7.right = f32[456,128]{1,0:T(8,128)S(1)} collective-permute-done((f32[456,128]{1,0:T(8,128)S(1)}, f32[456,128]{1,0:T(8,128)S(1)}, u32[]{:S(2)}, u32[]{:S(2)}) %collective-permute-start.7) | collective-permute-done | bytes 233504 | tf_op jit(solution)/shard_map/ppermute | solution.py:427
  46.8 0.1 gather_top.1
  46.9 0.3 collective-permute-start.8
  47.2 1.8 %collective-permute-start.9 = (f32[296,256]{1,0:T(8,128)S(1)}, f32[296,256]{1,0:T(8,128)S(1)}, u32[]{:S(2)}, u32[]{:S(2)}) collective-permute-start(f32[296,256]{1,0:T(8,128)S(1)} %get-tuple-element.74), channel_id=1, source_target_pairs={{0,15},{1,0},{2,1},{3,2},{4,3},{5,4},{6,5},{7,6},{8,7},{9,8},{10,9... | collective-permute-start | bytes 909320 | tf_op jit(solution)/shard_map/ppermute | solution.py:427
  49.0 3.6 %collective-permute-start.11 = (f32[80,128]{1,0:T(8,128)S(1)}, f32[80,128]{1,0:T(8,128)S(1)}, u32[]{:S(2)}, u32[]{:S(2)}) collective-permute-start(f32[80,128]{1,0:T(8,128)S(1)} %get-tuple-element.86), channel_id=1, source_target_pairs={{0,14},{1,15},{2,0},{3,1},{4,2},{5,3},{6,4},{7,5},{8,6},{9,7},{10,... | collective-permute-start | bytes 122888 | tf_op jit(solution)/shard_map/ppermute | solution.py:427
  52.5 3.4 %fine_level.1.mid_in = f32[18,32,128]{2,1,0:T(8,128)S(1)} custom-call(f32[3,3,21]{2,1,0:T(4,128)S(1)} %copy-done.2, f32[38,24,128]{2,1,0:T(8,128)S(1)} %get-tuple-element.76.l1x, f32[456,128]{1,0:T(8,128)S(1)} %collective-permute-done.6.left, f32[456,128]{1,0:T(8,128)S(1)} %collective-permute-done.7.right, bf16[96,144]{1,0:T(8,128)(2,1)S(1)} %get-tuple-element.79.y1, ...), custom_call_target="tpu_custom_call" | custom-call | flops 400000000 | bytes 4000000 | tf_op jit(solution)/shard_map/fine_level/pallas_call | solution.py:480
  55.9 1.1 %collective-permute-done.9.right = f32[296,256]{1,0:T(8,128)S(1)} collective-permute-done((f32[296,256]{1,0:T(8,128)S(1)}, f32[296,256]{1,0:T(8,128)S(1)}, u32[]{:S(2)}, u32[]{:S(2)}) %collective-permute-start.9) | collective-permute-done | bytes 303136 | tf_op jit(solution)/shard_map/ppermute | solution.py:427
  57.0 2.9 %collective-permute-done.10.left2 = f32[80,128]{1,0:T(8,128)S(1)} collective-permute-done((f32[80,128]{1,0:T(8,128)S(1)}, f32[80,128]{1,0:T(8,128)S(1)}, u32[]{:S(2)}, u32[]{:S(2)}) %collective-permute-start.10) | collective-permute-done | bytes 40992 | tf_op jit(solution)/shard_map/ppermute | solution.py:427
  59.9 6.1 %last.1 = f32[32,32,256]{2,1,0:T(8,128)} custom-call(f32[3,3,21]{2,1,0:T(4,128)S(1)} %copy-done.2, f32[344,256]{1,0:T(8,128)S(1)} %collective-permute-done.2.before, f32[344,256]{1,0:T(8,128)S(1)} %collective-permute-done.3.after, f32[296,256]{1,0:T(8,128)S(1)} %collective-permute-done.8.left, f32[296,256]{1,0:T(8,128)S(1)} %collective-permute-done.9.right, ...), custom_call_target="tpu_custom_call" | custom-call | flops 2000000000 | bytes 6000000 | tf_op jit(solution)/shard_map/last/pallas_call | solution.py:486
  (14 shorter events, 0.0 us)
Async XLA Ops:
  0.0 1.2 %copy-start = (f32[32,32,256]{2,1,0:T(8,128)S(1)}, f32[32,32,256]{2,1,0:T(8,128)}, u32[]{:S(2)}) copy-start(f32[32,32,256]{2,1,0:T(8,128)} %c.3) | copy-start | bytes 3145732
  2.2 11.1 %copy-start.2 = (f32[3,3,21]{2,1,0:T(4,128)S(1)}, f32[3,3,21]{2,1,0:T(4,128)}, u32[]{:S(2)}) copy-start(f32[3,3,21]{2,1,0:T(4,128)} %taps.3) | copy-start | bytes 2272
  2.3 14.1 %collective-permute-start = (f32[288,128]{1,0:T(8,128)S(1)}, f32[288,128]{1,0:T(8,128)S(1)}, u32[]{:S(2)}, u32[]{:S(2)}) collective-permute-start(f32[288,128]{1,0:T(8,128)S(1)} %get-tuple-element.52), channel_id=1, source_target_pairs={{0,16},{16,32},{32,48},{48,64},{64,80},{80,96},{96,112},{112,128},... | collective-permute-start | bytes 442376 | tf_op jit(solution)/shard_map/ppermute | solution.py:427
  6.2 11.2 %collective-permute-start.1 = (f32[288,128]{1,0:T(8,128)S(1)}, f32[288,128]{1,0:T(8,128)S(1)}, u32[]{:S(2)}, u32[]{:S(2)}) collective-permute-start(f32[288,128]{1,0:T(8,128)S(1)} %get-tuple-element.53), channel_id=1, source_target_pairs={{0,240},{16,0},{32,16},{48,32},{64,48},{80,64},{96,80},{112,96},{1... | collective-permute-start | bytes 442376 | tf_op jit(solution)/shard_map/ppermute | solution.py:427
  11.7 15.5 %collective-permute-start.4 = (f32[328,256]{1,0:T(8,128)S(1)}, f32[328,256]{1,0:T(8,128)S(1)}, u32[]{:S(2)}, u32[]{:S(2)}) collective-permute-start(f32[328,256]{1,0:T(8,128)S(1)} %get-tuple-element.59), channel_id=1, source_target_pairs={{0,1},{1,2},{2,3},{3,4},{4,5},{5,6},{6,7},{7,8},{8,9},{9,10},{10,1... | collective-permute-start | bytes 1007624 | tf_op jit(solution)/shard_map/ppermute | solution.py:427
  13.3 22.6 %collective-permute-start.5 = (f32[328,256]{1,0:T(8,128)S(1)}, f32[328,256]{1,0:T(8,128)S(1)}, u32[]{:S(2)}, u32[]{:S(2)}) collective-permute-start(f32[328,256]{1,0:T(8,128)S(1)} %get-tuple-element.60), channel_id=1, source_target_pairs={{0,15},{1,0},{2,1},{3,2},{4,3},{5,4},{6,5},{7,6},{8,7},{9,8},{10,9... | collective-permute-start | bytes 1007624 | tf_op jit(solution)/shard_map/ppermute | solution.py:427
  17.4 29.4 %collective-permute-start.2 = (f32[344,256]{1,0:T(8,128)S(1)}, f32[344,256]{1,0:T(8,128)S(1)}, u32[]{:S(2)}, u32[]{:S(2)}) collective-permute-start(f32[344,256]{1,0:T(8,128)S(1)} %get-tuple-element.57), channel_id=1, source_target_pairs={{0,16},{16,32},{32,48},{48,64},{64,80},{80,96},{96,112},{112,128},... | collective-permute-start | bytes 1056776 | tf_op jit(solution)/shard_map/ppermute | solution.py:427
  20.7 15.2 %copy-start.1 = (f32[32,32,256]{2,1,0:T(8,128)S(1)}, f32[32,32,256]{2,1,0:T(8,128)}, u32[]{:S(2)}) copy-start(f32[32,32,256]{2,1,0:T(8,128)} %c.3) | copy-start | bytes 3145732
  20.7 26.1 %collective-permute-start.3 = (f32[344,256]{1,0:T(8,128)S(1)}, f32[344,256]{1,0:T(8,128)S(1)}, u32[]{:S(2)}, u32[]{:S(2)}) collective-permute-start(f32[344,256]{1,0:T(8,128)S(1)} %get-tuple-element.58), channel_id=1, source_target_pairs={{0,240},{16,0},{32,16},{48,32},{64,48},{80,64},{96,80},{112,96},{1... | collective-permute-start | bytes 1056776 | tf_op jit(solution)/shard_map/ppermute | solution.py:427
  23.3 19.9 %collective-permute-start.6 = (f32[456,128]{1,0:T(8,128)S(1)}, f32[456,128]{1,0:T(8,128)S(1)}, u32[]{:S(2)}, u32[]{:S(2)}) collective-permute-start(f32[456,128]{1,0:T(8,128)S(1)} %get-tuple-element.65), channel_id=1, source_target_pairs={{0,1},{1,2},{2,3},{3,4},{4,5},{5,6},{6,7},{7,8},{8,9},{9,10},{10,1... | collective-permute-start | bytes 700424 | tf_op jit(solution)/shard_map/ppermute | solution.py:427
  27.2 19.6 %collective-permute-start.7 = (f32[456,128]{1,0:T(8,128)S(1)}, f32[456,128]{1,0:T(8,128)S(1)}, u32[]{:S(2)}, u32[]{:S(2)}) collective-permute-start(f32[456,128]{1,0:T(8,128)S(1)} %get-tuple-element.66), channel_id=1, source_target_pairs={{0,15},{1,0},{2,1},{3,2},{4,3},{5,4},{6,5},{7,6},{8,7},{9,8},{10,9... | collective-permute-start | bytes 700424 | tf_op jit(solution)/shard_map/ppermute | solution.py:427
  46.9 9.0 %collective-permute-start.8 = (f32[296,256]{1,0:T(8,128)S(1)}, f32[296,256]{1,0:T(8,128)S(1)}, u32[]{:S(2)}, u32[]{:S(2)}) collective-permute-start(f32[296,256]{1,0:T(8,128)S(1)} %get-tuple-element.73), channel_id=1, source_target_pairs={{0,1},{1,2},{2,3},{3,4},{4,5},{5,6},{6,7},{7,8},{8,9},{9,10},{10,1... | collective-permute-start | bytes 909320 | tf_op jit(solution)/shard_map/ppermute | solution.py:427
  47.2 9.8 %collective-permute-start.9 = (f32[296,256]{1,0:T(8,128)S(1)}, f32[296,256]{1,0:T(8,128)S(1)}, u32[]{:S(2)}, u32[]{:S(2)}) collective-permute-start(f32[296,256]{1,0:T(8,128)S(1)} %get-tuple-element.74), channel_id=1, source_target_pairs={{0,15},{1,0},{2,1},{3,2},{4,3},{5,4},{6,5},{7,6},{8,7},{9,8},{10,9... | collective-permute-start | bytes 909320 | tf_op jit(solution)/shard_map/ppermute | solution.py:427
  49.0 11.0 %collective-permute-start.10 = (f32[80,128]{1,0:T(8,128)S(1)}, f32[80,128]{1,0:T(8,128)S(1)}, u32[]{:S(2)}, u32[]{:S(2)}) collective-permute-start(f32[80,128]{1,0:T(8,128)S(1)} %get-tuple-element.85), channel_id=1, source_target_pairs={{0,2},{1,3},{2,4},{3,5},{4,6},{5,7},{6,8},{7,9},{8,10},{9,11},{10,... | collective-permute-start | bytes 122888 | tf_op jit(solution)/shard_map/ppermute | solution.py:427
  49.0 11.0 %collective-permute-start.11 = (f32[80,128]{1,0:T(8,128)S(1)}, f32[80,128]{1,0:T(8,128)S(1)}, u32[]{:S(2)}, u32[]{:S(2)}) collective-permute-start(f32[80,128]{1,0:T(8,128)S(1)} %get-tuple-element.86), channel_id=1, source_target_pairs={{0,14},{1,15},{2,0},{3,1},{4,2},{5,3},{6,4},{7,5},{8,6},{9,7},{10,... | collective-permute-start | bytes 122888 | tf_op jit(solution)/shard_map/ppermute | solution.py:427

commit v8 on v5

--- a/solution.py
+++ b/solution.py
@@ -118,9 +118,16 @@
     return spline_of(((fine - 2 * coarse + 2) & (fine_len - 1)) - 2)
 
 
-def restrict_kernel(c, l1, l2, up1, down1, last, first, face_up, face_down, s1, s2):
+def restrict_kernel(charges, l1, l2, up1, down1, last, first, face_up, face_down, s1, s2, c, sems):
+    copies = []
+    for q in range(4):
+        rows = pl.ds(8 * q, 8)
+        copies.append(pltpu.make_async_copy(charges.at[rows], c.at[rows], sems.at[q]))
+        copies[q].start()
     ry = spline_iota((24, 32), 2, 0, 1, 18).astype(BF)
     for i in range(-1, 17):
+        if i in (-1, 3, 7, 11):
+            copies[(i + 1) // 4].wait()
         high, low = halves(spline_sum(lambda r: c[r], i, 0, 31))
         s1[i + 1] = dot(ry, high) + dot(ry, low)
     for i in range(32):
@@ -385,18 +392,20 @@
                         sums[at] = term if sums[at] is None else sums[at] + term
                 for m in range(0, 20, 2):
                     high, low = halves(jnp.concatenate([sums[m], sums[m + 1]], 0))
-                    at = (pl.ds(8 * m, 16), pl.ds(256 * member + 128 * h, 128))
+                    at = (pl.ds(pl.multiple_of(160 * g, 32) + 8 * m, 16), pl.ds(256 * member + 128 * h, 128))
                     wh[at] = high
                     wl[at] = low
-        cols = pl.ds(pl.multiple_of(8 * g, 8), 8)
-        total = dot(wh[...], z0h[...]) + dot(wl[...], z0h[...]) + dot(wh[...], z0l[...])
-        total = total.reshape(20, 8, 256)
-        out[pl.ds(0, 10), cols] = inner[pl.ds(0, 10), cols] + total[:10]
+
+    total = dot(wh[...], z0h[...]) + dot(wl[...], z0h[...]) + dot(wh[...], z0l[...])
+    for g in range(4):
+        cols = pl.ds(8 * g, 8)
+        piece = total[160 * g:160 * g + 160].reshape(20, 8, 256)
+        out[pl.ds(0, 10), cols] = inner[pl.ds(0, 10), cols] + piece[:10]
         out[pl.ds(10, 12), cols] = inner[pl.ds(10, 12), cols]
-        out[pl.ds(22, 10), cols] = inner[pl.ds(22, 10), cols] + total[10:]
-
-
-def call(kernel, outs, scratch=(), scalars=0, count=0, flops=0, moved=0, name=None, sems=0, far=False):
+        out[pl.ds(22, 10), cols] = inner[pl.ds(22, 10), cols] + piece[10:]
+
+
+def call(kernel, outs, scratch=(), scalars=0, count=0, flops=0, moved=0, name=None, sems=0, far=False, near=True, limit=VMEM_LIMIT):
     vmem = pl.BlockSpec(memory_space=pltpu.VMEM)
     smem = pl.BlockSpec(memory_space=pltpu.SMEM)
     hbm = pl.BlockSpec(memory_space=pltpu.HBM)
@@ -404,10 +413,10 @@
     return pl.pallas_call(
         kernel,
         out_shape=shapes,
-        in_specs=[smem] * scalars + [vmem] * (count - scalars),
+        in_specs=[smem] * scalars + [vmem if near else hbm] * (count - scalars),
         out_specs=[hbm if far else vmem] * len(shapes),
         scratch_shapes=[pltpu.VMEM(*s) for s in scratch] + [pltpu.SemaphoreType.DMA((sems,))] * (sems > 0),
-        compiler_params=pltpu.CompilerParams(vmem_limit_bytes=VMEM_LIMIT),
+        compiler_params=pltpu.CompilerParams(vmem_limit_bytes=limit),
         cost_estimate=pl.CostEstimate(flops=flops, bytes_accessed=moved, transcendentals=0),
         name=name,
     )
@@ -424,7 +433,8 @@
         restrict_kernel,
         [((18, 24, 128), F32), ((6, 16, 128), F32), ((288, 128), F32), ((288, 128), F32),
          ((320, 256), F32), ((320, 256), F32), ((328, 256), F32), ((328, 256), F32)],
-        [((18, 24, 256), F32), ((12, 16, 128), F32)], 0, 1, 10**8, 2 * 10**6, name="restrict",
+        [((18, 24, 256), F32), ((12, 16, 128), F32), ((32, 32, 256), F32)],
+        0, 1, 10**8, 2 * 10**6, name="restrict", sems=4, near=False, limit=60 * 1024 * 1024,
     )(charges)
     x_left = shift(s_up, "gx", 1)
     x_right = shift(s_down, "gx", -1)
@@ -476,7 +486,7 @@
     left, right, mid = lax.optimization_barrier((left, right, mid))
     direct, = call(
         finest_kernel, [((32, 32, 256), F32)],
-        [((20, 96, 256), F32), ((160, 768), BF), ((160, 768), BF)],
+        [((20, 96, 256), F32), ((640, 768), BF), ((640, 768), BF)],
         1, 9, 2 * 10**9, 6 * 10**6, name="finest",
     )(taps, before, after, left, right, y0, z0h, z0l, inner)
     result, = call(

time: 64.5 us -> 65.6 us (1.017)
  starting transfers between devices: 35 us -> 29.3 us
  waiting for transfers between devices: 5.68 us -> 10.6 us
  Pallas kernels: 21.8 us -> 24 us
    ppermute x12, starting transfers between devices: 35 us -> 29.3 us  [shift(): return lax.ppermute(x, axis, [(i, (i + by) % n) for i in range(n)])]
    ppermute x12, waiting for transfers between devices: 5.68 us -> 10.6 us  [shift(): return lax.ppermute(x, axis, [(i, (i + by) % n) for i in range(n)])]
    pallas_call x1, Pallas kernels: 1.01 us -> 3.38 us  [body(): call(restrict_kernel, [((18, 24, 128), F32), ((6, 16, 128), F32), ((288,...]
  transfers between devices with their start and end apart: 12 -> 12, of which waited for: 3 -> 5; matrix products, arithmetic and copies ran while one was open for 0% -> 0% of each run, Pallas kernels for 27% -> 26%
where the time goes in v8:
time: 65.6 us; the launch traced here: 65.2 us
  starting transfers between devices  29.3 us (45%)
  Pallas kernels  24 us (37%)
  waiting for transfers between devices  10.6 us (16%)
  local copies, waits for them, and re-layouts  0.99 us (2%)
    ppermute x12, starting transfers between devices, shift(): return lax.ppermute(x, axis, [(i, (i + by) % n) for i in range(n)])  29.3 us
    ppermute x12, waiting for transfers between devices, shift(): return lax.ppermute(x, axis, [(i, (i + by) % n) for i in range(n)])  10.6 us
    pallas_call x1, Pallas kernels, body(): call(inner_kernel, [((32, 32, 256), F32)], [((32, 96, 256), F32), ((256,...  7.28 us
    pallas_call x1, Pallas kernels, body(): call(upper_kernel, [((32, 32, 256), F32)], [((16, 48, 128), F32), ((32, 9...  3.6 us
    pallas_call x1, Pallas kernels, body(): call(restrict_kernel, [((18, 24, 128), F32), ((6, 16, 128), F32), ((288,...  3.38 us
    pallas_call x1, Pallas kernels, body(): call(fine_level_kernel, [((18, 32, 128), F32)], [((38, 48, 128), F32), ((...  3.38 us
    pallas_call x1, Pallas kernels, body(): call(matrices_kernel, [((96, 192), BF), ((96, 144), BF), ((96, 144), BF),...  3.02 us
    pallas_call x1, Pallas kernels, body(): call(finest_kernel, [((32, 32, 256), F32)], [((20, 96, 256), F32), ((640,...  3 us
  transfers between devices with their start and end apart: 12, of which 5 were waited for; matrix products, arithmetic and copies ran while one was open for 0% of the time, Pallas kernels for 26%

profile of v8, /device:TPU:1, one launch (start us, length us, event | category | flops | bytes accessed | tf_op | source)
XLA Modules:
  0.0 65.2 jit_solution(10247260592016023065)
XLA Ops:
  0.0 3.4 %restrict.1 = (f32[18,24,128]{2,1,0:T(8,128)}, f32[6,16,128]{2,1,0:T(8,128)}, f32[288,128]{1,0:T(8,128)}, f32[288,128]{1,0:T(8,128)}, f32[320,256]{1,0:T(8,128)}...) custom-call(f32[32,32,256]{2,1,0:T(8,128)} %c.1), custom_call_target="tpu_custom_call" | custom-call | flops 100000000 | bytes 2000000 | tf_op jit(solution)/shard_map/restrict/pallas_call | solution.py:432
  3.4 3.9 %collective-permute-start = (f32[288,128]{1,0:T(8,128)}, f32[288,128]{1,0:T(8,128)S(1)}, u32[]{:S(2)}, u32[]{:S(2)}) collective-permute-start(f32[288,128]{1,0:T(8,128)} %get-tuple-element.52), channel_id=1, source_target_pairs={{0,16},{16,32},{32,48},{48,64},{64,80},{80,96},{96,112},{112,128},... | collective-permute-start | bytes 442376 | tf_op jit(solution)/shard_map/ppermute | solution.py:427
  7.3 5.6 %collective-permute-start.1 = (f32[288,128]{1,0:T(8,128)}, f32[288,128]{1,0:T(8,128)S(1)}, u32[]{:S(2)}, u32[]{:S(2)}) collective-permute-start(f32[288,128]{1,0:T(8,128)} %get-tuple-element.53), channel_id=1, source_target_pairs={{0,240},{16,0},{32,16},{48,32},{64,48},{80,64},{96,80},{112,96},{1... | collective-permute-start | bytes 442376 | tf_op jit(solution)/shard_map/ppermute | solution.py:427
  12.9 1.6 %collective-permute-start.4 = (f32[328,256]{1,0:T(8,128)}, f32[328,256]{1,0:T(8,128)S(1)}, u32[]{:S(2)}, u32[]{:S(2)}) collective-permute-start(f32[328,256]{1,0:T(8,128)} %get-tuple-element.59), channel_id=1, source_target_pairs={{0,1},{1,2},{2,3},{3,4},{4,5},{5,6},{6,7},{7,8},{8,9},{9,10},{10,1... | collective-permute-start | bytes 1007624 | tf_op jit(solution)/shard_map/ppermute | solution.py:427
  14.5 3.0 %matrices.1 = (bf16[96,192]{1,0:T(8,128)(2,1)S(1)}, bf16[96,144]{1,0:T(8,128)(2,1)S(1)}, bf16[96,144]{1,0:T(8,128)(2,1)S(1)}, bf16[768,256]{1,0:T(8,128)(2,1)S(1...) custom-call(f32[3,3,21]{2,1,0:T(4,128)S(1)} %copy-done.2), custom_call_target="tpu_custom_call" | custom-call | flops 100000000 | bytes 4000000 | tf_op jit(solution)/shard_map/matrices/pallas_call | solution.py:442
  17.5 1.2 %collective-permute-done.1.right = f32[288,128]{1,0:T(8,128)S(1)} collective-permute-done((f32[288,128]{1,0:T(8,128)}, f32[288,128]{1,0:T(8,128)S(1)}, u32[]{:S(2)}, u32[]{:S(2)}) %collective-permute-start.1) | collective-permute-done | bytes 147488 | tf_op jit(solution)/shard_map/ppermute | solution.py:427
  18.7 1.0 %copy-done.4 = f32[320,256]{1,0:T(8,128)S(1)} copy-done((f32[320,256]{1,0:T(8,128)S(1)}, f32[320,256]{1,0:T(8,128)}, u32[]{:S(2)}) %copy-start.4) | copy-done | bytes 327704
  19.8 3.3 %collective-permute-start.2 = (f32[344,256]{1,0:T(8,128)S(1)}, f32[344,256]{1,0:T(8,128)S(1)}, u32[]{:S(2)}, u32[]{:S(2)}) collective-permute-start(f32[344,256]{1,0:T(8,128)S(1)} %get-tuple-element.57), channel_id=1, source_target_pairs={{0,16},{16,32},{32,48},{48,64},{64,80},{80,96},{96,112},{112,128},... | collective-permute-start | bytes 1056776 | tf_op jit(solution)/shard_map/ppermute | solution.py:427
  23.1 2.5 %collective-permute-start.3 = (f32[344,256]{1,0:T(8,128)S(1)}, f32[344,256]{1,0:T(8,128)S(1)}, u32[]{:S(2)}, u32[]{:S(2)}) collective-permute-start(f32[344,256]{1,0:T(8,128)S(1)} %get-tuple-element.58), channel_id=1, source_target_pairs={{0,240},{16,0},{32,16},{48,32},{64,48},{80,64},{96,80},{112,96},{1... | collective-permute-start | bytes 1056776 | tf_op jit(solution)/shard_map/ppermute | solution.py:427
  25.6 4.0 %collective-permute-start.6 = (f32[456,128]{1,0:T(8,128)S(1)}, f32[456,128]{1,0:T(8,128)S(1)}, u32[]{:S(2)}, u32[]{:S(2)}) collective-permute-start(f32[456,128]{1,0:T(8,128)S(1)} %get-tuple-element.65), channel_id=1, source_target_pairs={{0,1},{1,2},{2,3},{3,4},{4,5},{5,6},{6,7},{7,8},{8,9},{9,10},{10,1... | collective-permute-start | bytes 700424 | tf_op jit(solution)/shard_map/ppermute | solution.py:427
  29.6 2.9 %collective-permute-start.7 = (f32[456,128]{1,0:T(8,128)S(1)}, f32[456,128]{1,0:T(8,128)S(1)}, u32[]{:S(2)}, u32[]{:S(2)}) collective-permute-start(f32[456,128]{1,0:T(8,128)S(1)} %get-tuple-element.66), channel_id=1, source_target_pairs={{0,15},{1,0},{2,1},{3,2},{4,3},{5,4},{6,5},{7,6},{8,7},{9,8},{10,9... | collective-permute-start | bytes 700424 | tf_op jit(solution)/shard_map/ppermute | solution.py:427
  32.5 3.3 %collective-permute-done.5.right = f32[328,256]{1,0:T(8,128)S(1)} collective-permute-done((f32[328,256]{1,0:T(8,128)}, f32[328,256]{1,0:T(8,128)S(1)}, u32[]{:S(2)}, u32[]{:S(2)}) %collective-permute-start.5) | collective-permute-done | bytes 335904 | tf_op jit(solution)/shard_map/ppermute | solution.py:427
  35.8 7.3 %inner.1 = f32[32,32,256]{2,1,0:T(8,128)S(1)} custom-call(f32[3,3,21]{2,1,0:T(4,128)S(1)} %copy-done.2, f32[32,32,256]{2,1,0:T(8,128)S(1)} %copy-done, f32[328,256]{1,0:T(8,128)S(1)} %collective-permute-done.4.left, f32[328,256]{1,0:T(8,128)S(1)} %collective-permute-done.5.right, bf16[96,192]{1,0:T(8,128)(2,1)S(1)} %get-tuple-element.67.y0, ...), custom_call_target="tpu_custom_call" | custom-call | flops 2000000000 | bytes 6000000 | tf_op jit(solution)/shard_map/inner/pallas_call | solution.py:464
  43.1 0.2 collective-permute-done.6.left
  43.3 4.9 %collective-permute-done.7.right = f32[456,128]{1,0:T(8,128)S(1)} collective-permute-done((f32[456,128]{1,0:T(8,128)S(1)}, f32[456,128]{1,0:T(8,128)S(1)}, u32[]{:S(2)}, u32[]{:S(2)}) %collective-permute-start.7) | collective-permute-done | bytes 233504 | tf_op jit(solution)/shard_map/ppermute | solution.py:427
  48.2 0.1 gather_top.1
  48.3 0.3 collective-permute-start.8
  48.6 1.8 %collective-permute-start.9 = (f32[296,256]{1,0:T(8,128)S(1)}, f32[296,256]{1,0:T(8,128)S(1)}, u32[]{:S(2)}, u32[]{:S(2)}) collective-permute-start(f32[296,256]{1,0:T(8,128)S(1)} %get-tuple-element.75), channel_id=1, source_target_pairs={{0,15},{1,0},{2,1},{3,2},{4,3},{5,4},{6,5},{7,6},{8,7},{9,8},{10,9... | collective-permute-start | bytes 909320 | tf_op jit(solution)/shard_map/ppermute | solution.py:427
  50.3 0.4 collective-permute-start.10
  50.8 3.1 %collective-permute-start.11 = (f32[80,128]{1,0:T(8,128)S(1)}, f32[80,128]{1,0:T(8,128)S(1)}, u32[]{:S(2)}, u32[]{:S(2)}) collective-permute-start(f32[80,128]{1,0:T(8,128)S(1)} %get-tuple-element.85), channel_id=1, source_target_pairs={{0,14},{1,15},{2,0},{3,1},{4,2},{5,3},{6,4},{7,5},{8,6},{9,7},{10,... | collective-permute-start | bytes 122888 | tf_op jit(solution)/shard_map/ppermute | solution.py:427
  53.9 3.4 %fine_level.1.mid_in = f32[18,32,128]{2,1,0:T(8,128)S(1)} custom-call(f32[3,3,21]{2,1,0:T(4,128)S(1)} %copy-done.2, f32[38,24,128]{2,1,0:T(8,128)S(1)} %get-tuple-element.77.l1x, f32[456,128]{1,0:T(8,128)S(1)} %collective-permute-done.6.left, f32[456,128]{1,0:T(8,128)S(1)} %collective-permute-done.7.right, bf16[96,144]{1,0:T(8,128)(2,1)S(1)} %get-tuple-element.80.y1, ...), custom_call_target="tpu_custom_call" | custom-call | flops 400000000 | bytes 4000000 | tf_op jit(solution)/shard_map/fine_level/pallas_call | solution.py:481
  57.3 1.0 %collective-permute-done.9.right = f32[296,256]{1,0:T(8,128)S(1)} collective-permute-done((f32[296,256]{1,0:T(8,128)S(1)}, f32[296,256]{1,0:T(8,128)S(1)}, u32[]{:S(2)}, u32[]{:S(2)}) %collective-permute-start.9) | collective-permute-done | bytes 303136 | tf_op jit(solution)/shard_map/ppermute | solution.py:427
  58.4 3.0 %finest.1.direct = f32[32,32,256]{2,1,0:T(8,128)S(1)} custom-call(f32[3,3,21]{2,1,0:T(4,128)S(1)} %copy-done.2, f32[344,256]{1,0:T(8,128)S(1)} %collective-permute-done.2.before, f32[344,256]{1,0:T(8,128)S(1)} %collective-permute-done.3.after, f32[296,256]{1,0:T(8,128)S(1)} %collective-permute-done.8.left, f32[296,256]{1,0:T(8,128)S(1)} %collective-permute-done.9.right, ...), custom_call_target="tpu_custom_call" | custom-call | flops 2000000000 | bytes 6000000 | tf_op jit(solution)/shard_map/finest/pallas_call | solution.py:487
  61.4 3.6 %upper.1 = f32[32,32,256]{2,1,0:T(8,128)} custom-call(f32[3,3,21]{2,1,0:T(4,128)S(1)} %copy-done.2, f32[16,16,128]{2,1,0:T(8,128)S(1)} %get-tuple-element.73.l2x, f32[296,256]{1,0:T(8,128)S(1)} %collective-permute-done.8.left, f32[296,256]{1,0:T(8,128)S(1)} %collective-permute-done.9.right, f32[80,128]{1,0:T(8,128)S(1)} %collective-permute-done.10.left2, ...), custom_call_target="tpu_custom_call" | custom-call | flops 400000000 | bytes 4000000 | tf_op jit(solution)/shard_map/upper/pallas_call | solution.py:492
  (21 shorter events, 0.2 us)
Async XLA Ops:
  3.4 11.1 %copy-start.2 = (f32[3,3,21]{2,1,0:T(4,128)S(1)}, f32[3,3,21]{2,1,0:T(4,128)}, u32[]{:S(2)}) copy-start(f32[3,3,21]{2,1,0:T(4,128)} %taps.4) | copy-start | bytes 2272
  3.4 15.3 %copy-start.3 = (f32[320,256]{1,0:T(8,128)S(1)}, f32[320,256]{1,0:T(8,128)}, u32[]{:S(2)}) copy-start(f32[320,256]{1,0:T(8,128)} %get-tuple-element.50.last) | copy-start | bytes 983044
  3.4 14.1 %collective-permute-start = (f32[288,128]{1,0:T(8,128)}, f32[288,128]{1,0:T(8,128)S(1)}, u32[]{:S(2)}, u32[]{:S(2)}) collective-permute-start(f32[288,128]{1,0:T(8,128)} %get-tuple-element.52), channel_id=1, source_target_pairs={{0,16},{16,32},{32,48},{48,64},{64,80},{80,96},{96,112},{112,128},... | collective-permute-start | bytes 442376 | tf_op jit(solution)/shard_map/ppermute | solution.py:427
  7.3 11.4 %collective-permute-start.1 = (f32[288,128]{1,0:T(8,128)}, f32[288,128]{1,0:T(8,128)S(1)}, u32[]{:S(2)}, u32[]{:S(2)}) collective-permute-start(f32[288,128]{1,0:T(8,128)} %get-tuple-element.53), channel_id=1, source_target_pairs={{0,240},{16,0},{32,16},{48,32},{64,48},{80,64},{96,80},{112,96},{1... | collective-permute-start | bytes 442376 | tf_op jit(solution)/shard_map/ppermute | solution.py:427
  12.9 16.7 %collective-permute-start.4 = (f32[328,256]{1,0:T(8,128)}, f32[328,256]{1,0:T(8,128)S(1)}, u32[]{:S(2)}, u32[]{:S(2)}) collective-permute-start(f32[328,256]{1,0:T(8,128)} %get-tuple-element.59), channel_id=1, source_target_pairs={{0,1},{1,2},{2,3},{3,4},{4,5},{5,6},{6,7},{7,8},{8,9},{9,10},{10,1... | collective-permute-start | bytes 1007624 | tf_op jit(solution)/shard_map/ppermute | solution.py:427
  14.5 21.4 %collective-permute-start.5 = (f32[328,256]{1,0:T(8,128)}, f32[328,256]{1,0:T(8,128)S(1)}, u32[]{:S(2)}, u32[]{:S(2)}) collective-permute-start(f32[328,256]{1,0:T(8,128)} %get-tuple-element.60), channel_id=1, source_target_pairs={{0,15},{1,0},{2,1},{3,2},{4,3},{5,4},{6,5},{7,6},{8,7},{9,8},{10,9... | collective-permute-start | bytes 1007624 | tf_op jit(solution)/shard_map/ppermute | solution.py:427
  18.7 1.0 %copy-start.4 = (f32[320,256]{1,0:T(8,128)S(1)}, f32[320,256]{1,0:T(8,128)}, u32[]{:S(2)}) copy-start(f32[320,256]{1,0:T(8,128)} %get-tuple-element.51.first) | copy-start | bytes 983044
  19.7 5.9 %copy-start.5 = (f32[18,24,128]{2,1,0:T(8,128)S(1)}, f32[18,24,128]{2,1,0:T(8,128)}, u32[]{:S(2)}) copy-start(f32[18,24,128]{2,1,0:T(8,128)} %get-tuple-element.62.l1) | copy-start | bytes 663556
  19.8 28.4 %collective-permute-start.2 = (f32[344,256]{1,0:T(8,128)S(1)}, f32[344,256]{1,0:T(8,128)S(1)}, u32[]{:S(2)}, u32[]{:S(2)}) collective-permute-start(f32[344,256]{1,0:T(8,128)S(1)} %get-tuple-element.57), channel_id=1, source_target_pairs={{0,16},{16,32},{32,48},{48,64},{64,80},{80,96},{96,112},{112,128},... | collective-permute-start | bytes 1056776 | tf_op jit(solution)/shard_map/ppermute | solution.py:427
  23.1 12.8 %copy-start = (f32[32,32,256]{2,1,0:T(8,128)S(1)}, f32[32,32,256]{2,1,0:T(8,128)}, u32[]{:S(2)}) copy-start(f32[32,32,256]{2,1,0:T(8,128)} %c.1) | copy-start | bytes 3145732
  23.1 25.1 %collective-permute-start.3 = (f32[344,256]{1,0:T(8,128)S(1)}, f32[344,256]{1,0:T(8,128)S(1)}, u32[]{:S(2)}, u32[]{:S(2)}) collective-permute-start(f32[344,256]{1,0:T(8,128)S(1)} %get-tuple-element.58), channel_id=1, source_target_pairs={{0,240},{16,0},{32,16},{48,32},{64,48},{80,64},{96,80},{112,96},{1... | collective-permute-start | bytes 1056776 | tf_op jit(solution)/shard_map/ppermute | solution.py:427
  25.6 17.6 %collective-permute-start.6 = (f32[456,128]{1,0:T(8,128)S(1)}, f32[456,128]{1,0:T(8,128)S(1)}, u32[]{:S(2)}, u32[]{:S(2)}) collective-permute-start(f32[456,128]{1,0:T(8,128)S(1)} %get-tuple-element.65), channel_id=1, source_target_pairs={{0,1},{1,2},{2,3},{3,4},{4,5},{5,6},{6,7},{7,8},{8,9},{9,10},{10,1... | collective-permute-start | bytes 700424 | tf_op jit(solution)/shard_map/ppermute | solution.py:427
  29.6 18.6 %collective-permute-start.7 = (f32[456,128]{1,0:T(8,128)S(1)}, f32[456,128]{1,0:T(8,128)S(1)}, u32[]{:S(2)}, u32[]{:S(2)}) collective-permute-start(f32[456,128]{1,0:T(8,128)S(1)} %get-tuple-element.66), channel_id=1, source_target_pairs={{0,15},{1,0},{2,1},{3,2},{4,3},{5,4},{6,5},{7,6},{8,7},{9,8},{10,9... | collective-permute-start | bytes 700424 | tf_op jit(solution)/shard_map/ppermute | solution.py:427
  35.8 12.4 %copy-start.1 = (f32[6,16,128]{2,1,0:T(8,128)S(1)}, f32[6,16,128]{2,1,0:T(8,128)}, u32[]{:S(2)}) copy-start(f32[6,16,128]{2,1,0:T(8,128)} %get-tuple-element.72.l2) | copy-start | bytes 147460
  48.3 9.0 %collective-permute-start.8 = (f32[296,256]{1,0:T(8,128)S(1)}, f32[296,256]{1,0:T(8,128)S(1)}, u32[]{:S(2)}, u32[]{:S(2)}) collective-permute-start(f32[296,256]{1,0:T(8,128)S(1)} %get-tuple-element.74), channel_id=1, source_target_pairs={{0,1},{1,2},{2,3},{3,4},{4,5},{5,6},{6,7},{7,8},{8,9},{9,10},{10,1... | collective-permute-start | bytes 909320 | tf_op jit(solution)/shard_map/ppermute | solution.py:427
  48.6 9.8 %collective-permute-start.9 = (f32[296,256]{1,0:T(8,128)S(1)}, f32[296,256]{1,0:T(8,128)S(1)}, u32[]{:S(2)}, u32[]{:S(2)}) collective-permute-start(f32[296,256]{1,0:T(8,128)S(1)} %get-tuple-element.75), channel_id=1, source_target_pairs={{0,15},{1,0},{2,1},{3,2},{4,3},{5,4},{6,5},{7,6},{8,7},{9,8},{10,9... | collective-permute-start | bytes 909320 | tf_op jit(solution)/shard_map/ppermute | solution.py:427
  50.3 11.0 %collective-permute-start.10 = (f32[80,128]{1,0:T(8,128)S(1)}, f32[80,128]{1,0:T(8,128)S(1)}, u32[]{:S(2)}, u32[]{:S(2)}) collective-permute-start(f32[80,128]{1,0:T(8,128)S(1)} %get-tuple-element.84), channel_id=1, source_target_pairs={{0,2},{1,3},{2,4},{3,5},{4,6},{5,7},{6,8},{7,9},{8,10},{9,11},{10,... | collective-permute-start | bytes 122888 | tf_op jit(solution)/shard_map/ppermute | solution.py:427
  50.8 10.6 %collective-permute-start.11 = (f32[80,128]{1,0:T(8,128)S(1)}, f32[80,128]{1,0:T(8,128)S(1)}, u32[]{:S(2)}, u32[]{:S(2)}) collective-permute-start(f32[80,128]{1,0:T(8,128)S(1)} %get-tuple-element.85), channel_id=1, source_target_pairs={{0,14},{1,15},{2,0},{3,1},{4,2},{5,3},{6,4},{7,5},{8,6},{9,7},{10,... | collective-permute-start | bytes 122888 | tf_op jit(solution)/shard_map/ppermute | solution.py:427

commit v9 on v5

--- a/solution.py
+++ b/solution.py
@@ -237,7 +237,7 @@
 
 
 def correlate_x(taps, level, v, w, count, many):
-    @pl.loop(0, 12)
+    @pl.loop(0, 12, unroll=4)
     def _(g):
         member = g // 4
         rows = pl.ds(pl.multiple_of(8 * g, 8), 8)
@@ -385,15 +385,17 @@
                         sums[at] = term if sums[at] is None else sums[at] + term
                 for m in range(0, 20, 2):
                     high, low = halves(jnp.concatenate([sums[m], sums[m + 1]], 0))
-                    at = (pl.ds(8 * m, 16), pl.ds(256 * member + 128 * h, 128))
+                    at = (pl.ds(pl.multiple_of(160 * g, 32) + 8 * m, 16), pl.ds(256 * member + 128 * h, 128))
                     wh[at] = high
                     wl[at] = low
-        cols = pl.ds(pl.multiple_of(8 * g, 8), 8)
-        total = dot(wh[...], z0h[...]) + dot(wl[...], z0h[...]) + dot(wh[...], z0l[...])
-        total = total.reshape(20, 8, 256)
-        out[pl.ds(0, 10), cols] = inner[pl.ds(0, 10), cols] + total[:10]
+
+    total = dot(wh[...], z0h[...]) + dot(wl[...], z0h[...]) + dot(wh[...], z0l[...])
+    for g in range(4):
+        cols = pl.ds(8 * g, 8)
+        piece = total[160 * g:160 * g + 160].reshape(20, 8, 256)
+        out[pl.ds(0, 10), cols] = inner[pl.ds(0, 10), cols] + piece[:10]
         out[pl.ds(10, 12), cols] = inner[pl.ds(10, 12), cols]
-        out[pl.ds(22, 10), cols] = inner[pl.ds(22, 10), cols] + total[10:]
+        out[pl.ds(22, 10), cols] = inner[pl.ds(22, 10), cols] + piece[10:]
 
 
 def call(kernel, outs, scratch=(), scalars=0, count=0, flops=0, moved=0, name=None, sems=0, far=False):
@@ -476,7 +478,7 @@
     left, right, mid = lax.optimization_barrier((left, right, mid))
     direct, = call(
         finest_kernel, [((32, 32, 256), F32)],
-        [((20, 96, 256), F32), ((160, 768), BF), ((160, 768), BF)],
+        [((20, 96, 256), F32), ((640, 768), BF), ((640, 768), BF)],
         1, 9, 2 * 10**9, 6 * 10**6, name="finest",
     )(taps, before, after, left, right, y0, z0h, z0l, inner)
     result, = call(

time: 64.5 us -> 63.9 us (level)
  transfers between devices with their start and end apart: 12 -> 12, of which waited for: 3 -> 3; matrix products, arithmetic and copies ran while one was open for 0% -> 0% of each run, Pallas kernels for 27% -> 26%
where the time goes in v9:
time: 63.9 us; the launch traced here: 63.6 us
  starting transfers between devices  35 us (55%)
  Pallas kernels  21.2 us (33%)
  waiting for transfers between devices  5.88 us (9%)
  local copies, waits for them, and re-layouts  1.23 us (2%)
    ppermute x12, starting transfers between devices, shift(): return lax.ppermute(x, axis, [(i, (i + by) % n) for i in range(n)])  35 us
    pallas_call x1, Pallas kernels, body(): call(inner_kernel, [((32, 32, 256), F32)], [((32, 96, 256), F32), ((256,...  7.25 us
    ppermute x12, waiting for transfers between devices, shift(): return lax.ppermute(x, axis, [(i, (i + by) % n) for i in range(n)])  5.88 us
    pallas_call x1, Pallas kernels, body(): call(upper_kernel, [((32, 32, 256), F32)], [((16, 48, 128), F32), ((32, 9...  3.43 us
    pallas_call x1, Pallas kernels, body(): call(fine_level_kernel, [((18, 32, 128), F32)], [((38, 48, 128), F32), ((...  3.19 us
    pallas_call x1, Pallas kernels, body(): call(matrices_kernel, [((96, 192), BF), ((96, 144), BF), ((96, 144), BF),...  3.02 us
    pallas_call x1, Pallas kernels, body(): call(finest_kernel, [((32, 32, 256), F32)], [((20, 96, 256), F32), ((640,...  3.02 us
  transfers between devices with their start and end apart: 12, of which 3 were waited for; matrix products, arithmetic and copies ran while one was open for 0% of the time, Pallas kernels for 26%

profile of v9, /device:TPU:1, one launch (start us, length us, event | category | flops | bytes accessed | tf_op | source)
XLA Modules:
  0.0 63.6 jit_solution(17957610776559430158)
XLA Ops:
  0.0 1.2 %copy-done = f32[32,32,256]{2,1,0:T(8,128)S(1)} copy-done((f32[32,32,256]{2,1,0:T(8,128)S(1)}, f32[32,32,256]{2,1,0:T(8,128)}, u32[]{:S(2)}) %copy-start) | copy-done | bytes 1048600
  1.2 1.0 %restrict.1 = (f32[18,24,128]{2,1,0:T(8,128)S(1)}, f32[6,16,128]{2,1,0:T(8,128)S(1)}, f32[288,128]{1,0:T(8,128)S(1)}, f32[288,128]{1,0:T(8,128)S(1)}, f32[320,25...) custom-call(f32[32,32,256]{2,1,0:T(8,128)S(1)} %copy-done), custom_call_target="tpu_custom_call" | custom-call | flops 100000000 | bytes 2000000 | tf_op jit(solution)/shard_map/restrict/pallas_call | solution.py:425
  2.2 0.0 copy-start.2
  2.3 3.9 %collective-permute-start = (f32[288,128]{1,0:T(8,128)S(1)}, f32[288,128]{1,0:T(8,128)S(1)}, u32[]{:S(2)}, u32[]{:S(2)}) collective-permute-start(f32[288,128]{1,0:T(8,128)S(1)} %get-tuple-element.52), channel_id=1, source_target_pairs={{0,16},{16,32},{32,48},{48,64},{64,80},{80,96},{96,112},{112,128},... | collective-permute-start | bytes 442376 | tf_op jit(solution)/shard_map/ppermute | solution.py:420
  6.2 5.6 %collective-permute-start.1 = (f32[288,128]{1,0:T(8,128)S(1)}, f32[288,128]{1,0:T(8,128)S(1)}, u32[]{:S(2)}, u32[]{:S(2)}) collective-permute-start(f32[288,128]{1,0:T(8,128)S(1)} %get-tuple-element.53), channel_id=1, source_target_pairs={{0,240},{16,0},{32,16},{48,32},{64,48},{80,64},{96,80},{112,96},{1... | collective-permute-start | bytes 442376 | tf_op jit(solution)/shard_map/ppermute | solution.py:420
  11.7 1.6 %collective-permute-start.4 = (f32[328,256]{1,0:T(8,128)S(1)}, f32[328,256]{1,0:T(8,128)S(1)}, u32[]{:S(2)}, u32[]{:S(2)}) collective-permute-start(f32[328,256]{1,0:T(8,128)S(1)} %get-tuple-element.59), channel_id=1, source_target_pairs={{0,1},{1,2},{2,3},{3,4},{4,5},{5,6},{6,7},{7,8},{8,9},{9,10},{10,1... | collective-permute-start | bytes 1007624 | tf_op jit(solution)/shard_map/ppermute | solution.py:420
  13.3 3.0 %matrices.1 = (bf16[96,192]{1,0:T(8,128)(2,1)S(1)}, bf16[96,144]{1,0:T(8,128)(2,1)S(1)}, bf16[96,144]{1,0:T(8,128)(2,1)S(1)}, bf16[768,256]{1,0:T(8,128)(2,1)S(1...) custom-call(f32[3,3,21]{2,1,0:T(4,128)S(1)} %copy-done.2), custom_call_target="tpu_custom_call" | custom-call | flops 100000000 | bytes 4000000 | tf_op jit(solution)/shard_map/matrices/pallas_call | solution.py:434
  16.3 1.0 %collective-permute-done.1.right = f32[288,128]{1,0:T(8,128)S(1)} collective-permute-done((f32[288,128]{1,0:T(8,128)S(1)}, f32[288,128]{1,0:T(8,128)S(1)}, u32[]{:S(2)}, u32[]{:S(2)}) %collective-permute-start.1) | collective-permute-done | bytes 147488 | tf_op jit(solution)/shard_map/ppermute | solution.py:420
  17.3 0.1 face_x.1
  17.4 3.3 %collective-permute-start.2 = (f32[344,256]{1,0:T(8,128)S(1)}, f32[344,256]{1,0:T(8,128)S(1)}, u32[]{:S(2)}, u32[]{:S(2)}) collective-permute-start(f32[344,256]{1,0:T(8,128)S(1)} %get-tuple-element.57), channel_id=1, source_target_pairs={{0,16},{16,32},{32,48},{48,64},{64,80},{80,96},{96,112},{112,128},... | collective-permute-start | bytes 1056776 | tf_op jit(solution)/shard_map/ppermute | solution.py:420
  20.7 2.5 %collective-permute-start.3 = (f32[344,256]{1,0:T(8,128)S(1)}, f32[344,256]{1,0:T(8,128)S(1)}, u32[]{:S(2)}, u32[]{:S(2)}) collective-permute-start(f32[344,256]{1,0:T(8,128)S(1)} %get-tuple-element.58), channel_id=1, source_target_pairs={{0,240},{16,0},{32,16},{48,32},{64,48},{80,64},{96,80},{112,96},{1... | collective-permute-start | bytes 1056776 | tf_op jit(solution)/shard_map/ppermute | solution.py:420
  23.2 0.1 gather_fine.1
  23.3 3.9 %collective-permute-start.6 = (f32[456,128]{1,0:T(8,128)S(1)}, f32[456,128]{1,0:T(8,128)S(1)}, u32[]{:S(2)}, u32[]{:S(2)}) collective-permute-start(f32[456,128]{1,0:T(8,128)S(1)} %get-tuple-element.65), channel_id=1, source_target_pairs={{0,1},{1,2},{2,3},{3,4},{4,5},{5,6},{6,7},{7,8},{8,9},{9,10},{10,1... | collective-permute-start | bytes 700424 | tf_op jit(solution)/shard_map/ppermute | solution.py:420
  27.2 8.7 %collective-permute-start.7 = (f32[456,128]{1,0:T(8,128)S(1)}, f32[456,128]{1,0:T(8,128)S(1)}, u32[]{:S(2)}, u32[]{:S(2)}) collective-permute-start(f32[456,128]{1,0:T(8,128)S(1)} %get-tuple-element.66), channel_id=1, source_target_pairs={{0,15},{1,0},{2,1},{3,2},{4,3},{5,4},{6,5},{7,6},{8,7},{9,8},{10,9... | collective-permute-start | bytes 700424 | tf_op jit(solution)/shard_map/ppermute | solution.py:420
  35.9 7.2 %inner.1 = f32[32,32,256]{2,1,0:T(8,128)S(1)} custom-call(f32[3,3,21]{2,1,0:T(4,128)S(1)} %copy-done.2, f32[32,32,256]{2,1,0:T(8,128)S(1)} %copy-done.1, f32[328,256]{1,0:T(8,128)S(1)} %collective-permute-done.4.left, f32[328,256]{1,0:T(8,128)S(1)} %collective-permute-done.5.right, bf16[96,192]{1,0:T(8,128)(2,1)S(1)} %get-tuple-element.67.y0, ...), custom_call_target="tpu_custom_call" | custom-call | flops 2000000000 | bytes 6000000 | tf_op jit(solution)/shard_map/inner/pallas_call | solution.py:456
  43.2 3.6 %collective-permute-done.7.right = f32[456,128]{1,0:T(8,128)S(1)} collective-permute-done((f32[456,128]{1,0:T(8,128)S(1)}, f32[456,128]{1,0:T(8,128)S(1)}, u32[]{:S(2)}, u32[]{:S(2)}) %collective-permute-start.7) | collective-permute-done | bytes 233504 | tf_op jit(solution)/shard_map/ppermute | solution.py:420
  46.8 0.1 gather_top.1
  46.9 0.3 collective-permute-start.8
  47.2 1.8 %collective-permute-start.9 = (f32[296,256]{1,0:T(8,128)S(1)}, f32[296,256]{1,0:T(8,128)S(1)}, u32[]{:S(2)}, u32[]{:S(2)}) collective-permute-start(f32[296,256]{1,0:T(8,128)S(1)} %get-tuple-element.75), channel_id=1, source_target_pairs={{0,15},{1,0},{2,1},{3,2},{4,3},{5,4},{6,5},{7,6},{8,7},{9,8},{10,9... | collective-permute-start | bytes 909320 | tf_op jit(solution)/shard_map/ppermute | solution.py:420
  49.0 3.6 %collective-permute-start.11 = (f32[80,128]{1,0:T(8,128)S(1)}, f32[80,128]{1,0:T(8,128)S(1)}, u32[]{:S(2)}, u32[]{:S(2)}) collective-permute-start(f32[80,128]{1,0:T(8,128)S(1)} %get-tuple-element.85), channel_id=1, source_target_pairs={{0,14},{1,15},{2,0},{3,1},{4,2},{5,3},{6,4},{7,5},{8,6},{9,7},{10,... | collective-permute-start | bytes 122888 | tf_op jit(solution)/shard_map/ppermute | solution.py:420
  52.5 3.2 %fine_level.1.mid_in = f32[18,32,128]{2,1,0:T(8,128)S(1)} custom-call(f32[3,3,21]{2,1,0:T(4,128)S(1)} %copy-done.2, f32[38,24,128]{2,1,0:T(8,128)S(1)} %get-tuple-element.77.l1x, f32[456,128]{1,0:T(8,128)S(1)} %collective-permute-done.6.left, f32[456,128]{1,0:T(8,128)S(1)} %collective-permute-done.7.right, bf16[96,144]{1,0:T(8,128)(2,1)S(1)} %get-tuple-element.80.y1, ...), custom_call_target="tpu_custom_call" | custom-call | flops 400000000 | bytes 4000000 | tf_op jit(solution)/shard_map/fine_level/pallas_call | solution.py:473
  55.7 1.2 %collective-permute-done.9.right = f32[296,256]{1,0:T(8,128)S(1)} collective-permute-done((f32[296,256]{1,0:T(8,128)S(1)}, f32[296,256]{1,0:T(8,128)S(1)}, u32[]{:S(2)}, u32[]{:S(2)}) %collective-permute-start.9) | collective-permute-done | bytes 303136 | tf_op jit(solution)/shard_map/ppermute | solution.py:420
  57.0 3.0 %finest.1.direct = f32[32,32,256]{2,1,0:T(8,128)S(1)} custom-call(f32[3,3,21]{2,1,0:T(4,128)S(1)} %copy-done.2, f32[344,256]{1,0:T(8,128)S(1)} %collective-permute-done.2.before, f32[344,256]{1,0:T(8,128)S(1)} %collective-permute-done.3.after, f32[296,256]{1,0:T(8,128)S(1)} %collective-permute-done.8.left, f32[296,256]{1,0:T(8,128)S(1)} %collective-permute-done.9.right, ...), custom_call_target="tpu_custom_call" | custom-call | flops 2000000000 | bytes 6000000 | tf_op jit(solution)/shard_map/finest/pallas_call | solution.py:479
  60.0 3.4 %upper.1 = f32[32,32,256]{2,1,0:T(8,128)} custom-call(f32[3,3,21]{2,1,0:T(4,128)S(1)} %copy-done.2, f32[16,16,128]{2,1,0:T(8,128)S(1)} %get-tuple-element.73.l2x, f32[296,256]{1,0:T(8,128)S(1)} %collective-permute-done.8.left, f32[296,256]{1,0:T(8,128)S(1)} %collective-permute-done.9.right, f32[80,128]{1,0:T(8,128)S(1)} %collective-permute-done.10.left2, ...), custom_call_target="tpu_custom_call" | custom-call | flops 400000000 | bytes 4000000 | tf_op jit(solution)/shard_map/upper/pallas_call | solution.py:484
  (15 shorter events, 0.0 us)
Async XLA Ops:
  0.0 1.2 %copy-start = (f32[32,32,256]{2,1,0:T(8,128)S(1)}, f32[32,32,256]{2,1,0:T(8,128)}, u32[]{:S(2)}) copy-start(f32[32,32,256]{2,1,0:T(8,128)} %c.3) | copy-start | bytes 3145732
  2.2 11.1 %copy-start.2 = (f32[3,3,21]{2,1,0:T(4,128)S(1)}, f32[3,3,21]{2,1,0:T(4,128)}, u32[]{:S(2)}) copy-start(f32[3,3,21]{2,1,0:T(4,128)} %taps.4) | copy-start | bytes 2272
  2.3 14.1 %collective-permute-start = (f32[288,128]{1,0:T(8,128)S(1)}, f32[288,128]{1,0:T(8,128)S(1)}, u32[]{:S(2)}, u32[]{:S(2)}) collective-permute-start(f32[288,128]{1,0:T(8,128)S(1)} %get-tuple-element.52), channel_id=1, source_target_pairs={{0,16},{16,32},{32,48},{48,64},{64,80},{80,96},{96,112},{112,128},... | collective-permute-start | bytes 442376 | tf_op jit(solution)/shard_map/ppermute | solution.py:420
  6.2 11.2 %collective-permute-start.1 = (f32[288,128]{1,0:T(8,128)S(1)}, f32[288,128]{1,0:T(8,128)S(1)}, u32[]{:S(2)}, u32[]{:S(2)}) collective-permute-start(f32[288,128]{1,0:T(8,128)S(1)} %get-tuple-element.53), channel_id=1, source_target_pairs={{0,240},{16,0},{32,16},{48,32},{64,48},{80,64},{96,80},{112,96},{1... | collective-permute-start | bytes 442376 | tf_op jit(solution)/shard_map/ppermute | solution.py:420
  11.7 15.5 %collective-permute-start.4 = (f32[328,256]{1,0:T(8,128)S(1)}, f32[328,256]{1,0:T(8,128)S(1)}, u32[]{:S(2)}, u32[]{:S(2)}) collective-permute-start(f32[328,256]{1,0:T(8,128)S(1)} %get-tuple-element.59), channel_id=1, source_target_pairs={{0,1},{1,2},{2,3},{3,4},{4,5},{5,6},{6,7},{7,8},{8,9},{9,10},{10,1... | collective-permute-start | bytes 1007624 | tf_op jit(solution)/shard_map/ppermute | solution.py:420
  13.3 22.6 %collective-permute-start.5 = (f32[328,256]{1,0:T(8,128)S(1)}, f32[328,256]{1,0:T(8,128)S(1)}, u32[]{:S(2)}, u32[]{:S(2)}) collective-permute-start(f32[328,256]{1,0:T(8,128)S(1)} %get-tuple-element.60), channel_id=1, source_target_pairs={{0,15},{1,0},{2,1},{3,2},{4,3},{5,4},{6,5},{7,6},{8,7},{9,8},{10,9... | collective-permute-start | bytes 1007624 | tf_op jit(solution)/shard_map/ppermute | solution.py:420
  17.4 29.4 %collective-permute-start.2 = (f32[344,256]{1,0:T(8,128)S(1)}, f32[344,256]{1,0:T(8,128)S(1)}, u32[]{:S(2)}, u32[]{:S(2)}) collective-permute-start(f32[344,256]{1,0:T(8,128)S(1)} %get-tuple-element.57), channel_id=1, source_target_pairs={{0,16},{16,32},{32,48},{48,64},{64,80},{80,96},{96,112},{112,128},... | collective-permute-start | bytes 1056776 | tf_op jit(solution)/shard_map/ppermute | solution.py:420
  20.7 15.2 %copy-start.1 = (f32[32,32,256]{2,1,0:T(8,128)S(1)}, f32[32,32,256]{2,1,0:T(8,128)}, u32[]{:S(2)}) copy-start(f32[32,32,256]{2,1,0:T(8,128)} %c.3) | copy-start | bytes 3145732
  20.7 26.1 %collective-permute-start.3 = (f32[344,256]{1,0:T(8,128)S(1)}, f32[344,256]{1,0:T(8,128)S(1)}, u32[]{:S(2)}, u32[]{:S(2)}) collective-permute-start(f32[344,256]{1,0:T(8,128)S(1)} %get-tuple-element.58), channel_id=1, source_target_pairs={{0,240},{16,0},{32,16},{48,32},{64,48},{80,64},{96,80},{112,96},{1... | collective-permute-start | bytes 1056776 | tf_op jit(solution)/shard_map/ppermute | solution.py:420
  23.3 19.9 %collective-permute-start.6 = (f32[456,128]{1,0:T(8,128)S(1)}, f32[456,128]{1,0:T(8,128)S(1)}, u32[]{:S(2)}, u32[]{:S(2)}) collective-permute-start(f32[456,128]{1,0:T(8,128)S(1)} %get-tuple-element.65), channel_id=1, source_target_pairs={{0,1},{1,2},{2,3},{3,4},{4,5},{5,6},{6,7},{7,8},{8,9},{9,10},{10,1... | collective-permute-start | bytes 700424 | tf_op jit(solution)/shard_map/ppermute | solution.py:420
  27.2 19.6 %collective-permute-start.7 = (f32[456,128]{1,0:T(8,128)S(1)}, f32[456,128]{1,0:T(8,128)S(1)}, u32[]{:S(2)}, u32[]{:S(2)}) collective-permute-start(f32[456,128]{1,0:T(8,128)S(1)} %get-tuple-element.66), channel_id=1, source_target_pairs={{0,15},{1,0},{2,1},{3,2},{4,3},{5,4},{6,5},{7,6},{8,7},{9,8},{10,9... | collective-permute-start | bytes 700424 | tf_op jit(solution)/shard_map/ppermute | solution.py:420
  46.9 8.8 %collective-permute-start.8 = (f32[296,256]{1,0:T(8,128)S(1)}, f32[296,256]{1,0:T(8,128)S(1)}, u32[]{:S(2)}, u32[]{:S(2)}) collective-permute-start(f32[296,256]{1,0:T(8,128)S(1)} %get-tuple-element.74), channel_id=1, source_target_pairs={{0,1},{1,2},{2,3},{3,4},{4,5},{5,6},{6,7},{7,8},{8,9},{9,10},{10,1... | collective-permute-start | bytes 909320 | tf_op jit(solution)/shard_map/ppermute | solution.py:420
  47.2 9.8 %collective-permute-start.9 = (f32[296,256]{1,0:T(8,128)S(1)}, f32[296,256]{1,0:T(8,128)S(1)}, u32[]{:S(2)}, u32[]{:S(2)}) collective-permute-start(f32[296,256]{1,0:T(8,128)S(1)} %get-tuple-element.75), channel_id=1, source_target_pairs={{0,15},{1,0},{2,1},{3,2},{4,3},{5,4},{6,5},{7,6},{8,7},{9,8},{10,9... | collective-permute-start | bytes 909320 | tf_op jit(solution)/shard_map/ppermute | solution.py:420
  49.0 11.1 %collective-permute-start.10 = (f32[80,128]{1,0:T(8,128)S(1)}, f32[80,128]{1,0:T(8,128)S(1)}, u32[]{:S(2)}, u32[]{:S(2)}) collective-permute-start(f32[80,128]{1,0:T(8,128)S(1)} %get-tuple-element.84), channel_id=1, source_target_pairs={{0,2},{1,3},{2,4},{3,5},{4,6},{5,7},{6,8},{7,9},{8,10},{9,11},{10,... | collective-permute-start | bytes 122888 | tf_op jit(solution)/shard_map/ppermute | solution.py:420
  49.0 11.1 %collective-permute-start.11 = (f32[80,128]{1,0:T(8,128)S(1)}, f32[80,128]{1,0:T(8,128)S(1)}, u32[]{:S(2)}, u32[]{:S(2)}) collective-permute-start(f32[80,128]{1,0:T(8,128)S(1)} %get-tuple-element.85), channel_id=1, source_target_pairs={{0,14},{1,15},{2,0},{3,1},{4,2},{5,3},{6,4},{7,5},{8,6},{9,7},{10,... | collective-permute-start | bytes 122888 | tf_op jit(solution)/shard_map/ppermute | solution.py:420

commit v10 on v9

--- a/solution.py
+++ b/solution.py
@@ -237,7 +237,7 @@
 
 
 def correlate_x(taps, level, v, w, count, many):
-    @pl.loop(0, 12, unroll=4)
+    @pl.loop(0, 12, unroll=12)
     def _(g):
         member = g // 4
         rows = pl.ds(pl.multiple_of(8 * g, 8), 8)
@@ -366,7 +366,7 @@
         high, low = halves(jnp.concatenate([own, b, a], 0))
         v[i] = dot(y0[...], jnp.concatenate([high, low, high], 0))
 
-    @pl.loop(0, 4)
+    @pl.loop(0, 4, unroll=4)
     def _(g):
         for member in range(3):
             rows = pl.ds(pl.multiple_of(32 * member + 8 * g, 8), 8)

time: 63.9 us -> 63.4 us (level)
  transfers between devices with their start and end apart: 12 -> 12, of which waited for: 3 -> 4; matrix products, arithmetic and copies ran while one was open for 0% -> 0% of each run, Pallas kernels for 26% -> 26%
where the time goes in v10:
time: 63.4 us; the launch traced here: 63 us
  starting transfers between devices  35.1 us (55%)
  Pallas kernels  20.7 us (33%)
  waiting for transfers between devices  5.82 us (9%)
  local copies, waits for them, and re-layouts  1.23 us (2%)
    ppermute x12, starting transfers between devices, shift(): return lax.ppermute(x, axis, [(i, (i + by) % n) for i in range(n)])  35.1 us
    pallas_call x1, Pallas kernels, body(): call(inner_kernel, [((32, 32, 256), F32)], [((32, 96, 256), F32), ((256,...  7.25 us
    ppermute x12, waiting for transfers between devices, shift(): return lax.ppermute(x, axis, [(i, (i + by) % n) for i in range(n)])  5.82 us
    pallas_call x1, Pallas kernels, body(): call(fine_level_kernel, [((18, 32, 128), F32)], [((38, 48, 128), F32), ((...  3.58 us
    pallas_call x1, Pallas kernels, body(): call(matrices_kernel, [((96, 192), BF), ((96, 144), BF), ((96, 144), BF),...  3.02 us
    pallas_call x1, Pallas kernels, body(): call(upper_kernel, [((32, 32, 256), F32)], [((16, 48, 128), F32), ((32, 9...  2.92 us
    pallas_call x1, Pallas kernels, body(): call(finest_kernel, [((32, 32, 256), F32)], [((20, 96, 256), F32), ((640,...  2.6 us
  transfers between devices with their start and end apart: 12, of which 4 were waited for; matrix products, arithmetic and copies ran while one was open for 0% of the time, Pallas kernels for 26%

profile of v10, /device:TPU:1, one launch (start us, length us, event | category | flops | bytes accessed | tf_op | source)
XLA Modules:
  0.0 63.0 jit_solution(6692975854044187833)
XLA Ops:
  0.0 1.2 %copy-done = f32[32,32,256]{2,1,0:T(8,128)S(1)} copy-done((f32[32,32,256]{2,1,0:T(8,128)S(1)}, f32[32,32,256]{2,1,0:T(8,128)}, u32[]{:S(2)}) %copy-start) | copy-done | bytes 1048600
  1.2 1.0 %restrict.1 = (f32[18,24,128]{2,1,0:T(8,128)S(1)}, f32[6,16,128]{2,1,0:T(8,128)S(1)}, f32[288,128]{1,0:T(8,128)S(1)}, f32[288,128]{1,0:T(8,128)S(1)}, f32[320,25...) custom-call(f32[32,32,256]{2,1,0:T(8,128)S(1)} %copy-done), custom_call_target="tpu_custom_call" | custom-call | flops 100000000 | bytes 2000000 | tf_op jit(solution)/shard_map/restrict/pallas_call | solution.py:425
  2.3 3.9 %collective-permute-start = (f32[288,128]{1,0:T(8,128)S(1)}, f32[288,128]{1,0:T(8,128)S(1)}, u32[]{:S(2)}, u32[]{:S(2)}) collective-permute-start(f32[288,128]{1,0:T(8,128)S(1)} %get-tuple-element.52), channel_id=1, source_target_pairs={{0,16},{16,32},{32,48},{48,64},{64,80},{80,96},{96,112},{112,128},... | collective-permute-start | bytes 442376 | tf_op jit(solution)/shard_map/ppermute | solution.py:420
  6.2 5.6 %collective-permute-start.1 = (f32[288,128]{1,0:T(8,128)S(1)}, f32[288,128]{1,0:T(8,128)S(1)}, u32[]{:S(2)}, u32[]{:S(2)}) collective-permute-start(f32[288,128]{1,0:T(8,128)S(1)} %get-tuple-element.53), channel_id=1, source_target_pairs={{0,240},{16,0},{32,16},{48,32},{64,48},{80,64},{96,80},{112,96},{1... | collective-permute-start | bytes 442376 | tf_op jit(solution)/shard_map/ppermute | solution.py:420
  11.7 1.6 %collective-permute-start.4 = (f32[328,256]{1,0:T(8,128)S(1)}, f32[328,256]{1,0:T(8,128)S(1)}, u32[]{:S(2)}, u32[]{:S(2)}) collective-permute-start(f32[328,256]{1,0:T(8,128)S(1)} %get-tuple-element.59), channel_id=1, source_target_pairs={{0,1},{1,2},{2,3},{3,4},{4,5},{5,6},{6,7},{7,8},{8,9},{9,10},{10,1... | collective-permute-start | bytes 1007624 | tf_op jit(solution)/shard_map/ppermute | solution.py:420
  13.3 3.0 %matrices.1 = (bf16[96,192]{1,0:T(8,128)(2,1)S(1)}, bf16[96,144]{1,0:T(8,128)(2,1)S(1)}, bf16[96,144]{1,0:T(8,128)(2,1)S(1)}, bf16[768,256]{1,0:T(8,128)(2,1)S(1...) custom-call(f32[3,3,21]{2,1,0:T(4,128)S(1)} %copy-done.2), custom_call_target="tpu_custom_call" | custom-call | flops 100000000 | bytes 4000000 | tf_op jit(solution)/shard_map/matrices/pallas_call | solution.py:434
  16.3 1.0 %collective-permute-done.1.right = f32[288,128]{1,0:T(8,128)S(1)} collective-permute-done((f32[288,128]{1,0:T(8,128)S(1)}, f32[288,128]{1,0:T(8,128)S(1)}, u32[]{:S(2)}, u32[]{:S(2)}) %collective-permute-start.1) | collective-permute-done | bytes 147488 | tf_op jit(solution)/shard_map/ppermute | solution.py:420
  17.3 0.1 face_x.1
  17.4 3.3 %collective-permute-start.2 = (f32[344,256]{1,0:T(8,128)S(1)}, f32[344,256]{1,0:T(8,128)S(1)}, u32[]{:S(2)}, u32[]{:S(2)}) collective-permute-start(f32[344,256]{1,0:T(8,128)S(1)} %get-tuple-element.57), channel_id=1, source_target_pairs={{0,16},{16,32},{32,48},{48,64},{64,80},{80,96},{96,112},{112,128},... | collective-permute-start | bytes 1056776 | tf_op jit(solution)/shard_map/ppermute | solution.py:420
  20.7 2.5 %collective-permute-start.3 = (f32[344,256]{1,0:T(8,128)S(1)}, f32[344,256]{1,0:T(8,128)S(1)}, u32[]{:S(2)}, u32[]{:S(2)}) collective-permute-start(f32[344,256]{1,0:T(8,128)S(1)} %get-tuple-element.58), channel_id=1, source_target_pairs={{0,240},{16,0},{32,16},{48,32},{64,48},{80,64},{96,80},{112,96},{1... | collective-permute-start | bytes 1056776 | tf_op jit(solution)/shard_map/ppermute | solution.py:420
  23.2 0.1 gather_fine.1
  23.3 3.9 %collective-permute-start.6 = (f32[456,128]{1,0:T(8,128)S(1)}, f32[456,128]{1,0:T(8,128)S(1)}, u32[]{:S(2)}, u32[]{:S(2)}) collective-permute-start(f32[456,128]{1,0:T(8,128)S(1)} %get-tuple-element.65), channel_id=1, source_target_pairs={{0,1},{1,2},{2,3},{3,4},{4,5},{5,6},{6,7},{7,8},{8,9},{9,10},{10,1... | collective-permute-start | bytes 700424 | tf_op jit(solution)/shard_map/ppermute | solution.py:420
  27.2 8.7 %collective-permute-start.7 = (f32[456,128]{1,0:T(8,128)S(1)}, f32[456,128]{1,0:T(8,128)S(1)}, u32[]{:S(2)}, u32[]{:S(2)}) collective-permute-start(f32[456,128]{1,0:T(8,128)S(1)} %get-tuple-element.66), channel_id=1, source_target_pairs={{0,15},{1,0},{2,1},{3,2},{4,3},{5,4},{6,5},{7,6},{8,7},{9,8},{10,9... | collective-permute-start | bytes 700424 | tf_op jit(solution)/shard_map/ppermute | solution.py:420
  35.9 7.2 %inner.1 = f32[32,32,256]{2,1,0:T(8,128)S(1)} custom-call(f32[3,3,21]{2,1,0:T(4,128)S(1)} %copy-done.2, f32[32,32,256]{2,1,0:T(8,128)S(1)} %copy-done.1, f32[328,256]{1,0:T(8,128)S(1)} %collective-permute-done.4.left, f32[328,256]{1,0:T(8,128)S(1)} %collective-permute-done.5.right, bf16[96,192]{1,0:T(8,128)(2,1)S(1)} %get-tuple-element.67.y0, ...), custom_call_target="tpu_custom_call" | custom-call | flops 2000000000 | bytes 6000000 | tf_op jit(solution)/shard_map/inner/pallas_call | solution.py:456
  43.2 3.6 %collective-permute-done.7.right = f32[456,128]{1,0:T(8,128)S(1)} collective-permute-done((f32[456,128]{1,0:T(8,128)S(1)}, f32[456,128]{1,0:T(8,128)S(1)}, u32[]{:S(2)}, u32[]{:S(2)}) %collective-permute-start.7) | collective-permute-done | bytes 233504 | tf_op jit(solution)/shard_map/ppermute | solution.py:420
  46.8 0.1 gather_top.1
  46.9 0.3 collective-permute-start.8
  47.2 1.8 %collective-permute-start.9 = (f32[296,256]{1,0:T(8,128)S(1)}, f32[296,256]{1,0:T(8,128)S(1)}, u32[]{:S(2)}, u32[]{:S(2)}) collective-permute-start(f32[296,256]{1,0:T(8,128)S(1)} %get-tuple-element.75), channel_id=1, source_target_pairs={{0,15},{1,0},{2,1},{3,2},{4,3},{5,4},{6,5},{7,6},{8,7},{9,8},{10,9... | collective-permute-start | bytes 909320 | tf_op jit(solution)/shard_map/ppermute | solution.py:420
  49.0 3.6 %collective-permute-start.11 = (f32[80,128]{1,0:T(8,128)S(1)}, f32[80,128]{1,0:T(8,128)S(1)}, u32[]{:S(2)}, u32[]{:S(2)}) collective-permute-start(f32[80,128]{1,0:T(8,128)S(1)} %get-tuple-element.85), channel_id=1, source_target_pairs={{0,14},{1,15},{2,0},{3,1},{4,2},{5,3},{6,4},{7,5},{8,6},{9,7},{10,... | collective-permute-start | bytes 122888 | tf_op jit(solution)/shard_map/ppermute | solution.py:420
  52.5 3.6 %fine_level.1.mid_in = f32[18,32,128]{2,1,0:T(8,128)S(1)} custom-call(f32[3,3,21]{2,1,0:T(4,128)S(1)} %copy-done.2, f32[38,24,128]{2,1,0:T(8,128)S(1)} %get-tuple-element.77.l1x, f32[456,128]{1,0:T(8,128)S(1)} %collective-permute-done.6.left, f32[456,128]{1,0:T(8,128)S(1)} %collective-permute-done.7.right, bf16[96,144]{1,0:T(8,128)(2,1)S(1)} %get-tuple-element.80.y1, ...), custom_call_target="tpu_custom_call" | custom-call | flops 400000000 | bytes 4000000 | tf_op jit(solution)/shard_map/fine_level/pallas_call | solution.py:473
  56.1 0.9 %collective-permute-done.9.right = f32[296,256]{1,0:T(8,128)S(1)} collective-permute-done((f32[296,256]{1,0:T(8,128)S(1)}, f32[296,256]{1,0:T(8,128)S(1)}, u32[]{:S(2)}, u32[]{:S(2)}) %collective-permute-start.9) | collective-permute-done | bytes 303136 | tf_op jit(solution)/shard_map/ppermute | solution.py:420
  57.0 2.6 %finest.1.direct = f32[32,32,256]{2,1,0:T(8,128)S(1)} custom-call(f32[3,3,21]{2,1,0:T(4,128)S(1)} %copy-done.2, f32[344,256]{1,0:T(8,128)S(1)} %collective-permute-done.2.before, f32[344,256]{1,0:T(8,128)S(1)} %collective-permute-done.3.after, f32[296,256]{1,0:T(8,128)S(1)} %collective-permute-done.8.left, f32[296,256]{1,0:T(8,128)S(1)} %collective-permute-done.9.right, ...), custom_call_target="tpu_custom_call" | custom-call | flops 2000000000 | bytes 6000000 | tf_op jit(solution)/shard_map/finest/pallas_call | solution.py:479
  59.6 0.3 collective-permute-done.10.left2
  59.9 2.9 %upper.1 = f32[32,32,256]{2,1,0:T(8,128)} custom-call(f32[3,3,21]{2,1,0:T(4,128)S(1)} %copy-done.2, f32[16,16,128]{2,1,0:T(8,128)S(1)} %get-tuple-element.73.l2x, f32[296,256]{1,0:T(8,128)S(1)} %collective-permute-done.8.left, f32[296,256]{1,0:T(8,128)S(1)} %collective-permute-done.9.right, f32[80,128]{1,0:T(8,128)S(1)} %collective-permute-done.10.left2, ...), custom_call_target="tpu_custom_call" | custom-call | flops 400000000 | bytes 4000000 | tf_op jit(solution)/shard_map/upper/pallas_call | solution.py:484
  (15 shorter events, 0.0 us)
Async XLA Ops:
  0.0 1.2 %copy-start = (f32[32,32,256]{2,1,0:T(8,128)S(1)}, f32[32,32,256]{2,1,0:T(8,128)}, u32[]{:S(2)}) copy-start(f32[32,32,256]{2,1,0:T(8,128)} %c.3) | copy-start | bytes 3145732
  2.2 11.1 %copy-start.2 = (f32[3,3,21]{2,1,0:T(4,128)S(1)}, f32[3,3,21]{2,1,0:T(4,128)}, u32[]{:S(2)}) copy-start(f32[3,3,21]{2,1,0:T(4,128)} %taps.4) | copy-start | bytes 2272
  2.3 14.1 %collective-permute-start = (f32[288,128]{1,0:T(8,128)S(1)}, f32[288,128]{1,0:T(8,128)S(1)}, u32[]{:S(2)}, u32[]{:S(2)}) collective-permute-start(f32[288,128]{1,0:T(8,128)S(1)} %get-tuple-element.52), channel_id=1, source_target_pairs={{0,16},{16,32},{32,48},{48,64},{64,80},{80,96},{96,112},{112,128},... | collective-permute-start | bytes 442376 | tf_op jit(solution)/shard_map/ppermute | solution.py:420
  6.2 11.2 %collective-permute-start.1 = (f32[288,128]{1,0:T(8,128)S(1)}, f32[288,128]{1,0:T(8,128)S(1)}, u32[]{:S(2)}, u32[]{:S(2)}) collective-permute-start(f32[288,128]{1,0:T(8,128)S(1)} %get-tuple-element.53), channel_id=1, source_target_pairs={{0,240},{16,0},{32,16},{48,32},{64,48},{80,64},{96,80},{112,96},{1... | collective-permute-start | bytes 442376 | tf_op jit(solution)/shard_map/ppermute | solution.py:420
  11.7 15.5 %collective-permute-start.4 = (f32[328,256]{1,0:T(8,128)S(1)}, f32[328,256]{1,0:T(8,128)S(1)}, u32[]{:S(2)}, u32[]{:S(2)}) collective-permute-start(f32[328,256]{1,0:T(8,128)S(1)} %get-tuple-element.59), channel_id=1, source_target_pairs={{0,1},{1,2},{2,3},{3,4},{4,5},{5,6},{6,7},{7,8},{8,9},{9,10},{10,1... | collective-permute-start | bytes 1007624 | tf_op jit(solution)/shard_map/ppermute | solution.py:420
  13.3 22.6 %collective-permute-start.5 = (f32[328,256]{1,0:T(8,128)S(1)}, f32[328,256]{1,0:T(8,128)S(1)}, u32[]{:S(2)}, u32[]{:S(2)}) collective-permute-start(f32[328,256]{1,0:T(8,128)S(1)} %get-tuple-element.60), channel_id=1, source_target_pairs={{0,15},{1,0},{2,1},{3,2},{4,3},{5,4},{6,5},{7,6},{8,7},{9,8},{10,9... | collective-permute-start | bytes 1007624 | tf_op jit(solution)/shard_map/ppermute | solution.py:420
  17.4 29.4 %collective-permute-start.2 = (f32[344,256]{1,0:T(8,128)S(1)}, f32[344,256]{1,0:T(8,128)S(1)}, u32[]{:S(2)}, u32[]{:S(2)}) collective-permute-start(f32[344,256]{1,0:T(8,128)S(1)} %get-tuple-element.57), channel_id=1, source_target_pairs={{0,16},{16,32},{32,48},{48,64},{64,80},{80,96},{96,112},{112,128},... | collective-permute-start | bytes 1056776 | tf_op jit(solution)/shard_map/ppermute | solution.py:420
  20.7 15.2 %copy-start.1 = (f32[32,32,256]{2,1,0:T(8,128)S(1)}, f32[32,32,256]{2,1,0:T(8,128)}, u32[]{:S(2)}) copy-start(f32[32,32,256]{2,1,0:T(8,128)} %c.3) | copy-start | bytes 3145732
  20.7 26.1 %collective-permute-start.3 = (f32[344,256]{1,0:T(8,128)S(1)}, f32[344,256]{1,0:T(8,128)S(1)}, u32[]{:S(2)}, u32[]{:S(2)}) collective-permute-start(f32[344,256]{1,0:T(8,128)S(1)} %get-tuple-element.58), channel_id=1, source_target_pairs={{0,240},{16,0},{32,16},{48,32},{64,48},{80,64},{96,80},{112,96},{1... | collective-permute-start | bytes 1056776 | tf_op jit(solution)/shard_map/ppermute | solution.py:420
  23.3 19.9 %collective-permute-start.6 = (f32[456,128]{1,0:T(8,128)S(1)}, f32[456,128]{1,0:T(8,128)S(1)}, u32[]{:S(2)}, u32[]{:S(2)}) collective-permute-start(f32[456,128]{1,0:T(8,128)S(1)} %get-tuple-element.65), channel_id=1, source_target_pairs={{0,1},{1,2},{2,3},{3,4},{4,5},{5,6},{6,7},{7,8},{8,9},{9,10},{10,1... | collective-permute-start | bytes 700424 | tf_op jit(solution)/shard_map/ppermute | solution.py:420
  27.2 19.6 %collective-permute-start.7 = (f32[456,128]{1,0:T(8,128)S(1)}, f32[456,128]{1,0:T(8,128)S(1)}, u32[]{:S(2)}, u32[]{:S(2)}) collective-permute-start(f32[456,128]{1,0:T(8,128)S(1)} %get-tuple-element.66), channel_id=1, source_target_pairs={{0,15},{1,0},{2,1},{3,2},{4,3},{5,4},{6,5},{7,6},{8,7},{9,8},{10,9... | collective-permute-start | bytes 700424 | tf_op jit(solution)/shard_map/ppermute | solution.py:420
  46.9 9.2 %collective-permute-start.8 = (f32[296,256]{1,0:T(8,128)S(1)}, f32[296,256]{1,0:T(8,128)S(1)}, u32[]{:S(2)}, u32[]{:S(2)}) collective-permute-start(f32[296,256]{1,0:T(8,128)S(1)} %get-tuple-element.74), channel_id=1, source_target_pairs={{0,1},{1,2},{2,3},{3,4},{4,5},{5,6},{6,7},{7,8},{8,9},{9,10},{10,1... | collective-permute-start | bytes 909320 | tf_op jit(solution)/shard_map/ppermute | solution.py:420
  47.2 9.8 %collective-permute-start.9 = (f32[296,256]{1,0:T(8,128)S(1)}, f32[296,256]{1,0:T(8,128)S(1)}, u32[]{:S(2)}, u32[]{:S(2)}) collective-permute-start(f32[296,256]{1,0:T(8,128)S(1)} %get-tuple-element.75), channel_id=1, source_target_pairs={{0,15},{1,0},{2,1},{3,2},{4,3},{5,4},{6,5},{7,6},{8,7},{9,8},{10,9... | collective-permute-start | bytes 909320 | tf_op jit(solution)/shard_map/ppermute | solution.py:420
  49.0 11.0 %collective-permute-start.10 = (f32[80,128]{1,0:T(8,128)S(1)}, f32[80,128]{1,0:T(8,128)S(1)}, u32[]{:S(2)}, u32[]{:S(2)}) collective-permute-start(f32[80,128]{1,0:T(8,128)S(1)} %get-tuple-element.84), channel_id=1, source_target_pairs={{0,2},{1,3},{2,4},{3,5},{4,6},{5,7},{6,8},{7,9},{8,10},{9,11},{10,... | collective-permute-start | bytes 122888 | tf_op jit(solution)/shard_map/ppermute | solution.py:420
  49.0 11.0 %collective-permute-start.11 = (f32[80,128]{1,0:T(8,128)S(1)}, f32[80,128]{1,0:T(8,128)S(1)}, u32[]{:S(2)}, u32[]{:S(2)}) collective-permute-start(f32[80,128]{1,0:T(8,128)S(1)} %get-tuple-element.85), channel_id=1, source_target_pairs={{0,14},{1,15},{2,0},{3,1},{4,2},{5,3},{6,4},{7,5},{8,6},{9,7},{10,... | collective-permute-start | bytes 122888 | tf_op jit(solution)/shard_map/ppermute | solution.py:420

commit v11 on v10

--- a/solution.py
+++ b/solution.py
@@ -237,7 +237,7 @@
 
 
 def correlate_x(taps, level, v, w, count, many):
-    @pl.loop(0, 12, unroll=12)
+    @pl.loop(0, 12, unroll=4 if level == 1 else 12)
     def _(g):
         member = g // 4
         rows = pl.ds(pl.multiple_of(8 * g, 8), 8)

time: 63.4 us -> 63.1 us (level)
  no operation moved by 1% of the time
where the time goes in v11:
time: 63.1 us; the launch traced here: 63 us
  starting transfers between devices  35 us (55%)
  Pallas kernels  20.3 us (32%)
  waiting for transfers between devices  6.21 us (10%)
  local copies, waits for them, and re-layouts  1.23 us (2%)
    ppermute x12, starting transfers between devices, shift(): return lax.ppermute(x, axis, [(i, (i + by) % n) for i in range(n)])  35 us
    pallas_call x1, Pallas kernels, body(): call(inner_kernel, [((32, 32, 256), F32)], [((32, 96, 256), F32), ((256,...  7.25 us
    ppermute x12, waiting for transfers between devices, shift(): return lax.ppermute(x, axis, [(i, (i + by) % n) for i in range(n)])  6.21 us
    pallas_call x1, Pallas kernels, body(): call(fine_level_kernel, [((18, 32, 128), F32)], [((38, 48, 128), F32), ((...  3.19 us
    pallas_call x1, Pallas kernels, body(): call(matrices_kernel, [((96, 192), BF), ((96, 144), BF), ((96, 144), BF),...  3.02 us
    pallas_call x1, Pallas kernels, body(): call(upper_kernel, [((32, 32, 256), F32)], [((16, 48, 128), F32), ((32, 9...  2.92 us
    pallas_call x1, Pallas kernels, body(): call(finest_kernel, [((32, 32, 256), F32)], [((20, 96, 256), F32), ((640,...  2.6 us
  transfers between devices with their start and end apart: 12, of which 4 were waited for; matrix products, arithmetic and copies ran while one was open for 0% of the time, Pallas kernels for 26%

profile of v11, /device:TPU:1, one launch (start us, length us, event | category | flops | bytes accessed | tf_op | source)
XLA Modules:
  0.0 63.0 jit_solution(10222565777427531637)
XLA Ops:
  0.0 1.2 %copy-done = f32[32,32,256]{2,1,0:T(8,128)S(1)} copy-done((f32[32,32,256]{2,1,0:T(8,128)S(1)}, f32[32,32,256]{2,1,0:T(8,128)}, u32[]{:S(2)}) %copy-start) | copy-done | bytes 1048600
  1.2 1.0 %restrict.1 = (f32[18,24,128]{2,1,0:T(8,128)S(1)}, f32[6,16,128]{2,1,0:T(8,128)S(1)}, f32[288,128]{1,0:T(8,128)S(1)}, f32[288,128]{1,0:T(8,128)S(1)}, f32[320,25...) custom-call(f32[32,32,256]{2,1,0:T(8,128)S(1)} %copy-done), custom_call_target="tpu_custom_call" | custom-call | flops 100000000 | bytes 2000000 | tf_op jit(solution)/shard_map/restrict/pallas_call | solution.py:425
  2.3 3.9 %collective-permute-start = (f32[288,128]{1,0:T(8,128)S(1)}, f32[288,128]{1,0:T(8,128)S(1)}, u32[]{:S(2)}, u32[]{:S(2)}) collective-permute-start(f32[288,128]{1,0:T(8,128)S(1)} %get-tuple-element.52), channel_id=1, source_target_pairs={{0,16},{16,32},{32,48},{48,64},{64,80},{80,96},{96,112},{112,128},... | collective-permute-start | bytes 442376 | tf_op jit(solution)/shard_map/ppermute | solution.py:420
  6.2 5.6 %collective-permute-start.1 = (f32[288,128]{1,0:T(8,128)S(1)}, f32[288,128]{1,0:T(8,128)S(1)}, u32[]{:S(2)}, u32[]{:S(2)}) collective-permute-start(f32[288,128]{1,0:T(8,128)S(1)} %get-tuple-element.53), channel_id=1, source_target_pairs={{0,240},{16,0},{32,16},{48,32},{64,48},{80,64},{96,80},{112,96},{1... | collective-permute-start | bytes 442376 | tf_op jit(solution)/shard_map/ppermute | solution.py:420
  11.7 1.6 %collective-permute-start.4 = (f32[328,256]{1,0:T(8,128)S(1)}, f32[328,256]{1,0:T(8,128)S(1)}, u32[]{:S(2)}, u32[]{:S(2)}) collective-permute-start(f32[328,256]{1,0:T(8,128)S(1)} %get-tuple-element.59), channel_id=1, source_target_pairs={{0,1},{1,2},{2,3},{3,4},{4,5},{5,6},{6,7},{7,8},{8,9},{9,10},{10,1... | collective-permute-start | bytes 1007624 | tf_op jit(solution)/shard_map/ppermute | solution.py:420
  13.3 3.0 %matrices.1 = (bf16[96,192]{1,0:T(8,128)(2,1)S(1)}, bf16[96,144]{1,0:T(8,128)(2,1)S(1)}, bf16[96,144]{1,0:T(8,128)(2,1)S(1)}, bf16[768,256]{1,0:T(8,128)(2,1)S(1...) custom-call(f32[3,3,21]{2,1,0:T(4,128)S(1)} %copy-done.2), custom_call_target="tpu_custom_call" | custom-call | flops 100000000 | bytes 4000000 | tf_op jit(solution)/shard_map/matrices/pallas_call | solution.py:434
  16.3 1.0 %collective-permute-done.1.right = f32[288,128]{1,0:T(8,128)S(1)} collective-permute-done((f32[288,128]{1,0:T(8,128)S(1)}, f32[288,128]{1,0:T(8,128)S(1)}, u32[]{:S(2)}, u32[]{:S(2)}) %collective-permute-start.1) | collective-permute-done | bytes 147488 | tf_op jit(solution)/shard_map/ppermute | solution.py:420
  17.3 0.1 face_x.1
  17.4 3.3 %collective-permute-start.2 = (f32[344,256]{1,0:T(8,128)S(1)}, f32[344,256]{1,0:T(8,128)S(1)}, u32[]{:S(2)}, u32[]{:S(2)}) collective-permute-start(f32[344,256]{1,0:T(8,128)S(1)} %get-tuple-element.57), channel_id=1, source_target_pairs={{0,16},{16,32},{32,48},{48,64},{64,80},{80,96},{96,112},{112,128},... | collective-permute-start | bytes 1056776 | tf_op jit(solution)/shard_map/ppermute | solution.py:420
  20.7 2.5 %collective-permute-start.3 = (f32[344,256]{1,0:T(8,128)S(1)}, f32[344,256]{1,0:T(8,128)S(1)}, u32[]{:S(2)}, u32[]{:S(2)}) collective-permute-start(f32[344,256]{1,0:T(8,128)S(1)} %get-tuple-element.58), channel_id=1, source_target_pairs={{0,240},{16,0},{32,16},{48,32},{64,48},{80,64},{96,80},{112,96},{1... | collective-permute-start | bytes 1056776 | tf_op jit(solution)/shard_map/ppermute | solution.py:420
  23.2 0.1 gather_fine.1
  23.3 3.9 %collective-permute-start.6 = (f32[456,128]{1,0:T(8,128)S(1)}, f32[456,128]{1,0:T(8,128)S(1)}, u32[]{:S(2)}, u32[]{:S(2)}) collective-permute-start(f32[456,128]{1,0:T(8,128)S(1)} %get-tuple-element.65), channel_id=1, source_target_pairs={{0,1},{1,2},{2,3},{3,4},{4,5},{5,6},{6,7},{7,8},{8,9},{9,10},{10,1... | collective-permute-start | bytes 700424 | tf_op jit(solution)/shard_map/ppermute | solution.py:420
  27.2 8.7 %collective-permute-start.7 = (f32[456,128]{1,0:T(8,128)S(1)}, f32[456,128]{1,0:T(8,128)S(1)}, u32[]{:S(2)}, u32[]{:S(2)}) collective-permute-start(f32[456,128]{1,0:T(8,128)S(1)} %get-tuple-element.66), channel_id=1, source_target_pairs={{0,15},{1,0},{2,1},{3,2},{4,3},{5,4},{6,5},{7,6},{8,7},{9,8},{10,9... | collective-permute-start | bytes 700424 | tf_op jit(solution)/shard_map/ppermute | solution.py:420
  35.9 7.2 %inner.1 = f32[32,32,256]{2,1,0:T(8,128)S(1)} custom-call(f32[3,3,21]{2,1,0:T(4,128)S(1)} %copy-done.2, f32[32,32,256]{2,1,0:T(8,128)S(1)} %copy-done.1, f32[328,256]{1,0:T(8,128)S(1)} %collective-permute-done.4.left, f32[328,256]{1,0:T(8,128)S(1)} %collective-permute-done.5.right, bf16[96,192]{1,0:T(8,128)(2,1)S(1)} %get-tuple-element.67.y0, ...), custom_call_target="tpu_custom_call" | custom-call | flops 2000000000 | bytes 6000000 | tf_op jit(solution)/shard_map/inner/pallas_call | solution.py:456
  43.2 3.6 %collective-permute-done.7.right = f32[456,128]{1,0:T(8,128)S(1)} collective-permute-done((f32[456,128]{1,0:T(8,128)S(1)}, f32[456,128]{1,0:T(8,128)S(1)}, u32[]{:S(2)}, u32[]{:S(2)}) %collective-permute-start.7) | collective-permute-done | bytes 233504 | tf_op jit(solution)/shard_map/ppermute | solution.py:420
  46.8 0.1 gather_top.1
  46.9 0.3 collective-permute-start.8
  47.2 1.8 %collective-permute-start.9 = (f32[296,256]{1,0:T(8,128)S(1)}, f32[296,256]{1,0:T(8,128)S(1)}, u32[]{:S(2)}, u32[]{:S(2)}) collective-permute-start(f32[296,256]{1,0:T(8,128)S(1)} %get-tuple-element.75), channel_id=1, source_target_pairs={{0,15},{1,0},{2,1},{3,2},{4,3},{5,4},{6,5},{7,6},{8,7},{9,8},{10,9... | collective-permute-start | bytes 909320 | tf_op jit(solution)/shard_map/ppermute | solution.py:420
  49.0 3.6 %collective-permute-start.11 = (f32[80,128]{1,0:T(8,128)S(1)}, f32[80,128]{1,0:T(8,128)S(1)}, u32[]{:S(2)}, u32[]{:S(2)}) collective-permute-start(f32[80,128]{1,0:T(8,128)S(1)} %get-tuple-element.85), channel_id=1, source_target_pairs={{0,14},{1,15},{2,0},{3,1},{4,2},{5,3},{6,4},{7,5},{8,6},{9,7},{10,... | collective-permute-start | bytes 122888 | tf_op jit(solution)/shard_map/ppermute | solution.py:420
  52.5 3.2 %fine_level.1.mid_in = f32[18,32,128]{2,1,0:T(8,128)S(1)} custom-call(f32[3,3,21]{2,1,0:T(4,128)S(1)} %copy-done.2, f32[38,24,128]{2,1,0:T(8,128)S(1)} %get-tuple-element.77.l1x, f32[456,128]{1,0:T(8,128)S(1)} %collective-permute-done.6.left, f32[456,128]{1,0:T(8,128)S(1)} %collective-permute-done.7.right, bf16[96,144]{1,0:T(8,128)(2,1)S(1)} %get-tuple-element.80.y1, ...), custom_call_target="tpu_custom_call" | custom-call | flops 400000000 | bytes 4000000 | tf_op jit(solution)/shard_map/fine_level/pallas_call | solution.py:473
  55.7 1.2 %collective-permute-done.9.right = f32[296,256]{1,0:T(8,128)S(1)} collective-permute-done((f32[296,256]{1,0:T(8,128)S(1)}, f32[296,256]{1,0:T(8,128)S(1)}, u32[]{:S(2)}, u32[]{:S(2)}) %collective-permute-start.9) | collective-permute-done | bytes 303136 | tf_op jit(solution)/shard_map/ppermute | solution.py:420
  57.0 2.6 %finest.1.direct = f32[32,32,256]{2,1,0:T(8,128)S(1)} custom-call(f32[3,3,21]{2,1,0:T(4,128)S(1)} %copy-done.2, f32[344,256]{1,0:T(8,128)S(1)} %collective-permute-done.2.before, f32[344,256]{1,0:T(8,128)S(1)} %collective-permute-done.3.after, f32[296,256]{1,0:T(8,128)S(1)} %collective-permute-done.8.left, f32[296,256]{1,0:T(8,128)S(1)} %collective-permute-done.9.right, ...), custom_call_target="tpu_custom_call" | custom-call | flops 2000000000 | bytes 6000000 | tf_op jit(solution)/shard_map/finest/pallas_call | solution.py:479
  59.6 0.3 collective-permute-done.10.left2
  59.9 2.9 %upper.1 = f32[32,32,256]{2,1,0:T(8,128)} custom-call(f32[3,3,21]{2,1,0:T(4,128)S(1)} %copy-done.2, f32[16,16,128]{2,1,0:T(8,128)S(1)} %get-tuple-element.73.l2x, f32[296,256]{1,0:T(8,128)S(1)} %collective-permute-done.8.left, f32[296,256]{1,0:T(8,128)S(1)} %collective-permute-done.9.right, f32[80,128]{1,0:T(8,128)S(1)} %collective-permute-done.10.left2, ...), custom_call_target="tpu_custom_call" | custom-call | flops 400000000 | bytes 4000000 | tf_op jit(solution)/shard_map/upper/pallas_call | solution.py:484
  (15 shorter events, 0.0 us)
Async XLA Ops:
  0.0 1.2 %copy-start = (f32[32,32,256]{2,1,0:T(8,128)S(1)}, f32[32,32,256]{2,1,0:T(8,128)}, u32[]{:S(2)}) copy-start(f32[32,32,256]{2,1,0:T(8,128)} %c.3) | copy-start | bytes 3145732
  2.2 11.1 %copy-start.2 = (f32[3,3,21]{2,1,0:T(4,128)S(1)}, f32[3,3,21]{2,1,0:T(4,128)}, u32[]{:S(2)}) copy-start(f32[3,3,21]{2,1,0:T(4,128)} %taps.4) | copy-start | bytes 2272
  2.3 14.1 %collective-permute-start = (f32[288,128]{1,0:T(8,128)S(1)}, f32[288,128]{1,0:T(8,128)S(1)}, u32[]{:S(2)}, u32[]{:S(2)}) collective-permute-start(f32[288,128]{1,0:T(8,128)S(1)} %get-tuple-element.52), channel_id=1, source_target_pairs={{0,16},{16,32},{32,48},{48,64},{64,80},{80,96},{96,112},{112,128},... | collective-permute-start | bytes 442376 | tf_op jit(solution)/shard_map/ppermute | solution.py:420
  6.2 11.2 %collective-permute-start.1 = (f32[288,128]{1,0:T(8,128)S(1)}, f32[288,128]{1,0:T(8,128)S(1)}, u32[]{:S(2)}, u32[]{:S(2)}) collective-permute-start(f32[288,128]{1,0:T(8,128)S(1)} %get-tuple-element.53), channel_id=1, source_target_pairs={{0,240},{16,0},{32,16},{48,32},{64,48},{80,64},{96,80},{112,96},{1... | collective-permute-start | bytes 442376 | tf_op jit(solution)/shard_map/ppermute | solution.py:420
  11.7 15.5 %collective-permute-start.4 = (f32[328,256]{1,0:T(8,128)S(1)}, f32[328,256]{1,0:T(8,128)S(1)}, u32[]{:S(2)}, u32[]{:S(2)}) collective-permute-start(f32[328,256]{1,0:T(8,128)S(1)} %get-tuple-element.59), channel_id=1, source_target_pairs={{0,1},{1,2},{2,3},{3,4},{4,5},{5,6},{6,7},{7,8},{8,9},{9,10},{10,1... | collective-permute-start | bytes 1007624 | tf_op jit(solution)/shard_map/ppermute | solution.py:420
  13.3 22.6 %collective-permute-start.5 = (f32[328,256]{1,0:T(8,128)S(1)}, f32[328,256]{1,0:T(8,128)S(1)}, u32[]{:S(2)}, u32[]{:S(2)}) collective-permute-start(f32[328,256]{1,0:T(8,128)S(1)} %get-tuple-element.60), channel_id=1, source_target_pairs={{0,15},{1,0},{2,1},{3,2},{4,3},{5,4},{6,5},{7,6},{8,7},{9,8},{10,9... | collective-permute-start | bytes 1007624 | tf_op jit(solution)/shard_map/ppermute | solution.py:420
  17.4 29.4 %collective-permute-start.2 = (f32[344,256]{1,0:T(8,128)S(1)}, f32[344,256]{1,0:T(8,128)S(1)}, u32[]{:S(2)}, u32[]{:S(2)}) collective-permute-start(f32[344,256]{1,0:T(8,128)S(1)} %get-tuple-element.57), channel_id=1, source_target_pairs={{0,16},{16,32},{32,48},{48,64},{64,80},{80,96},{96,112},{112,128},... | collective-permute-start | bytes 1056776 | tf_op jit(solution)/shard_map/ppermute | solution.py:420
  20.7 15.2 %copy-start.1 = (f32[32,32,256]{2,1,0:T(8,128)S(1)}, f32[32,32,256]{2,1,0:T(8,128)}, u32[]{:S(2)}) copy-start(f32[32,32,256]{2,1,0:T(8,128)} %c.3) | copy-start | bytes 3145732
  20.7 26.1 %collective-permute-start.3 = (f32[344,256]{1,0:T(8,128)S(1)}, f32[344,256]{1,0:T(8,128)S(1)}, u32[]{:S(2)}, u32[]{:S(2)}) collective-permute-start(f32[344,256]{1,0:T(8,128)S(1)} %get-tuple-element.58), channel_id=1, source_target_pairs={{0,240},{16,0},{32,16},{48,32},{64,48},{80,64},{96,80},{112,96},{1... | collective-permute-start | bytes 1056776 | tf_op jit(solution)/shard_map/ppermute | solution.py:420
  23.3 19.9 %collective-permute-start.6 = (f32[456,128]{1,0:T(8,128)S(1)}, f32[456,128]{1,0:T(8,128)S(1)}, u32[]{:S(2)}, u32[]{:S(2)}) collective-permute-start(f32[456,128]{1,0:T(8,128)S(1)} %get-tuple-element.65), channel_id=1, source_target_pairs={{0,1},{1,2},{2,3},{3,4},{4,5},{5,6},{6,7},{7,8},{8,9},{9,10},{10,1... | collective-permute-start | bytes 700424 | tf_op jit(solution)/shard_map/ppermute | solution.py:420
  27.2 19.6 %collective-permute-start.7 = (f32[456,128]{1,0:T(8,128)S(1)}, f32[456,128]{1,0:T(8,128)S(1)}, u32[]{:S(2)}, u32[]{:S(2)}) collective-permute-start(f32[456,128]{1,0:T(8,128)S(1)} %get-tuple-element.66), channel_id=1, source_target_pairs={{0,15},{1,0},{2,1},{3,2},{4,3},{5,4},{6,5},{7,6},{8,7},{9,8},{10,9... | collective-permute-start | bytes 700424 | tf_op jit(solution)/shard_map/ppermute | solution.py:420
  46.9 8.8 %collective-permute-start.8 = (f32[296,256]{1,0:T(8,128)S(1)}, f32[296,256]{1,0:T(8,128)S(1)}, u32[]{:S(2)}, u32[]{:S(2)}) collective-permute-start(f32[296,256]{1,0:T(8,128)S(1)} %get-tuple-element.74), channel_id=1, source_target_pairs={{0,1},{1,2},{2,3},{3,4},{4,5},{5,6},{6,7},{7,8},{8,9},{9,10},{10,1... | collective-permute-start | bytes 909320 | tf_op jit(solution)/shard_map/ppermute | solution.py:420
  47.2 9.8 %collective-permute-start.9 = (f32[296,256]{1,0:T(8,128)S(1)}, f32[296,256]{1,0:T(8,128)S(1)}, u32[]{:S(2)}, u32[]{:S(2)}) collective-permute-start(f32[296,256]{1,0:T(8,128)S(1)} %get-tuple-element.75), channel_id=1, source_target_pairs={{0,15},{1,0},{2,1},{3,2},{4,3},{5,4},{6,5},{7,6},{8,7},{9,8},{10,9... | collective-permute-start | bytes 909320 | tf_op jit(solution)/shard_map/ppermute | solution.py:420
  49.0 11.0 %collective-permute-start.10 = (f32[80,128]{1,0:T(8,128)S(1)}, f32[80,128]{1,0:T(8,128)S(1)}, u32[]{:S(2)}, u32[]{:S(2)}) collective-permute-start(f32[80,128]{1,0:T(8,128)S(1)} %get-tuple-element.84), channel_id=1, source_target_pairs={{0,2},{1,3},{2,4},{3,5},{4,6},{5,7},{6,8},{7,9},{8,10},{9,11},{10,... | collective-permute-start | bytes 122888 | tf_op jit(solution)/shard_map/ppermute | solution.py:420
  49.0 11.0 %collective-permute-start.11 = (f32[80,128]{1,0:T(8,128)S(1)}, f32[80,128]{1,0:T(8,128)S(1)}, u32[]{:S(2)}, u32[]{:S(2)}) collective-permute-start(f32[80,128]{1,0:T(8,128)S(1)} %get-tuple-element.85), channel_id=1, source_target_pairs={{0,14},{1,15},{2,0},{3,1},{4,2},{5,3},{6,4},{7,5},{8,6},{9,7},{10,... | collective-permute-start | bytes 122888 | tf_op jit(solution)/shard_map/ppermute | solution.py:420

commit v12 on v11

--- a/solution.py
+++ b/solution.py
@@ -307,10 +307,10 @@
         fine[2 * a] = 0.75 * mid[a + 1] + 0.125 * (mid[a] + mid[a + 2])
         fine[2 * a + 1] = 0.5 * (mid[a + 1] + mid[a + 2])
     copies = []
-    for q in range(4):
-        rows = pl.ds(8 * q, 8)
-        high, low = halves(fine[rows].reshape(256, 128))
-        done[rows] = direct[rows] + dot(jnp.concatenate([high, low], 1), up1[...]).reshape(8, 32, 256)
+    for q in range(8):
+        rows = pl.ds(4 * q, 4)
+        high, low = halves(fine[rows].reshape(128, 128))
+        done[rows] = direct[rows] + dot(jnp.concatenate([high, low], 1), up1[...]).reshape(4, 32, 256)
         copies.append(pltpu.make_async_copy(done.at[rows], out.at[rows], sems.at[q]))
         copies[q].start()
     for copy in copies:
@@ -485,7 +485,7 @@
         upper_kernel, [((32, 32, 256), F32)],
         [((16, 48, 128), F32), ((32, 96, 128), F32), ((11, 96, 128), F32), ((18, 32, 128), F32),
          ((32, 32, 128), F32), ((32, 32, 256), F32)],
-        1, 11, 4 * 10**8, 4 * 10**6, name="upper", sems=4, far=True,
+        1, 11, 4 * 10**8, 4 * 10**6, name="upper", sems=8, far=True,
     )(taps, l2x, left, right, left2, right2, y2, z2, up1, mid, direct)
     return result
 

time: 63.1 us -> 63.1 us (level)
  no operation moved by 1% of the time
where the time goes in v12:
time: 63.1 us; the launch traced here: 63 us
  starting transfers between devices  35 us (55%)
  Pallas kernels  20.3 us (32%)
  waiting for transfers between devices  6.21 us (10%)
  local copies, waits for them, and re-layouts  1.23 us (2%)
    ppermute x12, starting transfers between devices, shift(): return lax.ppermute(x, axis, [(i, (i + by) % n) for i in range(n)])  35 us
    pallas_call x1, Pallas kernels, body(): call(inner_kernel, [((32, 32, 256), F32)], [((32, 96, 256), F32), ((256,...  7.25 us
    ppermute x12, waiting for transfers between devices, shift(): return lax.ppermute(x, axis, [(i, (i + by) % n) for i in range(n)])  6.21 us
    pallas_call x1, Pallas kernels, body(): call(fine_level_kernel, [((18, 32, 128), F32)], [((38, 48, 128), F32), ((...  3.19 us
    pallas_call x1, Pallas kernels, body(): call(matrices_kernel, [((96, 192), BF), ((96, 144), BF), ((96, 144), BF),...  3.02 us
    pallas_call x1, Pallas kernels, body(): call(upper_kernel, [((32, 32, 256), F32)], [((16, 48, 128), F32), ((32, 9...  2.91 us
    pallas_call x1, Pallas kernels, body(): call(finest_kernel, [((32, 32, 256), F32)], [((20, 96, 256), F32), ((640,...  2.6 us
  transfers between devices with their start and end apart: 12, of which 4 were waited for; matrix products, arithmetic and copies ran while one was open for 0% of the time, Pallas kernels for 26%

profile of v12, /device:TPU:1, one launch (start us, length us, event | category | flops | bytes accessed | tf_op | source)
XLA Modules:
  0.0 63.0 jit_solution(10705729335837397005)
XLA Ops:
  0.0 1.2 %copy-done = f32[32,32,256]{2,1,0:T(8,128)S(1)} copy-done((f32[32,32,256]{2,1,0:T(8,128)S(1)}, f32[32,32,256]{2,1,0:T(8,128)}, u32[]{:S(2)}) %copy-start) | copy-done | bytes 1048600
  1.2 1.0 %restrict.1 = (f32[18,24,128]{2,1,0:T(8,128)S(1)}, f32[6,16,128]{2,1,0:T(8,128)S(1)}, f32[288,128]{1,0:T(8,128)S(1)}, f32[288,128]{1,0:T(8,128)S(1)}, f32[320,25...) custom-call(f32[32,32,256]{2,1,0:T(8,128)S(1)} %copy-done), custom_call_target="tpu_custom_call" | custom-call | flops 100000000 | bytes 2000000 | tf_op jit(solution)/shard_map/restrict/pallas_call | solution.py:425
  2.3 3.9 %collective-permute-start = (f32[288,128]{1,0:T(8,128)S(1)}, f32[288,128]{1,0:T(8,128)S(1)}, u32[]{:S(2)}, u32[]{:S(2)}) collective-permute-start(f32[288,128]{1,0:T(8,128)S(1)} %get-tuple-element.52), channel_id=1, source_target_pairs={{0,16},{16,32},{32,48},{48,64},{64,80},{80,96},{96,112},{112,128},... | collective-permute-start | bytes 442376 | tf_op jit(solution)/shard_map/ppermute | solution.py:420
  6.2 5.6 %collective-permute-start.1 = (f32[288,128]{1,0:T(8,128)S(1)}, f32[288,128]{1,0:T(8,128)S(1)}, u32[]{:S(2)}, u32[]{:S(2)}) collective-permute-start(f32[288,128]{1,0:T(8,128)S(1)} %get-tuple-element.53), channel_id=1, source_target_pairs={{0,240},{16,0},{32,16},{48,32},{64,48},{80,64},{96,80},{112,96},{1... | collective-permute-start | bytes 442376 | tf_op jit(solution)/shard_map/ppermute | solution.py:420
  11.7 1.6 %collective-permute-start.4 = (f32[328,256]{1,0:T(8,128)S(1)}, f32[328,256]{1,0:T(8,128)S(1)}, u32[]{:S(2)}, u32[]{:S(2)}) collective-permute-start(f32[328,256]{1,0:T(8,128)S(1)} %get-tuple-element.59), channel_id=1, source_target_pairs={{0,1},{1,2},{2,3},{3,4},{4,5},{5,6},{6,7},{7,8},{8,9},{9,10},{10,1... | collective-permute-start | bytes 1007624 | tf_op jit(solution)/shard_map/ppermute | solution.py:420
  13.3 3.0 %matrices.1 = (bf16[96,192]{1,0:T(8,128)(2,1)S(1)}, bf16[96,144]{1,0:T(8,128)(2,1)S(1)}, bf16[96,144]{1,0:T(8,128)(2,1)S(1)}, bf16[768,256]{1,0:T(8,128)(2,1)S(1...) custom-call(f32[3,3,21]{2,1,0:T(4,128)S(1)} %copy-done.2), custom_call_target="tpu_custom_call" | custom-call | flops 100000000 | bytes 4000000 | tf_op jit(solution)/shard_map/matrices/pallas_call | solution.py:434
  16.3 1.0 %collective-permute-done.1.right = f32[288,128]{1,0:T(8,128)S(1)} collective-permute-done((f32[288,128]{1,0:T(8,128)S(1)}, f32[288,128]{1,0:T(8,128)S(1)}, u32[]{:S(2)}, u32[]{:S(2)}) %collective-permute-start.1) | collective-permute-done | bytes 147488 | tf_op jit(solution)/shard_map/ppermute | solution.py:420
  17.3 0.1 face_x.1
  17.4 3.3 %collective-permute-start.2 = (f32[344,256]{1,0:T(8,128)S(1)}, f32[344,256]{1,0:T(8,128)S(1)}, u32[]{:S(2)}, u32[]{:S(2)}) collective-permute-start(f32[344,256]{1,0:T(8,128)S(1)} %get-tuple-element.57), channel_id=1, source_target_pairs={{0,16},{16,32},{32,48},{48,64},{64,80},{80,96},{96,112},{112,128},... | collective-permute-start | bytes 1056776 | tf_op jit(solution)/shard_map/ppermute | solution.py:420
  20.7 2.5 %collective-permute-start.3 = (f32[344,256]{1,0:T(8,128)S(1)}, f32[344,256]{1,0:T(8,128)S(1)}, u32[]{:S(2)}, u32[]{:S(2)}) collective-permute-start(f32[344,256]{1,0:T(8,128)S(1)} %get-tuple-element.58), channel_id=1, source_target_pairs={{0,240},{16,0},{32,16},{48,32},{64,48},{80,64},{96,80},{112,96},{1... | collective-permute-start | bytes 1056776 | tf_op jit(solution)/shard_map/ppermute | solution.py:420
  23.2 0.1 gather_fine.1
  23.3 3.9 %collective-permute-start.6 = (f32[456,128]{1,0:T(8,128)S(1)}, f32[456,128]{1,0:T(8,128)S(1)}, u32[]{:S(2)}, u32[]{:S(2)}) collective-permute-start(f32[456,128]{1,0:T(8,128)S(1)} %get-tuple-element.65), channel_id=1, source_target_pairs={{0,1},{1,2},{2,3},{3,4},{4,5},{5,6},{6,7},{7,8},{8,9},{9,10},{10,1... | collective-permute-start | bytes 700424 | tf_op jit(solution)/shard_map/ppermute | solution.py:420
  27.2 8.7 %collective-permute-start.7 = (f32[456,128]{1,0:T(8,128)S(1)}, f32[456,128]{1,0:T(8,128)S(1)}, u32[]{:S(2)}, u32[]{:S(2)}) collective-permute-start(f32[456,128]{1,0:T(8,128)S(1)} %get-tuple-element.66), channel_id=1, source_target_pairs={{0,15},{1,0},{2,1},{3,2},{4,3},{5,4},{6,5},{7,6},{8,7},{9,8},{10,9... | collective-permute-start | bytes 700424 | tf_op jit(solution)/shard_map/ppermute | solution.py:420
  35.9 7.2 %inner.1 = f32[32,32,256]{2,1,0:T(8,128)S(1)} custom-call(f32[3,3,21]{2,1,0:T(4,128)S(1)} %copy-done.2, f32[32,32,256]{2,1,0:T(8,128)S(1)} %copy-done.1, f32[328,256]{1,0:T(8,128)S(1)} %collective-permute-done.4.left, f32[328,256]{1,0:T(8,128)S(1)} %collective-permute-done.5.right, bf16[96,192]{1,0:T(8,128)(2,1)S(1)} %get-tuple-element.67.y0, ...), custom_call_target="tpu_custom_call" | custom-call | flops 2000000000 | bytes 6000000 | tf_op jit(solution)/shard_map/inner/pallas_call | solution.py:456
  43.2 3.6 %collective-permute-done.7.right = f32[456,128]{1,0:T(8,128)S(1)} collective-permute-done((f32[456,128]{1,0:T(8,128)S(1)}, f32[456,128]{1,0:T(8,128)S(1)}, u32[]{:S(2)}, u32[]{:S(2)}) %collective-permute-start.7) | collective-permute-done | bytes 233504 | tf_op jit(solution)/shard_map/ppermute | solution.py:420
  46.8 0.1 gather_top.1
  46.9 0.3 collective-permute-start.8
  47.2 1.8 %collective-permute-start.9 = (f32[296,256]{1,0:T(8,128)S(1)}, f32[296,256]{1,0:T(8,128)S(1)}, u32[]{:S(2)}, u32[]{:S(2)}) collective-permute-start(f32[296,256]{1,0:T(8,128)S(1)} %get-tuple-element.75), channel_id=1, source_target_pairs={{0,15},{1,0},{2,1},{3,2},{4,3},{5,4},{6,5},{7,6},{8,7},{9,8},{10,9... | collective-permute-start | bytes 909320 | tf_op jit(solution)/shard_map/ppermute | solution.py:420
  49.0 3.6 %collective-permute-start.11 = (f32[80,128]{1,0:T(8,128)S(1)}, f32[80,128]{1,0:T(8,128)S(1)}, u32[]{:S(2)}, u32[]{:S(2)}) collective-permute-start(f32[80,128]{1,0:T(8,128)S(1)} %get-tuple-element.85), channel_id=1, source_target_pairs={{0,14},{1,15},{2,0},{3,1},{4,2},{5,3},{6,4},{7,5},{8,6},{9,7},{10,... | collective-permute-start | bytes 122888 | tf_op jit(solution)/shard_map/ppermute | solution.py:420
  52.5 3.2 %fine_level.1.mid_in = f32[18,32,128]{2,1,0:T(8,128)S(1)} custom-call(f32[3,3,21]{2,1,0:T(4,128)S(1)} %copy-done.2, f32[38,24,128]{2,1,0:T(8,128)S(1)} %get-tuple-element.77.l1x, f32[456,128]{1,0:T(8,128)S(1)} %collective-permute-done.6.left, f32[456,128]{1,0:T(8,128)S(1)} %collective-permute-done.7.right, bf16[96,144]{1,0:T(8,128)(2,1)S(1)} %get-tuple-element.80.y1, ...), custom_call_target="tpu_custom_call" | custom-call | flops 400000000 | bytes 4000000 | tf_op jit(solution)/shard_map/fine_level/pallas_call | solution.py:473
  55.7 1.2 %collective-permute-done.9.right = f32[296,256]{1,0:T(8,128)S(1)} collective-permute-done((f32[296,256]{1,0:T(8,128)S(1)}, f32[296,256]{1,0:T(8,128)S(1)}, u32[]{:S(2)}, u32[]{:S(2)}) %collective-permute-start.9) | collective-permute-done | bytes 303136 | tf_op jit(solution)/shard_map/ppermute | solution.py:420
  57.0 2.6 %finest.1.direct = f32[32,32,256]{2,1,0:T(8,128)S(1)} custom-call(f32[3,3,21]{2,1,0:T(4,128)S(1)} %copy-done.2, f32[344,256]{1,0:T(8,128)S(1)} %collective-permute-done.2.before, f32[344,256]{1,0:T(8,128)S(1)} %collective-permute-done.3.after, f32[296,256]{1,0:T(8,128)S(1)} %collective-permute-done.8.left, f32[296,256]{1,0:T(8,128)S(1)} %collective-permute-done.9.right, ...), custom_call_target="tpu_custom_call" | custom-call | flops 2000000000 | bytes 6000000 | tf_op jit(solution)/shard_map/finest/pallas_call | solution.py:479
  59.6 0.3 collective-permute-done.10.left2
  59.9 2.9 %upper.1 = f32[32,32,256]{2,1,0:T(8,128)} custom-call(f32[3,3,21]{2,1,0:T(4,128)S(1)} %copy-done.2, f32[16,16,128]{2,1,0:T(8,128)S(1)} %get-tuple-element.73.l2x, f32[296,256]{1,0:T(8,128)S(1)} %collective-permute-done.8.left, f32[296,256]{1,0:T(8,128)S(1)} %collective-permute-done.9.right, f32[80,128]{1,0:T(8,128)S(1)} %collective-permute-done.10.left2, ...), custom_call_target="tpu_custom_call" | custom-call | flops 400000000 | bytes 4000000 | tf_op jit(solution)/shard_map/upper/pallas_call | solution.py:484
  (15 shorter events, 0.0 us)
Async XLA Ops:
  0.0 1.2 %copy-start = (f32[32,32,256]{2,1,0:T(8,128)S(1)}, f32[32,32,256]{2,1,0:T(8,128)}, u32[]{:S(2)}) copy-start(f32[32,32,256]{2,1,0:T(8,128)} %c.3) | copy-start | bytes 3145732
  2.2 11.1 %copy-start.2 = (f32[3,3,21]{2,1,0:T(4,128)S(1)}, f32[3,3,21]{2,1,0:T(4,128)}, u32[]{:S(2)}) copy-start(f32[3,3,21]{2,1,0:T(4,128)} %taps.4) | copy-start | bytes 2272
  2.3 14.1 %collective-permute-start = (f32[288,128]{1,0:T(8,128)S(1)}, f32[288,128]{1,0:T(8,128)S(1)}, u32[]{:S(2)}, u32[]{:S(2)}) collective-permute-start(f32[288,128]{1,0:T(8,128)S(1)} %get-tuple-element.52), channel_id=1, source_target_pairs={{0,16},{16,32},{32,48},{48,64},{64,80},{80,96},{96,112},{112,128},... | collective-permute-start | bytes 442376 | tf_op jit(solution)/shard_map/ppermute | solution.py:420
  6.2 11.2 %collective-permute-start.1 = (f32[288,128]{1,0:T(8,128)S(1)}, f32[288,128]{1,0:T(8,128)S(1)}, u32[]{:S(2)}, u32[]{:S(2)}) collective-permute-start(f32[288,128]{1,0:T(8,128)S(1)} %get-tuple-element.53), channel_id=1, source_target_pairs={{0,240},{16,0},{32,16},{48,32},{64,48},{80,64},{96,80},{112,96},{1... | collective-permute-start | bytes 442376 | tf_op jit(solution)/shard_map/ppermute | solution.py:420
  11.7 15.5 %collective-permute-start.4 = (f32[328,256]{1,0:T(8,128)S(1)}, f32[328,256]{1,0:T(8,128)S(1)}, u32[]{:S(2)}, u32[]{:S(2)}) collective-permute-start(f32[328,256]{1,0:T(8,128)S(1)} %get-tuple-element.59), channel_id=1, source_target_pairs={{0,1},{1,2},{2,3},{3,4},{4,5},{5,6},{6,7},{7,8},{8,9},{9,10},{10,1... | collective-permute-start | bytes 1007624 | tf_op jit(solution)/shard_map/ppermute | solution.py:420
  13.3 22.6 %collective-permute-start.5 = (f32[328,256]{1,0:T(8,128)S(1)}, f32[328,256]{1,0:T(8,128)S(1)}, u32[]{:S(2)}, u32[]{:S(2)}) collective-permute-start(f32[328,256]{1,0:T(8,128)S(1)} %get-tuple-element.60), channel_id=1, source_target_pairs={{0,15},{1,0},{2,1},{3,2},{4,3},{5,4},{6,5},{7,6},{8,7},{9,8},{10,9... | collective-permute-start | bytes 1007624 | tf_op jit(solution)/shard_map/ppermute | solution.py:420
  17.4 29.4 %collective-permute-start.2 = (f32[344,256]{1,0:T(8,128)S(1)}, f32[344,256]{1,0:T(8,128)S(1)}, u32[]{:S(2)}, u32[]{:S(2)}) collective-permute-start(f32[344,256]{1,0:T(8,128)S(1)} %get-tuple-element.57), channel_id=1, source_target_pairs={{0,16},{16,32},{32,48},{48,64},{64,80},{80,96},{96,112},{112,128},... | collective-permute-start | bytes 1056776 | tf_op jit(solution)/shard_map/ppermute | solution.py:420
  20.7 15.2 %copy-start.1 = (f32[32,32,256]{2,1,0:T(8,128)S(1)}, f32[32,32,256]{2,1,0:T(8,128)}, u32[]{:S(2)}) copy-start(f32[32,32,256]{2,1,0:T(8,128)} %c.3) | copy-start | bytes 3145732
  20.7 26.1 %collective-permute-start.3 = (f32[344,256]{1,0:T(8,128)S(1)}, f32[344,256]{1,0:T(8,128)S(1)}, u32[]{:S(2)}, u32[]{:S(2)}) collective-permute-start(f32[344,256]{1,0:T(8,128)S(1)} %get-tuple-element.58), channel_id=1, source_target_pairs={{0,240},{16,0},{32,16},{48,32},{64,48},{80,64},{96,80},{112,96},{1... | collective-permute-start | bytes 1056776 | tf_op jit(solution)/shard_map/ppermute | solution.py:420
  23.3 19.9 %collective-permute-start.6 = (f32[456,128]{1,0:T(8,128)S(1)}, f32[456,128]{1,0:T(8,128)S(1)}, u32[]{:S(2)}, u32[]{:S(2)}) collective-permute-start(f32[456,128]{1,0:T(8,128)S(1)} %get-tuple-element.65), channel_id=1, source_target_pairs={{0,1},{1,2},{2,3},{3,4},{4,5},{5,6},{6,7},{7,8},{8,9},{9,10},{10,1... | collective-permute-start | bytes 700424 | tf_op jit(solution)/shard_map/ppermute | solution.py:420
  27.2 19.6 %collective-permute-start.7 = (f32[456,128]{1,0:T(8,128)S(1)}, f32[456,128]{1,0:T(8,128)S(1)}, u32[]{:S(2)}, u32[]{:S(2)}) collective-permute-start(f32[456,128]{1,0:T(8,128)S(1)} %get-tuple-element.66), channel_id=1, source_target_pairs={{0,15},{1,0},{2,1},{3,2},{4,3},{5,4},{6,5},{7,6},{8,7},{9,8},{10,9... | collective-permute-start | bytes 700424 | tf_op jit(solution)/shard_map/ppermute | solution.py:420
  46.9 8.8 %collective-permute-start.8 = (f32[296,256]{1,0:T(8,128)S(1)}, f32[296,256]{1,0:T(8,128)S(1)}, u32[]{:S(2)}, u32[]{:S(2)}) collective-permute-start(f32[296,256]{1,0:T(8,128)S(1)} %get-tuple-element.74), channel_id=1, source_target_pairs={{0,1},{1,2},{2,3},{3,4},{4,5},{5,6},{6,7},{7,8},{8,9},{9,10},{10,1... | collective-permute-start | bytes 909320 | tf_op jit(solution)/shard_map/ppermute | solution.py:420
  47.2 9.8 %collective-permute-start.9 = (f32[296,256]{1,0:T(8,128)S(1)}, f32[296,256]{1,0:T(8,128)S(1)}, u32[]{:S(2)}, u32[]{:S(2)}) collective-permute-start(f32[296,256]{1,0:T(8,128)S(1)} %get-tuple-element.75), channel_id=1, source_target_pairs={{0,15},{1,0},{2,1},{3,2},{4,3},{5,4},{6,5},{7,6},{8,7},{9,8},{10,9... | collective-permute-start | bytes 909320 | tf_op jit(solution)/shard_map/ppermute | solution.py:420
  49.0 11.0 %collective-permute-start.10 = (f32[80,128]{1,0:T(8,128)S(1)}, f32[80,128]{1,0:T(8,128)S(1)}, u32[]{:S(2)}, u32[]{:S(2)}) collective-permute-start(f32[80,128]{1,0:T(8,128)S(1)} %get-tuple-element.84), channel_id=1, source_target_pairs={{0,2},{1,3},{2,4},{3,5},{4,6},{5,7},{6,8},{7,9},{8,10},{9,11},{10,... | collective-permute-start | bytes 122888 | tf_op jit(solution)/shard_map/ppermute | solution.py:420
  49.0 11.0 %collective-permute-start.11 = (f32[80,128]{1,0:T(8,128)S(1)}, f32[80,128]{1,0:T(8,128)S(1)}, u32[]{:S(2)}, u32[]{:S(2)}) collective-permute-start(f32[80,128]{1,0:T(8,128)S(1)} %get-tuple-element.85), channel_id=1, source_target_pairs={{0,14},{1,15},{2,0},{3,1},{4,2},{5,3},{6,4},{7,5},{8,6},{9,7},{10,... | collective-permute-start | bytes 122888 | tf_op jit(solution)/shard_map/ppermute | solution.py:420
